TPU v7x, 512 devices: a whole 4x4x16 slice. The times are simulated.
512 devices in a mesh: expert: 8 (over z_lo, core), row: 4 (over x), col: 16 (over y, z_hi).
Axes of the slice: x: 4, y: 4, z: 16 (z_hi: 4, z_lo: 4; z = z_hi * 4 + z_lo), core: 2. Of those that a mesh axis runs over, the one named last changes fastest.
Arguments:
- tokens: bfloat16 [8, 1024, 4096], P('expert', 'col', 'row'), may hold values from -6 to 6
- routes: int32 [8, 2], replicated, may hold values from 0 to 7, all different within a row; in each aligned block of 8 rows (0 to 7, 8 to 15, ...) at most 2 rows name the same one
- route_gates: float32 [8, 2], replicated, may hold values from 0.1 to 1
- w_in: bfloat16 [8, 4096, 2, 7168], P('expert', 'row', None, 'col'), may hold values from -0.09375 to 0.09375
- w_down: bfloat16 [8, 7168, 4096], P('expert', 'col', 'row'), may hold values from -0.0625 to 0.0625
Outputs:
- mixed: bfloat16 [8, 1024, 4096], P('expert', 'col', 'row')
Inputs may be any that keep to these rules, and one draw needn't show every extreme that they name: `routes`: each row names two different experts; every expert is named by exactly 2 rows.
All inputs are finite; a program needn't handle non-finite values.
Results may differ from a plain program's by a relative error of at most 0.03.
Values may be sent and summed in bfloat16 or wider, within the bound.
No kernel may reach another device: no remote copies, remote signals or barrier semaphores. Data moves between devices by JAX's collectives and lax.ppermute only.
A program may use at most 128 MiB of HBM per device.

v0:
```python
import jax
import jax.numpy as jnp
from jax import lax
from jax.sharding import PartitionSpec as P

CAP_MOST = 2


def on_device(tokens, routes, route_gates, w_in, w_down):
    experts = lax.axis_size("expert")
    owner = lax.axis_index("expert")
    local_seqs = tokens.shape[0]
    total_seqs = routes.shape[0]
    capacity = min(CAP_MOST, total_seqs)
    labels = jnp.arange(experts, dtype=jnp.int32)
    matches = routes[:, :, None] == labels[None, None, :]
    hit = jnp.sum(matches.astype(jnp.int32), axis=1)
    slot = jnp.cumsum(hit, axis=0) - hit
    taken = lax.dynamic_index_in_dim(hit, owner, 1, keepdims=False)
    where = lax.dynamic_index_in_dim(slot, owner, 1, keepdims=False)
    places = jnp.arange(capacity, dtype=jnp.int32)
    select = ((where[:, None] == places[None, :]) & (taken[:, None] == 1)).astype(jnp.bfloat16)
    local_hit = lax.dynamic_slice_in_dim(hit, owner * local_seqs, local_seqs, 0)
    keep = jnp.transpose(local_hit).astype(jnp.bfloat16)[:, :, None, None]
    arrived = lax.all_to_all(keep * tokens[None], "expert", split_axis=0, concat_axis=0, tiled=True)
    arrived = arrived.reshape(total_seqs, tokens.shape[1], tokens.shape[2])
    packed = jnp.einsum("sk,spd->pkd", select, arrived, preferred_element_type=jnp.float32).astype(
        jnp.bfloat16
    )
    packed = lax.all_gather(packed, "col", axis=0, tiled=True)
    rows = packed.reshape(packed.shape[0] * capacity, packed.shape[2])
    ff_cols = w_down.shape[1]
    w_both = w_in[0].reshape(w_in.shape[1], 2 * ff_cols)
    w_out = w_down[0]
    sums = lax.psum(
        jnp.dot(rows, w_both, preferred_element_type=jnp.float32).astype(jnp.bfloat16), "row"
    ).astype(jnp.float32)
    hidden = (jax.nn.silu(sums[:, :ff_cols]) * sums[:, ff_cols:]).astype(jnp.bfloat16)
    result = lax.psum_scatter(
        jnp.dot(hidden, w_out, preferred_element_type=jnp.float32).astype(jnp.bfloat16),
        "col",
        scatter_dimension=0,
        tiled=True,
    ).astype(jnp.float32)
    outputs = result.astype(jnp.bfloat16).reshape(
        result.shape[0] // capacity, capacity, result.shape[1]
    )
    going = jnp.einsum("sk,pkd->spd", select, outputs, preferred_element_type=jnp.float32).astype(
        jnp.bfloat16
    )
    going = going.reshape(experts, local_seqs, going.shape[1], going.shape[2])
    returned = lax.all_to_all(going, "expert", split_axis=0, concat_axis=0, tiled=True)
    weight_table = jnp.sum(route_gates[:, :, None] * matches.astype(jnp.float32), axis=1)
    local_weights = lax.dynamic_slice_in_dim(weight_table, owner * local_seqs, local_seqs, 0)
    scaled = jnp.transpose(local_weights)[:, :, None, None] * returned.astype(jnp.float32)
    return jnp.sum(scaled, axis=0).astype(jnp.bfloat16)


def solution(mesh):
    return jax.shard_map(
        on_device,
        mesh=mesh,
        in_specs=(
            P("expert", "col", "row"),
            P(),
            P(),
            P("expert", "row", None, "col"),
            P("expert", "col", "row"),
        ),
        out_specs=P("expert", "col", "row"),
        check_vma=False,
    )
```

profile of v0, /device:TPU:1, one launch (start us, length us, event | category | flops | bytes accessed | tf_op | source)
XLA Modules:
  0.0 497.8 jit_solution(2947054259841379689)
XLA Ops:
  6.5 0.0 copy-start
  6.5 0.9 convert_reduce_fusion
  7.4 2.0 broadcast_multiply_fusion
  9.5 10.3 %all-to-all-start = ((bf16[8,1,64,1024]{3,2,1,0:T(8,128)(2,1)}), bf16[8,1,64,1024]{3,2,1,0:T(8,128)(2,1)S(1)}, u32[]{:S(2)}, u32[]{:S(2)}) async-start(bf16[8,1,64,1024]{3,2,1,0:T(8,128)(2,1)} %broadcast_multiply_fusion), calls=%async_computation | async-start | bytes 2097152 | tf_op jit(solution)/shard_map/all_to_all | solution.py:25
  19.8 0.0 all-gather.2.cloned.1.call-start
  19.8 0.2 dynamic-slice_reduce_fusion
  20.0 0.2 fusion.7
  20.2 25.3 %all-to-all-done = bf16[8,1,64,1024]{3,2,1,0:T(8,128)(2,1)S(1)} async-done(((bf16[8,1,64,1024]{3,2,1,0:T(8,128)(2,1)}), bf16[8,1,64,1024]{3,2,1,0:T(8,128)(2,1)S(1)}, u32[]{:S(2)}, u32[]{:S(2)}) %all-to-all-start) | async-done | bytes 1048608 | tf_op jit(solution)/shard_map/all_to_all | solution.py:25
  45.6 1.4 fusion.3
  47.0 0.0 all-gather.2.cloned.1.call-update
  47.0 0.0 all-reduce.2.cloned.1.call-start
  47.1 132.9 %all-gather.2.cloned.1.call-done = bf16[1024,2,1024]{2,1,0:T(2,128)(2,1)} async-done(((bf16[64,2,1024]{2,1,0:T(2,128)(2,1)}), bf16[1024,2,1024]{2,1,0:T(2,128)(2,1)}) %all-gather.2.cloned.1.call-update) | async-done | bytes 4194320 | tf_op jit(solution)/shard_map/all_gather | solution.py:30
  179.9 7.2 %reshape.46 = bf16[2048,1024]{1,0:T(8,128)(2,1)} reshape(bf16[1024,2,1024]{2,1,0:T(2,128)(2,1)} %all-gather.2.cloned.1.call-done) | data formatting | bytes 8388608 | tf_op jit(solution)/shard_map/reshape | solution.py:31
  187.1 0.0 copy-done
  187.1 8.2 %convolution_convert_fusion.1 = bf16[2048,896]{1,0:T(8,128)(2,1)} fusion(bf16[2048,1024]{1,0:T(8,128)(2,1)} %reshape.46, bf16[1024,896]{0,1:T(8,128)(2,1)S(1)} %bitcast.27), kind=kOutput, calls=%fused_computation.3 | convolution fusion | flops 3759931392 | bytes 9699328 | tf_op jit(solution)/shard_map/dot_general | solution.py:36
  195.3 0.0 all-reduce.2.cloned.1.call-update
  195.3 0.0 copy-start.3
  195.3 0.0 reduce-scatter.2.cloned.1.call-start
  195.4 95.9 %all-reduce.2.cloned.1.call-done = bf16[2048,896]{1,0:T(8,128)(2,1)} async-done(((bf16[2048,896]{1,0:T(8,128)(2,1)}), bf16[2048,896]{1,0:T(8,128)(2,1)}) %all-reduce.2.cloned.1.call-update) | async-done | bytes 3670032 | tf_op jit(solution)/shard_map/psum | solution.py:35
  291.3 2.5 convert_element_type.63
  293.8 0.0 copy-done.3
  293.8 4.7 convolution_convert_fusion
  298.5 0.0 copy-start.1
  298.5 0.0 copy-start.2
  298.5 0.0 reduce-scatter.2.cloned.1.call-update
  298.5 158.0 %reduce-scatter.2.cloned.1.call-done = bf16[128,1024]{1,0:T(8,128)(2,1)} async-done(((bf16[2048,1024]{1,0:T(8,128)(2,1)}), bf16[128,1024]{1,0:T(8,128)(2,1)}) %reduce-scatter.2.cloned.1.call-update) | async-done | bytes 262160 | tf_op jit(solution)/shard_map/reduce_scatter | solution.py:39
  456.5 1.0 reshape.47
  457.6 0.5 fusion.2
  458.1 1.6 copy.15
  459.7 4.9 all-to-all-start.1
  464.6 0.0 copy-done.1
  464.6 0.0 copy-done.2
  464.6 0.1 select_reduce_fusion
  464.7 25.7 %all-to-all-done.1 = bf16[8,1,64,1024]{3,2,1,0:T(8,128)(2,1)S(1)} async-done(((bf16[8,1,64,1024]{3,2,1,0:T(8,128)(2,1)}), bf16[8,1,64,1024]{3,2,1,0:T(8,128)(2,1)S(1)}, u32[]{:S(2)}, u32[]{:S(2)}) %all-to-all-start.1) | async-done | bytes 1048608 | tf_op jit(solution)/shard_map/all_to_all | solution.py:52
  490.3 0.9 multiply_reduce_fusion
  (4 shorter events, 0.0 us)
Async XLA Ops:
  6.5 180.6 %copy-start = (bf16[1,1024,2,448]{1,3,2,0:T(8,128)(2,1)S(1)}, bf16[1,1024,2,448]{1,3,2,0:T(8,128)(2,1)}, u32[]{:S(2)}) copy-start(bf16[1,1024,2,448]{1,3,2,0:T(8,128)(2,1)} %param.8) | copy-start | bytes 5505028
  9.5 36.1 %all-to-all-start = ((bf16[8,1,64,1024]{3,2,1,0:T(8,128)(2,1)}), bf16[8,1,64,1024]{3,2,1,0:T(8,128)(2,1)S(1)}, u32[]{:S(2)}, u32[]{:S(2)}) async-start(bf16[8,1,64,1024]{3,2,1,0:T(8,128)(2,1)} %broadcast_multiply_fusion), calls=%async_computation | async-start | bytes 2097152 | tf_op jit(solution)/shard_map/all_to_all | solution.py:25
  19.8 160.1 %all-gather.2.cloned.1.call-start = ((), (), s32[]{:S(2)}) async-start(), calls=%async_computation.3 | async-start | bytes 4456448 | tf_op jit(solution)/shard_map/all_gather | solution.py:30
  47.0 244.3 %all-reduce.2.cloned.1.call-start = ((), (), s32[]{:S(2)}) async-start(), calls=%async_computation.4 | async-start | bytes 7340032 | tf_op jit(solution)/shard_map/psum | solution.py:35
  195.3 98.5 %copy-start.3 = (bf16[1,448,1024]{2,1,0:T(8,128)(2,1)S(1)}, bf16[1,448,1024]{2,1,0:T(8,128)(2,1)}, u32[]{:S(2)}) copy-start(bf16[1,448,1024]{2,1,0:T(8,128)(2,1)} %param.9) | copy-start | bytes 2752516
  195.3 261.2 %reduce-scatter.2.cloned.1.call-start = ((), (), s32[]{:S(2)}) async-start(), calls=%async_computation.5 | async-start | bytes 4456448 | tf_op jit(solution)/shard_map/reduce_scatter | solution.py:39
  298.5 166.1 %copy-start.1 = (s32[8,2]{0,1:T(2,128)S(1)}, s32[8,2]{0,1:T(2,128)}, u32[]{:S(2)}) copy-start(s32[8,2]{0,1:T(2,128)} %param.6) | copy-start | bytes 196
  298.5 166.1 %copy-start.2 = (f32[8,2]{0,1:T(2,128)S(1)}, f32[8,2]{0,1:T(2,128)}, u32[]{:S(2)}) copy-start(f32[8,2]{0,1:T(2,128)} %param.7) | copy-start | bytes 196
  459.7 30.7 %all-to-all-start.1 = ((bf16[8,1,64,1024]{3,2,1,0:T(8,128)(2,1)}), bf16[8,1,64,1024]{3,2,1,0:T(8,128)(2,1)S(1)}, u32[]{:S(2)}, u32[]{:S(2)}) async-start(bf16[8,1,64,1024]{3,2,1,0:T(8,128)(2,1)} %copy.15), calls=%async_computation.2 | async-start | bytes 2097152 | tf_op jit(solution)/shard_map/all_to_all | solution.py:52
Sparse Core Ops, SparseCore 0:
  47.1 132.7 all-gather.1
  195.4 95.7 all-reduce.1
  298.6 157.8 reduce-scatter.1
where the time goes:
time: 498 us
  waiting for transfers between devices  438 us (88%)
  starting transfers between devices  15.3 us (3%)
  matrix products  14.8 us (3%)
  between operations  13.2 us (3%)
  local copies, waits for them, and re-layouts  10 us (2%)
  other arithmetic  6.65 us (1%)
    reduce_scatter x1, waiting for transfers between devices, on_device(): lax.psum_scatter(jnp.dot(hidden, w_out, preferred_element_type=jnp.float3...  158 us
    all_gather x1, waiting for transfers between devices, on_device(): packed = lax.all_gather(packed, 'col', axis=0, tiled=True)  133 us
    psum x1, waiting for transfers between devices, on_device(): lax.psum(jnp.dot(rows, w_both, preferred_element_type=jnp.float32).astype...  95.9 us
    all_to_all x1, waiting for transfers between devices, on_device(): lax.all_to_all(going, 'expert', split_axis=0, concat_axis=0, tiled=True)  25.7 us
    all_to_all x1, waiting for transfers between devices, on_device(): lax.all_to_all(keep * tokens[None], 'expert', split_axis=0, concat_axis=0...  25.3 us
    all_to_all x1, starting transfers between devices, on_device(): lax.all_to_all(keep * tokens[None], 'expert', split_axis=0, concat_axis=0...  10.3 us
  transfers between devices with their start and end apart: 5, of which 5 were waited for; matrix products, arithmetic and copies ran while one was open for 0% of the time, Pallas kernels for 0%

commit v1 on v0

v1 whole, which is shorter than its diff:
```python
import jax
import jax.numpy as jnp
from jax import lax
from jax.sharding import Mesh, PartitionSpec as P


def shift(a, axis, by):
    n = lax.axis_size(axis)
    return lax.ppermute(a, axis, [(i, (i + by) % n) for i in range(n)])


def ring_gather(a, axis):
    half = a.shape[0] // 2
    below = shift(a, axis, 1)
    above = shift(a, axis, -1)
    low = shift(below[:half], axis, 1)
    high = shift(above[half:], axis, -1)
    return a, above, jnp.concatenate([low, high]), below


def ring_scatter(parts, axis):
    me, above, far, below = parts
    half = far.shape[0] // 2
    wide = jnp.float32
    up = shift(far[:half].astype(jnp.bfloat16), axis, 1)
    down = shift(far[half:].astype(jnp.bfloat16), axis, -1)
    above = jnp.concatenate([above[:half].astype(wide) + up.astype(wide), above[half:].astype(wide)])
    below = jnp.concatenate([below[:half].astype(wide), below[half:].astype(wide) + down.astype(wide)])
    up = shift(above.astype(jnp.bfloat16), axis, 1)
    down = shift(below.astype(jnp.bfloat16), axis, -1)
    return me.astype(wide) + up.astype(wide) + down.astype(wide)


def on_device(tokens, routes, route_gates, w_in, w_down):
    wide = jnp.float32
    core = lax.axis_index("core")
    expert = lax.axis_index("zlo") * 2 + core
    matches = routes[:, :, None] == jnp.arange(8, dtype=jnp.int32)[None, None, :]
    hit = jnp.sum(matches.astype(jnp.int32), axis=1)
    slot = jnp.cumsum(hit, axis=0) - hit
    weight = jnp.sum(route_gates[:, :, None] * matches.astype(wide), axis=1)
    taken = lax.dynamic_index_in_dim(hit, expert, 1, keepdims=False)
    place = lax.dynamic_index_in_dim(slot, expert, 1, keepdims=False)
    gates = lax.dynamic_index_in_dim(weight, expert, 1, keepdims=False)
    names = jnp.arange(8, dtype=jnp.int32)
    chosen = [(taken == 1) & (place == k) for k in range(2)]
    seqs = [jnp.sum(jnp.where(c, names, 0)) for c in chosen]
    scales = [jnp.sum(jnp.where(c, gates, 0.0)) for c in chosen]

    w_t = jnp.transpose(w_in[0], (1, 2, 0)).reshape(896, 1024)
    w_parts = ring_gather(w_t, "y")
    v_parts = ring_gather(w_down[0], "y")

    mine = lax.all_to_all(
        jnp.broadcast_to(tokens, (4, 64, 1024)), "zlo", split_axis=0, concat_axis=0, tiled=True
    )
    other = shift(mine, "core", 1)
    rows = []
    for s in seqs:
        a = lax.dynamic_index_in_dim(mine, s // 2, 0, keepdims=False)
        b = lax.dynamic_index_in_dim(other, s // 2, 0, keepdims=False)
        rows.append(jnp.where(s % 2 == core, a, b))
    rows = jnp.concatenate(ring_gather(jnp.concatenate(rows), "zhi"))

    w_all = jnp.concatenate([w[:448] for w in w_parts] + [w[448:] for w in w_parts])
    sums = lax.dot_general(
        rows, w_all, (((1,), (1,)), ((), ())), preferred_element_type=wide
    ).astype(jnp.bfloat16)
    parts = lax.all_to_all(sums.reshape(4, 128, 3584), "x", split_axis=0, concat_axis=0, tiled=True)
    total = jnp.sum(parts.astype(wide), axis=0)
    hidden = (jax.nn.silu(total[:, :1792]) * total[:, 1792:]).astype(jnp.bfloat16)
    hidden = lax.all_to_all(
        jnp.broadcast_to(hidden[None], (4, 128, 1792)), "x", split_axis=0, concat_axis=0, tiled=True
    ).reshape(512, 1792)

    v_all = jnp.concatenate(v_parts)
    out = jnp.dot(hidden, v_all, preferred_element_type=wide).astype(jnp.bfloat16).reshape(4, 128, 1024)
    result = ring_scatter((out[0], out[1], out[2], out[3]), "zhi").reshape(2, 64, 1024)

    ids = jnp.arange(4, dtype=jnp.int32)[:, None, None]
    def toward(parity):
        return sum(
            jnp.where((s // 2 == ids) & (s % 2 == parity), scale * result[k][None], 0.0)
            for k, (s, scale) in enumerate(zip(seqs, scales))
        )
    got = shift(toward(1 - core).astype(jnp.bfloat16), "core", 1)
    going = (toward(core) + got.astype(wide)).astype(jnp.bfloat16)
    back = lax.all_to_all(going, "zlo", split_axis=0, concat_axis=0, tiled=True)
    return jnp.sum(back.astype(wide), axis=0, keepdims=True).astype(jnp.bfloat16)


def solution(mesh):
    fine = Mesh(mesh.devices.reshape(4, 2, 4, 4, 4), ("zlo", "core", "x", "y", "zhi"))
    seqs, pos = ("zlo", "core"), ("y", "zhi")
    return jax.shard_map(
        on_device,
        mesh=fine,
        in_specs=(
            P(seqs, pos, "x"),
            P(),
            P(),
            P(seqs, "x", None, pos),
            P(seqs, pos, "x"),
        ),
        out_specs=P(seqs, pos, "x"),
        check_vma=False,
    )
```

time: 498 us -> 287 us (0.58)
  waiting for transfers between devices: 438 us -> 129 us
  starting transfers between devices: 15.3 us -> 97.5 us
  blocking collectives: 0 us -> 18.9 us
  between operations: 13.2 us -> 5.66 us
  local copies, waits for them, and re-layouts: 10 us -> 15.6 us
    reduce_scatter x1 -> x0, waiting for transfers between devices: 158 us -> none  [on_device(): lax.psum_scatter(jnp.dot(hidden, w_out, preferred_element_type=jnp.float3...]
    all_gather x1 -> x0, waiting for transfers between devices: 133 us -> none  [on_device(): packed = lax.all_gather(packed, 'col', axis=0, tiled=True)]
    psum x1 -> x0, waiting for transfers between devices: 95.9 us -> none  [on_device(): lax.psum(jnp.dot(rows, w_both, preferred_element_type=jnp.float32).astype...]
    ppermute x0 -> x18, waiting for transfers between devices: none -> 87.7 us  [shift(): return lax.ppermute(a, axis, [(i, (i + by) % n) for i in range(n)])]
    ppermute x0 -> x18, starting transfers between devices: none -> 82.6 us  [shift(): return lax.ppermute(a, axis, [(i, (i + by) % n) for i in range(n)])]
    all_to_all x0 -> x1, blocking collectives: none -> 18.9 us  [on_device(): back = lax.all_to_all(going, 'zlo', split_axis=0, concat_axis=0, tiled=True)]
    reshape x3 -> x0, local copies, waits for them, and re-layouts: 9.83 us -> none  [the longest x1 7.21 us: on_device(): rows = packed.reshape(packed.shape[0] * capacity, packed.shape[2])]
    all_to_all x2 -> x3, waiting for transfers between devices: 51 us -> 41.4 us  [the longest x1 37.5 us: on_device(): lax.all_to_all(sums.reshape(4, 128, 3584), 'x', split_axis=0, concat_axis...]
  transfers between devices with their start and end apart: 5 -> 21, of which waited for: 5 -> 13; matrix products, arithmetic and copies ran while one was open for 0% -> 7% of each run, Pallas kernels for 0% -> 0%
where the time goes in v1:
time: 287 us; the launch traced here: 285 us
  waiting for transfers between devices  129 us (45%)
  starting transfers between devices  97.5 us (34%)
  blocking collectives  18.9 us (7%)
  local copies, waits for them, and re-layouts  15.6 us (5%)
  matrix products  10.2 us (4%)
  other arithmetic  8.29 us (3%)
  between operations  5.66 us (2%)
    ppermute x18, waiting for transfers between devices, shift(): return lax.ppermute(a, axis, [(i, (i + by) % n) for i in range(n)])  87.7 us
    ppermute x18, starting transfers between devices, shift(): return lax.ppermute(a, axis, [(i, (i + by) % n) for i in range(n)])  82.6 us
    all_to_all x1, waiting for transfers between devices, on_device(): lax.all_to_all(sums.reshape(4, 128, 3584), 'x', split_axis=0, concat_axis...  37.5 us
    all_to_all x1, blocking collectives, on_device(): back = lax.all_to_all(going, 'zlo', split_axis=0, concat_axis=0, tiled=True)  18.9 us
    unnamed x21, local copies, waits for them, and re-layouts  7.71 us
  transfers between devices with their start and end apart: 21, of which 13 were waited for; matrix products, arithmetic and copies ran while one was open for 7% of the time, Pallas kernels for 0%

profile of v1, /device:TPU:1, one launch (start us, length us, event | category | flops | bytes accessed | tf_op | source)
XLA Modules:
  0.0 285.4 jit_solution(63972932620093252)
XLA Ops:
  0.0 4.0 %collective-permute-start.6 = (bf16[896,1024]{1,0:T(8,128)(2,1)}, bf16[896,1024]{1,0:T(8,128)(2,1)S(1)}, u32[]{:S(2)}, u32[]{:S(2)}) collective-permute-start(bf16[896,1024]{1,0:T(8,128)(2,1)} %bitcast.30), channel_id=1, source_target_pairs={{0,4},{4,8},{8,12},{12,0},{1,5},{5,9},{9,13},{13,1},{2,6},{6,10},{... | collective-permute-start | bytes 5505032 | tf_op jit(solution)/shard_map/ppermute | solution.py:9
  4.0 1.8 broadcast_in_dim.78
  5.8 5.6 %all-to-all-start = ((bf16[4,64,1024]{2,1,0:T(8,128)(2,1)}), bf16[4,64,1024]{2,1,0:T(8,128)(2,1)S(1)}, u32[]{:S(2)}, u32[]{:S(2)}) async-start(bf16[4,64,1024]{2,1,0:T(8,128)(2,1)} %broadcast_in_dim.78), calls=%async_computation | async-start | bytes 1048576 | tf_op jit(solution)/shard_map/all_to_all | solution.py:54
  11.4 3.3 %collective-permute-start.5 = (bf16[896,1024]{1,0:T(8,128)(2,1)}, bf16[896,1024]{1,0:T(8,128)(2,1)}, u32[]{:S(2)}, u32[]{:S(2)}) collective-permute-start(bf16[896,1024]{1,0:T(8,128)(2,1)} %bitcast.31), channel_id=1, source_target_pairs={{0,12},{4,0},{8,4},{12,8},{1,13},{5,1},{9,5},{13,9},{2,14},{6,2},{... | collective-permute-start | bytes 5505032 | tf_op jit(solution)/shard_map/ppermute | solution.py:9
  14.8 25.0 %collective-permute-done.6 = bf16[896,1024]{1,0:T(8,128)(2,1)S(1)} collective-permute-done((bf16[896,1024]{1,0:T(8,128)(2,1)}, bf16[896,1024]{1,0:T(8,128)(2,1)S(1)}, u32[]{:S(2)}, u32[]{:S(2)}) %collective-permute-start.6) | collective-permute-done | bytes 1835040 | tf_op jit(solution)/shard_map/ppermute | solution.py:9
  39.7 1.0 slice.118
  40.7 6.5 %collective-permute-start.7 = (bf16[448,1024]{1,0:T(8,128)(2,1)}, bf16[448,1024]{1,0:T(8,128)(2,1)S(1)}, u32[]{:S(2)}, u32[]{:S(2)}) collective-permute-start(bf16[448,1024]{1,0:T(8,128)(2,1)} %slice.118), channel_id=1, source_target_pairs={{0,4},{4,8},{8,12},{12,0},{1,5},{5,9},{9,13},{13,1},{2,6},{6,10},{... | collective-permute-start | bytes 2752520 | tf_op jit(solution)/shard_map/ppermute | solution.py:9
  54.1 4.5 %collective-permute-start = (bf16[4,64,1024]{2,1,0:T(8,128)(2,1)S(1)}, bf16[4,64,1024]{2,1,0:T(8,128)(2,1)S(1)}, u32[]{:S(2)}, u32[]{:S(2)}) collective-permute-start(bf16[4,64,1024]{2,1,0:T(8,128)(2,1)S(1)} %all-to-all-done), channel_id=1, source_target_pairs={{0,64},{64,0},{1,65},{65,1},{2,66},{66,2},{3,67},{67,3},{4,68},{68... | collective-permute-start | bytes 1572872 | tf_op jit(solution)/shard_map/ppermute | solution.py:9
  58.6 1.4 fusion.2
  60.0 1.2 slice_dynamic-update-slice_fusion.1
  61.3 6.1 %collective-permute-done.7 = bf16[448,1024]{1,0:T(8,128)(2,1)S(1)} collective-permute-done((bf16[448,1024]{1,0:T(8,128)(2,1)}, bf16[448,1024]{1,0:T(8,128)(2,1)S(1)}, u32[]{:S(2)}, u32[]{:S(2)}) %collective-permute-start.7) | collective-permute-done | bytes 917536 | tf_op jit(solution)/shard_map/ppermute | solution.py:9
  67.7 1.4 fusion.3
  69.1 4.6 %collective-permute-start.8 = (bf16[448,1024]{1,0:T(8,128)(2,1)S(1)}, bf16[448,1024]{1,0:T(8,128)(2,1)S(1)}, u32[]{:S(2)}, u32[]{:S(2)}) collective-permute-start(bf16[448,1024]{1,0:T(8,128)(2,1)S(1)} %get-tuple-element.13), channel_id=1, source_target_pairs={{0,12},{4,0},{8,4},{12,8},{1,13},{5,1},{9,5},{13,9},{2,14},{6,2},{... | collective-permute-start | bytes 2752520 | tf_op jit(solution)/shard_map/ppermute | solution.py:9
  73.7 8.8 %collective-permute-start.2 = (bf16[128,1024]{1,0:T(8,128)(2,1)S(1)}, bf16[128,1024]{1,0:T(8,128)(2,1)S(1)}, u32[]{:S(2)}, u32[]{:S(2)}) collective-permute-start(bf16[128,1024]{1,0:T(8,128)(2,1)S(1)} %pad_maximum_fusion), channel_id=1, source_target_pairs={{0,1},{1,2},{2,3},{3,0},{4,5},{5,6},{6,7},{7,4},{8,9},{9,10},{10,1... | collective-permute-start | bytes 786440 | tf_op jit(solution)/shard_map/ppermute | solution.py:9
  82.6 5.6 %collective-permute-start.1 = (bf16[128,1024]{1,0:T(8,128)(2,1)S(1)}, bf16[128,1024]{1,0:T(8,128)(2,1)S(1)}, u32[]{:S(2)}, u32[]{:S(2)}) collective-permute-start(bf16[128,1024]{1,0:T(8,128)(2,1)S(1)} %pad_maximum_fusion), channel_id=1, source_target_pairs={{0,3},{1,0},{2,1},{3,2},{4,7},{5,4},{6,5},{7,6},{8,11},{9,8},{10,9... | collective-permute-start | bytes 786440 | tf_op jit(solution)/shard_map/ppermute | solution.py:9
  88.1 2.3 collective-permute-done.2
  90.4 7.2 %collective-permute-start.3 = (bf16[64,1024]{1,0:T(8,128)(2,1)S(1)}, bf16[64,1024]{1,0:T(8,128)(2,1)S(1)}, u32[]{:S(2)}, u32[]{:S(2)}) collective-permute-start(bf16[64,1024]{1,0:T(8,128)(2,1)S(1)} %slice.114), channel_id=1, source_target_pairs={{0,1},{1,2},{2,3},{3,0},{4,5},{5,6},{6,7},{7,4},{8,9},{9,10},{10,1... | collective-permute-start | bytes 393224 | tf_op jit(solution)/shard_map/ppermute | solution.py:9
  97.7 16.9 %collective-permute-done.1 = bf16[128,1024]{1,0:T(8,128)(2,1)S(1)} collective-permute-done((bf16[128,1024]{1,0:T(8,128)(2,1)S(1)}, bf16[128,1024]{1,0:T(8,128)(2,1)S(1)}, u32[]{:S(2)}, u32[]{:S(2)}) %collective-permute-start.1) | collective-permute-done | bytes 262176 | tf_op jit(solution)/shard_map/ppermute | solution.py:9
  114.6 4.1 %collective-permute-start.4 = (bf16[64,1024]{1,0:T(8,128)(2,1)S(1)}, bf16[64,1024]{1,0:T(8,128)(2,1)S(1)}, u32[]{:S(2)}, u32[]{:S(2)}) collective-permute-start(bf16[64,1024]{1,0:T(8,128)(2,1)S(1)} %slice.115), channel_id=1, source_target_pairs={{0,3},{1,0},{2,1},{3,2},{4,7},{5,4},{6,5},{7,6},{8,11},{9,8},{10,9... | collective-permute-start | bytes 393224 | tf_op jit(solution)/shard_map/ppermute | solution.py:9
  118.7 10.4 %collective-permute-done.4 = bf16[64,1024]{1,0:T(8,128)(2,1)S(1)} collective-permute-done((bf16[64,1024]{1,0:T(8,128)(2,1)S(1)}, bf16[64,1024]{1,0:T(8,128)(2,1)S(1)}, u32[]{:S(2)}, u32[]{:S(2)}) %collective-permute-start.4) | collective-permute-done | bytes 131104 | tf_op jit(solution)/shard_map/ppermute | solution.py:9
  129.3 5.6 %convolution_convert_fusion = bf16[512,3584]{1,0:T(8,128)(2,1)} fusion(bf16[512,1024]{1,0:T(8,128)(2,1)S(1)} %constant_dynamic-update-slice_fusion, bf16[3584,1024]{1,0:T(8,128)(2,1)S(1)} %slice_dynamic-update-slice_fusion), kind=kOutput, calls=%fused_computation.1 | convolution fusion | flops 3759931392 | bytes 12058624 | tf_op jit(solution)/shard_map/dot_general | solution.py:66
  134.8 4.9 %all-to-all-start.1 = ((bf16[4,128,3584]{2,1,0:T(8,128)(2,1)}), bf16[4,128,3584]{2,1,0:T(8,128)(2,1)}, u32[]{:S(2)}, u32[]{:S(2)}) async-start(bf16[4,128,3584]{2,1,0:T(8,128)(2,1)} %bitcast.29), calls=%async_computation.1 | async-start | bytes 7340032 | tf_op jit(solution)/shard_map/all_to_all | solution.py:69
  139.7 2.4 collective-permute-start.9
  142.1 2.9 %collective-permute-start.10 = (bf16[448,1024]{1,0:T(8,128)(2,1)S(1)}, bf16[448,1024]{1,0:T(8,128)(2,1)S(1)}, u32[]{:S(2)}, u32[]{:S(2)}) collective-permute-start(bf16[448,1024]{1,0:T(8,128)(2,1)S(1)} %bitcast.35), channel_id=1, source_target_pairs={{0,4},{4,8},{8,12},{12,0},{1,5},{5,9},{9,13},{13,1},{2,6},{6,10},{... | collective-permute-start | bytes 2752520 | tf_op jit(solution)/shard_map/ppermute | solution.py:9
  145.0 37.5 %all-to-all-done.1 = bf16[4,128,3584]{2,1,0:T(8,128)(2,1)} async-done(((bf16[4,128,3584]{2,1,0:T(8,128)(2,1)}), bf16[4,128,3584]{2,1,0:T(8,128)(2,1)}, u32[]{:S(2)}, u32[]{:S(2)}) %all-to-all-start.1) | async-done | bytes 3670048 | tf_op jit(solution)/shard_map/all_to_all | solution.py:69
  182.6 2.7 convert_reduce_fusion
  185.6 1.4 broadcast_in_dim.79
  187.0 4.4 %all-to-all-start.2 = ((bf16[4,128,1792]{2,1,0:T(8,128)(2,1)}), bf16[4,128,1792]{2,1,0:T(8,128)(2,1)}, u32[]{:S(2)}, u32[]{:S(2)}) async-start(bf16[4,128,1792]{2,1,0:T(8,128)(2,1)} %broadcast_in_dim.79), calls=%async_computation.2 | async-start | bytes 3670016 | tf_op jit(solution)/shard_map/all_to_all | solution.py:72
  191.4 3.1 %collective-permute-start.11 = (bf16[224,1024]{1,0:T(8,128)(2,1)S(1)}, bf16[224,1024]{1,0:T(8,128)(2,1)S(1)}, u32[]{:S(2)}, u32[]{:S(2)}) collective-permute-start(bf16[224,1024]{1,0:T(8,128)(2,1)S(1)} %slice.124), channel_id=1, source_target_pairs={{0,4},{4,8},{8,12},{12,0},{1,5},{5,9},{9,13},{13,1},{2,6},{6,10},{... | collective-permute-start | bytes 1376264 | tf_op jit(solution)/shard_map/ppermute | solution.py:9
  194.5 1.1 slice.125
  195.6 3.4 %collective-permute-start.12 = (bf16[224,1024]{1,0:T(8,128)(2,1)S(1)}, bf16[224,1024]{1,0:T(8,128)(2,1)S(1)}, u32[]{:S(2)}, u32[]{:S(2)}) collective-permute-start(bf16[224,1024]{1,0:T(8,128)(2,1)S(1)} %slice.125), channel_id=1, source_target_pairs={{0,12},{4,0},{8,4},{12,8},{1,13},{5,1},{9,5},{13,9},{2,14},{6,2},{... | collective-permute-start | bytes 1376264 | tf_op jit(solution)/shard_map/ppermute | solution.py:9
  200.0 2.2 constant_dynamic-update-slice_fusion.13
  202.2 3.1 %collective-permute-done.11 = bf16[224,1024]{1,0:T(8,128)(2,1)S(1)} collective-permute-done((bf16[224,1024]{1,0:T(8,128)(2,1)S(1)}, bf16[224,1024]{1,0:T(8,128)(2,1)S(1)}, u32[]{:S(2)}, u32[]{:S(2)}) %collective-permute-start.11) | collective-permute-done | bytes 458784 | tf_op jit(solution)/shard_map/ppermute | solution.py:9
  206.1 1.9 collective-permute-done.12
  208.8 1.0 constant_dynamic-update-slice_fusion.10
  209.8 3.9 %all-to-all-done.2 = bf16[4,128,1792]{2,1,0:T(8,128)(2,1)} async-done(((bf16[4,128,1792]{2,1,0:T(8,128)(2,1)}), bf16[4,128,1792]{2,1,0:T(8,128)(2,1)}, u32[]{:S(2)}, u32[]{:S(2)}) %all-to-all-start.2) | async-done | bytes 1835040 | tf_op jit(solution)/shard_map/all_to_all | solution.py:72
  213.7 4.7 %convolution_convert_fusion.1 = bf16[512,1024]{1,0:T(8,128)(2,1)S(1)} fusion(bf16[512,1792]{1,0:T(8,128)(2,1)} %bitcast.11, bf16[1792,1024]{1,0:T(8,128)(2,1)} %constant_dynamic-update-slice_fusion.10), kind=kOutput, calls=%fused_computation.2 | convolution fusion | flops 1879572480 | bytes 6553600 | tf_op jit(solution)/shard_map/dot_general | solution.py:77
  218.4 2.8 collective-permute-start.13
  221.2 6.4 %collective-permute-start.15 = (bf16[64,1024]{1,0:T(8,128)(2,1)S(1)}, bf16[64,1024]{1,0:T(8,128)(2,1)S(1)}, u32[]{:S(2)}, u32[]{:S(2)}) collective-permute-start(bf16[64,1024]{1,0:T(8,128)(2,1)S(1)} %get-tuple-element.18), channel_id=1, source_target_pairs={{0,3},{1,0},{2,1},{3,2},{4,7},{5,4},{6,5},{7,6},{8,11},{9,8},{10,9... | collective-permute-start | bytes 393224 | tf_op jit(solution)/shard_map/ppermute | solution.py:9
  227.7 1.7 collective-permute-done.13
  229.4 2.3 collective-permute-done.15
  231.7 6.4 %collective-permute-start.14 = (bf16[128,1024]{1,0:T(8,128)(2,1)S(1)}, bf16[128,1024]{1,0:T(8,128)(2,1)S(1)}, u32[]{:S(2)}, u32[]{:S(2)}) collective-permute-start(bf16[128,1024]{1,0:T(8,128)(2,1)S(1)} %pad_maximum_fusion.1), channel_id=1, source_target_pairs={{0,1},{1,2},{2,3},{3,0},{4,5},{5,6},{6,7},{7,4},{8,9},{9,10},{10,1... | collective-permute-start | bytes 786440 | tf_op jit(solution)/shard_map/ppermute | solution.py:9
  238.2 2.7 collective-permute-start.16
  241.8 16.6 %collective-permute-done.14 = bf16[128,1024]{1,0:T(8,128)(2,1)S(1)} collective-permute-done((bf16[128,1024]{1,0:T(8,128)(2,1)S(1)}, bf16[128,1024]{1,0:T(8,128)(2,1)S(1)}, u32[]{:S(2)}, u32[]{:S(2)}) %collective-permute-start.14) | collective-permute-done | bytes 262176 | tf_op jit(solution)/shard_map/ppermute | solution.py:9
  258.6 1.3 slice_multiply_fusion.2
  260.1 3.9 %collective-permute-start.17 = (bf16[4,64,1024]{2,1,0:T(8,128)(2,1)S(1)}, bf16[4,64,1024]{2,1,0:T(8,128)(2,1)S(1)}, u32[]{:S(2)}, u32[]{:S(2)}) collective-permute-start(bf16[4,64,1024]{2,1,0:T(8,128)(2,1)S(1)} %add_convert_fusion.1), channel_id=1, source_target_pairs={{0,64},{64,0},{1,65},{65,1},{2,66},{66,2},{3,67},{67,3},{4,68},{68... | collective-permute-start | bytes 1572872 | tf_op jit(solution)/shard_map/ppermute | solution.py:9
  264.0 1.5 collective-permute-done.17
  265.7 18.9 %all_to_all.20 = bf16[4,64,1024]{2,1,0:T(8,128)(2,1)S(1)} all-to-all(bf16[4,64,1024]{2,1,0:T(8,128)(2,1)S(1)} %add_convert_fusion), channel_id=1, replica_groups=mesh['zlo'=4,'core'=2,'x'=4,'y'=4,'zhi'=4] {'zlo'}, dimensions={0} | all-to-all | bytes 1048576 | tf_op jit(solution)/shard_map/all_to_all | solution.py:88
  (55 shorter events, 7.5 us)
Async XLA Ops:
  0.0 39.7 %collective-permute-start.6 = (bf16[896,1024]{1,0:T(8,128)(2,1)}, bf16[896,1024]{1,0:T(8,128)(2,1)S(1)}, u32[]{:S(2)}, u32[]{:S(2)}) collective-permute-start(bf16[896,1024]{1,0:T(8,128)(2,1)} %bitcast.30), channel_id=1, source_target_pairs={{0,4},{4,8},{8,12},{12,0},{1,5},{5,9},{9,13},{13,1},{2,6},{6,10},{... | collective-permute-start | bytes 5505032 | tf_op jit(solution)/shard_map/ppermute | solution.py:9
  5.8 48.3 %all-to-all-start = ((bf16[4,64,1024]{2,1,0:T(8,128)(2,1)}), bf16[4,64,1024]{2,1,0:T(8,128)(2,1)S(1)}, u32[]{:S(2)}, u32[]{:S(2)}) async-start(bf16[4,64,1024]{2,1,0:T(8,128)(2,1)} %broadcast_in_dim.78), calls=%async_computation | async-start | bytes 1048576 | tf_op jit(solution)/shard_map/all_to_all | solution.py:54
  11.4 48.6 %collective-permute-start.5 = (bf16[896,1024]{1,0:T(8,128)(2,1)}, bf16[896,1024]{1,0:T(8,128)(2,1)}, u32[]{:S(2)}, u32[]{:S(2)}) collective-permute-start(bf16[896,1024]{1,0:T(8,128)(2,1)} %bitcast.31), channel_id=1, source_target_pairs={{0,12},{4,0},{8,4},{12,8},{1,13},{5,1},{9,5},{13,9},{2,14},{6,2},{... | collective-permute-start | bytes 5505032 | tf_op jit(solution)/shard_map/ppermute | solution.py:9
  40.7 26.7 %collective-permute-start.7 = (bf16[448,1024]{1,0:T(8,128)(2,1)}, bf16[448,1024]{1,0:T(8,128)(2,1)S(1)}, u32[]{:S(2)}, u32[]{:S(2)}) collective-permute-start(bf16[448,1024]{1,0:T(8,128)(2,1)} %slice.118), channel_id=1, source_target_pairs={{0,4},{4,8},{8,12},{12,0},{1,5},{5,9},{9,13},{13,1},{2,6},{6,10},{... | collective-permute-start | bytes 2752520 | tf_op jit(solution)/shard_map/ppermute | solution.py:9
  54.1 7.2 %collective-permute-start = (bf16[4,64,1024]{2,1,0:T(8,128)(2,1)S(1)}, bf16[4,64,1024]{2,1,0:T(8,128)(2,1)S(1)}, u32[]{:S(2)}, u32[]{:S(2)}) collective-permute-start(bf16[4,64,1024]{2,1,0:T(8,128)(2,1)S(1)} %all-to-all-done), channel_id=1, source_target_pairs={{0,64},{64,0},{1,65},{65,1},{2,66},{66,2},{3,67},{67,3},{4,68},{68... | collective-permute-start | bytes 1572872 | tf_op jit(solution)/shard_map/ppermute | solution.py:9
  58.6 9.0 %copy-start = (bf16[1,1024,2,448]{1,3,2,0:T(8,128)(2,1)S(1)}, bf16[1,1024,2,448]{1,3,2,0:T(8,128)(2,1)}, u32[]{:S(2)}) copy-start(bf16[1,1024,2,448]{1,3,2,0:T(8,128)(2,1)} %param.8) | copy-start | bytes 5505028
  69.1 60.0 %collective-permute-start.8 = (bf16[448,1024]{1,0:T(8,128)(2,1)S(1)}, bf16[448,1024]{1,0:T(8,128)(2,1)S(1)}, u32[]{:S(2)}, u32[]{:S(2)}) collective-permute-start(bf16[448,1024]{1,0:T(8,128)(2,1)S(1)} %get-tuple-element.13), channel_id=1, source_target_pairs={{0,12},{4,0},{8,4},{12,8},{1,13},{5,1},{9,5},{13,9},{2,14},{6,2},{... | collective-permute-start | bytes 2752520 | tf_op jit(solution)/shard_map/ppermute | solution.py:9
  73.7 16.7 %collective-permute-start.2 = (bf16[128,1024]{1,0:T(8,128)(2,1)S(1)}, bf16[128,1024]{1,0:T(8,128)(2,1)S(1)}, u32[]{:S(2)}, u32[]{:S(2)}) collective-permute-start(bf16[128,1024]{1,0:T(8,128)(2,1)S(1)} %pad_maximum_fusion), channel_id=1, source_target_pairs={{0,1},{1,2},{2,3},{3,0},{4,5},{5,6},{6,7},{7,4},{8,9},{9,10},{10,1... | collective-permute-start | bytes 786440 | tf_op jit(solution)/shard_map/ppermute | solution.py:9
  82.6 32.0 %collective-permute-start.1 = (bf16[128,1024]{1,0:T(8,128)(2,1)S(1)}, bf16[128,1024]{1,0:T(8,128)(2,1)S(1)}, u32[]{:S(2)}, u32[]{:S(2)}) collective-permute-start(bf16[128,1024]{1,0:T(8,128)(2,1)S(1)} %pad_maximum_fusion), channel_id=1, source_target_pairs={{0,3},{1,0},{2,1},{3,2},{4,7},{5,4},{6,5},{7,6},{8,11},{9,8},{10,9... | collective-permute-start | bytes 786440 | tf_op jit(solution)/shard_map/ppermute | solution.py:9
  90.4 28.2 %collective-permute-start.3 = (bf16[64,1024]{1,0:T(8,128)(2,1)S(1)}, bf16[64,1024]{1,0:T(8,128)(2,1)S(1)}, u32[]{:S(2)}, u32[]{:S(2)}) collective-permute-start(bf16[64,1024]{1,0:T(8,128)(2,1)S(1)} %slice.114), channel_id=1, source_target_pairs={{0,1},{1,2},{2,3},{3,0},{4,5},{5,6},{6,7},{7,4},{8,9},{9,10},{10,1... | collective-permute-start | bytes 393224 | tf_op jit(solution)/shard_map/ppermute | solution.py:9
  114.6 14.5 %collective-permute-start.4 = (bf16[64,1024]{1,0:T(8,128)(2,1)S(1)}, bf16[64,1024]{1,0:T(8,128)(2,1)S(1)}, u32[]{:S(2)}, u32[]{:S(2)}) collective-permute-start(bf16[64,1024]{1,0:T(8,128)(2,1)S(1)} %slice.115), channel_id=1, source_target_pairs={{0,3},{1,0},{2,1},{3,2},{4,7},{5,4},{6,5},{7,6},{8,11},{9,8},{10,9... | collective-permute-start | bytes 393224 | tf_op jit(solution)/shard_map/ppermute | solution.py:9
  134.8 4.9 %copy-start.1 = (bf16[1,448,1024]{2,1,0:T(8,128)(2,1)S(1)}, bf16[1,448,1024]{2,1,0:T(8,128)(2,1)}, u32[]{:S(2)}) copy-start(bf16[1,448,1024]{2,1,0:T(8,128)(2,1)} %param.9) | copy-start | bytes 2752516
  134.8 47.7 %all-to-all-start.1 = ((bf16[4,128,3584]{2,1,0:T(8,128)(2,1)}), bf16[4,128,3584]{2,1,0:T(8,128)(2,1)}, u32[]{:S(2)}, u32[]{:S(2)}) async-start(bf16[4,128,3584]{2,1,0:T(8,128)(2,1)} %bitcast.29), calls=%async_computation.1 | async-start | bytes 7340032 | tf_op jit(solution)/shard_map/all_to_all | solution.py:69
  139.7 54.8 %collective-permute-start.9 = (bf16[448,1024]{1,0:T(8,128)(2,1)S(1)}, bf16[448,1024]{1,0:T(8,128)(2,1)}, u32[]{:S(2)}, u32[]{:S(2)}) collective-permute-start(bf16[448,1024]{1,0:T(8,128)(2,1)S(1)} %bitcast.34), channel_id=1, source_target_pairs={{0,12},{4,0},{8,4},{12,8},{1,13},{5,1},{9,5},{13,9},{2,14},{6,2},{... | collective-permute-start | bytes 2752520 | tf_op jit(solution)/shard_map/ppermute | solution.py:9
  142.1 49.3 %collective-permute-start.10 = (bf16[448,1024]{1,0:T(8,128)(2,1)S(1)}, bf16[448,1024]{1,0:T(8,128)(2,1)S(1)}, u32[]{:S(2)}, u32[]{:S(2)}) collective-permute-start(bf16[448,1024]{1,0:T(8,128)(2,1)S(1)} %bitcast.35), channel_id=1, source_target_pairs={{0,4},{4,8},{8,12},{12,0},{1,5},{5,9},{9,13},{13,1},{2,6},{6,10},{... | collective-permute-start | bytes 2752520 | tf_op jit(solution)/shard_map/ppermute | solution.py:9
  187.0 26.7 %all-to-all-start.2 = ((bf16[4,128,1792]{2,1,0:T(8,128)(2,1)}), bf16[4,128,1792]{2,1,0:T(8,128)(2,1)}, u32[]{:S(2)}, u32[]{:S(2)}) async-start(bf16[4,128,1792]{2,1,0:T(8,128)(2,1)} %broadcast_in_dim.79), calls=%async_computation.2 | async-start | bytes 3670016 | tf_op jit(solution)/shard_map/all_to_all | solution.py:72
  191.4 13.9 %collective-permute-start.11 = (bf16[224,1024]{1,0:T(8,128)(2,1)S(1)}, bf16[224,1024]{1,0:T(8,128)(2,1)S(1)}, u32[]{:S(2)}, u32[]{:S(2)}) collective-permute-start(bf16[224,1024]{1,0:T(8,128)(2,1)S(1)} %slice.124), channel_id=1, source_target_pairs={{0,4},{4,8},{8,12},{12,0},{1,5},{5,9},{9,13},{13,1},{2,6},{6,10},{... | collective-permute-start | bytes 1376264 | tf_op jit(solution)/shard_map/ppermute | solution.py:9
  195.6 12.4 %collective-permute-start.12 = (bf16[224,1024]{1,0:T(8,128)(2,1)S(1)}, bf16[224,1024]{1,0:T(8,128)(2,1)S(1)}, u32[]{:S(2)}, u32[]{:S(2)}) collective-permute-start(bf16[224,1024]{1,0:T(8,128)(2,1)S(1)} %slice.125), channel_id=1, source_target_pairs={{0,12},{4,0},{8,4},{12,8},{1,13},{5,1},{9,5},{13,9},{2,14},{6,2},{... | collective-permute-start | bytes 1376264 | tf_op jit(solution)/shard_map/ppermute | solution.py:9
  213.7 13.9 %copy-start.2 = (s32[8,2]{0,1:T(2,128)S(1)}, s32[8,2]{0,1:T(2,128)}, u32[]{:S(2)}) copy-start(s32[8,2]{0,1:T(2,128)} %param.6) | copy-start | bytes 196
  213.7 14.0 %copy-start.3 = (f32[8,2]{0,1:T(2,128)S(1)}, f32[8,2]{0,1:T(2,128)}, u32[]{:S(2)}) copy-start(f32[8,2]{0,1:T(2,128)} %param.7) | copy-start | bytes 196
  218.4 11.0 %collective-permute-start.13 = (bf16[64,1024]{1,0:T(8,128)(2,1)S(1)}, bf16[64,1024]{1,0:T(8,128)(2,1)S(1)}, u32[]{:S(2)}, u32[]{:S(2)}) collective-permute-start(bf16[64,1024]{1,0:T(8,128)(2,1)S(1)} %get-tuple-element.17), channel_id=1, source_target_pairs={{0,1},{1,2},{2,3},{3,0},{4,5},{5,6},{6,7},{7,4},{8,9},{9,10},{10,1... | collective-permute-start | bytes 393224 | tf_op jit(solution)/shard_map/ppermute | solution.py:9
  221.2 10.5 %collective-permute-start.15 = (bf16[64,1024]{1,0:T(8,128)(2,1)S(1)}, bf16[64,1024]{1,0:T(8,128)(2,1)S(1)}, u32[]{:S(2)}, u32[]{:S(2)}) collective-permute-start(bf16[64,1024]{1,0:T(8,128)(2,1)S(1)} %get-tuple-element.18), channel_id=1, source_target_pairs={{0,3},{1,0},{2,1},{3,2},{4,7},{5,4},{6,5},{7,6},{8,11},{9,8},{10,9... | collective-permute-start | bytes 393224 | tf_op jit(solution)/shard_map/ppermute | solution.py:9
  231.7 26.7 %collective-permute-start.14 = (bf16[128,1024]{1,0:T(8,128)(2,1)S(1)}, bf16[128,1024]{1,0:T(8,128)(2,1)S(1)}, u32[]{:S(2)}, u32[]{:S(2)}) collective-permute-start(bf16[128,1024]{1,0:T(8,128)(2,1)S(1)} %pad_maximum_fusion.1), channel_id=1, source_target_pairs={{0,1},{1,2},{2,3},{3,0},{4,5},{5,6},{6,7},{7,4},{8,9},{9,10},{10,1... | collective-permute-start | bytes 786440 | tf_op jit(solution)/shard_map/ppermute | solution.py:9
  238.2 20.2 %collective-permute-start.16 = (bf16[128,1024]{1,0:T(8,128)(2,1)S(1)}, bf16[128,1024]{1,0:T(8,128)(2,1)S(1)}, u32[]{:S(2)}, u32[]{:S(2)}) collective-permute-start(bf16[128,1024]{1,0:T(8,128)(2,1)S(1)} %pad_maximum_fusion.2), channel_id=1, source_target_pairs={{0,3},{1,0},{2,1},{3,2},{4,7},{5,4},{6,5},{7,6},{8,11},{9,8},{10,9... | collective-permute-start | bytes 786440 | tf_op jit(solution)/shard_map/ppermute | solution.py:9
  260.1 5.4 %collective-permute-start.17 = (bf16[4,64,1024]{2,1,0:T(8,128)(2,1)S(1)}, bf16[4,64,1024]{2,1,0:T(8,128)(2,1)S(1)}, u32[]{:S(2)}, u32[]{:S(2)}) collective-permute-start(bf16[4,64,1024]{2,1,0:T(8,128)(2,1)S(1)} %add_convert_fusion.1), channel_id=1, source_target_pairs={{0,64},{64,0},{1,65},{65,1},{2,66},{66,2},{3,67},{67,3},{4,68},{68... | collective-permute-start | bytes 1572872 | tf_op jit(solution)/shard_map/ppermute | solution.py:9

commit v2 on v1

v2 whole, which is shorter than its diff:
```python
import jax
import jax.numpy as jnp
from jax import lax
from jax.experimental import pallas as pl
from jax.experimental.pallas import tpu as pltpu
from jax.sharding import Mesh, PartitionSpec as P

wide = jnp.float32
half = jnp.bfloat16


def shift(a, axis, by):
    n = lax.axis_size(axis)
    return lax.ppermute(a, axis, [(i, (i + by) % n) for i in range(n)])


def swap(a, axis):
    return lax.all_to_all(a, axis, split_axis=0, concat_axis=0, tiled=True)


def gate_up(pieces, w_all, after=None):
    n = len(pieces)
    rows = 128 * n

    def kernel(*refs):
        w_ref, out_ref, x_ref = refs[n], refs[-2], refs[-1]

        @pl.when(pl.program_id(0) == 0)
        def _():
            for j in range(4):
                for i in range(n):
                    x_ref[pl.ds(32 * (j * n + i), 32), :] = refs[i][pl.ds(32 * j, 32), :]

        w = w_ref[...].reshape(896, 1024)
        out = lax.dot_general(x_ref[...], w, (((1,), (1,)), ((), ())), preferred_element_type=wide)
        out_ref[...] = out.astype(half).reshape(4, 32 * n, 896)

    whole = pl.BlockSpec((128, 1024), lambda i: (0, 0))
    w_spec = pl.BlockSpec((2, 1, 448, 1024), lambda i: (i % 2, i // 2, 0, 0))
    extra = [] if after is None else [after]
    return pl.pallas_call(
        kernel,
        grid=(4,),
        in_specs=[whole] * n + [w_spec] + [pl.BlockSpec(memory_space=pl.ANY)] * len(extra),
        out_specs=pl.BlockSpec((4, 32 * n, 896), lambda i: (0, 0, i)),
        out_shape=jax.ShapeDtypeStruct((4, 32 * n, 3584), half),
        scratch_shapes=[pltpu.VMEM((rows, 1024), half)],
        compiler_params=pltpu.CompilerParams(vmem_limit_bytes=24 * 2**20),
        cost_estimate=pl.CostEstimate(
            flops=2 * rows * 1024 * 3584, bytes_accessed=3584 * 2048 + rows * 9216, transcendentals=0
        ),
    )(*pieces, w_all, *extra)


def activate(sums, cuts):
    rows = sums.shape[1]

    def kernel(gate_ref, up_ref, *outs):
        gate = jnp.sum(gate_ref[...].astype(wide), axis=0)
        up = jnp.sum(up_ref[...].astype(wide), axis=0)
        hidden = (gate / (1.0 + jnp.exp(-gate)) * up).astype(half)
        at = 0
        for cut, out in zip(cuts, outs):
            for j in range(4):
                out[j] = hidden[at : at + cut]
            at += cut

    return pl.pallas_call(
        kernel,
        grid=(2,),
        in_specs=[
            pl.BlockSpec((4, rows, 896), lambda i: (0, 0, i)),
            pl.BlockSpec((4, rows, 896), lambda i: (0, 0, i + 2)),
        ],
        out_specs=[pl.BlockSpec((4, c, 896), lambda i: (0, 0, i)) for c in cuts],
        out_shape=[jax.ShapeDtypeStruct((4, c, 1792), half) for c in cuts],
        compiler_params=pltpu.CompilerParams(vmem_limit_bytes=24 * 2**20),
        cost_estimate=pl.CostEstimate(
            flops=rows * 1792 * 12, bytes_accessed=rows * 3584 * 12, transcendentals=rows * 1792
        ),
    )(sums, sums)


def on_device(tokens, routes, route_gates, w_in, w_down):
    core = lax.axis_index("core")
    expert = lax.axis_index("zlo") * 2 + core
    w_t = jnp.transpose(w_in[0], (1, 2, 0)).reshape(896, 1024)
    w_all = lax.all_gather(w_t, "y", axis=0, tiled=True).reshape(4, 2, 448, 1024)

    matches = routes[:, :, None] == jnp.arange(8, dtype=jnp.int32)[None, None, :]
    hit = jnp.sum(matches.astype(jnp.int32), axis=1)
    slot = jnp.cumsum(hit, axis=0) - hit
    weight = jnp.sum(route_gates[:, :, None] * matches.astype(wide), axis=1)
    taken = lax.dynamic_index_in_dim(hit, expert, 1, keepdims=False)
    place = lax.dynamic_index_in_dim(slot, expert, 1, keepdims=False)
    gates = lax.dynamic_index_in_dim(weight, expert, 1, keepdims=False)
    names = jnp.arange(8, dtype=jnp.int32)
    chosen = [(taken == 1) & (place == k) for k in range(2)]
    owner = [jnp.sum(jnp.where(c, names >> 1, 0)) for c in chosen]
    side = [jnp.sum(jnp.where(c, names & 1, 0)) for c in chosen]
    scales = [jnp.sum(jnp.where(c, gates, 0.0)) for c in chosen]

    mine = swap(jnp.broadcast_to(tokens, (4, 64, 1024)), "zlo")
    other = shift(mine, "core", 1)
    rows = []
    for z, c in zip(owner, side):
        a = lax.dynamic_index_in_dim(mine, z, 0, keepdims=False)
        b = lax.dynamic_index_in_dim(other, z, 0, keepdims=False)
        rows.append(jnp.where(c == core, a, b))
    rows = jnp.concatenate(rows)

    above = shift(rows, "zhi", -1)
    below = shift(rows, "zhi", 1)
    low = shift(below[:64], "zhi", 1)
    high = shift(above[64:], "zhi", -1)
    far = jnp.concatenate([low, high])
    v_all = lax.all_gather(w_down[0], "y", axis=0, tiled=True)

    def down(hidden):
        return jnp.dot(hidden.reshape(-1, 1792), v_all, preferred_element_type=wide)

    sums = swap(gate_up([far, above, below], w_all), "x")
    far_h, near_h = activate(sums, (32, 64))
    far_h = swap(far_h, "x")
    far_out = down(far_h).astype(half)
    up1 = shift(far_out[:64], "zhi", 1)
    down1 = shift(far_out[64:], "zhi", -1)
    near_h = swap(near_h, "x")
    near_out = down(near_h).reshape(4, 2, 32, 1024)
    above_out = near_out[:, 0].reshape(128, 1024)
    below_out = near_out[:, 1].reshape(128, 1024)
    above_out = jnp.concatenate([above_out[:64] + up1.astype(wide), above_out[64:]]).astype(half)
    below_out = jnp.concatenate([below_out[:64], below_out[64:] + down1.astype(wide)]).astype(half)
    up2 = shift(above_out, "zhi", 1)
    down2 = shift(below_out, "zhi", -1)

    own = swap(gate_up([rows], w_all, near_h), "x")
    (own_h,) = activate(own, (32,))
    own_h = swap(own_h, "x")
    result = (down(own_h) + up2.astype(wide) + down2.astype(wide)).reshape(2, 64, 1024)

    ids = jnp.arange(4, dtype=jnp.int32)[:, None, None]

    def toward(parity):
        return sum(
            jnp.where((owner[k] == ids) & (side[k] == parity), scales[k] * result[k][None], 0.0)
            for k in range(2)
        )

    got = shift(toward(1 - core).astype(half), "core", 1)
    going = (toward(core) + got.astype(wide)).astype(half)
    back = swap(going, "zlo")
    return jnp.sum(back.astype(wide), axis=0, keepdims=True).astype(half)


def solution(mesh):
    fine = Mesh(mesh.devices.reshape(4, 2, 4, 4, 4), ("zlo", "core", "x", "y", "zhi"))
    seqs, pos = ("zlo", "core"), ("y", "zhi")
    return jax.shard_map(
        on_device,
        mesh=fine,
        in_specs=(
            P(seqs, pos, "x"),
            P(),
            P(),
            P(seqs, "x", None, pos),
            P(seqs, pos, "x"),
        ),
        out_specs=P(seqs, pos, "x"),
        check_vma=False,
    )
```

time: 287 us -> 259 us (0.902)
  waiting for transfers between devices: 129 us -> 73.9 us
  blocking collectives: 18.9 us -> 52.9 us
  starting transfers between devices: 97.5 us -> 76.3 us
  between operations: 5.66 us -> 19.8 us
  Pallas kernels: 0 us -> 11.6 us
  local copies, waits for them, and re-layouts: 15.6 us -> 8.21 us
    ppermute x18 -> x10, waiting for transfers between devices: 87.7 us -> 48.8 us  [shift(): return lax.ppermute(a, axis, [(i, (i + by) % n) for i in range(n)])]
    all_to_all x1 -> x2, blocking collectives: 18.9 us -> 52.9 us  [swap(): return lax.all_to_all(a, axis, split_axis=0, concat_axis=0, tiled=True)]
    ppermute x18 -> x10, starting transfers between devices: 82.6 us -> 54.5 us  [shift(): return lax.ppermute(a, axis, [(i, (i + by) % n) for i in range(n)])]
    all_to_all x3 -> x5, waiting for transfers between devices: 41.4 us -> 15.8 us  [swap(): return lax.all_to_all(a, axis, split_axis=0, concat_axis=0, tiled=True)]
    pallas_call x0 -> x4, Pallas kernels: none -> 11.6 us  [the longest x2 8.97 us: gate_up(): pl.pallas_call(kernel, grid=(4,), in_specs=[whole] * n + [w_spec] + [pl.B...]
    all_gather x0 -> x2, waiting for transfers between devices: none -> 7.91 us  [the longest x1 7.91 us: on_device(): lax.all_gather(w_t, 'y', axis=0, tiled=True).reshape(4, 2, 448, 1024)]
    all_to_all x3 -> x5, starting transfers between devices: 14.9 us -> 21.9 us  [swap(): return lax.all_to_all(a, axis, split_axis=0, concat_axis=0, tiled=True)]
    slice x7 -> x5, local copies, waits for them, and re-layouts: 3.52 us -> 0.1 us  [the longest x1 0.04 us: on_device(): above_out[:64] + up1.astype(wide)]
  transfers between devices with their start and end apart: 21 -> 17, of which waited for: 13 -> 8; matrix products, arithmetic and copies ran while one was open for 7% -> 6% of each run, Pallas kernels for 0% -> 4%
where the time goes in v2:
time: 259 us; the launch traced here: 258 us
  starting transfers between devices  76.3 us (29%)
  waiting for transfers between devices  73.9 us (29%)
  blocking collectives  52.9 us (20%)
  between operations  19.8 us (8%)
  Pallas kernels  11.6 us (4%)
  matrix products  8.51 us (3%)
  local copies, waits for them, and re-layouts  8.21 us (3%)
  other arithmetic  6.86 us (3%)
    ppermute x10, starting transfers between devices, shift(): return lax.ppermute(a, axis, [(i, (i + by) % n) for i in range(n)])  54.5 us
    all_to_all x2, blocking collectives, swap(): return lax.all_to_all(a, axis, split_axis=0, concat_axis=0, tiled=True)  52.9 us
    ppermute x10, waiting for transfers between devices, shift(): return lax.ppermute(a, axis, [(i, (i + by) % n) for i in range(n)])  48.8 us
    all_to_all x5, starting transfers between devices, swap(): return lax.all_to_all(a, axis, split_axis=0, concat_axis=0, tiled=True)  21.9 us
    all_to_all x5, waiting for transfers between devices, swap(): return lax.all_to_all(a, axis, split_axis=0, concat_axis=0, tiled=True)  15.8 us
    pallas_call x2, Pallas kernels, gate_up(): pl.pallas_call(kernel, grid=(4,), in_specs=[whole] * n + [w_spec] + [pl.B...  8.97 us
    dot_general x3, matrix products, down(): return jnp.dot(hidden.reshape(-1, 1792), v_all, preferred_element_type=wide)  8.51 us
    all_gather x1, waiting for transfers between devices, on_device(): lax.all_gather(w_t, 'y', axis=0, tiled=True).reshape(4, 2, 448, 1024)  7.91 us
  transfers between devices with their start and end apart: 17, of which 8 were waited for; matrix products, arithmetic and copies ran while one was open for 6% of the time, Pallas kernels for 4%

profile of v2, /device:TPU:1, one launch (start us, length us, event | category | flops | bytes accessed | tf_op | source)
XLA Modules:
  0.0 258.2 jit_solution(16417728497668530185)
XLA Ops:
  6.5 0.7 all-gather.4.cloned.1.call-update
  7.3 1.8 broadcast_in_dim.74
  9.0 6.4 %all-to-all-start = ((bf16[4,64,1024]{2,1,0:T(8,128)(2,1)}), bf16[4,64,1024]{2,1,0:T(8,128)(2,1)S(1)}, u32[]{:S(2)}, u32[]{:S(2)}) async-start(bf16[4,64,1024]{2,1,0:T(8,128)(2,1)} %broadcast_in_dim.74), calls=%async_computation | async-start | bytes 1048576 | tf_op jit(solution)/shard_map/all_to_all | solution.py:18
  15.5 0.7 all-gather.6.cloned.1.call-update
  16.2 10.1 %all-to-all-done = bf16[4,64,1024]{2,1,0:T(8,128)(2,1)S(1)} async-done(((bf16[4,64,1024]{2,1,0:T(8,128)(2,1)}), bf16[4,64,1024]{2,1,0:T(8,128)(2,1)S(1)}, u32[]{:S(2)}, u32[]{:S(2)}) %all-to-all-start) | async-done | bytes 524320 | tf_op jit(solution)/shard_map/all_to_all | solution.py:18
  26.3 6.5 %collective-permute-start = (bf16[4,64,1024]{2,1,0:T(8,128)(2,1)S(1)}, bf16[4,64,1024]{2,1,0:T(8,128)(2,1)S(1)}, u32[]{:S(2)}, u32[]{:S(2)}) collective-permute-start(bf16[4,64,1024]{2,1,0:T(8,128)(2,1)S(1)} %all-to-all-done), channel_id=1, source_target_pairs={{0,64},{64,0},{1,65},{65,1},{2,66},{66,2},{3,67},{67,3},{4,68},{68... | collective-permute-start | bytes 1572872 | tf_op jit(solution)/shard_map/ppermute | solution.py:14
  32.9 0.2 and_reduce_fusion.1
  33.2 0.7 select_reduce_fusion.3
  38.7 8.8 %collective-permute-start.1 = (bf16[128,1024]{1,0:T(8,128)(2,1)S(1)}, bf16[128,1024]{1,0:T(8,128)(2,1)S(1)}, u32[]{:S(2)}, u32[]{:S(2)}) collective-permute-start(bf16[128,1024]{1,0:T(8,128)(2,1)S(1)} %pad_maximum_fusion.refs_0_), channel_id=1, source_target_pairs={{0,1},{1,2},{2,3},{3,0},{4,5},{5,6},{6,7},{7,4},{8,9},{9,10},{10,1... | collective-permute-start | bytes 786440 | tf_op jit(solution)/shard_map/ppermute | solution.py:14
  47.6 3.4 %collective-permute-start.3 = (bf16[128,1024]{1,0:T(8,128)(2,1)S(1)}, bf16[128,1024]{1,0:T(8,128)(2,1)S(1)}, u32[]{:S(2)}, u32[]{:S(2)}) collective-permute-start(bf16[128,1024]{1,0:T(8,128)(2,1)S(1)} %pad_maximum_fusion.refs_0_), channel_id=1, source_target_pairs={{0,3},{1,0},{2,1},{3,2},{4,7},{5,4},{6,5},{7,6},{8,11},{9,8},{10,9... | collective-permute-start | bytes 786440 | tf_op jit(solution)/shard_map/ppermute | solution.py:14
  50.9 19.3 %collective-permute-done.1.refs_2_ = bf16[128,1024]{1,0:T(8,128)(2,1)S(1)} collective-permute-done((bf16[128,1024]{1,0:T(8,128)(2,1)S(1)}, bf16[128,1024]{1,0:T(8,128)(2,1)S(1)}, u32[]{:S(2)}, u32[]{:S(2)}) %collective-permute-start.1) | collective-permute-done | bytes 262176 | tf_op jit(solution)/shard_map/ppermute | solution.py:14
  70.2 7.0 %collective-permute-start.2 = (bf16[64,1024]{1,0:T(8,128)(2,1)S(1)}, bf16[64,1024]{1,0:T(8,128)(2,1)S(1)}, u32[]{:S(2)}, u32[]{:S(2)}) collective-permute-start(bf16[64,1024]{1,0:T(8,128)(2,1)S(1)} %slice.68), channel_id=1, source_target_pairs={{0,1},{1,2},{2,3},{3,0},{4,5},{5,6},{6,7},{7,4},{8,9},{9,10},{10,1... | collective-permute-start | bytes 393224 | tf_op jit(solution)/shard_map/ppermute | solution.py:14
  77.2 3.0 %collective-permute-start.4 = (bf16[64,1024]{1,0:T(8,128)(2,1)S(1)}, bf16[64,1024]{1,0:T(8,128)(2,1)S(1)}, u32[]{:S(2)}, u32[]{:S(2)}) collective-permute-start(bf16[64,1024]{1,0:T(8,128)(2,1)S(1)} %slice.69), channel_id=1, source_target_pairs={{0,3},{1,0},{2,1},{3,2},{4,7},{5,4},{6,5},{7,6},{8,11},{9,8},{10,9... | collective-permute-start | bytes 393224 | tf_op jit(solution)/shard_map/ppermute | solution.py:14
  80.2 8.7 %collective-permute-done.2 = bf16[64,1024]{1,0:T(8,128)(2,1)S(1)} collective-permute-done((bf16[64,1024]{1,0:T(8,128)(2,1)S(1)}, bf16[64,1024]{1,0:T(8,128)(2,1)S(1)}, u32[]{:S(2)}, u32[]{:S(2)}) %collective-permute-start.2) | collective-permute-done | bytes 131104 | tf_op jit(solution)/shard_map/ppermute | solution.py:14
  89.0 7.9 %all-gather.4.cloned.1.call-done = bf16[3584,1024]{1,0:T(8,128)(2,1)} async-done(((bf16[896,1024]{1,0:T(8,128)(2,1)}), bf16[3584,1024]{1,0:T(8,128)(2,1)}) %all-gather.4.cloned.1.call-update) | async-done | bytes 7340048 | tf_op jit(solution)/shard_map/all_gather | solution.py:88
  96.9 3.1 %copy-done = bf16[3584,1024]{1,0:T(8,128)(2,1)S(1)} copy-done((bf16[3584,1024]{1,0:T(8,128)(2,1)S(1)}, bf16[3584,1024]{1,0:T(8,128)(2,1)}, u32[]{:S(2)}) %copy-start) | copy-done | bytes 7340056
  100.0 4.9 %shard_map.55 = bf16[4,96,3584]{2,1,0:T(8,128)(2,1)S(1)} custom-call(bf16[128,1024]{1,0:T(8,128)(2,1)S(1)} %pad_maximum_fusion.1.refs_0_, bf16[128,1024]{1,0:T(8,128)(2,1)S(1)} %collective-permute-done.3.refs_1_, bf16[128,1024]{1,0:T(8,128)(2,1)S(1)} %collective-permute-done.1.refs_2_, bf16[4,2,448,1024]{3,2,1,0:T(8,128)(2,1)S(1)} %bitcast.43), custom_call_target="tpu_custom_call" | custom-call | flops 2818572288 | bytes 10878976 | tf_op jit(solution)/shard_map/pallas_call | solution.py:41
  104.8 36.3 %all_to_all.35.gate_ref.up_ref = bf16[4,96,3584]{2,1,0:T(8,128)(2,1)S(1)} all-to-all(bf16[4,96,3584]{2,1,0:T(8,128)(2,1)S(1)} %shard_map.55), channel_id=1, replica_groups=mesh['zlo'=4,'core'=2,'x'=4,'y'=4,'zhi'=4] {'x'}, dimensions={0} | all-to-all | bytes 5505024 | tf_op jit(solution)/shard_map/all_to_all | solution.py:18
  141.1 1.6 shard_map.56
  142.7 3.5 %all-to-all-start.5 = ((bf16[4,32,1792]{2,1,0:T(8,128)(2,1)}), bf16[4,32,1792]{2,1,0:T(8,128)(2,1)S(1)}, u32[]{:S(2)}, u32[]{:S(2)}) async-start(bf16[4,32,1792]{2,1,0:T(8,128)(2,1)} %get-tuple-element.8), calls=%async_computation.5 | async-start | bytes 917504 | tf_op jit(solution)/shard_map/all_to_all | solution.py:18
  147.4 0.6 compare_and_fusion
  148.2 4.6 %all-to-all-done.5 = bf16[4,32,1792]{2,1,0:T(8,128)(2,1)S(1)} async-done(((bf16[4,32,1792]{2,1,0:T(8,128)(2,1)}), bf16[4,32,1792]{2,1,0:T(8,128)(2,1)S(1)}, u32[]{:S(2)}, u32[]{:S(2)}) %all-to-all-start.5) | async-done | bytes 458784 | tf_op jit(solution)/shard_map/all_to_all | solution.py:18
  152.8 3.5 %all-to-all-start.2 = ((bf16[4,64,1792]{2,1,0:T(8,128)(2,1)}), bf16[4,64,1792]{2,1,0:T(8,128)(2,1)S(1)}, u32[]{:S(2)}, u32[]{:S(2)}) async-start(bf16[4,64,1792]{2,1,0:T(8,128)(2,1)} %get-tuple-element.7), calls=%async_computation.2 | async-start | bytes 1835008 | tf_op jit(solution)/shard_map/all_to_all | solution.py:18
  156.3 0.6 compare_and_fusion.2
  157.1 0.6 select_reduce_fusion.4
  157.7 2.7 %fusion.6 = bf16[128,1024]{1,0:T(8,128)(2,1)S(1)} fusion(bf16[128,1792]{1,0:T(8,128)(2,1)S(1)} %bitcast.46, bf16[1,1792,1024]{2,1,0:T(8,128)(2,1)} %all-gather.6.cloned.1.call-done), kind=kOutput, calls=%fused_computation.6 | convolution fusion | flops 469893120 | bytes 4390912 | tf_op jit(solution)/shard_map/dot_general | solution.py:120
  160.4 7.4 %collective-permute-start.5 = (bf16[64,1024]{1,0:T(8,128)(2,1)S(1)}, bf16[64,1024]{1,0:T(8,128)(2,1)S(1)}, u32[]{:S(2)}, u32[]{:S(2)}) collective-permute-start(bf16[64,1024]{1,0:T(8,128)(2,1)S(1)} %get-tuple-element.25), channel_id=1, source_target_pairs={{0,1},{1,2},{2,3},{3,0},{4,5},{5,6},{6,7},{7,4},{8,9},{9,10},{10,1... | collective-permute-start | bytes 393224 | tf_op jit(solution)/shard_map/ppermute | solution.py:14
  167.8 2.7 %collective-permute-start.7 = (bf16[64,1024]{1,0:T(8,128)(2,1)S(1)}, bf16[64,1024]{1,0:T(8,128)(2,1)S(1)}, u32[]{:S(2)}, u32[]{:S(2)}) collective-permute-start(bf16[64,1024]{1,0:T(8,128)(2,1)S(1)} %get-tuple-element.26), channel_id=1, source_target_pairs={{0,3},{1,0},{2,1},{3,2},{4,7},{5,4},{6,5},{7,6},{8,11},{9,8},{10,9... | collective-permute-start | bytes 393224 | tf_op jit(solution)/shard_map/ppermute | solution.py:14
  170.5 3.1 %copy-done.1 = bf16[3584,1024]{1,0:T(8,128)(2,1)S(1)} copy-done((bf16[3584,1024]{1,0:T(8,128)(2,1)S(1)}, bf16[3584,1024]{1,0:T(8,128)(2,1)}, u32[]{:S(2)}) %copy-start.1) | copy-done | bytes 7340056
  173.5 4.1 %shard_map.57 = bf16[4,32,3584]{2,1,0:T(8,128)(2,1)} custom-call(bf16[128,1024]{1,0:T(8,128)(2,1)S(1)} %pad_maximum_fusion.refs_0_, bf16[4,2,448,1024]{3,2,1,0:T(8,128)(2,1)S(1)} %bitcast.44, bf16[4,64,1792]{2,1,0:T(8,128)(2,1)S(1)} %all-to-all-done.2.refs_2_), custom_call_target="tpu_custom_call" | custom-call | flops 939524096 | bytes 8519680 | tf_op jit(solution)/shard_map/pallas_call | solution.py:41
  177.7 4.2 %all-to-all-start.3 = ((bf16[4,32,3584]{2,1,0:T(8,128)(2,1)}), bf16[4,32,3584]{2,1,0:T(8,128)(2,1)S(1)}, u32[]{:S(2)}, u32[]{:S(2)}) async-start(bf16[4,32,3584]{2,1,0:T(8,128)(2,1)} %shard_map.57), calls=%async_computation.3 | async-start | bytes 1835008 | tf_op jit(solution)/shard_map/all_to_all | solution.py:18
  181.9 3.1 %fusion.14 = (bf16[4,2,32,1024]{3,2,1,0:T(8,128)(2,1)S(1)}, f32[4,2,32,1024]{3,2,1,0:T(8,128)S(1)}) fusion(bf16[4,2,32,1792]{3,2,1,0:T(8,128)(2,1)S(1)} %bitcast.45, bf16[1,1792,1024]{2,1,0:T(8,128)(2,1)} %all-gather.6.cloned.1.call-done), kind=kOutput, calls=%fused_computation.44 | convolution fusion | flops 939786240 | bytes 6160384 | tf_op jit(solution)/shard_map/dot_general | solution.py:120
  185.2 6.6 %collective-permute-start.6 = (bf16[128,1024]{1,0:T(8,128)(2,1)S(1)}, bf16[128,1024]{1,0:T(8,128)(2,1)S(1)}, u32[]{:S(2)}, u32[]{:S(2)}) collective-permute-start(bf16[128,1024]{1,0:T(8,128)(2,1)S(1)} %pad_maximum_fusion.2), channel_id=1, source_target_pairs={{0,1},{1,2},{2,3},{3,0},{4,5},{5,6},{6,7},{7,4},{8,9},{9,10},{10,1... | collective-permute-start | bytes 786440 | tf_op jit(solution)/shard_map/ppermute | solution.py:14
  191.8 1.0 shard_map.58
  192.8 4.2 %all-to-all-start.4 = ((bf16[4,32,1792]{2,1,0:T(8,128)(2,1)}), bf16[4,32,1792]{2,1,0:T(8,128)(2,1)S(1)}, u32[]{:S(2)}, u32[]{:S(2)}) async-start(bf16[4,32,1792]{2,1,0:T(8,128)(2,1)} %shard_map.58), calls=%async_computation.4 | async-start | bytes 917504 | tf_op jit(solution)/shard_map/all_to_all | solution.py:18
  197.1 5.8 %collective-permute-start.8 = (bf16[128,1024]{1,0:T(8,128)(2,1)S(1)}, bf16[128,1024]{1,0:T(8,128)(2,1)S(1)}, u32[]{:S(2)}, u32[]{:S(2)}) collective-permute-start(bf16[128,1024]{1,0:T(8,128)(2,1)S(1)} %pad_maximum_fusion.3), channel_id=1, source_target_pairs={{0,3},{1,0},{2,1},{3,2},{4,7},{5,4},{6,5},{7,6},{8,11},{9,8},{10,9... | collective-permute-start | bytes 786440 | tf_op jit(solution)/shard_map/ppermute | solution.py:14
  202.9 1.0 all-to-all-done.4
  203.9 2.7 %fusion.4 = f32[128,1024]{1,0:T(8,128)S(1)} fusion(bf16[128,1792]{1,0:T(8,128)(2,1)S(1)} %bitcast.47, bf16[1,1792,1024]{2,1,0:T(8,128)(2,1)} %all-gather.6.cloned.1.call-done), kind=kOutput, calls=%fused_computation.4 | convolution fusion | flops 469762048 | bytes 4653056 | tf_op jit(solution)/shard_map/dot_general | solution.py:120
  206.6 20.5 %collective-permute-done.8 = bf16[128,1024]{1,0:T(8,128)(2,1)S(1)} collective-permute-done((bf16[128,1024]{1,0:T(8,128)(2,1)S(1)}, bf16[128,1024]{1,0:T(8,128)(2,1)S(1)}, u32[]{:S(2)}, u32[]{:S(2)}) %collective-permute-start.8) | collective-permute-done | bytes 262176 | tf_op jit(solution)/shard_map/ppermute | solution.py:14
  227.2 1.3 slice_multiply_fusion.1
  228.5 0.2 add_convert_fusion.1
  228.7 3.4 %collective-permute-start.9 = (bf16[4,64,1024]{2,1,0:T(8,128)(2,1)S(1)}, bf16[4,64,1024]{2,1,0:T(8,128)(2,1)S(1)}, u32[]{:S(2)}, u32[]{:S(2)}) collective-permute-start(bf16[4,64,1024]{2,1,0:T(8,128)(2,1)S(1)} %add_convert_fusion.1), channel_id=1, source_target_pairs={{0,64},{64,0},{1,65},{65,1},{2,66},{66,2},{3,67},{67,3},{4,68},{68... | collective-permute-start | bytes 1572872 | tf_op jit(solution)/shard_map/ppermute | solution.py:14
  232.2 0.6 compare_and_fusion.1
  232.8 0.6 compare_and_fusion.3
  233.4 0.3 collective-permute-done.9
  233.7 0.3 add_convert_fusion
  233.9 16.6 %all_to_all.36 = bf16[4,64,1024]{2,1,0:T(8,128)(2,1)S(1)} all-to-all(bf16[4,64,1024]{2,1,0:T(8,128)(2,1)S(1)} %add_convert_fusion), channel_id=1, replica_groups=mesh['zlo'=4,'core'=2,'x'=4,'y'=4,'zhi'=4] {'zlo'}, dimensions={0} | all-to-all | bytes 1048576 | tf_op jit(solution)/shard_map/all_to_all | solution.py:18
  250.6 0.7 reduce_sum.92
  (35 shorter events, 0.8 us)
Async XLA Ops:
  6.5 26.3 %copy-start.2 = (s32[8,2]{0,1:T(2,128)S(1)}, s32[8,2]{0,1:T(2,128)}, u32[]{:S(2)}) copy-start(s32[8,2]{0,1:T(2,128)} %param.6) | copy-start | bytes 196
  6.5 90.3 %all-gather.4.cloned.1.call-start = ((), (), s32[]{:S(2)}) async-start(), calls=%async_computation.7 | async-start | bytes 9175040 | tf_op jit(solution)/shard_map/all_gather | solution.py:88
  9.0 17.3 %all-to-all-start = ((bf16[4,64,1024]{2,1,0:T(8,128)(2,1)}), bf16[4,64,1024]{2,1,0:T(8,128)(2,1)S(1)}, u32[]{:S(2)}, u32[]{:S(2)}) async-start(bf16[4,64,1024]{2,1,0:T(8,128)(2,1)} %broadcast_in_dim.74), calls=%async_computation | async-start | bytes 1048576 | tf_op jit(solution)/shard_map/all_to_all | solution.py:18
  15.5 142.2 %all-gather.6.cloned.1.call-start = ((), (), s32[]{:S(2)}) async-start(), calls=%async_computation.8 | async-start | bytes 4587520 | tf_op jit(solution)/shard_map/all_gather | solution.py:117
  26.3 12.4 %collective-permute-start = (bf16[4,64,1024]{2,1,0:T(8,128)(2,1)S(1)}, bf16[4,64,1024]{2,1,0:T(8,128)(2,1)S(1)}, u32[]{:S(2)}, u32[]{:S(2)}) collective-permute-start(bf16[4,64,1024]{2,1,0:T(8,128)(2,1)S(1)} %all-to-all-done), channel_id=1, source_target_pairs={{0,64},{64,0},{1,65},{65,1},{2,66},{66,2},{3,67},{67,3},{4,68},{68... | collective-permute-start | bytes 1572872 | tf_op jit(solution)/shard_map/ppermute | solution.py:14
  38.7 31.5 %collective-permute-start.1 = (bf16[128,1024]{1,0:T(8,128)(2,1)S(1)}, bf16[128,1024]{1,0:T(8,128)(2,1)S(1)}, u32[]{:S(2)}, u32[]{:S(2)}) collective-permute-start(bf16[128,1024]{1,0:T(8,128)(2,1)S(1)} %pad_maximum_fusion.refs_0_), channel_id=1, source_target_pairs={{0,1},{1,2},{2,3},{3,0},{4,5},{5,6},{6,7},{7,4},{8,9},{9,10},{10,1... | collective-permute-start | bytes 786440 | tf_op jit(solution)/shard_map/ppermute | solution.py:14
  47.6 29.6 %collective-permute-start.3 = (bf16[128,1024]{1,0:T(8,128)(2,1)S(1)}, bf16[128,1024]{1,0:T(8,128)(2,1)S(1)}, u32[]{:S(2)}, u32[]{:S(2)}) collective-permute-start(bf16[128,1024]{1,0:T(8,128)(2,1)S(1)} %pad_maximum_fusion.refs_0_), channel_id=1, source_target_pairs={{0,3},{1,0},{2,1},{3,2},{4,7},{5,4},{6,5},{7,6},{8,11},{9,8},{10,9... | collective-permute-start | bytes 786440 | tf_op jit(solution)/shard_map/ppermute | solution.py:14
  70.2 18.7 %collective-permute-start.2 = (bf16[64,1024]{1,0:T(8,128)(2,1)S(1)}, bf16[64,1024]{1,0:T(8,128)(2,1)S(1)}, u32[]{:S(2)}, u32[]{:S(2)}) collective-permute-start(bf16[64,1024]{1,0:T(8,128)(2,1)S(1)} %slice.68), channel_id=1, source_target_pairs={{0,1},{1,2},{2,3},{3,0},{4,5},{5,6},{6,7},{7,4},{8,9},{9,10},{10,1... | collective-permute-start | bytes 393224 | tf_op jit(solution)/shard_map/ppermute | solution.py:14
  77.2 11.7 %collective-permute-start.4 = (bf16[64,1024]{1,0:T(8,128)(2,1)S(1)}, bf16[64,1024]{1,0:T(8,128)(2,1)S(1)}, u32[]{:S(2)}, u32[]{:S(2)}) collective-permute-start(bf16[64,1024]{1,0:T(8,128)(2,1)S(1)} %slice.69), channel_id=1, source_target_pairs={{0,3},{1,0},{2,1},{3,2},{4,7},{5,4},{6,5},{7,6},{8,11},{9,8},{10,9... | collective-permute-start | bytes 393224 | tf_op jit(solution)/shard_map/ppermute | solution.py:14
  96.9 3.1 %copy-start = (bf16[3584,1024]{1,0:T(8,128)(2,1)S(1)}, bf16[3584,1024]{1,0:T(8,128)(2,1)}, u32[]{:S(2)}) copy-start(bf16[3584,1024]{1,0:T(8,128)(2,1)} %all-gather.4.cloned.1.call-done) | copy-start | bytes 22020100
  141.1 7.0 %copy-start.3 = (f32[8,2]{0,1:T(2,128)S(1)}, f32[8,2]{0,1:T(2,128)}, u32[]{:S(2)}) copy-start(f32[8,2]{0,1:T(2,128)} %param.7) | copy-start | bytes 196
  142.7 10.1 %all-to-all-start.5 = ((bf16[4,32,1792]{2,1,0:T(8,128)(2,1)}), bf16[4,32,1792]{2,1,0:T(8,128)(2,1)S(1)}, u32[]{:S(2)}, u32[]{:S(2)}) async-start(bf16[4,32,1792]{2,1,0:T(8,128)(2,1)} %get-tuple-element.8), calls=%async_computation.5 | async-start | bytes 917504 | tf_op jit(solution)/shard_map/all_to_all | solution.py:18
  152.8 17.7 %all-to-all-start.2 = ((bf16[4,64,1792]{2,1,0:T(8,128)(2,1)}), bf16[4,64,1792]{2,1,0:T(8,128)(2,1)S(1)}, u32[]{:S(2)}, u32[]{:S(2)}) async-start(bf16[4,64,1792]{2,1,0:T(8,128)(2,1)} %get-tuple-element.7), calls=%async_computation.2 | async-start | bytes 1835008 | tf_op jit(solution)/shard_map/all_to_all | solution.py:18
  160.4 24.7 %collective-permute-start.5 = (bf16[64,1024]{1,0:T(8,128)(2,1)S(1)}, bf16[64,1024]{1,0:T(8,128)(2,1)S(1)}, u32[]{:S(2)}, u32[]{:S(2)}) collective-permute-start(bf16[64,1024]{1,0:T(8,128)(2,1)S(1)} %get-tuple-element.25), channel_id=1, source_target_pairs={{0,1},{1,2},{2,3},{3,0},{4,5},{5,6},{6,7},{7,4},{8,9},{9,10},{10,1... | collective-permute-start | bytes 393224 | tf_op jit(solution)/shard_map/ppermute | solution.py:14
  167.8 29.3 %collective-permute-start.7 = (bf16[64,1024]{1,0:T(8,128)(2,1)S(1)}, bf16[64,1024]{1,0:T(8,128)(2,1)S(1)}, u32[]{:S(2)}, u32[]{:S(2)}) collective-permute-start(bf16[64,1024]{1,0:T(8,128)(2,1)S(1)} %get-tuple-element.26), channel_id=1, source_target_pairs={{0,3},{1,0},{2,1},{3,2},{4,7},{5,4},{6,5},{7,6},{8,11},{9,8},{10,9... | collective-permute-start | bytes 393224 | tf_op jit(solution)/shard_map/ppermute | solution.py:14
  170.5 3.1 %copy-start.1 = (bf16[3584,1024]{1,0:T(8,128)(2,1)S(1)}, bf16[3584,1024]{1,0:T(8,128)(2,1)}, u32[]{:S(2)}) copy-start(bf16[3584,1024]{1,0:T(8,128)(2,1)} %all-gather.4.cloned.1.call-done) | copy-start | bytes 22020100
  177.7 14.1 %all-to-all-start.3 = ((bf16[4,32,3584]{2,1,0:T(8,128)(2,1)}), bf16[4,32,3584]{2,1,0:T(8,128)(2,1)S(1)}, u32[]{:S(2)}, u32[]{:S(2)}) async-start(bf16[4,32,3584]{2,1,0:T(8,128)(2,1)} %shard_map.57), calls=%async_computation.3 | async-start | bytes 1835008 | tf_op jit(solution)/shard_map/all_to_all | solution.py:18
  185.2 21.5 %collective-permute-start.6 = (bf16[128,1024]{1,0:T(8,128)(2,1)S(1)}, bf16[128,1024]{1,0:T(8,128)(2,1)S(1)}, u32[]{:S(2)}, u32[]{:S(2)}) collective-permute-start(bf16[128,1024]{1,0:T(8,128)(2,1)S(1)} %pad_maximum_fusion.2), channel_id=1, source_target_pairs={{0,1},{1,2},{2,3},{3,0},{4,5},{5,6},{6,7},{7,4},{8,9},{9,10},{10,1... | collective-permute-start | bytes 786440 | tf_op jit(solution)/shard_map/ppermute | solution.py:14
  192.8 11.1 %all-to-all-start.4 = ((bf16[4,32,1792]{2,1,0:T(8,128)(2,1)}), bf16[4,32,1792]{2,1,0:T(8,128)(2,1)S(1)}, u32[]{:S(2)}, u32[]{:S(2)}) async-start(bf16[4,32,1792]{2,1,0:T(8,128)(2,1)} %shard_map.58), calls=%async_computation.4 | async-start | bytes 917504 | tf_op jit(solution)/shard_map/all_to_all | solution.py:18
  197.1 30.0 %collective-permute-start.8 = (bf16[128,1024]{1,0:T(8,128)(2,1)S(1)}, bf16[128,1024]{1,0:T(8,128)(2,1)S(1)}, u32[]{:S(2)}, u32[]{:S(2)}) collective-permute-start(bf16[128,1024]{1,0:T(8,128)(2,1)S(1)} %pad_maximum_fusion.3), channel_id=1, source_target_pairs={{0,3},{1,0},{2,1},{3,2},{4,7},{5,4},{6,5},{7,6},{8,11},{9,8},{10,9... | collective-permute-start | bytes 786440 | tf_op jit(solution)/shard_map/ppermute | solution.py:14
  228.7 4.9 %collective-permute-start.9 = (bf16[4,64,1024]{2,1,0:T(8,128)(2,1)S(1)}, bf16[4,64,1024]{2,1,0:T(8,128)(2,1)S(1)}, u32[]{:S(2)}, u32[]{:S(2)}) collective-permute-start(bf16[4,64,1024]{2,1,0:T(8,128)(2,1)S(1)} %add_convert_fusion.1), channel_id=1, source_target_pairs={{0,64},{64,0},{1,65},{65,1},{2,66},{66,2},{3,67},{67,3},{4,68},{68... | collective-permute-start | bytes 1572872 | tf_op jit(solution)/shard_map/ppermute | solution.py:14
Sparse Core Ops, SparseCore 0:
  9.5 87.3 all-gather.3
  99.0 52.4 all-gather.5

commit v3 on v2

v3 whole, which is shorter than its diff:
```python
import jax
import jax.numpy as jnp
from jax import lax
from jax.experimental import pallas as pl
from jax.experimental.pallas import tpu as pltpu
from jax.sharding import Mesh, PartitionSpec as P

wide = jnp.float32
half = jnp.bfloat16
LIMIT = 60 * 2**20
ANY = pl.BlockSpec(memory_space=pl.ANY)


def shift(a, axis, by):
    n = lax.axis_size(axis)
    return lax.ppermute(a, axis, [(i, (i + by) % n) for i in range(n)])


def onward(a, axis):
    n = lax.axis_size(axis)
    return lax.ppermute(
        a, ("core", axis), [(c * n + i, c * n + (i + 1 - 2 * c) % n) for c in range(2) for i in range(n)]
    )


def swap(a, axis):
    return lax.all_to_all(a, axis, split_axis=0, concat_axis=0, tiled=True)


def hold(a, after):
    def kernel(a_ref, after_ref, out_ref, sem):
        copy = pltpu.make_async_copy(a_ref, out_ref, sem)
        copy.start()
        copy.wait()

    return pl.pallas_call(
        kernel,
        in_specs=[ANY, ANY],
        out_specs=ANY,
        out_shape=jax.ShapeDtypeStruct(a.shape, a.dtype),
        scratch_shapes=[pltpu.SemaphoreType.DMA],
        compiler_params=pltpu.CompilerParams(vmem_limit_bytes=LIMIT),
        cost_estimate=pl.CostEstimate(flops=0, bytes_accessed=4 * a.size, transcendentals=0),
    )(a, after)


def gate_up(pieces, weights, after=None):
    n = len(pieces)
    rows = 128 * n

    def kernel(*refs):
        w_refs, out_ref, x_ref = refs[n : n + 4], refs[-2], refs[-1]

        @pl.when(pl.program_id(0) == 0)
        def _():
            for j in range(4):
                for i in range(n):
                    x_ref[pl.ds(32 * (j * n + i), 32), :] = refs[i][pl.ds(32 * j, 32), :]

        for p in range(2):
            w = jnp.concatenate([w_refs[2 * p][...], w_refs[2 * p + 1][...]])
            out = lax.dot_general(x_ref[...], w, (((1,), (1,)), ((), ())), preferred_element_type=wide)
            out_ref[:, :, pl.ds(896 * p, 896)] = out.astype(half).reshape(4, 32 * n, 896)

    whole = pl.BlockSpec((128, 1024), lambda i: (0, 0))
    extra = [] if after is None else [after]
    return pl.pallas_call(
        kernel,
        grid=(2,),
        in_specs=[whole] * n + [pl.BlockSpec((448, 1024), lambda i: (i, 0))] * 4 + [ANY] * len(extra),
        out_specs=pl.BlockSpec((4, 32 * n, 1792), lambda i: (0, 0, i)),
        out_shape=jax.ShapeDtypeStruct((4, 32 * n, 3584), half),
        scratch_shapes=[pltpu.VMEM((rows, 1024), half)],
        compiler_params=pltpu.CompilerParams(vmem_limit_bytes=LIMIT),
        cost_estimate=pl.CostEstimate(
            flops=2 * rows * 1024 * 3584, bytes_accessed=3584 * 2048 + rows * 9216, transcendentals=0
        ),
    )(*pieces, *weights, *extra)


def activate(sums, *after):
    rows = sums.shape[1]

    def kernel(gate_ref, up_ref, *refs):
        out_ref = refs[-1]
        gate = jnp.sum(gate_ref[...].astype(wide), axis=0)
        up = jnp.sum(up_ref[...].astype(wide), axis=0)
        hidden = (gate / (1.0 + jnp.exp(-gate)) * up).astype(half)
        for j in range(4):
            out_ref[j] = hidden

    return pl.pallas_call(
        kernel,
        grid=(2,),
        in_specs=[
            pl.BlockSpec((4, rows, 896), lambda i: (0, 0, i)),
            pl.BlockSpec((4, rows, 896), lambda i: (0, 0, i + 2)),
        ]
        + [ANY] * len(after),
        out_specs=pl.BlockSpec((4, rows, 896), lambda i: (0, 0, i)),
        out_shape=jax.ShapeDtypeStruct((4, rows, 1792), half),
        compiler_params=pltpu.CompilerParams(vmem_limit_bytes=LIMIT),
        cost_estimate=pl.CostEstimate(
            flops=rows * 1792 * 12, bytes_accessed=rows * 3584 * 12, transcendentals=rows * 1792
        ),
    )(sums, sums, *after)


def down(hidden, weights, types):
    n = len(types)

    def kernel(*refs):
        hidden_ref, v_refs, outs = refs[0], refs[1:5], refs[5:]
        v = jnp.concatenate([ref[...] for ref in v_refs])
        for i, out in enumerate(outs):
            rows = hidden_ref[:, pl.ds(32 * i, 32), :].reshape(128, 1792)
            out[...] = jnp.dot(rows, v, preferred_element_type=wide).astype(out.dtype)

    return pl.pallas_call(
        kernel,
        grid=(2,),
        in_specs=[pl.BlockSpec((4, 32 * n, 1792), lambda i: (0, 0, 0))]
        + [pl.BlockSpec((448, 512), lambda i: (0, i))] * 4,
        out_specs=[pl.BlockSpec((128, 512), lambda i: (0, i))] * n,
        out_shape=[jax.ShapeDtypeStruct((128, 1024), t) for t in types],
        compiler_params=pltpu.CompilerParams(vmem_limit_bytes=LIMIT),
        cost_estimate=pl.CostEstimate(
            flops=2 * n * 128 * 1792 * 1024, bytes_accessed=1792 * 2048 + n * 128 * 8192, transcendentals=0
        ),
    )(hidden, *weights)


def on_device(tokens, routes, route_gates, w_in, w_down):
    core = lax.axis_index("core")
    zlo = lax.axis_index("zlo")
    expert = zlo * 2 + core

    mine = [tokens[0]] + [shift(tokens[0], "zlo", d) for d in (1, 2, 3)]
    w_own = jnp.transpose(w_in[0], (1, 2, 0)).reshape(896, 1024)
    weights = [w_own] + [shift(w_own, "y", d) for d in (1, 2, 3)]

    matches = routes[:, :, None] == jnp.arange(8, dtype=jnp.int32)[None, None, :]
    hit = jnp.sum(matches.astype(jnp.int32), axis=1)
    slot = jnp.cumsum(hit, axis=0) - hit
    weight = jnp.sum(route_gates[:, :, None] * matches.astype(wide), axis=1)
    names = jnp.arange(8, dtype=jnp.int32)

    def places(e):
        taken = lax.dynamic_index_in_dim(hit, e, 1, keepdims=False)
        place = lax.dynamic_index_in_dim(slot, e, 1, keepdims=False)
        chosen = [(taken == 1) & (place == k) for k in range(2)]
        owner = [jnp.sum(jnp.where(c, names >> 1, 0)) for c in chosen]
        side = [jnp.sum(jnp.where(c, names & 1, 0)) for c in chosen]
        return chosen, owner, side

    chosen, owner, side = places(expert)
    _, owner_too, _ = places(expert + 1 - 2 * core)
    gates = lax.dynamic_index_in_dim(weight, expert, 1, keepdims=False)
    scales = [jnp.sum(jnp.where(c, gates, 0.0)) for c in chosen]

    def taking(owners):
        out = []
        for z in owners:
            away = (zlo - z) & 3
            near = jnp.where(away == 0, mine[0], mine[1])
            out.append(jnp.where(away < 2, near, jnp.where(away == 2, mine[2], mine[3])))
        return out

    other = shift(jnp.concatenate(taking(owner_too)), "core", 1)
    rows = jnp.concatenate(
        [jnp.where(side[k] == core, a, other[64 * k : 64 * k + 64]) for k, a in enumerate(taking(owner))]
    )

    above = shift(rows, "zhi", -1)
    below = shift(rows, "zhi", 1)
    far = onward(jnp.where(core == 0, below, above), "zhi")

    part = gate_up([far, above, below], weights)
    v_own = hold(w_down[0], part)
    v_all = [v_own] + [shift(v_own, "y", d) for d in (1, 2, 3)]
    hidden = swap(activate(swap(part, "x"), v_all[1], v_all[3]), "x")
    far_out, above_out, below_out = down(hidden, v_all, (half, wide, wide))
    got = onward(far_out, "zhi").astype(wide)
    up = shift((above_out + jnp.where(core == 0, got, 0.0)).astype(half), "zhi", 1)
    back = shift((below_out + jnp.where(core == 1, got, 0.0)).astype(half), "zhi", -1)

    own = swap(gate_up([rows], weights, far_out), "x")
    own = swap(activate(own), "x")
    (own_out,) = down(own, v_all, (wide,))
    result = own_out + up.astype(wide) + back.astype(wide)

    def toward(away, parity):
        z = (zlo + away) & 3
        return sum(
            jnp.where((owner[k] == z) & (side[k] == parity), scales[k] * result[64 * k : 64 * k + 64], 0.0)
            for k in range(2)
        )

    got = shift(jnp.concatenate([toward(d, 1 - core).astype(half) for d in range(4)]), "core", 1)
    going = [toward(d, core) + got[64 * d : 64 * d + 64].astype(wide) for d in range(4)]
    total = going[0]
    for d in (1, 2, 3):
        total = total + shift(going[d].astype(half), "zlo", d).astype(wide)
    return total.astype(half)[None]


def solution(mesh):
    fine = Mesh(mesh.devices.reshape(4, 2, 4, 4, 4), ("zlo", "core", "x", "y", "zhi"))
    seqs, pos = ("zlo", "core"), ("y", "zhi")
    return jax.shard_map(
        on_device,
        mesh=fine,
        in_specs=(
            P(seqs, pos, "x"),
            P(),
            P(),
            P(seqs, "x", None, pos),
            P(seqs, pos, "x"),
        ),
        out_specs=P(seqs, pos, "x"),
        check_vma=False,
    )
```

time: 259 us -> 302 us (1.17)
  blocking collectives: 52.9 us -> 0 us
  Pallas kernels: 11.6 us -> 55.4 us
  waiting for transfers between devices: 73.9 us -> 116 us
  starting transfers between devices: 76.3 us -> 101 us
  between operations: 19.8 us -> 10.5 us
  matrix products: 8.51 us -> 0 us
  other arithmetic: 6.86 us -> 11.1 us
    ppermute x10 -> x18, waiting for transfers between devices: 48.8 us -> 107 us  [shift(): return lax.ppermute(a, axis, [(i, (i + by) % n) for i in range(n)])]
    all_to_all x2 -> x0, blocking collectives: 52.9 us -> none  [swap(): return lax.all_to_all(a, axis, split_axis=0, concat_axis=0, tiled=True)]
    pallas_call x2 -> x5, Pallas kernels: 8.97 us -> 50.4 us  [the longest x1 28.9 us: hold(): pl.pallas_call(kernel, in_specs=[ANY, ANY], out_specs=ANY, out_shape=jax....]
    all_to_all x5 -> x4, waiting for transfers between devices: 15.8 us -> 0.01 us  [swap(): return lax.all_to_all(a, axis, split_axis=0, concat_axis=0, tiled=True)]
    ppermute x0 -> x2, starting transfers between devices: none -> 15 us  [onward(): lax.ppermute(a, ('core', axis), [(c * n + i, c * n + (i + 1 - 2 * c) % n)...]
    ppermute x10 -> x18, starting transfers between devices: 54.5 us -> 69.2 us  [shift(): return lax.ppermute(a, axis, [(i, (i + by) % n) for i in range(n)])]
    ppermute x0 -> x2, waiting for transfers between devices: none -> 9.54 us  [onward(): lax.ppermute(a, ('core', axis), [(c * n + i, c * n + (i + 1 - 2 * c) % n)...]
    dot_general x3 -> x0, matrix products: 8.51 us -> none  [down(): return jnp.dot(hidden.reshape(-1, 1792), v_all, preferred_element_type=wide)]
  transfers between devices with their start and end apart: 17 -> 24, of which waited for: 8 -> 12; matrix products, arithmetic and copies ran while one was open for 6% -> 2% of each run, Pallas kernels for 4% -> 11%
where the time goes in v3:
time: 302 us; the launch traced here: 300 us
  waiting for transfers between devices  116 us (38%)
  starting transfers between devices  101 us (33%)
  Pallas kernels  55.4 us (18%)
  other arithmetic  11.1 us (4%)
  between operations  10.5 us (3%)
  local copies, waits for them, and re-layouts  6.46 us (2%)
    ppermute x18, waiting for transfers between devices, shift(): return lax.ppermute(a, axis, [(i, (i + by) % n) for i in range(n)])  107 us
    ppermute x18, starting transfers between devices, shift(): return lax.ppermute(a, axis, [(i, (i + by) % n) for i in range(n)])  69.2 us
    pallas_call x1, Pallas kernels, hold(): pl.pallas_call(kernel, in_specs=[ANY, ANY], out_specs=ANY, out_shape=jax....  28.9 us
    all_to_all x4, starting transfers between devices, swap(): return lax.all_to_all(a, axis, split_axis=0, concat_axis=0, tiled=True)  16.6 us
    ppermute x2, starting transfers between devices, onward(): lax.ppermute(a, ('core', axis), [(c * n + i, c * n + (i + 1 - 2 * c) % n)...  15 us
    pallas_call x2, Pallas kernels, gate_up(): pl.pallas_call(kernel, grid=(2,), in_specs=[whole] * n + [pl.BlockSpec((4...  13.4 us
    ppermute x2, waiting for transfers between devices, onward(): lax.ppermute(a, ('core', axis), [(c * n + i, c * n + (i + 1 - 2 * c) % n)...  9.54 us
    pallas_call x2, Pallas kernels, down(): pl.pallas_call(kernel, grid=(2,), in_specs=[pl.BlockSpec((4, 32 * n, 1792...  8.14 us
  transfers between devices with their start and end apart: 24, of which 12 were waited for; matrix products, arithmetic and copies ran while one was open for 2% of the time, Pallas kernels for 11%

profile of v3, /device:TPU:1, one launch (start us, length us, event | category | flops | bytes accessed | tf_op | source)
XLA Modules:
  0.0 300.5 jit_solution(6077349514138382852)
XLA Ops:
  0.0 5.7 %collective-permute-start.1 = (bf16[64,1024]{1,0:T(8,128)(2,1)}, bf16[64,1024]{1,0:T(8,128)(2,1)S(1)}, u32[]{:S(2)}, u32[]{:S(2)}) collective-permute-start(bf16[64,1024]{1,0:T(8,128)(2,1)} %bitcast.19), channel_id=1, source_target_pairs={{0,256},{128,384},{256,0},{384,128},{1,257},{129,385},{257,1},{385... | collective-permute-start | bytes 393224 | tf_op jit(solution)/shard_map/ppermute | solution.py:16
  5.7 3.3 %collective-permute-start.2 = (bf16[64,1024]{1,0:T(8,128)(2,1)}, bf16[64,1024]{1,0:T(8,128)(2,1)S(1)}, u32[]{:S(2)}, u32[]{:S(2)}) collective-permute-start(bf16[64,1024]{1,0:T(8,128)(2,1)} %bitcast.20), channel_id=1, source_target_pairs={{0,384},{128,0},{256,128},{384,256},{1,385},{129,1},{257,129},{385... | collective-permute-start | bytes 393224 | tf_op jit(solution)/shard_map/ppermute | solution.py:16
  9.0 2.2 collective-permute-start
  11.2 3.2 %collective-permute-start.4 = (bf16[896,1024]{1,0:T(8,128)(2,1)}, bf16[896,1024]{1,0:T(8,128)(2,1)S(1)}, u32[]{:S(2)}, u32[]{:S(2)}) collective-permute-start(bf16[896,1024]{1,0:T(8,128)(2,1)} %bitcast.13), channel_id=1, source_target_pairs={{0,4},{4,8},{8,12},{12,0},{1,5},{5,9},{9,13},{13,1},{2,6},{6,10},{... | collective-permute-start | bytes 5505032 | tf_op jit(solution)/shard_map/ppermute | solution.py:16
  14.4 4.5 %collective-permute-start.5 = (bf16[896,1024]{1,0:T(8,128)(2,1)}, bf16[896,1024]{1,0:T(8,128)(2,1)}, u32[]{:S(2)}, u32[]{:S(2)}) collective-permute-start(bf16[896,1024]{1,0:T(8,128)(2,1)} %bitcast.14), channel_id=1, source_target_pairs={{0,8},{4,12},{8,0},{12,4},{1,9},{5,13},{9,1},{13,5},{2,10},{6,14},... | collective-permute-start | bytes 5505032 | tf_op jit(solution)/shard_map/ppermute | solution.py:16
  21.4 3.0 collective-permute-start.6
  26.8 4.1 %collective-permute-start.3 = (bf16[128,1024]{1,0:T(8,128)(2,1)S(1)}, bf16[128,1024]{1,0:T(8,128)(2,1)S(1)}, u32[]{:S(2)}, u32[]{:S(2)}) collective-permute-start(bf16[128,1024]{1,0:T(8,128)(2,1)S(1)} %pad_maximum_fusion.1), channel_id=1, source_target_pairs={{0,64},{64,0},{1,65},{65,1},{2,66},{66,2},{3,67},{67,3},{4,68},{68... | collective-permute-start | bytes 786440 | tf_op jit(solution)/shard_map/ppermute | solution.py:16
  34.4 8.8 %collective-permute-start.7 = (bf16[128,1024]{1,0:T(8,128)(2,1)S(1)}, bf16[128,1024]{1,0:T(8,128)(2,1)S(1)}, u32[]{:S(2)}, u32[]{:S(2)}) collective-permute-start(bf16[128,1024]{1,0:T(8,128)(2,1)S(1)} %pad_maximum_fusion.2.refs_0_), channel_id=1, source_target_pairs={{0,1},{1,2},{2,3},{3,0},{4,5},{5,6},{6,7},{7,4},{8,9},{9,10},{10,1... | collective-permute-start | bytes 786440 | tf_op jit(solution)/shard_map/ppermute | solution.py:16
  43.3 3.8 %collective-permute-start.8 = (bf16[128,1024]{1,0:T(8,128)(2,1)S(1)}, bf16[128,1024]{1,0:T(8,128)(2,1)S(1)}, u32[]{:S(2)}, u32[]{:S(2)}) collective-permute-start(bf16[128,1024]{1,0:T(8,128)(2,1)S(1)} %pad_maximum_fusion.2.refs_0_), channel_id=1, source_target_pairs={{0,3},{1,0},{2,1},{3,2},{4,7},{5,4},{6,5},{7,6},{8,11},{9,8},{10,9... | collective-permute-start | bytes 786440 | tf_op jit(solution)/shard_map/ppermute | solution.py:16
  47.0 6.1 %collective-permute-done.7.refs_2_ = bf16[128,1024]{1,0:T(8,128)(2,1)S(1)} collective-permute-done((bf16[128,1024]{1,0:T(8,128)(2,1)S(1)}, bf16[128,1024]{1,0:T(8,128)(2,1)S(1)}, u32[]{:S(2)}, u32[]{:S(2)}) %collective-permute-start.7) | collective-permute-done | bytes 262176 | tf_op jit(solution)/shard_map/ppermute | solution.py:16
  53.2 18.8 %collective-permute-done.8.refs_1_ = bf16[128,1024]{1,0:T(8,128)(2,1)S(1)} collective-permute-done((bf16[128,1024]{1,0:T(8,128)(2,1)S(1)}, bf16[128,1024]{1,0:T(8,128)(2,1)S(1)}, u32[]{:S(2)}, u32[]{:S(2)}) %collective-permute-start.8) | collective-permute-done | bytes 262176 | tf_op jit(solution)/shard_map/ppermute | solution.py:16
  72.0 4.2 %collective-permute-start.9 = (bf16[128,1024]{1,0:T(8,128)(2,1)S(1)}, bf16[128,1024]{1,0:T(8,128)(2,1)S(1)}, u32[]{:S(2)}, u32[]{:S(2)}) collective-permute-start(bf16[128,1024]{1,0:T(8,128)(2,1)S(1)} %broadcast_select_fusion), channel_id=1, source_target_pairs={{0,1},{1,2},{2,3},{3,0},{64,67},{65,64},{66,65},{67,66},{4,5},{5,6... | collective-permute-start | bytes 786440 | tf_op jit(solution)/shard_map/ppermute | solution.py:21
  76.3 9.5 %collective-permute-done.9.refs_0_ = bf16[128,1024]{1,0:T(8,128)(2,1)S(1)} collective-permute-done((bf16[128,1024]{1,0:T(8,128)(2,1)S(1)}, bf16[128,1024]{1,0:T(8,128)(2,1)S(1)}, u32[]{:S(2)}, u32[]{:S(2)}) %collective-permute-start.9) | collective-permute-done | bytes 262176 | tf_op jit(solution)/shard_map/ppermute | solution.py:21
  85.8 9.6 %collective-permute-done.5.refs_5_.refs_3_ = bf16[896,1024]{1,0:T(8,128)(2,1)} collective-permute-done((bf16[896,1024]{1,0:T(8,128)(2,1)}, bf16[896,1024]{1,0:T(8,128)(2,1)}, u32[]{:S(2)}, u32[]{:S(2)}) %collective-permute-start.5) | collective-permute-done | bytes 1835040 | tf_op jit(solution)/shard_map/ppermute | solution.py:16
  95.4 2.1 collective-permute-done.6.refs_6_.refs_4_
  97.5 7.3 %shard_map.55.after_ref = bf16[4,96,3584]{2,1,0:T(8,128)(2,1)} custom-call(bf16[128,1024]{1,0:T(8,128)(2,1)} %copy-done.14, bf16[128,1024]{1,0:T(8,128)(2,1)} %copy-done.9, bf16[128,1024]{1,0:T(8,128)(2,1)} %copy-done.8, bf16[896,1024]{1,0:T(8,128)(2,1)} %bitcast.16, bf16[896,1024]{1,0:T(8,128)(2,1)} %copy-done.2, ...), custom_call_target="tpu_custom_call" | custom-call | flops 2818572288 | bytes 10878976 | tf_op jit(solution)/shard_map/pallas_call | solution.py:67
  104.8 4.0 %all-to-all-start = ((bf16[4,96,3584]{2,1,0:T(8,128)(2,1)}), bf16[4,96,3584]{2,1,0:T(8,128)(2,1)S(1)}, u32[]{:S(2)}, u32[]{:S(2)}) async-start(bf16[4,96,3584]{2,1,0:T(8,128)(2,1)} %shard_map.55.after_ref), calls=%async_computation | async-start | bytes 5505024 | tf_op jit(solution)/shard_map/all_to_all | solution.py:27
  108.8 28.9 %shard_map.56.refs_1_ = bf16[448,1024]{1,0:T(8,128)(2,1)} custom-call(bf16[448,1024]{1,0:T(8,128)(2,1)} %bitcast.18, bf16[4,96,3584]{2,1,0:T(8,128)(2,1)} %shard_map.55.after_ref), custom_call_target="tpu_custom_call" | custom-call | bytes 1835008 | tf_op jit(solution)/shard_map/pallas_call | solution.py:36
  137.7 5.2 %collective-permute-start.10 = (bf16[448,1024]{1,0:T(8,128)(2,1)}, bf16[448,1024]{1,0:T(8,128)(2,1)S(1)}, u32[]{:S(2)}, u32[]{:S(2)}) collective-permute-start(bf16[448,1024]{1,0:T(8,128)(2,1)} %shard_map.56.refs_1_), channel_id=1, source_target_pairs={{0,4},{4,8},{8,12},{12,0},{1,5},{5,9},{9,13},{13,1},{2,6},{6,10},{... | collective-permute-start | bytes 2752520 | tf_op jit(solution)/shard_map/ppermute | solution.py:16
  142.9 2.1 collective-permute-start.11
  145.0 17.6 %collective-permute-done.10.refs_0_.refs_2_ = bf16[448,1024]{1,0:T(8,128)(2,1)S(1)} collective-permute-done((bf16[448,1024]{1,0:T(8,128)(2,1)}, bf16[448,1024]{1,0:T(8,128)(2,1)S(1)}, u32[]{:S(2)}, u32[]{:S(2)}) %collective-permute-start.10) | collective-permute-done | bytes 917536 | tf_op jit(solution)/shard_map/ppermute | solution.py:16
  163.5 2.4 collective-permute-done.11.refs_1_.refs_4_
  165.9 1.5 copy-done
  167.4 2.9 shard_map.57
  170.3 4.1 %all-to-all-start.1 = ((bf16[4,96,1792]{2,1,0:T(8,128)(2,1)}), bf16[4,96,1792]{2,1,0:T(8,128)(2,1)S(1)}, u32[]{:S(2)}, u32[]{:S(2)}) async-start(bf16[4,96,1792]{2,1,0:T(8,128)(2,1)} %shard_map.57), calls=%async_computation.1 | async-start | bytes 2752512 | tf_op jit(solution)/shard_map/all_to_all | solution.py:27
  174.4 3.2 %collective-permute-start.12 = (bf16[448,1024]{1,0:T(8,128)(2,1)S(1)}, bf16[448,1024]{1,0:T(8,128)(2,1)S(1)}, u32[]{:S(2)}, u32[]{:S(2)}) collective-permute-start(bf16[448,1024]{1,0:T(8,128)(2,1)S(1)} %copy-done.4), channel_id=1, source_target_pairs={{0,8},{4,12},{8,0},{12,4},{1,9},{5,13},{9,1},{13,5},{2,10},{6,14},... | collective-permute-start | bytes 2752520 | tf_op jit(solution)/shard_map/ppermute | solution.py:16
  177.7 19.4 %collective-permute-done.12.refs_3_ = bf16[448,1024]{1,0:T(8,128)(2,1)S(1)} collective-permute-done((bf16[448,1024]{1,0:T(8,128)(2,1)S(1)}, bf16[448,1024]{1,0:T(8,128)(2,1)S(1)}, u32[]{:S(2)}, u32[]{:S(2)}) %collective-permute-start.12) | collective-permute-done | bytes 917536 | tf_op jit(solution)/shard_map/ppermute | solution.py:16
  199.1 4.7 %shard_map.58 = (bf16[128,1024]{1,0:T(8,128)(2,1)}, f32[128,1024]{1,0:T(8,128)}, f32[128,1024]{1,0:T(8,128)}) custom-call(bf16[4,96,1792]{2,1,0:T(8,128)(2,1)} %copy-done.6, bf16[448,1024]{1,0:T(8,128)(2,1)} %shard_map.56.refs_1_, bf16[448,1024]{1,0:T(8,128)(2,1)} %copy-done.3, bf16[448,1024]{1,0:T(8,128)(2,1)} %copy-done.10, ...), custom_call_target="tpu_custom_call" | custom-call | flops 1409286144 | bytes 6815744 | tf_op jit(solution)/shard_map/pallas_call | solution.py:119
  203.9 6.0 %shard_map.59 = bf16[4,32,3584]{2,1,0:T(8,128)(2,1)} custom-call(bf16[128,1024]{1,0:T(8,128)(2,1)} %copy-done.7, bf16[896,1024]{1,0:T(8,128)(2,1)} %bitcast.17, bf16[896,1024]{1,0:T(8,128)(2,1)} %copy-done.2, bf16[896,1024]{1,0:T(8,128)(2,1)} %collective-permute-done.5.refs_5_.refs_3_, bf16[896,1024]{1,0:T(8,128)(2,1)} %collective-permute-done.6.refs_6_.refs_4_, ...), custom_call_target="tpu_custom_call" | custom-call | flops 939524096 | bytes 8519680 | tf_op jit(solution)/shard_map/pallas_call | solution.py:67
  209.9 4.1 %all-to-all-start.2 = ((bf16[4,32,3584]{2,1,0:T(8,128)(2,1)}), bf16[4,32,3584]{2,1,0:T(8,128)(2,1)S(1)}, u32[]{:S(2)}, u32[]{:S(2)}) async-start(bf16[4,32,3584]{2,1,0:T(8,128)(2,1)} %shard_map.59), calls=%async_computation.2 | async-start | bytes 1835008 | tf_op jit(solution)/shard_map/all_to_all | solution.py:27
  214.0 10.8 %collective-permute-start.13 = (bf16[128,1024]{1,0:T(8,128)(2,1)S(1)}, bf16[128,1024]{1,0:T(8,128)(2,1)S(1)}, u32[]{:S(2)}, u32[]{:S(2)}) collective-permute-start(bf16[128,1024]{1,0:T(8,128)(2,1)S(1)} %copy-done.13), channel_id=1, source_target_pairs={{0,1},{1,2},{2,3},{3,0},{64,67},{65,64},{66,65},{67,66},{4,5},{5,6... | collective-permute-start | bytes 786440 | tf_op jit(solution)/shard_map/ppermute | solution.py:21
  232.0 2.1 shard_map.60
  234.1 4.4 %all-to-all-start.3 = ((bf16[4,32,1792]{2,1,0:T(8,128)(2,1)}), bf16[4,32,1792]{2,1,0:T(8,128)(2,1)S(1)}, u32[]{:S(2)}, u32[]{:S(2)}) async-start(bf16[4,32,1792]{2,1,0:T(8,128)(2,1)} %shard_map.60), calls=%async_computation.3 | async-start | bytes 917504 | tf_op jit(solution)/shard_map/all_to_all | solution.py:27
  238.6 5.1 %collective-permute-start.15 = (bf16[128,1024]{1,0:T(8,128)(2,1)S(1)}, bf16[128,1024]{1,0:T(8,128)(2,1)S(1)}, u32[]{:S(2)}, u32[]{:S(2)}) collective-permute-start(bf16[128,1024]{1,0:T(8,128)(2,1)S(1)} %get-tuple-element.35), channel_id=1, source_target_pairs={{0,3},{1,0},{2,1},{3,2},{4,7},{5,4},{6,5},{7,6},{8,11},{9,8},{10,9... | collective-permute-start | bytes 786440 | tf_op jit(solution)/shard_map/ppermute | solution.py:16
  243.7 4.0 %collective-permute-start.14 = (bf16[128,1024]{1,0:T(8,128)(2,1)S(1)}, bf16[128,1024]{1,0:T(8,128)(2,1)S(1)}, u32[]{:S(2)}, u32[]{:S(2)}) collective-permute-start(bf16[128,1024]{1,0:T(8,128)(2,1)S(1)} %get-tuple-element.34), channel_id=1, source_target_pairs={{0,1},{1,2},{2,3},{3,0},{4,5},{5,6},{6,7},{7,4},{8,9},{9,10},{10,1... | collective-permute-start | bytes 786440 | tf_op jit(solution)/shard_map/ppermute | solution.py:16
  249.6 3.4 %shard_map.61 = f32[128,1024]{1,0:T(8,128)} custom-call(bf16[4,32,1792]{2,1,0:T(8,128)(2,1)} %copy-done.5, bf16[448,1024]{1,0:T(8,128)(2,1)} %shard_map.56.refs_1_, bf16[448,1024]{1,0:T(8,128)(2,1)} %copy-done.3, bf16[448,1024]{1,0:T(8,128)(2,1)} %copy-done.10, bf16[448,1024]{1,0:T(8,128)(2,1)} %collective-permute-done.11.refs_1_.refs_4_), custom_call_target="tpu_custom_call" | custom-call | flops 469762048 | bytes 4718592 | tf_op jit(solution)/shard_map/pallas_call | solution.py:119
  253.0 8.3 %collective-permute-done.15 = bf16[128,1024]{1,0:T(8,128)(2,1)S(1)} collective-permute-done((bf16[128,1024]{1,0:T(8,128)(2,1)S(1)}, bf16[128,1024]{1,0:T(8,128)(2,1)S(1)}, u32[]{:S(2)}, u32[]{:S(2)}) %collective-permute-start.15) | collective-permute-done | bytes 262176 | tf_op jit(solution)/shard_map/ppermute | solution.py:16
  261.2 12.5 %collective-permute-done.14 = bf16[128,1024]{1,0:T(8,128)(2,1)S(1)} collective-permute-done((bf16[128,1024]{1,0:T(8,128)(2,1)S(1)}, bf16[128,1024]{1,0:T(8,128)(2,1)S(1)}, u32[]{:S(2)}, u32[]{:S(2)}) %collective-permute-start.14) | collective-permute-done | bytes 262176 | tf_op jit(solution)/shard_map/ppermute | solution.py:16
  273.8 1.1 convert_add_fusion
  274.9 1.3 add_convert_fusion.7
  276.3 2.4 collective-permute-start.16
  278.7 1.5 collective-permute-done.16
  280.2 1.3 add_convert_fusion.3
  281.6 4.5 %collective-permute-start.19 = (bf16[64,1024]{1,0:T(8,128)(2,1)S(1)}, bf16[64,1024]{1,0:T(8,128)(2,1)S(1)}, u32[]{:S(2)}, u32[]{:S(2)}) collective-permute-start(bf16[64,1024]{1,0:T(8,128)(2,1)S(1)} %get-tuple-element.24), channel_id=1, source_target_pairs={{0,384},{128,0},{256,128},{384,256},{1,385},{129,1},{257,129},{385... | collective-permute-start | bytes 393224 | tf_op jit(solution)/shard_map/ppermute | solution.py:16
  286.0 1.9 collective-permute-start.18
  288.0 2.2 collective-permute-start.17
  290.2 8.3 %collective-permute-done.18 = bf16[64,1024]{1,0:T(8,128)(2,1)S(1)} collective-permute-done((bf16[64,1024]{1,0:T(8,128)(2,1)S(1)}, bf16[64,1024]{1,0:T(8,128)(2,1)S(1)}, u32[]{:S(2)}, u32[]{:S(2)}) %collective-permute-start.18) | collective-permute-done | bytes 131104 | tf_op jit(solution)/shard_map/ppermute | solution.py:16
  298.5 2.0 fusion.4
  (62 shorter events, 10.3 us)
Async XLA Ops:
  0.0 21.4 %collective-permute-start.1 = (bf16[64,1024]{1,0:T(8,128)(2,1)}, bf16[64,1024]{1,0:T(8,128)(2,1)S(1)}, u32[]{:S(2)}, u32[]{:S(2)}) collective-permute-start(bf16[64,1024]{1,0:T(8,128)(2,1)} %bitcast.19), channel_id=1, source_target_pairs={{0,256},{128,384},{256,0},{384,128},{1,257},{129,385},{257,1},{385... | collective-permute-start | bytes 393224 | tf_op jit(solution)/shard_map/ppermute | solution.py:16
  5.7 20.1 %collective-permute-start.2 = (bf16[64,1024]{1,0:T(8,128)(2,1)}, bf16[64,1024]{1,0:T(8,128)(2,1)S(1)}, u32[]{:S(2)}, u32[]{:S(2)}) collective-permute-start(bf16[64,1024]{1,0:T(8,128)(2,1)} %bitcast.20), channel_id=1, source_target_pairs={{0,384},{128,0},{256,128},{384,256},{1,385},{129,1},{257,129},{385... | collective-permute-start | bytes 393224 | tf_op jit(solution)/shard_map/ppermute | solution.py:16
  9.0 16.8 %collective-permute-start = (bf16[64,1024]{1,0:T(8,128)(2,1)}, bf16[64,1024]{1,0:T(8,128)(2,1)S(1)}, u32[]{:S(2)}, u32[]{:S(2)}) collective-permute-start(bf16[64,1024]{1,0:T(8,128)(2,1)} %bitcast.21), channel_id=1, source_target_pairs={{0,128},{128,256},{256,384},{384,0},{1,129},{129,257},{257,385},{3... | collective-permute-start | bytes 393224 | tf_op jit(solution)/shard_map/ppermute | solution.py:16
  11.2 74.6 %collective-permute-start.4 = (bf16[896,1024]{1,0:T(8,128)(2,1)}, bf16[896,1024]{1,0:T(8,128)(2,1)S(1)}, u32[]{:S(2)}, u32[]{:S(2)}) collective-permute-start(bf16[896,1024]{1,0:T(8,128)(2,1)} %bitcast.13), channel_id=1, source_target_pairs={{0,4},{4,8},{8,12},{12,0},{1,5},{5,9},{9,13},{13,1},{2,6},{6,10},{... | collective-permute-start | bytes 5505032 | tf_op jit(solution)/shard_map/ppermute | solution.py:16
  14.4 80.9 %collective-permute-start.5 = (bf16[896,1024]{1,0:T(8,128)(2,1)}, bf16[896,1024]{1,0:T(8,128)(2,1)}, u32[]{:S(2)}, u32[]{:S(2)}) collective-permute-start(bf16[896,1024]{1,0:T(8,128)(2,1)} %bitcast.14), channel_id=1, source_target_pairs={{0,8},{4,12},{8,0},{12,4},{1,9},{5,13},{9,1},{13,5},{2,10},{6,14},... | collective-permute-start | bytes 5505032 | tf_op jit(solution)/shard_map/ppermute | solution.py:16
  21.4 76.0 %collective-permute-start.6 = (bf16[896,1024]{1,0:T(8,128)(2,1)}, bf16[896,1024]{1,0:T(8,128)(2,1)}, u32[]{:S(2)}, u32[]{:S(2)}) collective-permute-start(bf16[896,1024]{1,0:T(8,128)(2,1)} %bitcast.15), channel_id=1, source_target_pairs={{0,12},{4,0},{8,4},{12,8},{1,13},{5,1},{9,5},{13,9},{2,14},{6,2},{... | collective-permute-start | bytes 5505032 | tf_op jit(solution)/shard_map/ppermute | solution.py:16
  26.8 6.6 %collective-permute-start.3 = (bf16[128,1024]{1,0:T(8,128)(2,1)S(1)}, bf16[128,1024]{1,0:T(8,128)(2,1)S(1)}, u32[]{:S(2)}, u32[]{:S(2)}) collective-permute-start(bf16[128,1024]{1,0:T(8,128)(2,1)S(1)} %pad_maximum_fusion.1), channel_id=1, source_target_pairs={{0,64},{64,0},{1,65},{65,1},{2,66},{66,2},{3,67},{67,3},{4,68},{68... | collective-permute-start | bytes 786440 | tf_op jit(solution)/shard_map/ppermute | solution.py:16
  34.4 70.4 %copy-start.7 = (bf16[128,1024]{1,0:T(8,128)(2,1)}, bf16[128,1024]{1,0:T(8,128)(2,1)S(1)}, u32[]{:S(2)}) copy-start(bf16[128,1024]{1,0:T(8,128)(2,1)S(1)} %pad_maximum_fusion.2.refs_0_) | copy-start | bytes 786436
  34.4 18.7 %collective-permute-start.7 = (bf16[128,1024]{1,0:T(8,128)(2,1)S(1)}, bf16[128,1024]{1,0:T(8,128)(2,1)S(1)}, u32[]{:S(2)}, u32[]{:S(2)}) collective-permute-start(bf16[128,1024]{1,0:T(8,128)(2,1)S(1)} %pad_maximum_fusion.2.refs_0_), channel_id=1, source_target_pairs={{0,1},{1,2},{2,3},{3,0},{4,5},{5,6},{6,7},{7,4},{8,9},{9,10},{10,1... | collective-permute-start | bytes 786440 | tf_op jit(solution)/shard_map/ppermute | solution.py:16
  43.3 28.7 %collective-permute-start.8 = (bf16[128,1024]{1,0:T(8,128)(2,1)S(1)}, bf16[128,1024]{1,0:T(8,128)(2,1)S(1)}, u32[]{:S(2)}, u32[]{:S(2)}) collective-permute-start(bf16[128,1024]{1,0:T(8,128)(2,1)S(1)} %pad_maximum_fusion.2.refs_0_), channel_id=1, source_target_pairs={{0,3},{1,0},{2,1},{3,2},{4,7},{5,4},{6,5},{7,6},{8,11},{9,8},{10,9... | collective-permute-start | bytes 786440 | tf_op jit(solution)/shard_map/ppermute | solution.py:16
  53.2 44.3 %copy-start.8 = (bf16[128,1024]{1,0:T(8,128)(2,1)}, bf16[128,1024]{1,0:T(8,128)(2,1)S(1)}, u32[]{:S(2)}) copy-start(bf16[128,1024]{1,0:T(8,128)(2,1)S(1)} %collective-permute-done.7.refs_2_) | copy-start | bytes 786436
  72.0 25.5 %copy-start.9 = (bf16[128,1024]{1,0:T(8,128)(2,1)}, bf16[128,1024]{1,0:T(8,128)(2,1)S(1)}, u32[]{:S(2)}) copy-start(bf16[128,1024]{1,0:T(8,128)(2,1)S(1)} %collective-permute-done.8.refs_1_) | copy-start | bytes 786436
  72.0 13.8 %collective-permute-start.9 = (bf16[128,1024]{1,0:T(8,128)(2,1)S(1)}, bf16[128,1024]{1,0:T(8,128)(2,1)S(1)}, u32[]{:S(2)}, u32[]{:S(2)}) collective-permute-start(bf16[128,1024]{1,0:T(8,128)(2,1)S(1)} %broadcast_select_fusion), channel_id=1, source_target_pairs={{0,1},{1,2},{2,3},{3,0},{64,67},{65,64},{66,65},{67,66},{4,5},{5,6... | collective-permute-start | bytes 786440 | tf_op jit(solution)/shard_map/ppermute | solution.py:21
  85.8 11.7 %copy-start.14 = (bf16[128,1024]{1,0:T(8,128)(2,1)}, bf16[128,1024]{1,0:T(8,128)(2,1)S(1)}, u32[]{:S(2)}) copy-start(bf16[128,1024]{1,0:T(8,128)(2,1)S(1)} %collective-permute-done.9.refs_0_) | copy-start | bytes 786436
  85.8 11.7 %copy-start.2 = (bf16[896,1024]{1,0:T(8,128)(2,1)}, bf16[896,1024]{1,0:T(8,128)(2,1)S(1)}, u32[]{:S(2)}) copy-start(bf16[896,1024]{1,0:T(8,128)(2,1)S(1)} %collective-permute-done.4.refs_4_.refs_2_) | copy-start | bytes 5505028
  104.8 61.1 %all-to-all-start = ((bf16[4,96,3584]{2,1,0:T(8,128)(2,1)}), bf16[4,96,3584]{2,1,0:T(8,128)(2,1)S(1)}, u32[]{:S(2)}, u32[]{:S(2)}) async-start(bf16[4,96,3584]{2,1,0:T(8,128)(2,1)} %shard_map.55.after_ref), calls=%async_computation | async-start | bytes 5505024 | tf_op jit(solution)/shard_map/all_to_all | solution.py:27
  137.7 24.8 %collective-permute-start.10 = (bf16[448,1024]{1,0:T(8,128)(2,1)}, bf16[448,1024]{1,0:T(8,128)(2,1)S(1)}, u32[]{:S(2)}, u32[]{:S(2)}) collective-permute-start(bf16[448,1024]{1,0:T(8,128)(2,1)} %shard_map.56.refs_1_), channel_id=1, source_target_pairs={{0,4},{4,8},{8,12},{12,0},{1,5},{5,9},{9,13},{13,1},{2,6},{6,10},{... | collective-permute-start | bytes 2752520 | tf_op jit(solution)/shard_map/ppermute | solution.py:16
  142.9 23.0 %collective-permute-start.11 = (bf16[448,1024]{1,0:T(8,128)(2,1)}, bf16[448,1024]{1,0:T(8,128)(2,1)}, u32[]{:S(2)}, u32[]{:S(2)}) collective-permute-start(bf16[448,1024]{1,0:T(8,128)(2,1)} %shard_map.56.refs_1_), channel_id=1, source_target_pairs={{0,12},{4,0},{8,4},{12,8},{1,13},{5,1},{9,5},{13,9},{2,14},{6,2},{... | collective-permute-start | bytes 2752520 | tf_op jit(solution)/shard_map/ppermute | solution.py:16
  162.6 0.9 copy-start.3
  165.9 1.5 copy-start
  170.3 4.1 %copy-start.4 = (bf16[448,1024]{1,0:T(8,128)(2,1)S(1)}, bf16[448,1024]{1,0:T(8,128)(2,1)}, u32[]{:S(2)}) copy-start(bf16[448,1024]{1,0:T(8,128)(2,1)} %shard_map.56.refs_1_) | copy-start | bytes 2752516
  170.3 26.8 %all-to-all-start.1 = ((bf16[4,96,1792]{2,1,0:T(8,128)(2,1)}), bf16[4,96,1792]{2,1,0:T(8,128)(2,1)S(1)}, u32[]{:S(2)}, u32[]{:S(2)}) async-start(bf16[4,96,1792]{2,1,0:T(8,128)(2,1)} %shard_map.57), calls=%async_computation.1 | async-start | bytes 2752512 | tf_op jit(solution)/shard_map/all_to_all | solution.py:27
  174.4 22.7 %collective-permute-start.12 = (bf16[448,1024]{1,0:T(8,128)(2,1)S(1)}, bf16[448,1024]{1,0:T(8,128)(2,1)S(1)}, u32[]{:S(2)}, u32[]{:S(2)}) collective-permute-start(bf16[448,1024]{1,0:T(8,128)(2,1)S(1)} %copy-done.4), channel_id=1, source_target_pairs={{0,8},{4,12},{8,0},{12,4},{1,9},{5,13},{9,1},{13,5},{2,10},{6,14},... | collective-permute-start | bytes 2752520 | tf_op jit(solution)/shard_map/ppermute | solution.py:16
  197.1 0.9 copy-start.10
  198.0 1.1 copy-start.6
  209.9 4.1 %copy-start.13 = (bf16[128,1024]{1,0:T(8,128)(2,1)S(1)}, bf16[128,1024]{1,0:T(8,128)(2,1)}, u32[]{:S(2)}) copy-start(bf16[128,1024]{1,0:T(8,128)(2,1)} %get-tuple-element.8.refs_5_) | copy-start | bytes 786436
  209.9 21.1 %all-to-all-start.2 = ((bf16[4,32,3584]{2,1,0:T(8,128)(2,1)}), bf16[4,32,3584]{2,1,0:T(8,128)(2,1)S(1)}, u32[]{:S(2)}, u32[]{:S(2)}) async-start(bf16[4,32,3584]{2,1,0:T(8,128)(2,1)} %shard_map.59), calls=%async_computation.2 | async-start | bytes 1835008 | tf_op jit(solution)/shard_map/all_to_all | solution.py:27
  214.0 24.4 %copy-start.11 = (f32[128,1024]{1,0:T(8,128)S(1)}, f32[128,1024]{1,0:T(8,128)}, u32[]{:S(2)}) copy-start(f32[128,1024]{1,0:T(8,128)} %get-tuple-element.9) | copy-start | bytes 1572868
  214.0 24.4 %copy-start.12 = (f32[128,1024]{1,0:T(8,128)S(1)}, f32[128,1024]{1,0:T(8,128)}, u32[]{:S(2)}) copy-start(f32[128,1024]{1,0:T(8,128)} %get-tuple-element.10) | copy-start | bytes 1572868
  214.0 24.4 %collective-permute-start.13 = (bf16[128,1024]{1,0:T(8,128)(2,1)S(1)}, bf16[128,1024]{1,0:T(8,128)(2,1)S(1)}, u32[]{:S(2)}, u32[]{:S(2)}) collective-permute-start(bf16[128,1024]{1,0:T(8,128)(2,1)S(1)} %copy-done.13), channel_id=1, source_target_pairs={{0,1},{1,2},{2,3},{3,0},{64,67},{65,64},{66,65},{67,66},{4,5},{5,6... | collective-permute-start | bytes 786440 | tf_op jit(solution)/shard_map/ppermute | solution.py:21
  231.1 0.9 copy-start.1
  234.1 13.7 %copy-start.15 = (s32[8,2]{0,1:T(2,128)S(1)}, s32[8,2]{0,1:T(2,128)}, u32[]{:S(2)}) copy-start(s32[8,2]{0,1:T(2,128)} %param.6) | copy-start | bytes 196
  234.1 13.7 %copy-start.16 = (f32[8,2]{0,1:T(2,128)S(1)}, f32[8,2]{0,1:T(2,128)}, u32[]{:S(2)}) copy-start(f32[8,2]{0,1:T(2,128)} %param.7) | copy-start | bytes 196
  234.1 14.7 %all-to-all-start.3 = ((bf16[4,32,1792]{2,1,0:T(8,128)(2,1)}), bf16[4,32,1792]{2,1,0:T(8,128)(2,1)S(1)}, u32[]{:S(2)}, u32[]{:S(2)}) async-start(bf16[4,32,1792]{2,1,0:T(8,128)(2,1)} %shard_map.60), calls=%async_computation.3 | async-start | bytes 917504 | tf_op jit(solution)/shard_map/all_to_all | solution.py:27
  238.6 22.7 %collective-permute-start.15 = (bf16[128,1024]{1,0:T(8,128)(2,1)S(1)}, bf16[128,1024]{1,0:T(8,128)(2,1)S(1)}, u32[]{:S(2)}, u32[]{:S(2)}) collective-permute-start(bf16[128,1024]{1,0:T(8,128)(2,1)S(1)} %get-tuple-element.35), channel_id=1, source_target_pairs={{0,3},{1,0},{2,1},{3,2},{4,7},{5,4},{6,5},{7,6},{8,11},{9,8},{10,9... | collective-permute-start | bytes 786440 | tf_op jit(solution)/shard_map/ppermute | solution.py:16
  243.7 30.0 %collective-permute-start.14 = (bf16[128,1024]{1,0:T(8,128)(2,1)S(1)}, bf16[128,1024]{1,0:T(8,128)(2,1)S(1)}, u32[]{:S(2)}, u32[]{:S(2)}) collective-permute-start(bf16[128,1024]{1,0:T(8,128)(2,1)S(1)} %get-tuple-element.34), channel_id=1, source_target_pairs={{0,1},{1,2},{2,3},{3,0},{4,5},{5,6},{6,7},{7,4},{8,9},{9,10},{10,1... | collective-permute-start | bytes 786440 | tf_op jit(solution)/shard_map/ppermute | solution.py:16
  248.8 0.8 copy-start.5
  276.3 3.9 %collective-permute-start.16 = (bf16[256,1024]{1,0:T(8,128)(2,1)S(1)}, bf16[256,1024]{1,0:T(8,128)(2,1)S(1)}, u32[]{:S(2)}, u32[]{:S(2)}) collective-permute-start(bf16[256,1024]{1,0:T(8,128)(2,1)S(1)} %pad_maximum_fusion), channel_id=1, source_target_pairs={{0,64},{64,0},{1,65},{65,1},{2,66},{66,2},{3,67},{67,3},{4,68},{68... | collective-permute-start | bytes 1572872 | tf_op jit(solution)/shard_map/ppermute | solution.py:16
  281.6 8.6 %collective-permute-start.19 = (bf16[64,1024]{1,0:T(8,128)(2,1)S(1)}, bf16[64,1024]{1,0:T(8,128)(2,1)S(1)}, u32[]{:S(2)}, u32[]{:S(2)}) collective-permute-start(bf16[64,1024]{1,0:T(8,128)(2,1)S(1)} %get-tuple-element.24), channel_id=1, source_target_pairs={{0,384},{128,0},{256,128},{384,256},{1,385},{129,1},{257,129},{385... | collective-permute-start | bytes 393224 | tf_op jit(solution)/shard_map/ppermute | solution.py:16
  286.0 12.5 %collective-permute-start.18 = (bf16[64,1024]{1,0:T(8,128)(2,1)S(1)}, bf16[64,1024]{1,0:T(8,128)(2,1)S(1)}, u32[]{:S(2)}, u32[]{:S(2)}) collective-permute-start(bf16[64,1024]{1,0:T(8,128)(2,1)S(1)} %get-tuple-element.25), channel_id=1, source_target_pairs={{0,256},{128,384},{256,0},{384,128},{1,257},{129,385},{257,1},{385... | collective-permute-start | bytes 393224 | tf_op jit(solution)/shard_map/ppermute | solution.py:16
  288.0 10.5 %collective-permute-start.17 = (bf16[64,1024]{1,0:T(8,128)(2,1)S(1)}, bf16[64,1024]{1,0:T(8,128)(2,1)S(1)}, u32[]{:S(2)}, u32[]{:S(2)}) collective-permute-start(bf16[64,1024]{1,0:T(8,128)(2,1)S(1)} %get-tuple-element.23), channel_id=1, source_target_pairs={{0,128},{128,256},{256,384},{384,0},{1,129},{129,257},{257,385},{3... | collective-permute-start | bytes 393224 | tf_op jit(solution)/shard_map/ppermute | solution.py:16

commit v4 on v3

v4 whole, which is shorter than its diff:
```python
import jax
import jax.numpy as jnp
from jax import lax
from jax.experimental import pallas as pl
from jax.experimental.pallas import tpu as pltpu
from jax.sharding import Mesh, PartitionSpec as P

wide = jnp.float32
half = jnp.bfloat16
LIMIT = 60 * 2**20
COST = pl.CostEstimate(flops=1024, bytes_accessed=1024, transcendentals=0)
ANY = pl.BlockSpec(memory_space=pl.ANY)


def shift(a, axis, by):
    n = lax.axis_size(axis)
    return lax.ppermute(a, axis, [(i, (i + by) % n) for i in range(n)])


def onward(a, axis):
    n = lax.axis_size(axis)
    return lax.ppermute(
        a, ("core", axis), [(c * n + i, c * n + (i + 1 - 2 * c) % n) for c in range(2) for i in range(n)]
    )


def swap(a, axis):
    return lax.all_to_all(a, axis, split_axis=0, concat_axis=0, tiled=True)


def pick(first, second, after):
    rows = first.shape[0] // 7

    def kernel(a_ref, b_ref, core_ref, after_ref, out_ref):
        out_ref[...] = jnp.where(core_ref[0] == 0, a_ref[...], b_ref[...])

    block = pl.BlockSpec((rows, 1024), lambda i: (i, 0))
    return pl.pallas_call(
        kernel,
        grid=(7,),
        in_specs=[block, block, pl.BlockSpec(memory_space=pltpu.SMEM), ANY],
        out_specs=block,
        out_shape=jax.ShapeDtypeStruct(first.shape, first.dtype),
        compiler_params=pltpu.CompilerParams(vmem_limit_bytes=LIMIT),
        cost_estimate=COST,
    )(first, second, lax.axis_index("core").reshape(1), after)


def hold(a, after):
    def kernel(a_ref, after_ref, out_ref):
        out_ref[...] = a_ref[...]

    block = pl.BlockSpec((a.shape[0] // 4, 1024), lambda i: (i, 0))
    return pl.pallas_call(
        kernel,
        grid=(4,),
        in_specs=[block, ANY],
        out_specs=block,
        out_shape=jax.ShapeDtypeStruct(a.shape, a.dtype),
        compiler_params=pltpu.CompilerParams(vmem_limit_bytes=LIMIT),
        cost_estimate=COST,
    )(a, after)


def early(pieces, weights):
    n = len(pieces)

    def kernel(*refs):
        x = jnp.concatenate([ref[...] for ref in refs[:n]])
        w = [ref[...] for ref in refs[n : n + 3]]
        w = jnp.concatenate([a[:448] for a in w] + [a[448:] for a in w])
        out = lax.dot_general(x, w, (((1,), (1,)), ((), ())), preferred_element_type=wide).astype(half)
        for i in range(n):
            refs[-1][:, pl.ds(32 * i, 32), :] = out[128 * i : 128 * i + 128].reshape(4, 32, 2688)

    return pl.pallas_call(
        kernel,
        out_shape=jax.ShapeDtypeStruct((4, 32 * n, 2688), half),
        compiler_params=pltpu.CompilerParams(vmem_limit_bytes=LIMIT),
        cost_estimate=COST,
    )(*pieces, *weights)


def late(far, pieces, weights, after):
    def kernel(far_ref, *refs):
        out_ref = refs[-1]
        w = [ref[...] for ref in refs[3:7]]
        w_all = jnp.concatenate([a[:448] for a in w] + [a[448:] for a in w])
        dims = (((1,), (1,)), ((), ()))
        out = lax.dot_general(far_ref[...], w_all, dims, preferred_element_type=wide).astype(half)
        out_ref[:, :, :3584] = out.reshape(4, 32, 3584)
        x = jnp.concatenate([ref[...] for ref in refs[:3]])
        out = lax.dot_general(x, w[3], dims, preferred_element_type=wide).astype(half)
        for i in range(3):
            out_ref[:, :, pl.ds(3584 + 896 * i, 896)] = out[128 * i : 128 * i + 128].reshape(4, 32, 896)

    whole = pl.BlockSpec(memory_space=pltpu.VMEM)
    return pl.pallas_call(
        kernel,
        in_specs=[whole] * 8 + [ANY] * len(after),
        out_shape=jax.ShapeDtypeStruct((4, 32, 6272), half),
        compiler_params=pltpu.CompilerParams(vmem_limit_bytes=LIMIT),
        cost_estimate=COST,
    )(far, *pieces, *weights, *after)


def act(gate, up):
    return (gate / (1.0 + jnp.exp(-gate)) * up).astype(half)


def activate_early(sums, after):
    rows = sums.shape[1]

    def kernel(sums_ref, after_ref, out_ref):
        total = jnp.sum(sums_ref[...].astype(wide), axis=0)
        out_ref[...] = act(total[:, :1344], total[:, 1344:])

    return pl.pallas_call(
        kernel,
        in_specs=[pl.BlockSpec(memory_space=pltpu.VMEM), ANY],
        out_shape=jax.ShapeDtypeStruct((rows, 1344), half),
        compiler_params=pltpu.CompilerParams(vmem_limit_bytes=LIMIT),
        cost_estimate=COST,
    )(sums, after)


def activate_late(sums, first):
    def kernel(sums_ref, first_ref, *outs):
        total = jnp.sum(sums_ref[...].astype(wide), axis=0)
        parts = [act(total[:, :1792], total[:, 1792:3584])]
        rest = []
        for i in range(3):
            at = 3584 + 896 * i
            rest.append(act(total[:, at : at + 448], total[:, at + 448 : at + 896]))
        whole = jnp.concatenate([first_ref[...], jnp.concatenate(rest)], axis=1)
        parts += [whole[:64], whole[64:]]
        for part, out in zip(parts, outs):
            for j in range(4):
                out[j] = part

    return pl.pallas_call(
        kernel,
        out_shape=[jax.ShapeDtypeStruct((4, r, 1792), half) for r in (32, 64, 32)],
        compiler_params=pltpu.CompilerParams(vmem_limit_bytes=LIMIT),
        cost_estimate=COST,
    )(sums, first)


def down(hidden, weights, types):
    n = len(types)

    def kernel(*refs):
        hidden_ref, v_refs, outs = refs[0], refs[1:5], refs[5:]
        v = jnp.concatenate([ref[...] for ref in v_refs])
        for i, out in enumerate(outs):
            rows = hidden_ref[:, pl.ds(32 * i, 32), :].reshape(128, 1792)
            out[...] = jnp.dot(rows, v, preferred_element_type=wide).astype(out.dtype)

    return pl.pallas_call(
        kernel,
        grid=(2,),
        in_specs=[pl.BlockSpec((4, 32 * n, 1792), lambda i: (0, 0, 0))]
        + [pl.BlockSpec((448, 512), lambda i: (0, i))] * 4,
        out_specs=[pl.BlockSpec((128, 512), lambda i: (0, i))] * n,
        out_shape=[jax.ShapeDtypeStruct((128, 1024), t) for t in types],
        compiler_params=pltpu.CompilerParams(vmem_limit_bytes=LIMIT),
        cost_estimate=COST,
    )(hidden, *weights)


def on_device(tokens, routes, route_gates, w_in, w_down):
    core = lax.axis_index("core")
    zlo = lax.axis_index("zlo")
    expert = zlo * 2 + core

    mine = [tokens[0]] + [shift(tokens[0], "zlo", d) for d in (1, 2, 3)]
    w_own = jnp.transpose(w_in[0], (1, 2, 0)).reshape(896, 1024)
    w_above = shift(w_own, "y", -1)
    w_below = shift(w_own, "y", 1)
    weights = [w_own, w_above, w_below]

    matches = routes[:, :, None] == jnp.arange(8, dtype=jnp.int32)[None, None, :]
    hit = jnp.sum(matches.astype(jnp.int32), axis=1)
    slot = jnp.cumsum(hit, axis=0) - hit
    weight = jnp.sum(route_gates[:, :, None] * matches.astype(wide), axis=1)
    names = jnp.arange(8, dtype=jnp.int32)

    def places(e):
        taken = lax.dynamic_index_in_dim(hit, e, 1, keepdims=False)
        place = lax.dynamic_index_in_dim(slot, e, 1, keepdims=False)
        chosen = [(taken == 1) & (place == k) for k in range(2)]
        owner = [jnp.sum(jnp.where(c, names >> 1, 0)) for c in chosen]
        side = [jnp.sum(jnp.where(c, names & 1, 0)) for c in chosen]
        return chosen, owner, side

    chosen, owner, side = places(expert)
    _, owner_too, _ = places(expert + 1 - 2 * core)
    gates = lax.dynamic_index_in_dim(weight, expert, 1, keepdims=False)
    scales = [jnp.sum(jnp.where(c, gates, 0.0)) for c in chosen]

    def taking(owners):
        out = []
        for z in owners:
            away = (zlo - z) & 3
            near = jnp.where(away == 0, mine[0], mine[1])
            out.append(jnp.where(away < 2, near, jnp.where(away == 2, mine[2], mine[3])))
        return out

    other = shift(jnp.concatenate(taking(owner_too)), "core", 1)
    rows = jnp.concatenate(
        [jnp.where(side[k] == core, a, other[64 * k : 64 * k + 64]) for k, a in enumerate(taking(owner))]
    )

    above = shift(rows, "zhi", -1)
    below = shift(rows, "zhi", 1)
    v_own = hold(w_down[0], rows)
    v_above = shift(v_own, "y", -1)
    v_below = shift(v_own, "y", 1)
    next_z = jnp.where(core == 0, below, above)
    far = onward(next_z, "zhi")
    w_far = onward(pick(w_below, w_above, next_z), "y")
    part = early([above, below, rows], weights)

    v_far = onward(pick(v_below, v_above, part), "y")
    v_all = [v_own, v_above, v_below, v_far]
    first = activate_early(swap(part, "x"), v_far)
    rest = swap(late(far, [above, below, rows], weights + [w_far], [v_above, v_below]), "x")
    far_h, near_h, own_h = activate_late(rest, first)

    (far_out,) = down(swap(far_h, "x"), v_all, (half,))
    got = onward(far_out, "zhi").astype(wide)
    above_out, below_out = down(swap(near_h, "x"), v_all, (wide, wide))
    up = shift((above_out + jnp.where(core == 0, got, 0.0)).astype(half), "zhi", 1)
    back = shift((below_out + jnp.where(core == 1, got, 0.0)).astype(half), "zhi", -1)

    (own_out,) = down(swap(own_h, "x"), v_all, (wide,))
    result = own_out + up.astype(wide) + back.astype(wide)

    def toward(away, parity):
        z = (zlo + away) & 3
        return sum(
            jnp.where((owner[k] == z) & (side[k] == parity), scales[k] * result[64 * k : 64 * k + 64], 0.0)
            for k in range(2)
        )

    got = shift(jnp.concatenate([toward(d, 1 - core).astype(half) for d in range(4)]), "core", 1)
    going = [toward(d, core) + got[64 * d : 64 * d + 64].astype(wide) for d in range(4)]
    total = going[0]
    for d in (1, 2, 3):
        total = total + shift(going[d].astype(half), "zlo", d).astype(wide)
    return total.astype(half)[None]


def solution(mesh):
    fine = Mesh(mesh.devices.reshape(4, 2, 4, 4, 4), ("zlo", "core", "x", "y", "zhi"))
    seqs, pos = ("zlo", "core"), ("y", "zhi")
    return jax.shard_map(
        on_device,
        mesh=fine,
        in_specs=(
            P(seqs, pos, "x"),
            P(),
            P(),
            P(seqs, "x", None, pos),
            P(seqs, pos, "x"),
        ),
        out_specs=P(seqs, pos, "x"),
        check_vma=False,
    )
```

time: 302 us -> 260 us (0.86)
  waiting for transfers between devices: 116 us -> 65.2 us
  blocking collectives: 0 us -> 10.9 us
  Pallas kernels: 55.4 us -> 45 us
  starting transfers between devices: 101 us -> 110 us
    ppermute x18 -> x16, waiting for transfers between devices: 107 us -> 44.7 us  [shift(): return lax.ppermute(a, axis, [(i, (i + by) % n) for i in range(n)])]
    pallas_call x5 -> x7, Pallas kernels: 47.2 us -> 34.1 us  [the longest x2 10.5 us: pick(): pl.pallas_call(kernel, grid=(7,), in_specs=[block, block, pl.BlockSpec(me...]
    all_to_all x0 -> x1, blocking collectives: none -> 10.9 us  [swap(): return lax.all_to_all(a, axis, split_axis=0, concat_axis=0, tiled=True)]
    ppermute x2 -> x4, waiting for transfers between devices: 9.54 us -> 19.2 us  [onward(): lax.ppermute(a, ('core', axis), [(c * n + i, c * n + (i + 1 - 2 * c) % n)...]
    ppermute x18 -> x16, starting transfers between devices: 69.2 us -> 76 us  [shift(): return lax.ppermute(a, axis, [(i, (i + by) % n) for i in range(n)])]
    ppermute x2 -> x4, starting transfers between devices: 15 us -> 18.2 us  [onward(): lax.ppermute(a, ('core', axis), [(c * n + i, c * n + (i + 1 - 2 * c) % n)...]
    pallas_call x2 -> x3, Pallas kernels: 8.14 us -> 10.9 us  [down(): pl.pallas_call(kernel, grid=(2,), in_specs=[pl.BlockSpec((4, 32 * n, 1792...]
    unnamed x34 -> x26, local copies, waits for them, and re-layouts: 6.27 us -> 3.99 us
  transfers between devices with their start and end apart: 24 -> 24, of which waited for: 12 -> 10; matrix products, arithmetic and copies ran while one was open for 2% -> 3% of each run, Pallas kernels for 11% -> 14%
where the time goes in v4:
time: 260 us; the launch traced here: 258 us
  starting transfers between devices  110 us (42%)
  waiting for transfers between devices  65.2 us (25%)
  Pallas kernels  45 us (17%)
  other arithmetic  13 us (5%)
  blocking collectives  10.9 us (4%)
  between operations  10.4 us (4%)
  local copies, waits for them, and re-layouts  4.17 us (2%)
    ppermute x16, starting transfers between devices, shift(): return lax.ppermute(a, axis, [(i, (i + by) % n) for i in range(n)])  76 us
    ppermute x16, waiting for transfers between devices, shift(): return lax.ppermute(a, axis, [(i, (i + by) % n) for i in range(n)])  44.7 us
    ppermute x4, waiting for transfers between devices, onward(): lax.ppermute(a, ('core', axis), [(c * n + i, c * n + (i + 1 - 2 * c) % n)...  19.2 us
    ppermute x4, starting transfers between devices, onward(): lax.ppermute(a, ('core', axis), [(c * n + i, c * n + (i + 1 - 2 * c) % n)...  18.2 us
    all_to_all x4, starting transfers between devices, swap(): return lax.all_to_all(a, axis, split_axis=0, concat_axis=0, tiled=True)  15.3 us
    pallas_call x3, Pallas kernels, down(): pl.pallas_call(kernel, grid=(2,), in_specs=[pl.BlockSpec((4, 32 * n, 1792...  10.9 us
    all_to_all x1, blocking collectives, swap(): return lax.all_to_all(a, axis, split_axis=0, concat_axis=0, tiled=True)  10.9 us
    pallas_call x2, Pallas kernels, pick(): pl.pallas_call(kernel, grid=(7,), in_specs=[block, block, pl.BlockSpec(me...  10.5 us
  transfers between devices with their start and end apart: 24, of which 10 were waited for; matrix products, arithmetic and copies ran while one was open for 3% of the time, Pallas kernels for 14%

profile of v4, /device:TPU:1, one launch (start us, length us, event | category | flops | bytes accessed | tf_op | source)
XLA Modules:
  0.0 258.3 jit_solution(2624001879385416565)
XLA Ops:
  0.0 5.7 %collective-permute-start.1 = (bf16[64,1024]{1,0:T(8,128)(2,1)}, bf16[64,1024]{1,0:T(8,128)(2,1)S(1)}, u32[]{:S(2)}, u32[]{:S(2)}) collective-permute-start(bf16[64,1024]{1,0:T(8,128)(2,1)} %bitcast.19), channel_id=1, source_target_pairs={{0,256},{128,384},{256,0},{384,128},{1,257},{129,385},{257,1},{385... | collective-permute-start | bytes 393224 | tf_op jit(solution)/shard_map/ppermute | solution.py:17
  5.7 3.3 %collective-permute-start.2 = (bf16[64,1024]{1,0:T(8,128)(2,1)}, bf16[64,1024]{1,0:T(8,128)(2,1)S(1)}, u32[]{:S(2)}, u32[]{:S(2)}) collective-permute-start(bf16[64,1024]{1,0:T(8,128)(2,1)} %bitcast.20), channel_id=1, source_target_pairs={{0,384},{128,0},{256,128},{384,256},{1,385},{129,1},{257,129},{385... | collective-permute-start | bytes 393224 | tf_op jit(solution)/shard_map/ppermute | solution.py:17
  9.0 2.2 collective-permute-start
  11.2 4.6 %collective-permute-start.7 = (bf16[896,1024]{1,0:T(8,128)(2,1)}, bf16[896,1024]{1,0:T(8,128)(2,1)S(1)}, u32[]{:S(2)}, u32[]{:S(2)}) collective-permute-start(bf16[896,1024]{1,0:T(8,128)(2,1)} %bitcast.14), channel_id=1, source_target_pairs={{0,12},{4,0},{8,4},{12,8},{1,13},{5,1},{9,5},{13,9},{2,14},{6,2},{... | collective-permute-start | bytes 5505032 | tf_op jit(solution)/shard_map/ppermute | solution.py:17
  15.9 1.9 collective-permute-start.8
  22.4 4.6 %collective-permute-start.3 = (bf16[128,1024]{1,0:T(8,128)(2,1)S(1)}, bf16[128,1024]{1,0:T(8,128)(2,1)S(1)}, u32[]{:S(2)}, u32[]{:S(2)}) collective-permute-start(bf16[128,1024]{1,0:T(8,128)(2,1)S(1)} %pad_maximum_fusion.1), channel_id=1, source_target_pairs={{0,64},{64,0},{1,65},{65,1},{2,66},{66,2},{3,67},{67,3},{4,68},{68... | collective-permute-start | bytes 786440 | tf_op jit(solution)/shard_map/ppermute | solution.py:17
  30.6 7.7 %collective-permute-start.4 = (bf16[128,1024]{1,0:T(8,128)(2,1)S(1)}, bf16[128,1024]{1,0:T(8,128)(2,1)S(1)}, u32[]{:S(2)}, u32[]{:S(2)}) collective-permute-start(bf16[128,1024]{1,0:T(8,128)(2,1)S(1)} %pad_maximum_fusion.2.after_ref.refs_2_), channel_id=1, source_target_pairs={{0,1},{1,2},{2,3},{3,0},{4,5},{5,6},{6,7},{7,4},{8,9},{9,10},{10,1... | collective-permute-start | bytes 786440 | tf_op jit(solution)/shard_map/ppermute | solution.py:17
  38.3 3.8 %collective-permute-start.5 = (bf16[128,1024]{1,0:T(8,128)(2,1)S(1)}, bf16[128,1024]{1,0:T(8,128)(2,1)S(1)}, u32[]{:S(2)}, u32[]{:S(2)}) collective-permute-start(bf16[128,1024]{1,0:T(8,128)(2,1)S(1)} %pad_maximum_fusion.2.after_ref.refs_2_), channel_id=1, source_target_pairs={{0,3},{1,0},{2,1},{3,2},{4,7},{5,4},{6,5},{7,6},{8,11},{9,8},{10,9... | collective-permute-start | bytes 786440 | tf_op jit(solution)/shard_map/ppermute | solution.py:17
  42.1 6.1 %collective-permute-done.4.refs_1_ = bf16[128,1024]{1,0:T(8,128)(2,1)S(1)} collective-permute-done((bf16[128,1024]{1,0:T(8,128)(2,1)S(1)}, bf16[128,1024]{1,0:T(8,128)(2,1)S(1)}, u32[]{:S(2)}, u32[]{:S(2)}) %collective-permute-start.4) | collective-permute-done | bytes 262176 | tf_op jit(solution)/shard_map/ppermute | solution.py:17
  48.2 18.8 %collective-permute-done.5.refs_0_ = bf16[128,1024]{1,0:T(8,128)(2,1)S(1)} collective-permute-done((bf16[128,1024]{1,0:T(8,128)(2,1)S(1)}, bf16[128,1024]{1,0:T(8,128)(2,1)S(1)}, u32[]{:S(2)}, u32[]{:S(2)}) %collective-permute-start.5) | collective-permute-done | bytes 262176 | tf_op jit(solution)/shard_map/ppermute | solution.py:17
  69.1 5.5 %shard_map.55 = bf16[896,1024]{1,0:T(8,128)(2,1)} custom-call(bf16[896,1024]{1,0:T(8,128)(2,1)} %collective-permute-done.8.a_ref.refs_5_, bf16[896,1024]{1,0:T(8,128)(2,1)} %copy-done.2, s32[1]{0:T(128)} %bitcast.6.core_ref, bf16[128,1024]{1,0:T(8,128)(2,1)} %broadcast_select_fusion.after_ref), custom_call_target="tpu_custom_call" | custom-call | flops 1024 | bytes 1024 | tf_op jit(solution)/shard_map/pallas_call | solution.py:38
  74.6 4.9 %collective-permute-start.9 = (bf16[896,1024]{1,0:T(8,128)(2,1)}, bf16[896,1024]{1,0:T(8,128)(2,1)}, u32[]{:S(2)}, u32[]{:S(2)}) collective-permute-start(bf16[896,1024]{1,0:T(8,128)(2,1)} %shard_map.55), channel_id=1, source_target_pairs={{0,4},{4,8},{8,12},{12,0},{64,76},{68,64},{72,68},{76,72},{1,5},{5... | collective-permute-start | bytes 5505032 | tf_op jit(solution)/shard_map/ppermute | solution.py:22
  79.4 6.6 %shard_map.58.after_ref = bf16[4,96,2688]{2,1,0:T(8,128)(2,1)} custom-call(bf16[128,1024]{1,0:T(8,128)(2,1)} %copy-done.8, bf16[128,1024]{1,0:T(8,128)(2,1)} %copy-done.7, bf16[128,1024]{1,0:T(8,128)(2,1)} %copy-done.5, bf16[896,1024]{1,0:T(8,128)(2,1)} %bitcast.16, bf16[896,1024]{1,0:T(8,128)(2,1)} %copy-done.2, ...), custom_call_target="tpu_custom_call" | custom-call | flops 1024 | bytes 1024 | tf_op jit(solution)/shard_map/pallas_call | solution.py:76
  86.1 4.0 %all-to-all-start.1 = ((bf16[4,96,2688]{2,1,0:T(8,128)(2,1)}), bf16[4,96,2688]{2,1,0:T(8,128)(2,1)S(1)}, u32[]{:S(2)}, u32[]{:S(2)}) async-start(bf16[4,96,2688]{2,1,0:T(8,128)(2,1)} %shard_map.58.after_ref), calls=%async_computation.1 | async-start | bytes 4128768 | tf_op jit(solution)/shard_map/all_to_all | solution.py:28
  90.1 3.3 %shard_map.56.refs_1_ = bf16[448,1024]{1,0:T(8,128)(2,1)} custom-call(bf16[448,1024]{1,0:T(8,128)(2,1)} %bitcast.18, bf16[128,1024]{1,0:T(8,128)(2,1)} %copy-done.5), custom_call_target="tpu_custom_call" | custom-call | flops 1024 | bytes 1024 | tf_op jit(solution)/shard_map/pallas_call | solution.py:54
  93.4 1.9 collective-permute-start.10
  95.3 3.4 %collective-permute-start.11 = (bf16[448,1024]{1,0:T(8,128)(2,1)}, bf16[448,1024]{1,0:T(8,128)(2,1)S(1)}, u32[]{:S(2)}, u32[]{:S(2)}) collective-permute-start(bf16[448,1024]{1,0:T(8,128)(2,1)} %shard_map.56.refs_1_), channel_id=1, source_target_pairs={{0,4},{4,8},{8,12},{12,0},{1,5},{5,9},{9,13},{13,1},{2,6},{6,10},{... | collective-permute-start | bytes 2752520 | tf_op jit(solution)/shard_map/ppermute | solution.py:17
  98.7 4.2 %collective-permute-start.6 = (bf16[128,1024]{1,0:T(8,128)(2,1)}, bf16[128,1024]{1,0:T(8,128)(2,1)S(1)}, u32[]{:S(2)}, u32[]{:S(2)}) collective-permute-start(bf16[128,1024]{1,0:T(8,128)(2,1)} %broadcast_select_fusion.after_ref), channel_id=1, source_target_pairs={{0,1},{1,2},{2,3},{3,0},{64,67},{65,64},{66,65},{67,66},{4,5},{5,6... | collective-permute-start | bytes 786440 | tf_op jit(solution)/shard_map/ppermute | solution.py:22
  102.9 8.5 %collective-permute-done.6.far_ref = bf16[128,1024]{1,0:T(8,128)(2,1)S(1)} collective-permute-done((bf16[128,1024]{1,0:T(8,128)(2,1)}, bf16[128,1024]{1,0:T(8,128)(2,1)S(1)}, u32[]{:S(2)}, u32[]{:S(2)}) %collective-permute-start.6) | collective-permute-done | bytes 262176 | tf_op jit(solution)/shard_map/ppermute | solution.py:22
  111.5 8.1 %collective-permute-done.10.refs_7_.b_ref.refs_2_ = bf16[448,1024]{1,0:T(8,128)(2,1)S(1)} collective-permute-done((bf16[448,1024]{1,0:T(8,128)(2,1)}, bf16[448,1024]{1,0:T(8,128)(2,1)S(1)}, u32[]{:S(2)}, u32[]{:S(2)}) %collective-permute-start.10) | collective-permute-done | bytes 917536 | tf_op jit(solution)/shard_map/ppermute | solution.py:17
  120.8 8.1 %shard_map.57 = bf16[4,32,6272]{2,1,0:T(8,128)(2,1)} custom-call(bf16[128,1024]{1,0:T(8,128)(2,1)} %copy-done.10, bf16[128,1024]{1,0:T(8,128)(2,1)} %copy-done.8, bf16[128,1024]{1,0:T(8,128)(2,1)} %copy-done.7, bf16[128,1024]{1,0:T(8,128)(2,1)} %copy-done.5, bf16[896,1024]{1,0:T(8,128)(2,1)} %bitcast.17, bf16[896,1024]{1,0:T(8,128)(2,1)} %copy-done.2, ...), custom_call_target="tpu_custom_call" | custom-call | flops 1024 | bytes 1024 | tf_op jit(solution)/shard_map/pallas_call | solution.py:98
  128.9 4.3 %all-to-all-start = ((bf16[4,32,6272]{2,1,0:T(8,128)(2,1)}), bf16[4,32,6272]{2,1,0:T(8,128)(2,1)}, u32[]{:S(2)}, u32[]{:S(2)}) async-start(bf16[4,32,6272]{2,1,0:T(8,128)(2,1)} %shard_map.57), calls=%async_computation | async-start | bytes 3211264 | tf_op jit(solution)/shard_map/all_to_all | solution.py:28
  133.3 5.0 %shard_map.59 = bf16[448,1024]{1,0:T(8,128)(2,1)} custom-call(bf16[448,1024]{1,0:T(8,128)(2,1)} %copy-done.1, bf16[448,1024]{1,0:T(8,128)(2,1)} %copy-done, s32[1]{0:T(128)} %bitcast.6.core_ref, bf16[4,96,2688]{2,1,0:T(8,128)(2,1)} %shard_map.58.after_ref), custom_call_target="tpu_custom_call" | custom-call | flops 1024 | bytes 1024 | tf_op jit(solution)/shard_map/pallas_call | solution.py:38
  138.3 4.9 %collective-permute-start.12 = (bf16[448,1024]{1,0:T(8,128)(2,1)}, bf16[448,1024]{1,0:T(8,128)(2,1)S(1)}, u32[]{:S(2)}, u32[]{:S(2)}) collective-permute-start(bf16[448,1024]{1,0:T(8,128)(2,1)} %shard_map.59), channel_id=1, source_target_pairs={{0,4},{4,8},{8,12},{12,0},{64,76},{68,64},{72,68},{76,72},{1,5},{5... | collective-permute-start | bytes 2752520 | tf_op jit(solution)/shard_map/ppermute | solution.py:22
  143.2 10.6 %collective-permute-done.12.after_ref.refs_4_ = bf16[448,1024]{1,0:T(8,128)(2,1)S(1)} collective-permute-done((bf16[448,1024]{1,0:T(8,128)(2,1)}, bf16[448,1024]{1,0:T(8,128)(2,1)S(1)}, u32[]{:S(2)}, u32[]{:S(2)}) %collective-permute-start.12) | collective-permute-done | bytes 917536 | tf_op jit(solution)/shard_map/ppermute | solution.py:22
  154.8 2.7 %shard_map.60.first_ref = bf16[96,1344]{1,0:T(8,128)(2,1)} custom-call(bf16[4,96,2688]{2,1,0:T(8,128)(2,1)} %copy-done.4, bf16[448,1024]{1,0:T(8,128)(2,1)} %copy-done.3), custom_call_target="tpu_custom_call" | custom-call | flops 1024 | bytes 1024 | tf_op jit(solution)/shard_map/pallas_call | solution.py:118
  157.4 2.9 %shard_map.61 = (bf16[4,32,1792]{2,1,0:T(8,128)(2,1)}, bf16[4,64,1792]{2,1,0:T(8,128)(2,1)}, bf16[4,32,1792]{2,1,0:T(8,128)(2,1)}) custom-call(bf16[4,32,6272]{2,1,0:T(8,128)(2,1)} %all-to-all-done.sums_ref, bf16[96,1344]{1,0:T(8,128)(2,1)} %shard_map.60.first_ref), custom_call_target="tpu_custom_call" | custom-call | flops 1024 | bytes 1024 | tf_op jit(solution)/shard_map/pallas_call | solution.py:141
  160.3 10.9 %all_to_all.25.refs_0_ = bf16[4,32,1792]{2,1,0:T(8,128)(2,1)} all-to-all(bf16[4,32,1792]{2,1,0:T(8,128)(2,1)} %get-tuple-element.13), channel_id=1, replica_groups=mesh['zlo'=4,'core'=2,'x'=4,'y'=4,'zhi'=4] {'x'}, dimensions={0} | all-to-all | bytes 917504 | tf_op jit(solution)/shard_map/all_to_all | solution.py:28
  171.2 3.5 %all-to-all-start.3 = ((bf16[4,64,1792]{2,1,0:T(8,128)(2,1)}), bf16[4,64,1792]{2,1,0:T(8,128)(2,1)S(1)}, u32[]{:S(2)}, u32[]{:S(2)}) async-start(bf16[4,64,1792]{2,1,0:T(8,128)(2,1)} %get-tuple-element.11), calls=%async_computation.3 | async-start | bytes 1835008 | tf_op jit(solution)/shard_map/all_to_all | solution.py:28
  174.7 3.4 %shard_map.64 = bf16[128,1024]{1,0:T(8,128)(2,1)} custom-call(bf16[4,32,1792]{2,1,0:T(8,128)(2,1)} %all_to_all.25.refs_0_, bf16[448,1024]{1,0:T(8,128)(2,1)} %shard_map.56.refs_1_, bf16[448,1024]{1,0:T(8,128)(2,1)} %copy-done, bf16[448,1024]{1,0:T(8,128)(2,1)} %copy-done.1, bf16[448,1024]{1,0:T(8,128)(2,1)} %copy-done.3), custom_call_target="tpu_custom_call" | custom-call | flops 1024 | bytes 1024 | tf_op jit(solution)/shard_map/pallas_call | solution.py:159
  178.1 4.2 %collective-permute-start.13 = (bf16[128,1024]{1,0:T(8,128)(2,1)}, bf16[128,1024]{1,0:T(8,128)(2,1)S(1)}, u32[]{:S(2)}, u32[]{:S(2)}) collective-permute-start(bf16[128,1024]{1,0:T(8,128)(2,1)} %shard_map.64), channel_id=1, source_target_pairs={{0,1},{1,2},{2,3},{3,0},{64,67},{65,64},{66,65},{67,66},{4,5},{5,6... | collective-permute-start | bytes 786440 | tf_op jit(solution)/shard_map/ppermute | solution.py:22
  182.3 1.4 all-to-all-done.3.refs_0_
  183.7 3.5 %all-to-all-start.2 = ((bf16[4,32,1792]{2,1,0:T(8,128)(2,1)}), bf16[4,32,1792]{2,1,0:T(8,128)(2,1)S(1)}, u32[]{:S(2)}, u32[]{:S(2)}) async-start(bf16[4,32,1792]{2,1,0:T(8,128)(2,1)} %get-tuple-element.10), calls=%async_computation.2 | async-start | bytes 917504 | tf_op jit(solution)/shard_map/all_to_all | solution.py:28
  187.2 4.1 %shard_map.63 = (f32[128,1024]{1,0:T(8,128)}, f32[128,1024]{1,0:T(8,128)}) custom-call(bf16[4,64,1792]{2,1,0:T(8,128)(2,1)} %copy-done.6, bf16[448,1024]{1,0:T(8,128)(2,1)} %shard_map.56.refs_1_, bf16[448,1024]{1,0:T(8,128)(2,1)} %copy-done, bf16[448,1024]{1,0:T(8,128)(2,1)} %copy-done.1, bf16[448,1024]{1,0:T(8,128)(2,1)} %copy-done.3), custom_call_target="tpu_custom_call" | custom-call | flops 1024 | bytes 1024 | tf_op jit(solution)/shard_map/pallas_call | solution.py:159
  191.3 1.3 fusion.1
  192.7 6.3 %collective-permute-start.15 = (bf16[128,1024]{1,0:T(8,128)(2,1)S(1)}, bf16[128,1024]{1,0:T(8,128)(2,1)S(1)}, u32[]{:S(2)}, u32[]{:S(2)}) collective-permute-start(bf16[128,1024]{1,0:T(8,128)(2,1)S(1)} %get-tuple-element.39), channel_id=1, source_target_pairs={{0,3},{1,0},{2,1},{3,2},{4,7},{5,4},{6,5},{7,6},{8,11},{9,8},{10,9... | collective-permute-start | bytes 786440 | tf_op jit(solution)/shard_map/ppermute | solution.py:17
  199.0 2.9 %collective-permute-start.14 = (bf16[128,1024]{1,0:T(8,128)(2,1)S(1)}, bf16[128,1024]{1,0:T(8,128)(2,1)S(1)}, u32[]{:S(2)}, u32[]{:S(2)}) collective-permute-start(bf16[128,1024]{1,0:T(8,128)(2,1)S(1)} %get-tuple-element.38), channel_id=1, source_target_pairs={{0,1},{1,2},{2,3},{3,0},{4,5},{5,6},{6,7},{7,4},{8,9},{9,10},{10,1... | collective-permute-start | bytes 786440 | tf_op jit(solution)/shard_map/ppermute | solution.py:17
  209.9 3.4 %shard_map.62 = f32[128,1024]{1,0:T(8,128)} custom-call(bf16[4,32,1792]{2,1,0:T(8,128)(2,1)} %copy-done.9, bf16[448,1024]{1,0:T(8,128)(2,1)} %shard_map.56.refs_1_, bf16[448,1024]{1,0:T(8,128)(2,1)} %copy-done, bf16[448,1024]{1,0:T(8,128)(2,1)} %copy-done.1, bf16[448,1024]{1,0:T(8,128)(2,1)} %copy-done.3), custom_call_target="tpu_custom_call" | custom-call | flops 1024 | bytes 1024 | tf_op jit(solution)/shard_map/pallas_call | solution.py:159
  213.3 3.2 %collective-permute-done.14 = bf16[128,1024]{1,0:T(8,128)(2,1)S(1)} collective-permute-done((bf16[128,1024]{1,0:T(8,128)(2,1)S(1)}, bf16[128,1024]{1,0:T(8,128)(2,1)S(1)}, u32[]{:S(2)}, u32[]{:S(2)}) %collective-permute-start.14) | collective-permute-done | bytes 262176 | tf_op jit(solution)/shard_map/ppermute | solution.py:17
  217.7 1.3 add_convert_fusion.7
  219.0 10.0 %collective-permute-start.16 = (bf16[256,1024]{1,0:T(8,128)(2,1)S(1)}, bf16[256,1024]{1,0:T(8,128)(2,1)S(1)}, u32[]{:S(2)}, u32[]{:S(2)}) collective-permute-start(bf16[256,1024]{1,0:T(8,128)(2,1)S(1)} %pad_maximum_fusion), channel_id=1, source_target_pairs={{0,64},{64,0},{1,65},{65,1},{2,66},{66,2},{3,67},{67,3},{4,68},{68... | collective-permute-start | bytes 1572872 | tf_op jit(solution)/shard_map/ppermute | solution.py:17
  229.1 1.5 collective-permute-done.16
  230.6 1.3 add_convert_fusion.3
  231.9 3.0 %collective-permute-start.19 = (bf16[64,1024]{1,0:T(8,128)(2,1)S(1)}, bf16[64,1024]{1,0:T(8,128)(2,1)S(1)}, u32[]{:S(2)}, u32[]{:S(2)}) collective-permute-start(bf16[64,1024]{1,0:T(8,128)(2,1)S(1)} %get-tuple-element.28), channel_id=1, source_target_pairs={{0,384},{128,0},{256,128},{384,256},{1,385},{129,1},{257,129},{385... | collective-permute-start | bytes 393224 | tf_op jit(solution)/shard_map/ppermute | solution.py:17
  235.0 11.2 %collective-permute-start.18 = (bf16[64,1024]{1,0:T(8,128)(2,1)S(1)}, bf16[64,1024]{1,0:T(8,128)(2,1)S(1)}, u32[]{:S(2)}, u32[]{:S(2)}) collective-permute-start(bf16[64,1024]{1,0:T(8,128)(2,1)S(1)} %get-tuple-element.29), channel_id=1, source_target_pairs={{0,256},{128,384},{256,0},{384,128},{1,257},{129,385},{257,1},{385... | collective-permute-start | bytes 393224 | tf_op jit(solution)/shard_map/ppermute | solution.py:17
  246.2 3.4 %collective-permute-start.17 = (bf16[64,1024]{1,0:T(8,128)(2,1)S(1)}, bf16[64,1024]{1,0:T(8,128)(2,1)S(1)}, u32[]{:S(2)}, u32[]{:S(2)}) collective-permute-start(bf16[64,1024]{1,0:T(8,128)(2,1)S(1)} %get-tuple-element.27), channel_id=1, source_target_pairs={{0,128},{128,256},{256,384},{384,0},{1,129},{129,257},{257,385},{3... | collective-permute-start | bytes 393224 | tf_op jit(solution)/shard_map/ppermute | solution.py:17
  249.6 6.7 %collective-permute-done.18 = bf16[64,1024]{1,0:T(8,128)(2,1)S(1)} collective-permute-done((bf16[64,1024]{1,0:T(8,128)(2,1)S(1)}, bf16[64,1024]{1,0:T(8,128)(2,1)S(1)}, u32[]{:S(2)}, u32[]{:S(2)}) %collective-permute-start.18) | collective-permute-done | bytes 131104 | tf_op jit(solution)/shard_map/ppermute | solution.py:17
  256.3 2.0 fusion.4
  (58 shorter events, 11.5 us)
Async XLA Ops:
  0.0 21.4 %collective-permute-start.1 = (bf16[64,1024]{1,0:T(8,128)(2,1)}, bf16[64,1024]{1,0:T(8,128)(2,1)S(1)}, u32[]{:S(2)}, u32[]{:S(2)}) collective-permute-start(bf16[64,1024]{1,0:T(8,128)(2,1)} %bitcast.19), channel_id=1, source_target_pairs={{0,256},{128,384},{256,0},{384,128},{1,257},{129,385},{257,1},{385... | collective-permute-start | bytes 393224 | tf_op jit(solution)/shard_map/ppermute | solution.py:17
  5.7 15.7 %collective-permute-start.2 = (bf16[64,1024]{1,0:T(8,128)(2,1)}, bf16[64,1024]{1,0:T(8,128)(2,1)S(1)}, u32[]{:S(2)}, u32[]{:S(2)}) collective-permute-start(bf16[64,1024]{1,0:T(8,128)(2,1)} %bitcast.20), channel_id=1, source_target_pairs={{0,384},{128,0},{256,128},{384,256},{1,385},{129,1},{257,129},{385... | collective-permute-start | bytes 393224 | tf_op jit(solution)/shard_map/ppermute | solution.py:17
  9.0 12.4 %collective-permute-start = (bf16[64,1024]{1,0:T(8,128)(2,1)}, bf16[64,1024]{1,0:T(8,128)(2,1)S(1)}, u32[]{:S(2)}, u32[]{:S(2)}) collective-permute-start(bf16[64,1024]{1,0:T(8,128)(2,1)} %bitcast.21), channel_id=1, source_target_pairs={{0,128},{128,256},{256,384},{384,0},{1,129},{129,257},{257,385},{3... | collective-permute-start | bytes 393224 | tf_op jit(solution)/shard_map/ppermute | solution.py:17
  11.2 56.6 %collective-permute-start.7 = (bf16[896,1024]{1,0:T(8,128)(2,1)}, bf16[896,1024]{1,0:T(8,128)(2,1)S(1)}, u32[]{:S(2)}, u32[]{:S(2)}) collective-permute-start(bf16[896,1024]{1,0:T(8,128)(2,1)} %bitcast.14), channel_id=1, source_target_pairs={{0,12},{4,0},{8,4},{12,8},{1,13},{5,1},{9,5},{13,9},{2,14},{6,2},{... | collective-permute-start | bytes 5505032 | tf_op jit(solution)/shard_map/ppermute | solution.py:17
  15.9 52.0 %collective-permute-start.8 = (bf16[896,1024]{1,0:T(8,128)(2,1)}, bf16[896,1024]{1,0:T(8,128)(2,1)}, u32[]{:S(2)}, u32[]{:S(2)}) collective-permute-start(bf16[896,1024]{1,0:T(8,128)(2,1)} %bitcast.15), channel_id=1, source_target_pairs={{0,4},{4,8},{8,12},{12,0},{1,5},{5,9},{9,13},{13,1},{2,6},{6,10},{... | collective-permute-start | bytes 5505032 | tf_op jit(solution)/shard_map/ppermute | solution.py:17
  22.4 7.2 %collective-permute-start.3 = (bf16[128,1024]{1,0:T(8,128)(2,1)S(1)}, bf16[128,1024]{1,0:T(8,128)(2,1)S(1)}, u32[]{:S(2)}, u32[]{:S(2)}) collective-permute-start(bf16[128,1024]{1,0:T(8,128)(2,1)S(1)} %pad_maximum_fusion.1), channel_id=1, source_target_pairs={{0,64},{64,0},{1,65},{65,1},{2,66},{66,2},{3,67},{67,3},{4,68},{68... | collective-permute-start | bytes 786440 | tf_op jit(solution)/shard_map/ppermute | solution.py:17
  30.6 44.0 %copy-start.5 = (bf16[128,1024]{1,0:T(8,128)(2,1)}, bf16[128,1024]{1,0:T(8,128)(2,1)S(1)}, u32[]{:S(2)}) copy-start(bf16[128,1024]{1,0:T(8,128)(2,1)S(1)} %pad_maximum_fusion.2.after_ref.refs_2_) | copy-start | bytes 786436
  30.6 17.6 %collective-permute-start.4 = (bf16[128,1024]{1,0:T(8,128)(2,1)S(1)}, bf16[128,1024]{1,0:T(8,128)(2,1)S(1)}, u32[]{:S(2)}, u32[]{:S(2)}) collective-permute-start(bf16[128,1024]{1,0:T(8,128)(2,1)S(1)} %pad_maximum_fusion.2.after_ref.refs_2_), channel_id=1, source_target_pairs={{0,1},{1,2},{2,3},{3,0},{4,5},{5,6},{6,7},{7,4},{8,9},{9,10},{10,1... | collective-permute-start | bytes 786440 | tf_op jit(solution)/shard_map/ppermute | solution.py:17
  38.3 28.7 %collective-permute-start.5 = (bf16[128,1024]{1,0:T(8,128)(2,1)S(1)}, bf16[128,1024]{1,0:T(8,128)(2,1)S(1)}, u32[]{:S(2)}, u32[]{:S(2)}) collective-permute-start(bf16[128,1024]{1,0:T(8,128)(2,1)S(1)} %pad_maximum_fusion.2.after_ref.refs_2_), channel_id=1, source_target_pairs={{0,3},{1,0},{2,1},{3,2},{4,7},{5,4},{6,5},{7,6},{8,11},{9,8},{10,9... | collective-permute-start | bytes 786440 | tf_op jit(solution)/shard_map/ppermute | solution.py:17
  48.2 26.3 %copy-start.7 = (bf16[128,1024]{1,0:T(8,128)(2,1)}, bf16[128,1024]{1,0:T(8,128)(2,1)S(1)}, u32[]{:S(2)}) copy-start(bf16[128,1024]{1,0:T(8,128)(2,1)S(1)} %collective-permute-done.4.refs_1_) | copy-start | bytes 786436
  67.0 7.6 %copy-start.8 = (bf16[128,1024]{1,0:T(8,128)(2,1)}, bf16[128,1024]{1,0:T(8,128)(2,1)S(1)}, u32[]{:S(2)}) copy-start(bf16[128,1024]{1,0:T(8,128)(2,1)S(1)} %collective-permute-done.5.refs_0_) | copy-start | bytes 786436
  67.8 1.3 copy-start.2
  74.6 45.2 %collective-permute-start.9 = (bf16[896,1024]{1,0:T(8,128)(2,1)}, bf16[896,1024]{1,0:T(8,128)(2,1)}, u32[]{:S(2)}, u32[]{:S(2)}) collective-permute-start(bf16[896,1024]{1,0:T(8,128)(2,1)} %shard_map.55), channel_id=1, source_target_pairs={{0,4},{4,8},{8,12},{12,0},{64,76},{68,64},{72,68},{76,72},{1,5},{5... | collective-permute-start | bytes 5505032 | tf_op jit(solution)/shard_map/ppermute | solution.py:22
  86.1 42.9 %all-to-all-start.1 = ((bf16[4,96,2688]{2,1,0:T(8,128)(2,1)}), bf16[4,96,2688]{2,1,0:T(8,128)(2,1)S(1)}, u32[]{:S(2)}, u32[]{:S(2)}) async-start(bf16[4,96,2688]{2,1,0:T(8,128)(2,1)} %shard_map.58.after_ref), calls=%async_computation.1 | async-start | bytes 4128768 | tf_op jit(solution)/shard_map/all_to_all | solution.py:28
  93.4 26.2 %collective-permute-start.10 = (bf16[448,1024]{1,0:T(8,128)(2,1)}, bf16[448,1024]{1,0:T(8,128)(2,1)S(1)}, u32[]{:S(2)}, u32[]{:S(2)}) collective-permute-start(bf16[448,1024]{1,0:T(8,128)(2,1)} %shard_map.56.refs_1_), channel_id=1, source_target_pairs={{0,12},{4,0},{8,4},{12,8},{1,13},{5,1},{9,5},{13,9},{2,14},{6,2},{... | collective-permute-start | bytes 2752520 | tf_op jit(solution)/shard_map/ppermute | solution.py:17
  95.3 24.5 %collective-permute-start.11 = (bf16[448,1024]{1,0:T(8,128)(2,1)}, bf16[448,1024]{1,0:T(8,128)(2,1)S(1)}, u32[]{:S(2)}, u32[]{:S(2)}) collective-permute-start(bf16[448,1024]{1,0:T(8,128)(2,1)} %shard_map.56.refs_1_), channel_id=1, source_target_pairs={{0,4},{4,8},{8,12},{12,0},{1,5},{5,9},{9,13},{13,1},{2,6},{6,10},{... | collective-permute-start | bytes 2752520 | tf_op jit(solution)/shard_map/ppermute | solution.py:17
  98.7 12.8 %collective-permute-start.6 = (bf16[128,1024]{1,0:T(8,128)(2,1)}, bf16[128,1024]{1,0:T(8,128)(2,1)S(1)}, u32[]{:S(2)}, u32[]{:S(2)}) collective-permute-start(bf16[128,1024]{1,0:T(8,128)(2,1)} %broadcast_select_fusion.after_ref), channel_id=1, source_target_pairs={{0,1},{1,2},{2,3},{3,0},{64,67},{65,64},{66,65},{67,66},{4,5},{5,6... | collective-permute-start | bytes 786440 | tf_op jit(solution)/shard_map/ppermute | solution.py:22
  111.5 8.4 %copy-start.10 = (bf16[128,1024]{1,0:T(8,128)(2,1)}, bf16[128,1024]{1,0:T(8,128)(2,1)S(1)}, u32[]{:S(2)}) copy-start(bf16[128,1024]{1,0:T(8,128)(2,1)S(1)} %collective-permute-done.6.far_ref) | copy-start | bytes 786436
  119.6 0.9 copy-start
  119.8 1.0 copy-start.1
  128.9 9.3 %copy-start.4 = (bf16[4,96,2688]{2,1,0:T(8,128)(2,1)}, bf16[4,96,2688]{2,1,0:T(8,128)(2,1)S(1)}, u32[]{:S(2)}) copy-start(bf16[4,96,2688]{2,1,0:T(8,128)(2,1)S(1)} %all-to-all-done.1.sums_ref) | copy-start | bytes 6193156
  128.9 28.5 %all-to-all-start = ((bf16[4,32,6272]{2,1,0:T(8,128)(2,1)}), bf16[4,32,6272]{2,1,0:T(8,128)(2,1)}, u32[]{:S(2)}, u32[]{:S(2)}) async-start(bf16[4,32,6272]{2,1,0:T(8,128)(2,1)} %shard_map.57), calls=%async_computation | async-start | bytes 3211264 | tf_op jit(solution)/shard_map/all_to_all | solution.py:28
  138.3 15.6 %collective-permute-start.12 = (bf16[448,1024]{1,0:T(8,128)(2,1)}, bf16[448,1024]{1,0:T(8,128)(2,1)S(1)}, u32[]{:S(2)}, u32[]{:S(2)}) collective-permute-start(bf16[448,1024]{1,0:T(8,128)(2,1)} %shard_map.59), channel_id=1, source_target_pairs={{0,4},{4,8},{8,12},{12,0},{64,76},{68,64},{72,68},{76,72},{1,5},{5... | collective-permute-start | bytes 2752520 | tf_op jit(solution)/shard_map/ppermute | solution.py:22
  153.8 0.9 copy-start.3
  171.2 12.5 %all-to-all-start.3 = ((bf16[4,64,1792]{2,1,0:T(8,128)(2,1)}), bf16[4,64,1792]{2,1,0:T(8,128)(2,1)S(1)}, u32[]{:S(2)}, u32[]{:S(2)}) async-start(bf16[4,64,1792]{2,1,0:T(8,128)(2,1)} %get-tuple-element.11), calls=%async_computation.3 | async-start | bytes 1835008 | tf_op jit(solution)/shard_map/all_to_all | solution.py:28
  178.1 13.2 %collective-permute-start.13 = (bf16[128,1024]{1,0:T(8,128)(2,1)}, bf16[128,1024]{1,0:T(8,128)(2,1)S(1)}, u32[]{:S(2)}, u32[]{:S(2)}) collective-permute-start(bf16[128,1024]{1,0:T(8,128)(2,1)} %shard_map.64), channel_id=1, source_target_pairs={{0,1},{1,2},{2,3},{3,0},{64,67},{65,64},{66,65},{67,66},{4,5},{5,6... | collective-permute-start | bytes 786440 | tf_op jit(solution)/shard_map/ppermute | solution.py:22
  183.7 3.5 %copy-start.6 = (bf16[4,64,1792]{2,1,0:T(8,128)(2,1)}, bf16[4,64,1792]{2,1,0:T(8,128)(2,1)S(1)}, u32[]{:S(2)}) copy-start(bf16[4,64,1792]{2,1,0:T(8,128)(2,1)S(1)} %all-to-all-done.3.refs_0_) | copy-start | bytes 2752516
  183.7 25.4 %all-to-all-start.2 = ((bf16[4,32,1792]{2,1,0:T(8,128)(2,1)}), bf16[4,32,1792]{2,1,0:T(8,128)(2,1)S(1)}, u32[]{:S(2)}, u32[]{:S(2)}) async-start(bf16[4,32,1792]{2,1,0:T(8,128)(2,1)} %get-tuple-element.10), calls=%async_computation.2 | async-start | bytes 917504 | tf_op jit(solution)/shard_map/all_to_all | solution.py:28
  191.3 16.9 %copy-start.11 = (s32[8,2]{0,1:T(2,128)S(1)}, s32[8,2]{0,1:T(2,128)}, u32[]{:S(2)}) copy-start(s32[8,2]{0,1:T(2,128)} %param.6) | copy-start | bytes 196
  191.3 16.9 %copy-start.12 = (f32[8,2]{0,1:T(2,128)S(1)}, f32[8,2]{0,1:T(2,128)}, u32[]{:S(2)}) copy-start(f32[8,2]{0,1:T(2,128)} %param.7) | copy-start | bytes 196
  192.7 20.7 %collective-permute-start.15 = (bf16[128,1024]{1,0:T(8,128)(2,1)S(1)}, bf16[128,1024]{1,0:T(8,128)(2,1)S(1)}, u32[]{:S(2)}, u32[]{:S(2)}) collective-permute-start(bf16[128,1024]{1,0:T(8,128)(2,1)S(1)} %get-tuple-element.39), channel_id=1, source_target_pairs={{0,3},{1,0},{2,1},{3,2},{4,7},{5,4},{6,5},{7,6},{8,11},{9,8},{10,9... | collective-permute-start | bytes 786440 | tf_op jit(solution)/shard_map/ppermute | solution.py:17
  199.0 17.5 %collective-permute-start.14 = (bf16[128,1024]{1,0:T(8,128)(2,1)S(1)}, bf16[128,1024]{1,0:T(8,128)(2,1)S(1)}, u32[]{:S(2)}, u32[]{:S(2)}) collective-permute-start(bf16[128,1024]{1,0:T(8,128)(2,1)S(1)} %get-tuple-element.38), channel_id=1, source_target_pairs={{0,1},{1,2},{2,3},{3,0},{4,5},{5,6},{6,7},{7,4},{8,9},{9,10},{10,1... | collective-permute-start | bytes 786440 | tf_op jit(solution)/shard_map/ppermute | solution.py:17
  209.1 0.8 copy-start.9
  219.0 11.6 %collective-permute-start.16 = (bf16[256,1024]{1,0:T(8,128)(2,1)S(1)}, bf16[256,1024]{1,0:T(8,128)(2,1)S(1)}, u32[]{:S(2)}, u32[]{:S(2)}) collective-permute-start(bf16[256,1024]{1,0:T(8,128)(2,1)S(1)} %pad_maximum_fusion), channel_id=1, source_target_pairs={{0,64},{64,0},{1,65},{65,1},{2,66},{66,2},{3,67},{67,3},{4,68},{68... | collective-permute-start | bytes 1572872 | tf_op jit(solution)/shard_map/ppermute | solution.py:17
  231.9 17.7 %collective-permute-start.19 = (bf16[64,1024]{1,0:T(8,128)(2,1)S(1)}, bf16[64,1024]{1,0:T(8,128)(2,1)S(1)}, u32[]{:S(2)}, u32[]{:S(2)}) collective-permute-start(bf16[64,1024]{1,0:T(8,128)(2,1)S(1)} %get-tuple-element.28), channel_id=1, source_target_pairs={{0,384},{128,0},{256,128},{384,256},{1,385},{129,1},{257,129},{385... | collective-permute-start | bytes 393224 | tf_op jit(solution)/shard_map/ppermute | solution.py:17
  235.0 21.3 %collective-permute-start.18 = (bf16[64,1024]{1,0:T(8,128)(2,1)S(1)}, bf16[64,1024]{1,0:T(8,128)(2,1)S(1)}, u32[]{:S(2)}, u32[]{:S(2)}) collective-permute-start(bf16[64,1024]{1,0:T(8,128)(2,1)S(1)} %get-tuple-element.29), channel_id=1, source_target_pairs={{0,256},{128,384},{256,0},{384,128},{1,257},{129,385},{257,1},{385... | collective-permute-start | bytes 393224 | tf_op jit(solution)/shard_map/ppermute | solution.py:17
  246.2 10.1 %collective-permute-start.17 = (bf16[64,1024]{1,0:T(8,128)(2,1)S(1)}, bf16[64,1024]{1,0:T(8,128)(2,1)S(1)}, u32[]{:S(2)}, u32[]{:S(2)}) collective-permute-start(bf16[64,1024]{1,0:T(8,128)(2,1)S(1)} %get-tuple-element.27), channel_id=1, source_target_pairs={{0,128},{128,256},{256,384},{384,0},{1,129},{129,257},{257,385},{3... | collective-permute-start | bytes 393224 | tf_op jit(solution)/shard_map/ppermute | solution.py:17

commit v5 on v4

v5 whole, which is shorter than its diff:
```python
import jax
import jax.numpy as jnp
from jax import lax
from jax.experimental import pallas as pl
from jax.experimental.pallas import tpu as pltpu
from jax.sharding import Mesh, PartitionSpec as P

wide = jnp.float32
half = jnp.bfloat16
LIMIT = 60 * 2**20
COST = pl.CostEstimate(flops=1024, bytes_accessed=1024, transcendentals=0)
ANY = pl.BlockSpec(memory_space=pl.ANY)
WHOLE = pl.BlockSpec(memory_space=pltpu.VMEM)


def shift(a, axis, by):
    n = lax.axis_size(axis)
    return lax.ppermute(a, axis, [(i, (i + by) % n) for i in range(n)])


def pass_on(a, axis, by):
    n = lax.axis_size(axis)
    return lax.ppermute(
        a, ("core", axis), [(c * n + i, c * n + (i + by * (1 - 2 * c)) % n) for c in range(2) for i in range(n)]
    )


def swap(a, axis):
    return lax.all_to_all(a, axis, split_axis=0, concat_axis=0, tiled=True)


DIMS = (((1,), (1,)), ((), ()))


def hold(a, after):
    def kernel(a_ref, after_ref, out_ref):
        out_ref[...] = a_ref[...]

    return pl.pallas_call(
        kernel,
        in_specs=[WHOLE, ANY],
        out_specs=WHOLE,
        out_shape=jax.ShapeDtypeStruct(a.shape, a.dtype),
        compiler_params=pltpu.CompilerParams(vmem_limit_bytes=LIMIT),
        cost_estimate=COST,
    )(a, after)


def fetch(refs, held, sems):
    copies = [pltpu.make_async_copy(ref, held.at[i], sems.at[i]) for i, ref in enumerate(refs)]
    for copy in copies:
        copy.start()
    return copies


def early(pieces, weights, after):
    def kernel(*refs):
        out_ref, copy_ref, held, sems, sem = refs[-5:]
        copies = fetch(refs[3:6], held, sems)
        x = jnp.concatenate([ref[...] for ref in refs[:3]])
        spare = pltpu.make_async_copy(held.at[1], copy_ref, sem)
        for i in range(3):
            copies[i].wait()
            if i == 1:
                spare.start()
            out = lax.dot_general(x, held[i], DIMS, preferred_element_type=wide).astype(half)
            for p in range(3):
                out_ref[:, pl.ds(32 * p, 32), pl.ds(896 * i, 896)] = out[128 * p : 128 * p + 128].reshape(4, 32, 896)
        spare.wait()

    return pl.pallas_call(
        kernel,
        in_specs=[WHOLE] * 3 + [ANY] * (3 + len(after)),
        out_specs=[WHOLE, ANY],
        out_shape=[jax.ShapeDtypeStruct((4, 96, 2688), half), jax.ShapeDtypeStruct((896, 1024), half)],
        scratch_shapes=[
            pltpu.VMEM((3, 896, 1024), half),
            pltpu.SemaphoreType.DMA((3,)),
            pltpu.SemaphoreType.DMA,
        ],
        compiler_params=pltpu.CompilerParams(vmem_limit_bytes=LIMIT),
        cost_estimate=COST,
    )(*pieces, *weights, *after)


def late_near(far, weights):
    def kernel(far_ref, *refs):
        out_ref, held, sums, sems, sem = refs[-5:]
        copies = fetch(refs[:3], held, sems)
        x = far_ref[...]
        for i in range(3):
            copies[i].wait()
            out = lax.dot_general(x, held[i], DIMS, preferred_element_type=wide).astype(half)
            sums[:, :, pl.ds(896 * i, 896)] = out.reshape(4, 32, 896)
        copy = pltpu.make_async_copy(sums, out_ref.at[:, :, pl.ds(0, 2688)], sem)
        copy.start()
        copy.wait()

    return pl.pallas_call(
        kernel,
        in_specs=[WHOLE] + [ANY] * 3,
        out_specs=ANY,
        out_shape=jax.ShapeDtypeStruct((4, 32, 6272), half),
        scratch_shapes=[
            pltpu.VMEM((3, 896, 1024), half),
            pltpu.VMEM((4, 32, 2688), half),
            pltpu.SemaphoreType.DMA((3,)),
            pltpu.SemaphoreType.DMA,
        ],
        compiler_params=pltpu.CompilerParams(vmem_limit_bytes=LIMIT),
        cost_estimate=COST,
    )(far, *weights)


def late_far(pieces, w_far, begun):
    def kernel(*refs):
        w_ref, out_ref, sums, sem = refs[4], refs[6], refs[7], refs[8]
        x = jnp.concatenate([ref[...] for ref in refs[:4]])
        out = lax.dot_general(x, w_ref[...], DIMS, preferred_element_type=wide).astype(half)
        for p in range(4):
            sums[:, :, pl.ds(896 * p, 896)] = out[128 * p : 128 * p + 128].reshape(4, 32, 896)
        copy = pltpu.make_async_copy(sums, out_ref.at[:, :, pl.ds(2688, 3584)], sem)
        copy.start()
        copy.wait()

    return pl.pallas_call(
        kernel,
        in_specs=[WHOLE] * 5 + [ANY],
        out_specs=ANY,
        out_shape=jax.ShapeDtypeStruct((4, 32, 6272), half),
        scratch_shapes=[pltpu.VMEM((4, 32, 3584), half), pltpu.SemaphoreType.DMA],
        input_output_aliases={5: 0},
        compiler_params=pltpu.CompilerParams(vmem_limit_bytes=LIMIT),
        cost_estimate=COST,
    )(*pieces, w_far, begun)


def act(gate, up):
    return (gate / (1.0 + jnp.exp(-gate)) * up).astype(half)


def block(sums, i):
    at = 896 * i
    return act(sums[:, at : at + 448], sums[:, at + 448 : at + 896])


def activate_early(sums, after):
    def kernel(sums_ref, *refs):
        out_ref = refs[-1]
        total = jnp.sum(sums_ref[...].astype(wide), axis=0)
        out_ref[...] = jnp.concatenate([block(total, i) for i in range(3)], axis=1)

    return pl.pallas_call(
        kernel,
        in_specs=[WHOLE] + [ANY] * len(after),
        out_specs=WHOLE,
        out_shape=jax.ShapeDtypeStruct((96, 1344), half),
        compiler_params=pltpu.CompilerParams(vmem_limit_bytes=LIMIT),
        cost_estimate=COST,
    )(sums, *after)


def activate_late(sums, first):
    def kernel(sums_ref, first_ref, *outs):
        total = jnp.sum(sums_ref[...].astype(wide), axis=0)
        blocks = [block(total, i) for i in range(7)]
        far = jnp.concatenate(blocks[:4], axis=1)
        rest = jnp.concatenate([first_ref[...], jnp.concatenate(blocks[4:])], axis=1)
        for part, out in zip((far, rest[:64], rest[64:]), outs):
            for j in range(4):
                out[j] = part

    return pl.pallas_call(
        kernel,
        out_shape=[jax.ShapeDtypeStruct((4, r, 1792), half) for r in (32, 64, 32)],
        compiler_params=pltpu.CompilerParams(vmem_limit_bytes=LIMIT),
        cost_estimate=COST,
    )(sums, first)


def down(hidden, weights, types):
    n = len(types)

    def kernel(*refs):
        hidden_ref, v_refs, outs = refs[0], refs[1:5], refs[5:]
        v = jnp.concatenate([ref[...] for ref in v_refs])
        for i, out in enumerate(outs):
            rows = hidden_ref[:, pl.ds(32 * i, 32), :].reshape(128, 1792)
            out[...] = jnp.dot(rows, v, preferred_element_type=wide).astype(out.dtype)

    return pl.pallas_call(
        kernel,
        grid=(2,),
        in_specs=[pl.BlockSpec((4, 32 * n, 1792), lambda i: (0, 0, 0))]
        + [pl.BlockSpec((448, 512), lambda i: (0, i))] * 4,
        out_specs=[pl.BlockSpec((128, 512), lambda i: (0, i))] * n,
        out_shape=[jax.ShapeDtypeStruct((128, 1024), t) for t in types],
        compiler_params=pltpu.CompilerParams(vmem_limit_bytes=LIMIT),
        cost_estimate=COST,
    )(hidden, *weights)


def on_device(tokens, routes, route_gates, w_in, w_down):
    core = lax.axis_index("core")
    zlo = lax.axis_index("zlo")
    expert = zlo * 2 + core

    mine = [tokens[0]] + [shift(tokens[0], "zlo", d) for d in (1, 2, 3)]
    w_own, v_own = jnp.transpose(w_in[0], (1, 2, 0)).reshape(896, 1024), w_down[0]
    w_first, w_second = pass_on(w_own, "y", 1), pass_on(w_own, "y", -1)
    v_first, v_second = pass_on(v_own, "y", 1), pass_on(v_own, "y", -1)
    weights = [w_own, w_first, w_second]

    matches = routes[:, :, None] == jnp.arange(8, dtype=jnp.int32)[None, None, :]
    hit = jnp.sum(matches.astype(jnp.int32), axis=1)
    slot = jnp.cumsum(hit, axis=0) - hit
    weight = jnp.sum(route_gates[:, :, None] * matches.astype(wide), axis=1)
    names = jnp.arange(8, dtype=jnp.int32)

    def places(e):
        taken = lax.dynamic_index_in_dim(hit, e, 1, keepdims=False)
        place = lax.dynamic_index_in_dim(slot, e, 1, keepdims=False)
        chosen = [(taken == 1) & (place == k) for k in range(2)]
        owner = [jnp.sum(jnp.where(c, names >> 1, 0)) for c in chosen]
        side = [jnp.sum(jnp.where(c, names & 1, 0)) for c in chosen]
        return chosen, owner, side

    chosen, owner, side = places(expert)
    _, owner_too, _ = places(expert + 1 - 2 * core)
    gates = lax.dynamic_index_in_dim(weight, expert, 1, keepdims=False)
    scales = [jnp.sum(jnp.where(c, gates, 0.0)) for c in chosen]

    def taking(owners):
        out = []
        for z in owners:
            away = (zlo - z) & 3
            near = jnp.where(away == 0, mine[0], mine[1])
            out.append(jnp.where(away < 2, near, jnp.where(away == 2, mine[2], mine[3])))
        return out

    other = shift(jnp.concatenate(taking(owner_too)), "core", 1)
    rows = jnp.concatenate(
        [jnp.where(side[k] == core, a, other[64 * k : 64 * k + 64]) for k, a in enumerate(taking(owner))]
    )

    first, second = pass_on(rows, "zhi", 1), pass_on(rows, "zhi", -1)
    part, w_next = early([first, second, rows], weights, [v_first])

    far = pass_on(hold(first, second), "zhi", 1)
    w_far = pass_on(w_next, "y", 1)
    v_far = pass_on(v_first, "y", 1)
    v_all = [v_own, v_first, v_second, v_far]
    begun = activate_early(swap(part, "x"), [v_second, v_far])
    rest = swap(late_far([far, first, second, rows], w_far, late_near(far, weights)), "x")
    far_h, near_h, own_h = activate_late(rest, begun)

    (far_out,) = down(swap(far_h, "x"), v_all, (half,))
    got = pass_on(far_out, "zhi", 1)
    first_out, second_out = down(swap(near_h, "x"), v_all, (half, wide))
    back = pass_on(first_out, "zhi", -1)
    ahead = pass_on((second_out + got.astype(wide)).astype(half), "zhi", 1)

    (own_out,) = down(swap(own_h, "x"), v_all, (wide,))
    result = (own_out + ahead.astype(wide) + back.astype(wide)).reshape(2, 64, 1024)

    ids = jnp.arange(4, dtype=jnp.int32)[:, None, None]

    def toward(parity):
        return sum(
            jnp.where((owner[k] == ids) & (side[k] == parity), scales[k] * result[k][None], 0.0)
            for k in range(2)
        )

    got = shift(toward(1 - core).astype(half), "core", 1)
    going = (toward(core) + got.astype(wide)).astype(half)
    return jnp.sum(swap(going, "zlo").astype(wide), axis=0, keepdims=True).astype(half)


def solution(mesh):
    fine = Mesh(mesh.devices.reshape(4, 2, 4, 4, 4), ("zlo", "core", "x", "y", "zhi"))
    seqs, pos = ("zlo", "core"), ("y", "zhi")
    return jax.shard_map(
        on_device,
        mesh=fine,
        in_specs=(
            P(seqs, pos, "x"),
            P(),
            P(),
            P(seqs, "x", None, pos),
            P(seqs, pos, "x"),
        ),
        out_specs=P(seqs, pos, "x"),
        check_vma=False,
    )
```

time: 260 us -> 244 us (0.938)
  blocking collectives: 10.9 us -> 38.9 us
  waiting for transfers between devices: 65.2 us -> 49.5 us
  starting transfers between devices: 110 us -> 95 us
  Pallas kernels: 45 us -> 35 us
  between operations: 10.4 us -> 5.57 us
    ppermute x16 -> x5, starting transfers between devices: 76 us -> 26 us  [shift(): return lax.ppermute(a, axis, [(i, (i + by) % n) for i in range(n)])]
    ppermute x16 -> x5, waiting for transfers between devices: 44.7 us -> 0.23 us  [shift(): return lax.ppermute(a, axis, [(i, (i + by) % n) for i in range(n)])]
    ppermute x4 -> x12, starting transfers between devices: 18.2 us -> 54.1 us  [pass_on(): lax.ppermute(a, ('core', axis), [(c * n + i, c * n + (i + by * (1 - 2 * c...]
    all_to_all x1 -> x2, blocking collectives: 10.9 us -> 38.9 us  [swap(): return lax.all_to_all(a, axis, split_axis=0, concat_axis=0, tiled=True)]
    ppermute x4 -> x12, waiting for transfers between devices: 19.2 us -> 45.2 us  [pass_on(): lax.ppermute(a, ('core', axis), [(c * n + i, c * n + (i + by * (1 - 2 * c...]
    pallas_call x6 -> x5, Pallas kernels: 31.2 us -> 21.1 us  [the longest x1 7 us: early(): pl.pallas_call(kernel, in_specs=[WHOLE] * 3 + [ANY] * (3 + len(after)), o...]
    all_to_all x4, waiting for transfers between devices: 1.39 us -> 4 us  [swap(): return lax.all_to_all(a, axis, split_axis=0, concat_axis=0, tiled=True)]
    unnamed x26 -> x28, local copies, waits for them, and re-layouts: 3.99 us -> 5.45 us
  transfers between devices with their start and end apart: 24 -> 21, of which waited for: 10 -> 8; matrix products, arithmetic and copies ran while one was open for 3% -> 4% of each run, Pallas kernels for 14% -> 10%
where the time goes in v5:
time: 244 us; the launch traced here: 242 us
  starting transfers between devices  95 us (39%)
  waiting for transfers between devices  49.5 us (20%)
  blocking collectives  38.9 us (16%)
  Pallas kernels  35 us (14%)
  other arithmetic  12.8 us (5%)
  local copies, waits for them, and re-layouts  5.64 us (2%)
  between operations  5.57 us (2%)
    ppermute x12, starting transfers between devices, pass_on(): lax.ppermute(a, ('core', axis), [(c * n + i, c * n + (i + by * (1 - 2 * c...  54.1 us
    ppermute x12, waiting for transfers between devices, pass_on(): lax.ppermute(a, ('core', axis), [(c * n + i, c * n + (i + by * (1 - 2 * c...  45.2 us
    all_to_all x2, blocking collectives, swap(): return lax.all_to_all(a, axis, split_axis=0, concat_axis=0, tiled=True)  38.9 us
    ppermute x5, starting transfers between devices, shift(): return lax.ppermute(a, axis, [(i, (i + by) % n) for i in range(n)])  26 us
    all_to_all x4, starting transfers between devices, swap(): return lax.all_to_all(a, axis, split_axis=0, concat_axis=0, tiled=True)  15 us
    pallas_call x3, Pallas kernels, down(): pl.pallas_call(kernel, grid=(2,), in_specs=[pl.BlockSpec((4, 32 * n, 1792...  10.9 us
    pallas_call x1, Pallas kernels, early(): pl.pallas_call(kernel, in_specs=[WHOLE] * 3 + [ANY] * (3 + len(after)), o...  7 us
    pallas_call x1, Pallas kernels, late_near(): pl.pallas_call(kernel, in_specs=[WHOLE] + [ANY] * 3, out_specs=ANY, out_s...  5.59 us
  transfers between devices with their start and end apart: 21, of which 8 were waited for; matrix products, arithmetic and copies ran while one was open for 4% of the time, Pallas kernels for 10%

profile of v5, /device:TPU:1, one launch (start us, length us, event | category | flops | bytes accessed | tf_op | source)
XLA Modules:
  0.0 242.4 jit_solution(12388752968371743787)
XLA Ops:
  0.0 5.5 %collective-permute-start.7 = (bf16[896,1024]{1,0:T(8,128)(2,1)}, bf16[896,1024]{1,0:T(8,128)(2,1)S(1)}, u32[]{:S(2)}, u32[]{:S(2)}) collective-permute-start(bf16[896,1024]{1,0:T(8,128)(2,1)} %bitcast.17), channel_id=1, source_target_pairs={{0,4},{4,8},{8,12},{12,0},{64,76},{68,64},{72,68},{76,72},{1,5},{5... | collective-permute-start | bytes 5505032 | tf_op jit(solution)/shard_map/ppermute | solution.py:23
  5.5 1.9 collective-permute-start.8
  7.4 3.5 %collective-permute-start = (bf16[64,1024]{1,0:T(8,128)(2,1)}, bf16[64,1024]{1,0:T(8,128)(2,1)S(1)}, u32[]{:S(2)}, u32[]{:S(2)}) collective-permute-start(bf16[64,1024]{1,0:T(8,128)(2,1)} %bitcast.21), channel_id=1, source_target_pairs={{0,128},{128,256},{256,384},{384,0},{1,129},{129,257},{257,385},{3... | collective-permute-start | bytes 393224 | tf_op jit(solution)/shard_map/ppermute | solution.py:18
  11.0 4.9 %collective-permute-start.1 = (bf16[64,1024]{1,0:T(8,128)(2,1)}, bf16[64,1024]{1,0:T(8,128)(2,1)S(1)}, u32[]{:S(2)}, u32[]{:S(2)}) collective-permute-start(bf16[64,1024]{1,0:T(8,128)(2,1)} %bitcast.22), channel_id=1, source_target_pairs={{0,256},{128,384},{256,0},{384,128},{1,257},{129,385},{257,1},{385... | collective-permute-start | bytes 393224 | tf_op jit(solution)/shard_map/ppermute | solution.py:18
  15.9 2.6 %collective-permute-start.2 = (bf16[64,1024]{1,0:T(8,128)(2,1)}, bf16[64,1024]{1,0:T(8,128)(2,1)S(1)}, u32[]{:S(2)}, u32[]{:S(2)}) collective-permute-start(bf16[64,1024]{1,0:T(8,128)(2,1)} %bitcast.23), channel_id=1, source_target_pairs={{0,384},{128,0},{256,128},{384,256},{1,385},{129,1},{257,129},{385... | collective-permute-start | bytes 393224 | tf_op jit(solution)/shard_map/ppermute | solution.py:18
  18.5 0.8 convert_reduce_fusion
  22.5 4.6 %collective-permute-start.9 = (bf16[448,1024]{1,0:T(8,128)(2,1)}, bf16[448,1024]{1,0:T(8,128)(2,1)S(1)}, u32[]{:S(2)}, u32[]{:S(2)}) collective-permute-start(bf16[448,1024]{1,0:T(8,128)(2,1)} %bitcast.12), channel_id=1, source_target_pairs={{0,4},{4,8},{8,12},{12,0},{64,76},{68,64},{72,68},{76,72},{1,5},{5... | collective-permute-start | bytes 2752520 | tf_op jit(solution)/shard_map/ppermute | solution.py:23
  27.1 0.9 select_select_fusion.1
  28.1 4.3 %collective-permute-start.3 = (bf16[128,1024]{1,0:T(8,128)(2,1)S(1)}, bf16[128,1024]{1,0:T(8,128)(2,1)}, u32[]{:S(2)}, u32[]{:S(2)}) collective-permute-start(bf16[128,1024]{1,0:T(8,128)(2,1)S(1)} %pad_maximum_fusion), channel_id=1, source_target_pairs={{0,64},{64,0},{1,65},{65,1},{2,66},{66,2},{3,67},{67,3},{4,68},{68... | collective-permute-start | bytes 786440 | tf_op jit(solution)/shard_map/ppermute | solution.py:18
  34.9 1.1 slice_select_fusion.1
  36.0 8.3 %collective-permute-start.4 = (bf16[128,1024]{1,0:T(8,128)(2,1)S(1)}, bf16[128,1024]{1,0:T(8,128)(2,1)S(1)}, u32[]{:S(2)}, u32[]{:S(2)}) collective-permute-start(bf16[128,1024]{1,0:T(8,128)(2,1)S(1)} %pad_maximum_fusion.1.refs_2_.refs_3_), channel_id=1, source_target_pairs={{0,1},{1,2},{2,3},{3,0},{64,67},{65,64},{66,65},{67,66},{4,5},{5,6... | collective-permute-start | bytes 786440 | tf_op jit(solution)/shard_map/ppermute | solution.py:23
  44.3 1.9 collective-permute-start.5
  46.3 18.3 %collective-permute-done.4.a_ref.refs_0_.refs_1_ = bf16[128,1024]{1,0:T(8,128)(2,1)S(1)} collective-permute-done((bf16[128,1024]{1,0:T(8,128)(2,1)S(1)}, bf16[128,1024]{1,0:T(8,128)(2,1)S(1)}, u32[]{:S(2)}, u32[]{:S(2)}) %collective-permute-start.4) | collective-permute-done | bytes 262176 | tf_op jit(solution)/shard_map/ppermute | solution.py:23
  66.3 7.0 %shard_map.56 = (bf16[4,96,2688]{2,1,0:T(8,128)(2,1)}, bf16[896,1024]{1,0:T(8,128)(2,1)}) custom-call(bf16[128,1024]{1,0:T(8,128)(2,1)} %copy-done.7, bf16[128,1024]{1,0:T(8,128)(2,1)} %copy-done.8, bf16[128,1024]{1,0:T(8,128)(2,1)} %copy-done.9, bf16[896,1024]{1,0:T(8,128)(2,1)} %bitcast.19, bf16[896,1024]{1,0:T(8,128)(2,1)} %copy-done.5, ...), custom_call_target="tpu_custom_call" | custom-call | flops 1024 | bytes 1024 | tf_op jit(solution)/shard_map/pallas_call | solution.py:71
  73.3 4.9 %collective-permute-start.10 = (bf16[896,1024]{1,0:T(8,128)(2,1)}, bf16[896,1024]{1,0:T(8,128)(2,1)}, u32[]{:S(2)}, u32[]{:S(2)}) collective-permute-start(bf16[896,1024]{1,0:T(8,128)(2,1)} %get-tuple-element.12), channel_id=1, source_target_pairs={{0,4},{4,8},{8,12},{12,0},{64,76},{68,64},{72,68},{76,72},{1,5},{5... | collective-permute-start | bytes 5505032 | tf_op jit(solution)/shard_map/ppermute | solution.py:23
  78.1 3.6 %all-to-all-start.1 = ((bf16[4,96,2688]{2,1,0:T(8,128)(2,1)}), bf16[4,96,2688]{2,1,0:T(8,128)(2,1)S(1)}, u32[]{:S(2)}, u32[]{:S(2)}) async-start(bf16[4,96,2688]{2,1,0:T(8,128)(2,1)} %get-tuple-element.13), calls=%async_computation.1 | async-start | bytes 4128768 | tf_op jit(solution)/shard_map/all_to_all | solution.py:29
  81.8 1.7 shard_map.55
  83.5 5.6 %collective-permute-start.6 = (bf16[128,1024]{1,0:T(8,128)(2,1)}, bf16[128,1024]{1,0:T(8,128)(2,1)S(1)}, u32[]{:S(2)}, u32[]{:S(2)}) collective-permute-start(bf16[128,1024]{1,0:T(8,128)(2,1)} %shard_map.55), channel_id=1, source_target_pairs={{0,1},{1,2},{2,3},{3,0},{64,67},{65,64},{66,65},{67,66},{4,5},{5,6... | collective-permute-start | bytes 786440 | tf_op jit(solution)/shard_map/ppermute | solution.py:23
  89.1 6.5 %collective-permute-done.6.far_ref.refs_0_ = bf16[128,1024]{1,0:T(8,128)(2,1)S(1)} collective-permute-done((bf16[128,1024]{1,0:T(8,128)(2,1)}, bf16[128,1024]{1,0:T(8,128)(2,1)S(1)}, u32[]{:S(2)}, u32[]{:S(2)}) %collective-permute-start.6) | collective-permute-done | bytes 262176 | tf_op jit(solution)/shard_map/ppermute | solution.py:23
  96.3 5.6 %shard_map.57.refs_5_ = bf16[4,32,6272]{2,1,0:T(8,128)(2,1)} custom-call(bf16[128,1024]{1,0:T(8,128)(2,1)} %copy-done.11, bf16[896,1024]{1,0:T(8,128)(2,1)} %bitcast.20, bf16[896,1024]{1,0:T(8,128)(2,1)} %copy-done.5, bf16[896,1024]{1,0:T(8,128)(2,1)} %collective-permute-done.8.refs_5_.refs_2_), custom_call_target="tpu_custom_call" | custom-call | flops 1024 | bytes 1024 | tf_op jit(solution)/shard_map/pallas_call | solution.py:99
  102.0 4.1 %shard_map.58 = bf16[4,32,6272]{2,1,0:T(8,128)(2,1)} custom-call(bf16[128,1024]{1,0:T(8,128)(2,1)} %copy-done.11, bf16[128,1024]{1,0:T(8,128)(2,1)} %copy-done.7, bf16[128,1024]{1,0:T(8,128)(2,1)} %copy-done.8, bf16[128,1024]{1,0:T(8,128)(2,1)} %copy-done.9, bf16[896,1024]{1,0:T(8,128)(2,1)} %collective-permute-done.10.refs_4_, ...), custom_call_target="tpu_custom_call", output_to_operand_aliasing={{}: (5, {})} | custom-call | flops 1024 | bytes 1024 | tf_op jit(solution)/shard_map/pallas_call | solution.py:126
  106.0 1.6 all-to-all-done.1.sums_ref
  107.7 1.3 copy-done.4
  109.0 4.4 %all-to-all-start = ((bf16[4,32,6272]{2,1,0:T(8,128)(2,1)}), bf16[4,32,6272]{2,1,0:T(8,128)(2,1)}, u32[]{:S(2)}, u32[]{:S(2)}) async-start(bf16[4,32,6272]{2,1,0:T(8,128)(2,1)} %shard_map.58), calls=%async_computation | async-start | bytes 3211264 | tf_op jit(solution)/shard_map/all_to_all | solution.py:29
  113.4 3.3 %collective-permute-start.11 = (bf16[448,1024]{1,0:T(8,128)(2,1)}, bf16[448,1024]{1,0:T(8,128)(2,1)S(1)}, u32[]{:S(2)}, u32[]{:S(2)}) collective-permute-start(bf16[448,1024]{1,0:T(8,128)(2,1)} %bitcast.13), channel_id=1, source_target_pairs={{0,12},{4,0},{8,4},{12,8},{64,68},{68,72},{72,76},{76,64},{1,13},{... | collective-permute-start | bytes 2752520 | tf_op jit(solution)/shard_map/ppermute | solution.py:23
  116.7 3.2 %collective-permute-start.12 = (bf16[448,1024]{1,0:T(8,128)(2,1)S(1)}, bf16[448,1024]{1,0:T(8,128)(2,1)S(1)}, u32[]{:S(2)}, u32[]{:S(2)}) collective-permute-start(bf16[448,1024]{1,0:T(8,128)(2,1)S(1)} %copy-done.1), channel_id=1, source_target_pairs={{0,4},{4,8},{8,12},{12,0},{64,76},{68,64},{72,68},{76,72},{1,5},{5... | collective-permute-start | bytes 2752520 | tf_op jit(solution)/shard_map/ppermute | solution.py:23
  119.9 14.6 %collective-permute-done.11.refs_0_.refs_3_ = bf16[448,1024]{1,0:T(8,128)(2,1)S(1)} collective-permute-done((bf16[448,1024]{1,0:T(8,128)(2,1)}, bf16[448,1024]{1,0:T(8,128)(2,1)S(1)}, u32[]{:S(2)}, u32[]{:S(2)}) %collective-permute-start.11) | collective-permute-done | bytes 917536 | tf_op jit(solution)/shard_map/ppermute | solution.py:23
  134.5 4.5 %collective-permute-done.12.refs_1_.refs_4_ = bf16[448,1024]{1,0:T(8,128)(2,1)S(1)} collective-permute-done((bf16[448,1024]{1,0:T(8,128)(2,1)S(1)}, bf16[448,1024]{1,0:T(8,128)(2,1)S(1)}, u32[]{:S(2)}, u32[]{:S(2)}) %collective-permute-start.12) | collective-permute-done | bytes 917536 | tf_op jit(solution)/shard_map/ppermute | solution.py:23
  139.1 0.9 copy-done.3
  140.0 2.7 %shard_map.59.first_ref = bf16[96,1344]{1,0:T(8,128)(2,1)} custom-call(bf16[4,96,2688]{2,1,0:T(8,128)(2,1)} %copy-done.4, bf16[448,1024]{1,0:T(8,128)(2,1)} %copy-done.2, bf16[448,1024]{1,0:T(8,128)(2,1)} %copy-done.3), custom_call_target="tpu_custom_call" | custom-call | flops 1024 | bytes 1024 | tf_op jit(solution)/shard_map/pallas_call | solution.py:153
  142.7 3.1 %shard_map.60 = (bf16[4,32,1792]{2,1,0:T(8,128)(2,1)}, bf16[4,64,1792]{2,1,0:T(8,128)(2,1)}, bf16[4,32,1792]{2,1,0:T(8,128)(2,1)}) custom-call(bf16[4,32,6272]{2,1,0:T(8,128)(2,1)} %all-to-all-done.sums_ref, bf16[96,1344]{1,0:T(8,128)(2,1)} %shard_map.59.first_ref), custom_call_target="tpu_custom_call" | custom-call | flops 1024 | bytes 1024 | tf_op jit(solution)/shard_map/pallas_call | solution.py:173
  145.8 12.7 %all_to_all.30.refs_0_ = bf16[4,32,1792]{2,1,0:T(8,128)(2,1)} all-to-all(bf16[4,32,1792]{2,1,0:T(8,128)(2,1)} %get-tuple-element.17), channel_id=1, replica_groups=mesh['zlo'=4,'core'=2,'x'=4,'y'=4,'zhi'=4] {'x'}, dimensions={0} | all-to-all | bytes 917504 | tf_op jit(solution)/shard_map/all_to_all | solution.py:29
  158.5 3.5 %all-to-all-start.3 = ((bf16[4,64,1792]{2,1,0:T(8,128)(2,1)}), bf16[4,64,1792]{2,1,0:T(8,128)(2,1)S(1)}, u32[]{:S(2)}, u32[]{:S(2)}) async-start(bf16[4,64,1792]{2,1,0:T(8,128)(2,1)} %get-tuple-element.15), calls=%async_computation.3 | async-start | bytes 1835008 | tf_op jit(solution)/shard_map/all_to_all | solution.py:29
  162.1 3.4 %shard_map.63 = bf16[128,1024]{1,0:T(8,128)(2,1)} custom-call(bf16[4,32,1792]{2,1,0:T(8,128)(2,1)} %all_to_all.30.refs_0_, bf16[448,1024]{1,0:T(8,128)(2,1)} %bitcast.14, bf16[448,1024]{1,0:T(8,128)(2,1)} %copy-done, bf16[448,1024]{1,0:T(8,128)(2,1)} %copy-done.2, bf16[448,1024]{1,0:T(8,128)(2,1)} %copy-done.3), custom_call_target="tpu_custom_call" | custom-call | flops 1024 | bytes 1024 | tf_op jit(solution)/shard_map/pallas_call | solution.py:191
  165.5 5.7 %collective-permute-start.13 = (bf16[128,1024]{1,0:T(8,128)(2,1)}, bf16[128,1024]{1,0:T(8,128)(2,1)S(1)}, u32[]{:S(2)}, u32[]{:S(2)}) collective-permute-start(bf16[128,1024]{1,0:T(8,128)(2,1)} %shard_map.63), channel_id=1, source_target_pairs={{0,1},{1,2},{2,3},{3,0},{64,67},{65,64},{66,65},{67,66},{4,5},{5,6... | collective-permute-start | bytes 786440 | tf_op jit(solution)/shard_map/ppermute | solution.py:23
  171.8 2.4 all-to-all-done.3.refs_0_
  174.2 3.5 %all-to-all-start.2 = ((bf16[4,32,1792]{2,1,0:T(8,128)(2,1)}), bf16[4,32,1792]{2,1,0:T(8,128)(2,1)S(1)}, u32[]{:S(2)}, u32[]{:S(2)}) async-start(bf16[4,32,1792]{2,1,0:T(8,128)(2,1)} %get-tuple-element.14), calls=%async_computation.2 | async-start | bytes 917504 | tf_op jit(solution)/shard_map/all_to_all | solution.py:29
  177.6 4.1 %shard_map.62 = (bf16[128,1024]{1,0:T(8,128)(2,1)}, f32[128,1024]{1,0:T(8,128)}) custom-call(bf16[4,64,1792]{2,1,0:T(8,128)(2,1)} %copy-done.6, bf16[448,1024]{1,0:T(8,128)(2,1)} %bitcast.15, bf16[448,1024]{1,0:T(8,128)(2,1)} %copy-done, bf16[448,1024]{1,0:T(8,128)(2,1)} %copy-done.2, bf16[448,1024]{1,0:T(8,128)(2,1)} %copy-done.3), custom_call_target="tpu_custom_call" | custom-call | flops 1024 | bytes 1024 | tf_op jit(solution)/shard_map/pallas_call | solution.py:191
  181.7 1.1 add_convert_fusion.2
  182.8 4.5 %collective-permute-start.14 = (bf16[128,1024]{1,0:T(8,128)(2,1)S(1)}, bf16[128,1024]{1,0:T(8,128)(2,1)S(1)}, u32[]{:S(2)}, u32[]{:S(2)}) collective-permute-start(bf16[128,1024]{1,0:T(8,128)(2,1)S(1)} %add_convert_fusion.2), channel_id=1, source_target_pairs={{0,1},{1,2},{2,3},{3,0},{64,67},{65,64},{66,65},{67,66},{4,5},{5,6... | collective-permute-start | bytes 786440 | tf_op jit(solution)/shard_map/ppermute | solution.py:23
  187.4 4.7 %collective-permute-start.15 = (bf16[128,1024]{1,0:T(8,128)(2,1)}, bf16[128,1024]{1,0:T(8,128)(2,1)S(1)}, u32[]{:S(2)}, u32[]{:S(2)}) collective-permute-start(bf16[128,1024]{1,0:T(8,128)(2,1)} %get-tuple-element.18), channel_id=1, source_target_pairs={{0,3},{1,0},{2,1},{3,2},{64,65},{65,66},{66,67},{67,64},{4,7},{5,4... | collective-permute-start | bytes 786440 | tf_op jit(solution)/shard_map/ppermute | solution.py:23
  194.8 0.8 copy-done.10
  195.6 3.4 %shard_map.61 = f32[128,1024]{1,0:T(8,128)} custom-call(bf16[4,32,1792]{2,1,0:T(8,128)(2,1)} %copy-done.10, bf16[448,1024]{1,0:T(8,128)(2,1)} %bitcast.16, bf16[448,1024]{1,0:T(8,128)(2,1)} %copy-done, bf16[448,1024]{1,0:T(8,128)(2,1)} %copy-done.2, bf16[448,1024]{1,0:T(8,128)(2,1)} %copy-done.3), custom_call_target="tpu_custom_call" | custom-call | flops 1024 | bytes 1024 | tf_op jit(solution)/shard_map/pallas_call | solution.py:191
  199.0 1.3 collective-permute-done.15
  200.3 1.1 convert_add_fusion
  201.4 1.4 slice_multiply_fusion.1
  203.0 10.6 %collective-permute-start.16 = (bf16[4,64,1024]{2,1,0:T(8,128)(2,1)S(1)}, bf16[4,64,1024]{2,1,0:T(8,128)(2,1)S(1)}, u32[]{:S(2)}, u32[]{:S(2)}) collective-permute-start(bf16[4,64,1024]{2,1,0:T(8,128)(2,1)S(1)} %add_convert_fusion.1), channel_id=1, source_target_pairs={{0,64},{64,0},{1,65},{65,1},{2,66},{66,2},{3,67},{67,3},{4,68},{68... | collective-permute-start | bytes 1572872 | tf_op jit(solution)/shard_map/ppermute | solution.py:18
  215.4 26.2 %all_to_all.31 = bf16[4,64,1024]{2,1,0:T(8,128)(2,1)S(1)} all-to-all(bf16[4,64,1024]{2,1,0:T(8,128)(2,1)S(1)} %add_convert_fusion), channel_id=1, replica_groups=mesh['zlo'=4,'core'=2,'x'=4,'y'=4,'zhi'=4] {'zlo'}, dimensions={0} | all-to-all | bytes 1048576 | tf_op jit(solution)/shard_map/all_to_all | solution.py:29
  (57 shorter events, 9.2 us)
Async XLA Ops:
  0.0 64.5 %collective-permute-start.7 = (bf16[896,1024]{1,0:T(8,128)(2,1)}, bf16[896,1024]{1,0:T(8,128)(2,1)S(1)}, u32[]{:S(2)}, u32[]{:S(2)}) collective-permute-start(bf16[896,1024]{1,0:T(8,128)(2,1)} %bitcast.17), channel_id=1, source_target_pairs={{0,4},{4,8},{8,12},{12,0},{64,76},{68,64},{72,68},{76,72},{1,5},{5... | collective-permute-start | bytes 5505032 | tf_op jit(solution)/shard_map/ppermute | solution.py:23
  5.5 59.1 %collective-permute-start.8 = (bf16[896,1024]{1,0:T(8,128)(2,1)}, bf16[896,1024]{1,0:T(8,128)(2,1)}, u32[]{:S(2)}, u32[]{:S(2)}) collective-permute-start(bf16[896,1024]{1,0:T(8,128)(2,1)} %bitcast.18), channel_id=1, source_target_pairs={{0,12},{4,0},{8,4},{12,8},{64,68},{68,72},{72,76},{76,64},{1,13},{... | collective-permute-start | bytes 5505032 | tf_op jit(solution)/shard_map/ppermute | solution.py:23
  7.4 15.1 %collective-permute-start = (bf16[64,1024]{1,0:T(8,128)(2,1)}, bf16[64,1024]{1,0:T(8,128)(2,1)S(1)}, u32[]{:S(2)}, u32[]{:S(2)}) collective-permute-start(bf16[64,1024]{1,0:T(8,128)(2,1)} %bitcast.21), channel_id=1, source_target_pairs={{0,128},{128,256},{256,384},{384,0},{1,129},{129,257},{257,385},{3... | collective-permute-start | bytes 393224 | tf_op jit(solution)/shard_map/ppermute | solution.py:18
  11.0 16.2 %collective-permute-start.1 = (bf16[64,1024]{1,0:T(8,128)(2,1)}, bf16[64,1024]{1,0:T(8,128)(2,1)S(1)}, u32[]{:S(2)}, u32[]{:S(2)}) collective-permute-start(bf16[64,1024]{1,0:T(8,128)(2,1)} %bitcast.22), channel_id=1, source_target_pairs={{0,256},{128,384},{256,0},{384,128},{1,257},{129,385},{257,1},{385... | collective-permute-start | bytes 393224 | tf_op jit(solution)/shard_map/ppermute | solution.py:18
  15.9 11.3 %collective-permute-start.2 = (bf16[64,1024]{1,0:T(8,128)(2,1)}, bf16[64,1024]{1,0:T(8,128)(2,1)S(1)}, u32[]{:S(2)}, u32[]{:S(2)}) collective-permute-start(bf16[64,1024]{1,0:T(8,128)(2,1)} %bitcast.23), channel_id=1, source_target_pairs={{0,384},{128,0},{256,128},{384,256},{1,385},{129,1},{257,129},{385... | collective-permute-start | bytes 393224 | tf_op jit(solution)/shard_map/ppermute | solution.py:18
  22.5 42.0 %collective-permute-start.9 = (bf16[448,1024]{1,0:T(8,128)(2,1)}, bf16[448,1024]{1,0:T(8,128)(2,1)S(1)}, u32[]{:S(2)}, u32[]{:S(2)}) collective-permute-start(bf16[448,1024]{1,0:T(8,128)(2,1)} %bitcast.12), channel_id=1, source_target_pairs={{0,4},{4,8},{8,12},{12,0},{64,76},{68,64},{72,68},{76,72},{1,5},{5... | collective-permute-start | bytes 2752520 | tf_op jit(solution)/shard_map/ppermute | solution.py:23
  28.1 6.8 %collective-permute-start.3 = (bf16[128,1024]{1,0:T(8,128)(2,1)S(1)}, bf16[128,1024]{1,0:T(8,128)(2,1)}, u32[]{:S(2)}, u32[]{:S(2)}) collective-permute-start(bf16[128,1024]{1,0:T(8,128)(2,1)S(1)} %pad_maximum_fusion), channel_id=1, source_target_pairs={{0,64},{64,0},{1,65},{65,1},{2,66},{66,2},{3,67},{67,3},{4,68},{68... | collective-permute-start | bytes 786440 | tf_op jit(solution)/shard_map/ppermute | solution.py:18
  36.0 28.6 %copy-start.9 = (bf16[128,1024]{1,0:T(8,128)(2,1)}, bf16[128,1024]{1,0:T(8,128)(2,1)S(1)}, u32[]{:S(2)}) copy-start(bf16[128,1024]{1,0:T(8,128)(2,1)S(1)} %pad_maximum_fusion.1.refs_2_.refs_3_) | copy-start | bytes 786436
  36.0 28.5 %collective-permute-start.4 = (bf16[128,1024]{1,0:T(8,128)(2,1)S(1)}, bf16[128,1024]{1,0:T(8,128)(2,1)S(1)}, u32[]{:S(2)}, u32[]{:S(2)}) collective-permute-start(bf16[128,1024]{1,0:T(8,128)(2,1)S(1)} %pad_maximum_fusion.1.refs_2_.refs_3_), channel_id=1, source_target_pairs={{0,1},{1,2},{2,3},{3,0},{64,67},{65,64},{66,65},{67,66},{4,5},{5,6... | collective-permute-start | bytes 786440 | tf_op jit(solution)/shard_map/ppermute | solution.py:23
  44.3 20.2 %collective-permute-start.5 = (bf16[128,1024]{1,0:T(8,128)(2,1)S(1)}, bf16[128,1024]{1,0:T(8,128)(2,1)S(1)}, u32[]{:S(2)}, u32[]{:S(2)}) collective-permute-start(bf16[128,1024]{1,0:T(8,128)(2,1)S(1)} %pad_maximum_fusion.1.refs_2_.refs_3_), channel_id=1, source_target_pairs={{0,3},{1,0},{2,1},{3,2},{64,65},{65,66},{66,67},{67,64},{4,7},{5,4... | collective-permute-start | bytes 786440 | tf_op jit(solution)/shard_map/ppermute | solution.py:23
  64.5 0.7 copy-start.7
  64.5 0.8 copy-start.8
  64.5 1.1 copy-start
  64.6 1.7 copy-start.5
  73.3 28.7 %collective-permute-start.10 = (bf16[896,1024]{1,0:T(8,128)(2,1)}, bf16[896,1024]{1,0:T(8,128)(2,1)}, u32[]{:S(2)}, u32[]{:S(2)}) collective-permute-start(bf16[896,1024]{1,0:T(8,128)(2,1)} %get-tuple-element.12), channel_id=1, source_target_pairs={{0,4},{4,8},{8,12},{12,0},{64,76},{68,64},{72,68},{76,72},{1,5},{5... | collective-permute-start | bytes 5505032 | tf_op jit(solution)/shard_map/ppermute | solution.py:23
  78.1 29.5 %all-to-all-start.1 = ((bf16[4,96,2688]{2,1,0:T(8,128)(2,1)}), bf16[4,96,2688]{2,1,0:T(8,128)(2,1)S(1)}, u32[]{:S(2)}, u32[]{:S(2)}) async-start(bf16[4,96,2688]{2,1,0:T(8,128)(2,1)} %get-tuple-element.13), calls=%async_computation.1 | async-start | bytes 4128768 | tf_op jit(solution)/shard_map/all_to_all | solution.py:29
  83.5 12.2 %collective-permute-start.6 = (bf16[128,1024]{1,0:T(8,128)(2,1)}, bf16[128,1024]{1,0:T(8,128)(2,1)S(1)}, u32[]{:S(2)}, u32[]{:S(2)}) collective-permute-start(bf16[128,1024]{1,0:T(8,128)(2,1)} %shard_map.55), channel_id=1, source_target_pairs={{0,1},{1,2},{2,3},{3,0},{64,67},{65,64},{66,65},{67,66},{4,5},{5,6... | collective-permute-start | bytes 786440 | tf_op jit(solution)/shard_map/ppermute | solution.py:23
  95.6 0.7 copy-start.11
  106.0 10.7 %copy-start.1 = (bf16[448,1024]{1,0:T(8,128)(2,1)S(1)}, bf16[448,1024]{1,0:T(8,128)(2,1)}, u32[]{:S(2)}) copy-start(bf16[448,1024]{1,0:T(8,128)(2,1)} %copy-done) | copy-start | bytes 2752516
  107.7 1.3 copy-start.4
  109.0 33.7 %all-to-all-start = ((bf16[4,32,6272]{2,1,0:T(8,128)(2,1)}), bf16[4,32,6272]{2,1,0:T(8,128)(2,1)}, u32[]{:S(2)}, u32[]{:S(2)}) async-start(bf16[4,32,6272]{2,1,0:T(8,128)(2,1)} %shard_map.58), calls=%async_computation | async-start | bytes 3211264 | tf_op jit(solution)/shard_map/all_to_all | solution.py:29
  113.4 21.2 %collective-permute-start.11 = (bf16[448,1024]{1,0:T(8,128)(2,1)}, bf16[448,1024]{1,0:T(8,128)(2,1)S(1)}, u32[]{:S(2)}, u32[]{:S(2)}) collective-permute-start(bf16[448,1024]{1,0:T(8,128)(2,1)} %bitcast.13), channel_id=1, source_target_pairs={{0,12},{4,0},{8,4},{12,8},{64,68},{68,72},{72,76},{76,64},{1,13},{... | collective-permute-start | bytes 2752520 | tf_op jit(solution)/shard_map/ppermute | solution.py:23
  116.7 22.4 %collective-permute-start.12 = (bf16[448,1024]{1,0:T(8,128)(2,1)S(1)}, bf16[448,1024]{1,0:T(8,128)(2,1)S(1)}, u32[]{:S(2)}, u32[]{:S(2)}) collective-permute-start(bf16[448,1024]{1,0:T(8,128)(2,1)S(1)} %copy-done.1), channel_id=1, source_target_pairs={{0,4},{4,8},{8,12},{12,0},{64,76},{68,64},{72,68},{76,72},{1,5},{5... | collective-permute-start | bytes 2752520 | tf_op jit(solution)/shard_map/ppermute | solution.py:23
  134.5 4.5 %copy-start.2 = (bf16[448,1024]{1,0:T(8,128)(2,1)}, bf16[448,1024]{1,0:T(8,128)(2,1)S(1)}, u32[]{:S(2)}) copy-start(bf16[448,1024]{1,0:T(8,128)(2,1)S(1)} %collective-permute-done.11.refs_0_.refs_3_) | copy-start | bytes 2752516
  139.1 0.9 copy-start.3
  158.5 15.6 %all-to-all-start.3 = ((bf16[4,64,1792]{2,1,0:T(8,128)(2,1)}), bf16[4,64,1792]{2,1,0:T(8,128)(2,1)S(1)}, u32[]{:S(2)}, u32[]{:S(2)}) async-start(bf16[4,64,1792]{2,1,0:T(8,128)(2,1)} %get-tuple-element.15), calls=%async_computation.3 | async-start | bytes 1835008 | tf_op jit(solution)/shard_map/all_to_all | solution.py:29
  162.0 9.7 %copy-start.12 = (s32[8,2]{0,1:T(2,128)S(1)}, s32[8,2]{0,1:T(2,128)}, u32[]{:S(2)}) copy-start(s32[8,2]{0,1:T(2,128)} %param.6) | copy-start | bytes 196
  162.0 9.7 %copy-start.13 = (f32[8,2]{0,1:T(2,128)S(1)}, f32[8,2]{0,1:T(2,128)}, u32[]{:S(2)}) copy-start(f32[8,2]{0,1:T(2,128)} %param.7) | copy-start | bytes 196
  165.5 16.3 %collective-permute-start.13 = (bf16[128,1024]{1,0:T(8,128)(2,1)}, bf16[128,1024]{1,0:T(8,128)(2,1)S(1)}, u32[]{:S(2)}, u32[]{:S(2)}) collective-permute-start(bf16[128,1024]{1,0:T(8,128)(2,1)} %shard_map.63), channel_id=1, source_target_pairs={{0,1},{1,2},{2,3},{3,0},{64,67},{65,64},{66,65},{67,66},{4,5},{5,6... | collective-permute-start | bytes 786440 | tf_op jit(solution)/shard_map/ppermute | solution.py:23
  174.2 3.5 %copy-start.6 = (bf16[4,64,1792]{2,1,0:T(8,128)(2,1)}, bf16[4,64,1792]{2,1,0:T(8,128)(2,1)S(1)}, u32[]{:S(2)}) copy-start(bf16[4,64,1792]{2,1,0:T(8,128)(2,1)S(1)} %all-to-all-done.3.refs_0_) | copy-start | bytes 2752516
  174.2 20.7 %all-to-all-start.2 = ((bf16[4,32,1792]{2,1,0:T(8,128)(2,1)}), bf16[4,32,1792]{2,1,0:T(8,128)(2,1)S(1)}, u32[]{:S(2)}, u32[]{:S(2)}) async-start(bf16[4,32,1792]{2,1,0:T(8,128)(2,1)} %get-tuple-element.14), calls=%async_computation.2 | async-start | bytes 917504 | tf_op jit(solution)/shard_map/all_to_all | solution.py:29
  182.8 16.2 %collective-permute-start.14 = (bf16[128,1024]{1,0:T(8,128)(2,1)S(1)}, bf16[128,1024]{1,0:T(8,128)(2,1)S(1)}, u32[]{:S(2)}, u32[]{:S(2)}) collective-permute-start(bf16[128,1024]{1,0:T(8,128)(2,1)S(1)} %add_convert_fusion.2), channel_id=1, source_target_pairs={{0,1},{1,2},{2,3},{3,0},{64,67},{65,64},{66,65},{67,66},{4,5},{5,6... | collective-permute-start | bytes 786440 | tf_op jit(solution)/shard_map/ppermute | solution.py:23
  187.4 13.0 %collective-permute-start.15 = (bf16[128,1024]{1,0:T(8,128)(2,1)}, bf16[128,1024]{1,0:T(8,128)(2,1)S(1)}, u32[]{:S(2)}, u32[]{:S(2)}) collective-permute-start(bf16[128,1024]{1,0:T(8,128)(2,1)} %get-tuple-element.18), channel_id=1, source_target_pairs={{0,3},{1,0},{2,1},{3,2},{64,65},{65,66},{66,67},{67,64},{4,7},{5,4... | collective-permute-start | bytes 786440 | tf_op jit(solution)/shard_map/ppermute | solution.py:23
  194.8 0.8 copy-start.10
  203.0 12.2 %collective-permute-start.16 = (bf16[4,64,1024]{2,1,0:T(8,128)(2,1)S(1)}, bf16[4,64,1024]{2,1,0:T(8,128)(2,1)S(1)}, u32[]{:S(2)}, u32[]{:S(2)}) collective-permute-start(bf16[4,64,1024]{2,1,0:T(8,128)(2,1)S(1)} %add_convert_fusion.1), channel_id=1, source_target_pairs={{0,64},{64,0},{1,65},{65,1},{2,66},{66,2},{3,67},{67,3},{4,68},{68... | collective-permute-start | bytes 1572872 | tf_op jit(solution)/shard_map/ppermute | solution.py:18

commit v6 on v5

--- a/solution.py
+++ b/solution.py
@@ -32,20 +32,6 @@
 DIMS = (((1,), (1,)), ((), ()))
 
 
-def hold(a, after):
-    def kernel(a_ref, after_ref, out_ref):
-        out_ref[...] = a_ref[...]
-
-    return pl.pallas_call(
-        kernel,
-        in_specs=[WHOLE, ANY],
-        out_specs=WHOLE,
-        out_shape=jax.ShapeDtypeStruct(a.shape, a.dtype),
-        compiler_params=pltpu.CompilerParams(vmem_limit_bytes=LIMIT),
-        cost_estimate=COST,
-    )(a, after)
-
-
 def fetch(refs, held, sems):
     copies = [pltpu.make_async_copy(ref, held.at[i], sems.at[i]) for i, ref in enumerate(refs)]
     for copy in copies:
@@ -53,34 +39,48 @@
     return copies
 
 
-def early(pieces, weights, after):
+def early(pieces, weights):
     def kernel(*refs):
-        out_ref, copy_ref, held, sems, sem = refs[-5:]
+        out_ref, piece_ref, copy_ref, held, sums, sems, out_sems, sem, piece_sem = refs[-9:]
         copies = fetch(refs[3:6], held, sems)
+        piece = pltpu.make_async_copy(refs[0], piece_ref, piece_sem)
+        piece.start()
         x = jnp.concatenate([ref[...] for ref in refs[:3]])
         spare = pltpu.make_async_copy(held.at[1], copy_ref, sem)
+        going = []
         for i in range(3):
             copies[i].wait()
             if i == 1:
                 spare.start()
+            columns = pl.ds(896 * i, 896)
             out = lax.dot_general(x, held[i], DIMS, preferred_element_type=wide).astype(half)
             for p in range(3):
-                out_ref[:, pl.ds(32 * p, 32), pl.ds(896 * i, 896)] = out[128 * p : 128 * p + 128].reshape(4, 32, 896)
-        spare.wait()
-
-    return pl.pallas_call(
-        kernel,
-        in_specs=[WHOLE] * 3 + [ANY] * (3 + len(after)),
-        out_specs=[WHOLE, ANY],
-        out_shape=[jax.ShapeDtypeStruct((4, 96, 2688), half), jax.ShapeDtypeStruct((896, 1024), half)],
+                sums[:, pl.ds(32 * p, 32), columns] = out[128 * p : 128 * p + 128].reshape(4, 32, 896)
+            going.append(pltpu.make_async_copy(sums.at[:, :, columns], out_ref.at[:, :, columns], out_sems.at[i]))
+            going[i].start()
+        for copy in going + [spare, piece]:
+            copy.wait()
+
+    return pl.pallas_call(
+        kernel,
+        in_specs=[WHOLE] * 3 + [ANY] * 3,
+        out_specs=[ANY] * 3,
+        out_shape=[
+            jax.ShapeDtypeStruct((4, 96, 2688), half),
+            jax.ShapeDtypeStruct((128, 1024), half),
+            jax.ShapeDtypeStruct((896, 1024), half),
+        ],
         scratch_shapes=[
             pltpu.VMEM((3, 896, 1024), half),
+            pltpu.VMEM((4, 96, 2688), half),
+            pltpu.SemaphoreType.DMA((3,)),
             pltpu.SemaphoreType.DMA((3,)),
             pltpu.SemaphoreType.DMA,
+            pltpu.SemaphoreType.DMA,
         ],
         compiler_params=pltpu.CompilerParams(vmem_limit_bytes=LIMIT),
         cost_estimate=COST,
-    )(*pieces, *weights, *after)
+    )(*pieces, *weights)
 
 
 def late_near(far, weights):
@@ -144,38 +144,47 @@
     return act(sums[:, at : at + 448], sums[:, at + 448 : at + 896])
 
 
-def activate_early(sums, after):
-    def kernel(sums_ref, *refs):
-        out_ref = refs[-1]
+def activate_early(sums):
+    def kernel(sums_ref, out_ref):
         total = jnp.sum(sums_ref[...].astype(wide), axis=0)
         out_ref[...] = jnp.concatenate([block(total, i) for i in range(3)], axis=1)
 
     return pl.pallas_call(
         kernel,
-        in_specs=[WHOLE] + [ANY] * len(after),
-        out_specs=WHOLE,
+        grid=(1,),
+        in_specs=[pl.BlockSpec((4, 96, 2688), lambda i: (0, 0, 0))],
+        out_specs=pl.BlockSpec((96, 1344), lambda i: (0, 0)),
         out_shape=jax.ShapeDtypeStruct((96, 1344), half),
         compiler_params=pltpu.CompilerParams(vmem_limit_bytes=LIMIT),
         cost_estimate=COST,
-    )(sums, *after)
-
-
-def activate_late(sums, first):
-    def kernel(sums_ref, first_ref, *outs):
+    )(sums)
+
+
+def activate_late(sums, begun, after):
+    def kernel(sums_ref, begun_ref, *refs):
+        others_ref, own_ref = refs[-2:]
         total = jnp.sum(sums_ref[...].astype(wide), axis=0)
         blocks = [block(total, i) for i in range(7)]
         far = jnp.concatenate(blocks[:4], axis=1)
-        rest = jnp.concatenate([first_ref[...], jnp.concatenate(blocks[4:])], axis=1)
-        for part, out in zip((far, rest[:64], rest[64:]), outs):
-            for j in range(4):
-                out[j] = part
-
-    return pl.pallas_call(
-        kernel,
-        out_shape=[jax.ShapeDtypeStruct((4, r, 1792), half) for r in (32, 64, 32)],
-        compiler_params=pltpu.CompilerParams(vmem_limit_bytes=LIMIT),
-        cost_estimate=COST,
-    )(sums, first)
+        rest = jnp.concatenate([begun_ref[...], jnp.concatenate(blocks[4:])], axis=1)
+        for j in range(4):
+            others_ref[j, :32] = far
+            others_ref[j, 32:] = rest[:64]
+            own_ref[j] = rest[64:]
+
+    return pl.pallas_call(
+        kernel,
+        grid=(1,),
+        in_specs=[
+            pl.BlockSpec((4, 32, 6272), lambda i: (0, 0, 0)),
+            pl.BlockSpec((96, 1344), lambda i: (0, 0)),
+        ]
+        + [ANY] * len(after),
+        out_specs=[pl.BlockSpec((4, r, 1792), lambda i: (0, 0, 0)) for r in (96, 32)],
+        out_shape=[jax.ShapeDtypeStruct((4, r, 1792), half) for r in (96, 32)],
+        compiler_params=pltpu.CompilerParams(vmem_limit_bytes=LIMIT),
+        cost_estimate=COST,
+    )(sums, begun, *after)
 
 
 def down(hidden, weights, types):
@@ -244,19 +253,16 @@
     )
 
     first, second = pass_on(rows, "zhi", 1), pass_on(rows, "zhi", -1)
-    part, w_next = early([first, second, rows], weights, [v_first])
-
-    far = pass_on(hold(first, second), "zhi", 1)
-    w_far = pass_on(w_next, "y", 1)
-    v_far = pass_on(v_first, "y", 1)
+    part, z_next, w_next = early([first, second, rows], weights)
+
+    far, w_far, v_far = pass_on(z_next, "zhi", 1), pass_on(w_next, "y", 1), pass_on(v_first, "y", 1)
     v_all = [v_own, v_first, v_second, v_far]
-    begun = activate_early(swap(part, "x"), [v_second, v_far])
+    begun = activate_early(swap(part, "x"))
     rest = swap(late_far([far, first, second, rows], w_far, late_near(far, weights)), "x")
-    far_h, near_h, own_h = activate_late(rest, begun)
-
-    (far_out,) = down(swap(far_h, "x"), v_all, (half,))
+    others_h, own_h = activate_late(rest, begun, [v_first, v_second])
+
+    far_out, first_out, second_out = down(swap(others_h, "x"), v_all, (half, half, wide))
     got = pass_on(far_out, "zhi", 1)
-    first_out, second_out = down(swap(near_h, "x"), v_all, (half, wide))
     back = pass_on(first_out, "zhi", -1)
     ahead = pass_on((second_out + got.astype(wide)).astype(half), "zhi", 1)
 

time: 244 us -> 249 us (1.020)
  waiting for transfers between devices: 49.5 us -> 75.2 us
  blocking collectives: 38.9 us -> 16.6 us
  starting transfers between devices: 95 us -> 103 us
  Pallas kernels: 35 us -> 30.3 us
    ppermute x12, waiting for transfers between devices: 45.2 us -> 68.8 us  [pass_on(): lax.ppermute(a, ('core', axis), [(c * n + i, c * n + (i + by * (1 - 2 * c...]
    all_to_all x2 -> x1, blocking collectives: 38.9 us -> 16.6 us  [swap(): return lax.all_to_all(a, axis, split_axis=0, concat_axis=0, tiled=True)]
    ppermute x5, starting transfers between devices: 26 us -> 31.4 us  [shift(): return lax.ppermute(a, axis, [(i, (i + by) % n) for i in range(n)])]
    pallas_call x3 -> x2, Pallas kernels: 10.9 us -> 8.13 us  [down(): pl.pallas_call(kernel, grid=(2,), in_specs=[pl.BlockSpec((4, 32 * n, 1792...]
    pallas_call x4 -> x3, Pallas kernels: 14.5 us -> 12.5 us  [the longest x1 6.69 us: early(): pl.pallas_call(kernel, in_specs=[WHOLE] * 3 + [ANY] * 3, out_specs=[ANY]...]
    unnamed x28 -> x32, local copies, waits for them, and re-layouts: 5.45 us -> 4.94 us
  transfers between devices with their start and end apart: 21 -> 21, of which waited for: 8 -> 11; matrix products, arithmetic and copies ran while one was open for 4% -> 4% of each run, Pallas kernels for 10% -> 6%
where the time goes in v6:
time: 249 us; the launch traced here: 248 us
  starting transfers between devices  103 us (41%)
  waiting for transfers between devices  75.2 us (30%)
  Pallas kernels  30.3 us (12%)
  blocking collectives  16.6 us (7%)
  other arithmetic  12.4 us (5%)
  between operations  5.44 us (2%)
  local copies, waits for them, and re-layouts  5.12 us (2%)
    ppermute x12, waiting for transfers between devices, pass_on(): lax.ppermute(a, ('core', axis), [(c * n + i, c * n + (i + by * (1 - 2 * c...  68.8 us
    ppermute x12, starting transfers between devices, pass_on(): lax.ppermute(a, ('core', axis), [(c * n + i, c * n + (i + by * (1 - 2 * c...  54.9 us
    ppermute x5, starting transfers between devices, shift(): return lax.ppermute(a, axis, [(i, (i + by) % n) for i in range(n)])  31.4 us
    all_to_all x1, blocking collectives, swap(): return lax.all_to_all(a, axis, split_axis=0, concat_axis=0, tiled=True)  16.6 us
    all_to_all x4, starting transfers between devices, swap(): return lax.all_to_all(a, axis, split_axis=0, concat_axis=0, tiled=True)  16.6 us
    pallas_call x2, Pallas kernels, down(): pl.pallas_call(kernel, grid=(2,), in_specs=[pl.BlockSpec((4, 32 * n, 1792...  8.13 us
    pallas_call x1, Pallas kernels, early(): pl.pallas_call(kernel, in_specs=[WHOLE] * 3 + [ANY] * 3, out_specs=[ANY]...  6.69 us
    pallas_call x1, Pallas kernels, late_near(): pl.pallas_call(kernel, in_specs=[WHOLE] + [ANY] * 3, out_specs=ANY, out_s...  5.62 us
  transfers between devices with their start and end apart: 21, of which 11 were waited for; matrix products, arithmetic and copies ran while one was open for 4% of the time, Pallas kernels for 6%

profile of v6, /device:TPU:1, one launch (start us, length us, event | category | flops | bytes accessed | tf_op | source)
XLA Modules:
  0.0 248.0 jit_solution(15300492155792316739)
XLA Ops:
  0.0 5.5 %collective-permute-start.6 = (bf16[896,1024]{1,0:T(8,128)(2,1)}, bf16[896,1024]{1,0:T(8,128)(2,1)S(1)}, u32[]{:S(2)}, u32[]{:S(2)}) collective-permute-start(bf16[896,1024]{1,0:T(8,128)(2,1)} %bitcast.12), channel_id=1, source_target_pairs={{0,4},{4,8},{8,12},{12,0},{64,76},{68,64},{72,68},{76,72},{1,5},{5... | collective-permute-start | bytes 5505032 | tf_op jit(solution)/shard_map/ppermute | solution.py:23
  5.5 1.9 collective-permute-start.7
  7.4 3.5 %collective-permute-start = (bf16[64,1024]{1,0:T(8,128)(2,1)}, bf16[64,1024]{1,0:T(8,128)(2,1)S(1)}, u32[]{:S(2)}, u32[]{:S(2)}) collective-permute-start(bf16[64,1024]{1,0:T(8,128)(2,1)} %bitcast.20), channel_id=1, source_target_pairs={{0,128},{128,256},{256,384},{384,0},{1,129},{129,257},{257,385},{3... | collective-permute-start | bytes 393224 | tf_op jit(solution)/shard_map/ppermute | solution.py:18
  11.0 4.9 %collective-permute-start.1 = (bf16[64,1024]{1,0:T(8,128)(2,1)}, bf16[64,1024]{1,0:T(8,128)(2,1)S(1)}, u32[]{:S(2)}, u32[]{:S(2)}) collective-permute-start(bf16[64,1024]{1,0:T(8,128)(2,1)} %bitcast.21), channel_id=1, source_target_pairs={{0,256},{128,384},{256,0},{384,128},{1,257},{129,385},{257,1},{385... | collective-permute-start | bytes 393224 | tf_op jit(solution)/shard_map/ppermute | solution.py:18
  15.9 2.6 %collective-permute-start.2 = (bf16[64,1024]{1,0:T(8,128)(2,1)}, bf16[64,1024]{1,0:T(8,128)(2,1)S(1)}, u32[]{:S(2)}, u32[]{:S(2)}) collective-permute-start(bf16[64,1024]{1,0:T(8,128)(2,1)} %bitcast.22), channel_id=1, source_target_pairs={{0,384},{128,0},{256,128},{384,256},{1,385},{129,1},{257,129},{385... | collective-permute-start | bytes 393224 | tf_op jit(solution)/shard_map/ppermute | solution.py:18
  18.5 0.8 convert_reduce_fusion
  22.4 1.4 collective-permute-done.2
  23.7 0.9 select_select_fusion.1
  24.7 6.0 %collective-permute-start.3 = (bf16[128,1024]{1,0:T(8,128)(2,1)S(1)}, bf16[128,1024]{1,0:T(8,128)(2,1)S(1)}, u32[]{:S(2)}, u32[]{:S(2)}) collective-permute-start(bf16[128,1024]{1,0:T(8,128)(2,1)S(1)} %pad_maximum_fusion), channel_id=1, source_target_pairs={{0,64},{64,0},{1,65},{65,1},{2,66},{66,2},{3,67},{67,3},{4,68},{68... | collective-permute-start | bytes 786440 | tf_op jit(solution)/shard_map/ppermute | solution.py:18
  33.2 0.9 slice_select_fusion.1
  34.2 8.7 %collective-permute-start.4 = (bf16[128,1024]{1,0:T(8,128)(2,1)S(1)}, bf16[128,1024]{1,0:T(8,128)(2,1)S(1)}, u32[]{:S(2)}, u32[]{:S(2)}) collective-permute-start(bf16[128,1024]{1,0:T(8,128)(2,1)S(1)} %pad_maximum_fusion.1.refs_2_.refs_3_), channel_id=1, source_target_pairs={{0,1},{1,2},{2,3},{3,0},{64,67},{65,64},{66,65},{67,66},{4,5},{5,6... | collective-permute-start | bytes 786440 | tf_op jit(solution)/shard_map/ppermute | solution.py:23
  42.9 1.9 collective-permute-start.5
  44.9 15.9 %collective-permute-done.4.refs_0_.refs_1_ = bf16[128,1024]{1,0:T(8,128)(2,1)S(1)} collective-permute-done((bf16[128,1024]{1,0:T(8,128)(2,1)S(1)}, bf16[128,1024]{1,0:T(8,128)(2,1)S(1)}, u32[]{:S(2)}, u32[]{:S(2)}) %collective-permute-start.4) | collective-permute-done | bytes 262176 | tf_op jit(solution)/shard_map/ppermute | solution.py:23
  62.3 6.7 %shard_map.55 = (bf16[4,96,2688]{2,1,0:T(8,128)(2,1)}, bf16[128,1024]{1,0:T(8,128)(2,1)}, bf16[896,1024]{1,0:T(8,128)(2,1)}) custom-call(bf16[128,1024]{1,0:T(8,128)(2,1)} %copy-done.10, bf16[128,1024]{1,0:T(8,128)(2,1)} %copy-done.11, bf16[128,1024]{1,0:T(8,128)(2,1)} %copy-done.8, bf16[896,1024]{1,0:T(8,128)(2,1)} %bitcast.14, ...), custom_call_target="tpu_custom_call" | custom-call | flops 1024 | bytes 1024 | tf_op jit(solution)/shard_map/pallas_call | solution.py:64
  69.0 6.1 %collective-permute-start.9 = (bf16[896,1024]{1,0:T(8,128)(2,1)}, bf16[896,1024]{1,0:T(8,128)(2,1)}, u32[]{:S(2)}, u32[]{:S(2)}) collective-permute-start(bf16[896,1024]{1,0:T(8,128)(2,1)} %get-tuple-element.14), channel_id=1, source_target_pairs={{0,4},{4,8},{8,12},{12,0},{64,76},{68,64},{72,68},{76,72},{1,5},{5... | collective-permute-start | bytes 5505032 | tf_op jit(solution)/shard_map/ppermute | solution.py:23
  75.0 4.2 %all-to-all-start.1 = ((bf16[4,96,2688]{2,1,0:T(8,128)(2,1)}), bf16[4,96,2688]{2,1,0:T(8,128)(2,1)S(1)}, u32[]{:S(2)}, u32[]{:S(2)}) async-start(bf16[4,96,2688]{2,1,0:T(8,128)(2,1)} %get-tuple-element.15), calls=%async_computation.1 | async-start | bytes 4128768 | tf_op jit(solution)/shard_map/all_to_all | solution.py:29
  79.2 5.7 %collective-permute-start.8 = (bf16[128,1024]{1,0:T(8,128)(2,1)S(1)}, bf16[128,1024]{1,0:T(8,128)(2,1)S(1)}, u32[]{:S(2)}, u32[]{:S(2)}) collective-permute-start(bf16[128,1024]{1,0:T(8,128)(2,1)S(1)} %copy-done.15), channel_id=1, source_target_pairs={{0,1},{1,2},{2,3},{3,0},{64,67},{65,64},{66,65},{67,66},{4,5},{5,6... | collective-permute-start | bytes 786440 | tf_op jit(solution)/shard_map/ppermute | solution.py:23
  84.9 8.7 %collective-permute-done.8.far_ref.refs_0_ = bf16[128,1024]{1,0:T(8,128)(2,1)S(1)} collective-permute-done((bf16[128,1024]{1,0:T(8,128)(2,1)S(1)}, bf16[128,1024]{1,0:T(8,128)(2,1)S(1)}, u32[]{:S(2)}, u32[]{:S(2)}) %collective-permute-start.8) | collective-permute-done | bytes 262176 | tf_op jit(solution)/shard_map/ppermute | solution.py:23
  94.3 5.6 %shard_map.56.refs_5_ = bf16[4,32,6272]{2,1,0:T(8,128)(2,1)} custom-call(bf16[128,1024]{1,0:T(8,128)(2,1)} %copy-done.12, bf16[896,1024]{1,0:T(8,128)(2,1)} %bitcast.15, bf16[896,1024]{1,0:T(8,128)(2,1)} %copy-done.4, bf16[896,1024]{1,0:T(8,128)(2,1)} %collective-permute-done.7.refs_5_.refs_2_), custom_call_target="tpu_custom_call" | custom-call | flops 1024 | bytes 1024 | tf_op jit(solution)/shard_map/pallas_call | solution.py:99
  100.0 4.1 %shard_map.57 = bf16[4,32,6272]{2,1,0:T(8,128)(2,1)} custom-call(bf16[128,1024]{1,0:T(8,128)(2,1)} %copy-done.12, bf16[128,1024]{1,0:T(8,128)(2,1)} %copy-done.10, bf16[128,1024]{1,0:T(8,128)(2,1)} %copy-done.11, bf16[128,1024]{1,0:T(8,128)(2,1)} %copy-done.8, bf16[896,1024]{1,0:T(8,128)(2,1)} %collective-permute-done.9.refs_4_, ...), custom_call_target="tpu_custom_call", output_to_operand_aliasing={{}: (5, {})} | custom-call | flops 1024 | bytes 1024 | tf_op jit(solution)/shard_map/pallas_call | solution.py:126
  104.4 4.4 %all-to-all-start = ((bf16[4,32,6272]{2,1,0:T(8,128)(2,1)}), bf16[4,32,6272]{2,1,0:T(8,128)(2,1)}, u32[]{:S(2)}, u32[]{:S(2)}) async-start(bf16[4,32,6272]{2,1,0:T(8,128)(2,1)} %shard_map.57), calls=%async_computation | async-start | bytes 3211264 | tf_op jit(solution)/shard_map/all_to_all | solution.py:29
  108.8 1.9 collective-permute-start.10
  110.7 3.4 %collective-permute-start.11 = (bf16[448,1024]{1,0:T(8,128)(2,1)S(1)}, bf16[448,1024]{1,0:T(8,128)(2,1)S(1)}, u32[]{:S(2)}, u32[]{:S(2)}) collective-permute-start(bf16[448,1024]{1,0:T(8,128)(2,1)S(1)} %bitcast.19), channel_id=1, source_target_pairs={{0,12},{4,0},{8,4},{12,8},{64,68},{68,72},{72,76},{76,64},{1,13},{... | collective-permute-start | bytes 2752520 | tf_op jit(solution)/shard_map/ppermute | solution.py:23
  114.1 2.7 %shard_map.58.begun_ref = bf16[96,1344]{1,0:T(8,128)(2,1)} custom-call(bf16[4,96,2688]{2,1,0:T(8,128)(2,1)} %copy-done.3), custom_call_target="tpu_custom_call" | custom-call | flops 1024 | bytes 1024 | tf_op jit(solution)/shard_map/pallas_call | solution.py:152
  116.8 9.1 %collective-permute-done.10.refs_0_.refs_2_ = bf16[448,1024]{1,0:T(8,128)(2,1)S(1)} collective-permute-done((bf16[448,1024]{1,0:T(8,128)(2,1)S(1)}, bf16[448,1024]{1,0:T(8,128)(2,1)S(1)}, u32[]{:S(2)}, u32[]{:S(2)}) %collective-permute-start.10) | collective-permute-done | bytes 917536 | tf_op jit(solution)/shard_map/ppermute | solution.py:23
  125.9 8.1 %collective-permute-done.11.refs_1_.refs_3_ = bf16[448,1024]{1,0:T(8,128)(2,1)S(1)} collective-permute-done((bf16[448,1024]{1,0:T(8,128)(2,1)S(1)}, bf16[448,1024]{1,0:T(8,128)(2,1)S(1)}, u32[]{:S(2)}, u32[]{:S(2)}) %collective-permute-start.11) | collective-permute-done | bytes 917536 | tf_op jit(solution)/shard_map/ppermute | solution.py:23
  134.0 0.9 copy-done.2
  134.9 3.1 %shard_map.59 = (bf16[4,96,1792]{2,1,0:T(8,128)(2,1)}, bf16[4,32,1792]{2,1,0:T(8,128)(2,1)}) custom-call(bf16[4,32,6272]{2,1,0:T(8,128)(2,1)} %all-to-all-done.sums_ref, bf16[96,1344]{1,0:T(8,128)(2,1)} %shard_map.58.begun_ref, bf16[448,1024]{1,0:T(8,128)(2,1)} %copy-done, bf16[448,1024]{1,0:T(8,128)(2,1)} %copy-done.2), custom_call_target="tpu_custom_call" | custom-call | flops 1024 | bytes 1024 | tf_op jit(solution)/shard_map/pallas_call | solution.py:175
  138.1 4.6 %all-to-all-start.3 = ((bf16[4,96,1792]{2,1,0:T(8,128)(2,1)}), bf16[4,96,1792]{2,1,0:T(8,128)(2,1)S(1)}, u32[]{:S(2)}, u32[]{:S(2)}) async-start(bf16[4,96,1792]{2,1,0:T(8,128)(2,1)} %get-tuple-element.17), calls=%async_computation.3 | async-start | bytes 2752512 | tf_op jit(solution)/shard_map/all_to_all | solution.py:29
  142.7 2.1 collective-permute-start.12
  144.7 12.5 %collective-permute-done.12.refs_4_ = bf16[448,1024]{1,0:T(8,128)(2,1)S(1)} collective-permute-done((bf16[448,1024]{1,0:T(8,128)(2,1)S(1)}, bf16[448,1024]{1,0:T(8,128)(2,1)S(1)}, u32[]{:S(2)}, u32[]{:S(2)}) %collective-permute-start.12) | collective-permute-done | bytes 917536 | tf_op jit(solution)/shard_map/ppermute | solution.py:23
  157.2 4.6 %all-to-all-done.3.refs_0_ = bf16[4,96,1792]{2,1,0:T(8,128)(2,1)S(1)} async-done(((bf16[4,96,1792]{2,1,0:T(8,128)(2,1)}), bf16[4,96,1792]{2,1,0:T(8,128)(2,1)S(1)}, u32[]{:S(2)}, u32[]{:S(2)}) %all-to-all-start.3) | async-done | bytes 1376288 | tf_op jit(solution)/shard_map/all_to_all | solution.py:29
  161.8 1.1 copy-done.5
  162.9 4.7 %shard_map.61 = (bf16[128,1024]{1,0:T(8,128)(2,1)}, bf16[128,1024]{1,0:T(8,128)(2,1)}, f32[128,1024]{1,0:T(8,128)}) custom-call(bf16[4,96,1792]{2,1,0:T(8,128)(2,1)} %copy-done.5, bf16[448,1024]{1,0:T(8,128)(2,1)} %bitcast.16, bf16[448,1024]{1,0:T(8,128)(2,1)} %copy-done, bf16[448,1024]{1,0:T(8,128)(2,1)} %copy-done.2, bf16[448,1024]{1,0:T(8,128)(2,1)} %copy-done.7), custom_call_target="tpu_custom_call" | custom-call | flops 1024 | bytes 1024 | tf_op jit(solution)/shard_map/pallas_call | solution.py:200
  167.6 7.8 %collective-permute-start.13 = (bf16[128,1024]{1,0:T(8,128)(2,1)}, bf16[128,1024]{1,0:T(8,128)(2,1)S(1)}, u32[]{:S(2)}, u32[]{:S(2)}) collective-permute-start(bf16[128,1024]{1,0:T(8,128)(2,1)} %get-tuple-element.19), channel_id=1, source_target_pairs={{0,1},{1,2},{2,3},{3,0},{64,67},{65,64},{66,65},{67,66},{4,5},{5,6... | collective-permute-start | bytes 786440 | tf_op jit(solution)/shard_map/ppermute | solution.py:23
  176.0 3.5 %all-to-all-start.2 = ((bf16[4,32,1792]{2,1,0:T(8,128)(2,1)}), bf16[4,32,1792]{2,1,0:T(8,128)(2,1)S(1)}, u32[]{:S(2)}, u32[]{:S(2)}) async-start(bf16[4,32,1792]{2,1,0:T(8,128)(2,1)} %get-tuple-element.16), calls=%async_computation.2 | async-start | bytes 917504 | tf_op jit(solution)/shard_map/all_to_all | solution.py:29
  179.5 1.9 collective-permute-start.15
  181.4 10.0 %collective-permute-done.13 = bf16[128,1024]{1,0:T(8,128)(2,1)S(1)} collective-permute-done((bf16[128,1024]{1,0:T(8,128)(2,1)}, bf16[128,1024]{1,0:T(8,128)(2,1)S(1)}, u32[]{:S(2)}, u32[]{:S(2)}) %collective-permute-start.13) | collective-permute-done | bytes 262176 | tf_op jit(solution)/shard_map/ppermute | solution.py:23
  191.4 1.1 add_convert_fusion.2
  192.5 8.1 %collective-permute-start.14 = (bf16[128,1024]{1,0:T(8,128)(2,1)S(1)}, bf16[128,1024]{1,0:T(8,128)(2,1)S(1)}, u32[]{:S(2)}, u32[]{:S(2)}) collective-permute-start(bf16[128,1024]{1,0:T(8,128)(2,1)S(1)} %add_convert_fusion.2), channel_id=1, source_target_pairs={{0,1},{1,2},{2,3},{3,0},{64,67},{65,64},{66,65},{67,66},{4,5},{5,6... | collective-permute-start | bytes 786440 | tf_op jit(solution)/shard_map/ppermute | solution.py:23
  203.4 0.8 copy-done.9
  204.1 3.4 %shard_map.60 = f32[128,1024]{1,0:T(8,128)} custom-call(bf16[4,32,1792]{2,1,0:T(8,128)(2,1)} %copy-done.9, bf16[448,1024]{1,0:T(8,128)(2,1)} %bitcast.17, bf16[448,1024]{1,0:T(8,128)(2,1)} %copy-done, bf16[448,1024]{1,0:T(8,128)(2,1)} %copy-done.2, bf16[448,1024]{1,0:T(8,128)(2,1)} %copy-done.7), custom_call_target="tpu_custom_call" | custom-call | flops 1024 | bytes 1024 | tf_op jit(solution)/shard_map/pallas_call | solution.py:200
  207.6 4.4 %collective-permute-done.14 = bf16[128,1024]{1,0:T(8,128)(2,1)S(1)} collective-permute-done((bf16[128,1024]{1,0:T(8,128)(2,1)S(1)}, bf16[128,1024]{1,0:T(8,128)(2,1)S(1)}, u32[]{:S(2)}, u32[]{:S(2)}) %collective-permute-start.14) | collective-permute-done | bytes 262176 | tf_op jit(solution)/shard_map/ppermute | solution.py:23
  212.0 1.1 convert_add_fusion
  213.1 1.2 slice_multiply_fusion.1
  214.5 14.2 %collective-permute-start.16 = (bf16[4,64,1024]{2,1,0:T(8,128)(2,1)S(1)}, bf16[4,64,1024]{2,1,0:T(8,128)(2,1)S(1)}, u32[]{:S(2)}, u32[]{:S(2)}) collective-permute-start(bf16[4,64,1024]{2,1,0:T(8,128)(2,1)S(1)} %add_convert_fusion.1), channel_id=1, source_target_pairs={{0,64},{64,0},{1,65},{65,1},{2,66},{66,2},{3,67},{67,3},{4,68},{68... | collective-permute-start | bytes 1572872 | tf_op jit(solution)/shard_map/ppermute | solution.py:18
  230.6 16.6 %all_to_all.25 = bf16[4,64,1024]{2,1,0:T(8,128)(2,1)S(1)} all-to-all(bf16[4,64,1024]{2,1,0:T(8,128)(2,1)S(1)} %add_convert_fusion), channel_id=1, replica_groups=mesh['zlo'=4,'core'=2,'x'=4,'y'=4,'zhi'=4] {'zlo'}, dimensions={0} | all-to-all | bytes 1048576 | tf_op jit(solution)/shard_map/all_to_all | solution.py:29
  247.2 0.7 reduce_sum.112
  (58 shorter events, 8.4 us)
Async XLA Ops:
  0.0 60.8 %collective-permute-start.6 = (bf16[896,1024]{1,0:T(8,128)(2,1)}, bf16[896,1024]{1,0:T(8,128)(2,1)S(1)}, u32[]{:S(2)}, u32[]{:S(2)}) collective-permute-start(bf16[896,1024]{1,0:T(8,128)(2,1)} %bitcast.12), channel_id=1, source_target_pairs={{0,4},{4,8},{8,12},{12,0},{64,76},{68,64},{72,68},{76,72},{1,5},{5... | collective-permute-start | bytes 5505032 | tf_op jit(solution)/shard_map/ppermute | solution.py:23
  5.5 55.4 %collective-permute-start.7 = (bf16[896,1024]{1,0:T(8,128)(2,1)}, bf16[896,1024]{1,0:T(8,128)(2,1)}, u32[]{:S(2)}, u32[]{:S(2)}) collective-permute-start(bf16[896,1024]{1,0:T(8,128)(2,1)} %bitcast.13), channel_id=1, source_target_pairs={{0,12},{4,0},{8,4},{12,8},{64,68},{68,72},{72,76},{76,64},{1,13},{... | collective-permute-start | bytes 5505032 | tf_op jit(solution)/shard_map/ppermute | solution.py:23
  7.4 14.9 %collective-permute-start = (bf16[64,1024]{1,0:T(8,128)(2,1)}, bf16[64,1024]{1,0:T(8,128)(2,1)S(1)}, u32[]{:S(2)}, u32[]{:S(2)}) collective-permute-start(bf16[64,1024]{1,0:T(8,128)(2,1)} %bitcast.20), channel_id=1, source_target_pairs={{0,128},{128,256},{256,384},{384,0},{1,129},{129,257},{257,385},{3... | collective-permute-start | bytes 393224 | tf_op jit(solution)/shard_map/ppermute | solution.py:18
  11.0 11.4 %collective-permute-start.1 = (bf16[64,1024]{1,0:T(8,128)(2,1)}, bf16[64,1024]{1,0:T(8,128)(2,1)S(1)}, u32[]{:S(2)}, u32[]{:S(2)}) collective-permute-start(bf16[64,1024]{1,0:T(8,128)(2,1)} %bitcast.21), channel_id=1, source_target_pairs={{0,256},{128,384},{256,0},{384,128},{1,257},{129,385},{257,1},{385... | collective-permute-start | bytes 393224 | tf_op jit(solution)/shard_map/ppermute | solution.py:18
  15.9 7.9 %collective-permute-start.2 = (bf16[64,1024]{1,0:T(8,128)(2,1)}, bf16[64,1024]{1,0:T(8,128)(2,1)S(1)}, u32[]{:S(2)}, u32[]{:S(2)}) collective-permute-start(bf16[64,1024]{1,0:T(8,128)(2,1)} %bitcast.22), channel_id=1, source_target_pairs={{0,384},{128,0},{256,128},{384,256},{1,385},{129,1},{257,129},{385... | collective-permute-start | bytes 393224 | tf_op jit(solution)/shard_map/ppermute | solution.py:18
  24.7 8.5 %collective-permute-start.3 = (bf16[128,1024]{1,0:T(8,128)(2,1)S(1)}, bf16[128,1024]{1,0:T(8,128)(2,1)S(1)}, u32[]{:S(2)}, u32[]{:S(2)}) collective-permute-start(bf16[128,1024]{1,0:T(8,128)(2,1)S(1)} %pad_maximum_fusion), channel_id=1, source_target_pairs={{0,64},{64,0},{1,65},{65,1},{2,66},{66,2},{3,67},{67,3},{4,68},{68... | collective-permute-start | bytes 786440 | tf_op jit(solution)/shard_map/ppermute | solution.py:18
  34.2 26.6 %copy-start.8 = (bf16[128,1024]{1,0:T(8,128)(2,1)}, bf16[128,1024]{1,0:T(8,128)(2,1)S(1)}, u32[]{:S(2)}) copy-start(bf16[128,1024]{1,0:T(8,128)(2,1)S(1)} %pad_maximum_fusion.1.refs_2_.refs_3_) | copy-start | bytes 786436
  34.2 26.6 %collective-permute-start.4 = (bf16[128,1024]{1,0:T(8,128)(2,1)S(1)}, bf16[128,1024]{1,0:T(8,128)(2,1)S(1)}, u32[]{:S(2)}, u32[]{:S(2)}) collective-permute-start(bf16[128,1024]{1,0:T(8,128)(2,1)S(1)} %pad_maximum_fusion.1.refs_2_.refs_3_), channel_id=1, source_target_pairs={{0,1},{1,2},{2,3},{3,0},{64,67},{65,64},{66,65},{67,66},{4,5},{5,6... | collective-permute-start | bytes 786440 | tf_op jit(solution)/shard_map/ppermute | solution.py:23
  42.9 17.9 %collective-permute-start.5 = (bf16[128,1024]{1,0:T(8,128)(2,1)S(1)}, bf16[128,1024]{1,0:T(8,128)(2,1)S(1)}, u32[]{:S(2)}, u32[]{:S(2)}) collective-permute-start(bf16[128,1024]{1,0:T(8,128)(2,1)S(1)} %pad_maximum_fusion.1.refs_2_.refs_3_), channel_id=1, source_target_pairs={{0,3},{1,0},{2,1},{3,2},{64,65},{65,66},{66,67},{67,64},{4,7},{5,4... | collective-permute-start | bytes 786440 | tf_op jit(solution)/shard_map/ppermute | solution.py:23
  60.8 0.7 copy-start.10
  60.8 0.8 copy-start.11
  60.8 1.4 copy-start.4
  69.0 31.0 %collective-permute-start.9 = (bf16[896,1024]{1,0:T(8,128)(2,1)}, bf16[896,1024]{1,0:T(8,128)(2,1)}, u32[]{:S(2)}, u32[]{:S(2)}) collective-permute-start(bf16[896,1024]{1,0:T(8,128)(2,1)} %get-tuple-element.14), channel_id=1, source_target_pairs={{0,4},{4,8},{8,12},{12,0},{64,76},{68,64},{72,68},{76,72},{1,5},{5... | collective-permute-start | bytes 5505032 | tf_op jit(solution)/shard_map/ppermute | solution.py:23
  75.0 4.2 %copy-start.15 = (bf16[128,1024]{1,0:T(8,128)(2,1)S(1)}, bf16[128,1024]{1,0:T(8,128)(2,1)}, u32[]{:S(2)}) copy-start(bf16[128,1024]{1,0:T(8,128)(2,1)} %get-tuple-element.13) | copy-start | bytes 786436
  75.0 29.3 %all-to-all-start.1 = ((bf16[4,96,2688]{2,1,0:T(8,128)(2,1)}), bf16[4,96,2688]{2,1,0:T(8,128)(2,1)S(1)}, u32[]{:S(2)}, u32[]{:S(2)}) async-start(bf16[4,96,2688]{2,1,0:T(8,128)(2,1)} %get-tuple-element.15), calls=%async_computation.1 | async-start | bytes 4128768 | tf_op jit(solution)/shard_map/all_to_all | solution.py:29
  79.2 14.4 %collective-permute-start.8 = (bf16[128,1024]{1,0:T(8,128)(2,1)S(1)}, bf16[128,1024]{1,0:T(8,128)(2,1)S(1)}, u32[]{:S(2)}, u32[]{:S(2)}) collective-permute-start(bf16[128,1024]{1,0:T(8,128)(2,1)S(1)} %copy-done.15), channel_id=1, source_target_pairs={{0,1},{1,2},{2,3},{3,0},{64,67},{65,64},{66,65},{67,66},{4,5},{5,6... | collective-permute-start | bytes 786440 | tf_op jit(solution)/shard_map/ppermute | solution.py:23
  93.6 0.7 copy-start.12
  104.0 4.7 %copy-start.6 = (bf16[1,448,1024]{2,1,0:T(8,128)(2,1)S(1)}, bf16[1,448,1024]{2,1,0:T(8,128)(2,1)}, u32[]{:S(2)}) copy-start(bf16[1,448,1024]{2,1,0:T(8,128)(2,1)} %param.9) | copy-start | bytes 2752516
  104.4 4.4 %copy-start.3 = (bf16[4,96,2688]{2,1,0:T(8,128)(2,1)}, bf16[4,96,2688]{2,1,0:T(8,128)(2,1)S(1)}, u32[]{:S(2)}) copy-start(bf16[4,96,2688]{2,1,0:T(8,128)(2,1)S(1)} %all-to-all-done.1.sums_ref) | copy-start | bytes 6193156
  104.4 29.6 %all-to-all-start = ((bf16[4,32,6272]{2,1,0:T(8,128)(2,1)}), bf16[4,32,6272]{2,1,0:T(8,128)(2,1)}, u32[]{:S(2)}, u32[]{:S(2)}) async-start(bf16[4,32,6272]{2,1,0:T(8,128)(2,1)} %shard_map.57), calls=%async_computation | async-start | bytes 3211264 | tf_op jit(solution)/shard_map/all_to_all | solution.py:29
  108.8 17.1 %collective-permute-start.10 = (bf16[448,1024]{1,0:T(8,128)(2,1)S(1)}, bf16[448,1024]{1,0:T(8,128)(2,1)S(1)}, u32[]{:S(2)}, u32[]{:S(2)}) collective-permute-start(bf16[448,1024]{1,0:T(8,128)(2,1)S(1)} %bitcast.18), channel_id=1, source_target_pairs={{0,4},{4,8},{8,12},{12,0},{64,76},{68,64},{72,68},{76,72},{1,5},{5... | collective-permute-start | bytes 2752520 | tf_op jit(solution)/shard_map/ppermute | solution.py:23
  110.7 23.3 %collective-permute-start.11 = (bf16[448,1024]{1,0:T(8,128)(2,1)S(1)}, bf16[448,1024]{1,0:T(8,128)(2,1)S(1)}, u32[]{:S(2)}, u32[]{:S(2)}) collective-permute-start(bf16[448,1024]{1,0:T(8,128)(2,1)S(1)} %bitcast.19), channel_id=1, source_target_pairs={{0,12},{4,0},{8,4},{12,8},{64,68},{68,72},{72,76},{76,64},{1,13},{... | collective-permute-start | bytes 2752520 | tf_op jit(solution)/shard_map/ppermute | solution.py:23
  125.9 8.2 %copy-start = (bf16[448,1024]{1,0:T(8,128)(2,1)}, bf16[448,1024]{1,0:T(8,128)(2,1)S(1)}, u32[]{:S(2)}) copy-start(bf16[448,1024]{1,0:T(8,128)(2,1)S(1)} %collective-permute-done.10.refs_0_.refs_2_) | copy-start | bytes 2752516
  134.0 0.9 copy-start.2
  138.1 4.6 %copy-start.1 = (bf16[448,1024]{1,0:T(8,128)(2,1)S(1)}, bf16[448,1024]{1,0:T(8,128)(2,1)}, u32[]{:S(2)}) copy-start(bf16[448,1024]{1,0:T(8,128)(2,1)} %copy-done) | copy-start | bytes 2752516
  138.1 23.7 %all-to-all-start.3 = ((bf16[4,96,1792]{2,1,0:T(8,128)(2,1)}), bf16[4,96,1792]{2,1,0:T(8,128)(2,1)S(1)}, u32[]{:S(2)}, u32[]{:S(2)}) async-start(bf16[4,96,1792]{2,1,0:T(8,128)(2,1)} %get-tuple-element.17), calls=%async_computation.3 | async-start | bytes 2752512 | tf_op jit(solution)/shard_map/all_to_all | solution.py:29
  142.7 33.3 %copy-start.13 = (s32[8,2]{0,1:T(2,128)S(1)}, s32[8,2]{0,1:T(2,128)}, u32[]{:S(2)}) copy-start(s32[8,2]{0,1:T(2,128)} %param.6) | copy-start | bytes 196
  142.7 33.3 %copy-start.14 = (f32[8,2]{0,1:T(2,128)S(1)}, f32[8,2]{0,1:T(2,128)}, u32[]{:S(2)}) copy-start(f32[8,2]{0,1:T(2,128)} %param.7) | copy-start | bytes 196
  142.7 14.6 %collective-permute-start.12 = (bf16[448,1024]{1,0:T(8,128)(2,1)S(1)}, bf16[448,1024]{1,0:T(8,128)(2,1)S(1)}, u32[]{:S(2)}, u32[]{:S(2)}) collective-permute-start(bf16[448,1024]{1,0:T(8,128)(2,1)S(1)} %copy-done.1), channel_id=1, source_target_pairs={{0,4},{4,8},{8,12},{12,0},{64,76},{68,64},{72,68},{76,72},{1,5},{5... | collective-permute-start | bytes 2752520 | tf_op jit(solution)/shard_map/ppermute | solution.py:23
  157.2 4.6 %copy-start.7 = (bf16[448,1024]{1,0:T(8,128)(2,1)}, bf16[448,1024]{1,0:T(8,128)(2,1)S(1)}, u32[]{:S(2)}) copy-start(bf16[448,1024]{1,0:T(8,128)(2,1)S(1)} %collective-permute-done.12.refs_4_) | copy-start | bytes 2752516
  161.8 1.1 copy-start.5
  167.6 23.8 %collective-permute-start.13 = (bf16[128,1024]{1,0:T(8,128)(2,1)}, bf16[128,1024]{1,0:T(8,128)(2,1)S(1)}, u32[]{:S(2)}, u32[]{:S(2)}) collective-permute-start(bf16[128,1024]{1,0:T(8,128)(2,1)} %get-tuple-element.19), channel_id=1, source_target_pairs={{0,1},{1,2},{2,3},{3,0},{64,67},{65,64},{66,65},{67,66},{4,5},{5,6... | collective-permute-start | bytes 786440 | tf_op jit(solution)/shard_map/ppermute | solution.py:23
  176.0 27.4 %all-to-all-start.2 = ((bf16[4,32,1792]{2,1,0:T(8,128)(2,1)}), bf16[4,32,1792]{2,1,0:T(8,128)(2,1)S(1)}, u32[]{:S(2)}, u32[]{:S(2)}) async-start(bf16[4,32,1792]{2,1,0:T(8,128)(2,1)} %get-tuple-element.16), calls=%async_computation.2 | async-start | bytes 917504 | tf_op jit(solution)/shard_map/all_to_all | solution.py:29
  179.5 28.1 %collective-permute-start.15 = (bf16[128,1024]{1,0:T(8,128)(2,1)}, bf16[128,1024]{1,0:T(8,128)(2,1)S(1)}, u32[]{:S(2)}, u32[]{:S(2)}) collective-permute-start(bf16[128,1024]{1,0:T(8,128)(2,1)} %get-tuple-element.20), channel_id=1, source_target_pairs={{0,3},{1,0},{2,1},{3,2},{64,65},{65,66},{66,67},{67,64},{4,7},{5,4... | collective-permute-start | bytes 786440 | tf_op jit(solution)/shard_map/ppermute | solution.py:23
  192.5 19.4 %collective-permute-start.14 = (bf16[128,1024]{1,0:T(8,128)(2,1)S(1)}, bf16[128,1024]{1,0:T(8,128)(2,1)S(1)}, u32[]{:S(2)}, u32[]{:S(2)}) collective-permute-start(bf16[128,1024]{1,0:T(8,128)(2,1)S(1)} %add_convert_fusion.2), channel_id=1, source_target_pairs={{0,1},{1,2},{2,3},{3,0},{64,67},{65,64},{66,65},{67,66},{4,5},{5,6... | collective-permute-start | bytes 786440 | tf_op jit(solution)/shard_map/ppermute | solution.py:23
  203.4 0.8 copy-start.9
  214.5 15.8 %collective-permute-start.16 = (bf16[4,64,1024]{2,1,0:T(8,128)(2,1)S(1)}, bf16[4,64,1024]{2,1,0:T(8,128)(2,1)S(1)}, u32[]{:S(2)}, u32[]{:S(2)}) collective-permute-start(bf16[4,64,1024]{2,1,0:T(8,128)(2,1)S(1)} %add_convert_fusion.1), channel_id=1, source_target_pairs={{0,64},{64,0},{1,65},{65,1},{2,66},{66,2},{3,67},{67,3},{4,68},{68... | collective-permute-start | bytes 1572872 | tf_op jit(solution)/shard_map/ppermute | solution.py:18

commit v7 on v6

--- a/solution.py
+++ b/solution.py
@@ -39,7 +39,7 @@
     return copies
 
 
-def early(pieces, weights):
+def early(pieces, weights, after):
     def kernel(*refs):
         out_ref, piece_ref, copy_ref, held, sums, sems, out_sems, sem, piece_sem = refs[-9:]
         copies = fetch(refs[3:6], held, sems)
@@ -63,7 +63,7 @@
 
     return pl.pallas_call(
         kernel,
-        in_specs=[WHOLE] * 3 + [ANY] * 3,
+        in_specs=[WHOLE] * 3 + [ANY] * 4,
         out_specs=[ANY] * 3,
         out_shape=[
             jax.ShapeDtypeStruct((4, 96, 2688), half),
@@ -80,7 +80,7 @@
         ],
         compiler_params=pltpu.CompilerParams(vmem_limit_bytes=LIMIT),
         cost_estimate=COST,
-    )(*pieces, *weights)
+    )(*pieces, *weights, after)
 
 
 def late_near(far, weights):
@@ -162,14 +162,14 @@
 
 def activate_late(sums, begun, after):
     def kernel(sums_ref, begun_ref, *refs):
-        others_ref, own_ref = refs[-2:]
+        far_ref, near_ref, own_ref = refs[-3:]
         total = jnp.sum(sums_ref[...].astype(wide), axis=0)
         blocks = [block(total, i) for i in range(7)]
         far = jnp.concatenate(blocks[:4], axis=1)
         rest = jnp.concatenate([begun_ref[...], jnp.concatenate(blocks[4:])], axis=1)
         for j in range(4):
-            others_ref[j, :32] = far
-            others_ref[j, 32:] = rest[:64]
+            far_ref[j] = far
+            near_ref[j] = rest[:64]
             own_ref[j] = rest[64:]
 
     return pl.pallas_call(
@@ -180,8 +180,8 @@
             pl.BlockSpec((96, 1344), lambda i: (0, 0)),
         ]
         + [ANY] * len(after),
-        out_specs=[pl.BlockSpec((4, r, 1792), lambda i: (0, 0, 0)) for r in (96, 32)],
-        out_shape=[jax.ShapeDtypeStruct((4, r, 1792), half) for r in (96, 32)],
+        out_specs=[pl.BlockSpec((4, r, 1792), lambda i: (0, 0, 0)) for r in (32, 64, 32)],
+        out_shape=[jax.ShapeDtypeStruct((4, r, 1792), half) for r in (32, 64, 32)],
         compiler_params=pltpu.CompilerParams(vmem_limit_bytes=LIMIT),
         cost_estimate=COST,
     )(sums, begun, *after)
@@ -214,7 +214,7 @@
     zlo = lax.axis_index("zlo")
     expert = zlo * 2 + core
 
-    mine = [tokens[0]] + [shift(tokens[0], "zlo", d) for d in (1, 2, 3)]
+    mine = swap(jnp.broadcast_to(tokens, (4, 64, 1024)), "zlo")
     w_own, v_own = jnp.transpose(w_in[0], (1, 2, 0)).reshape(896, 1024), w_down[0]
     w_first, w_second = pass_on(w_own, "y", 1), pass_on(w_own, "y", -1)
     v_first, v_second = pass_on(v_own, "y", 1), pass_on(v_own, "y", -1)
@@ -240,12 +240,7 @@
     scales = [jnp.sum(jnp.where(c, gates, 0.0)) for c in chosen]
 
     def taking(owners):
-        out = []
-        for z in owners:
-            away = (zlo - z) & 3
-            near = jnp.where(away == 0, mine[0], mine[1])
-            out.append(jnp.where(away < 2, near, jnp.where(away == 2, mine[2], mine[3])))
-        return out
+        return [lax.dynamic_index_in_dim(mine, z, 0, keepdims=False) for z in owners]
 
     other = shift(jnp.concatenate(taking(owner_too)), "core", 1)
     rows = jnp.concatenate(
@@ -253,16 +248,17 @@
     )
 
     first, second = pass_on(rows, "zhi", 1), pass_on(rows, "zhi", -1)
-    part, z_next, w_next = early([first, second, rows], weights)
+    part, z_next, w_next = early([first, second, rows], weights, v_first)
 
     far, w_far, v_far = pass_on(z_next, "zhi", 1), pass_on(w_next, "y", 1), pass_on(v_first, "y", 1)
     v_all = [v_own, v_first, v_second, v_far]
     begun = activate_early(swap(part, "x"))
     rest = swap(late_far([far, first, second, rows], w_far, late_near(far, weights)), "x")
-    others_h, own_h = activate_late(rest, begun, [v_first, v_second])
-
-    far_out, first_out, second_out = down(swap(others_h, "x"), v_all, (half, half, wide))
+    far_h, near_h, own_h = activate_late(rest, begun, [v_second, v_far])
+
+    (far_out,) = down(swap(far_h, "x"), v_all, (half,))
     got = pass_on(far_out, "zhi", 1)
+    first_out, second_out = down(swap(near_h, "x"), v_all, (half, wide))
     back = pass_on(first_out, "zhi", -1)
     ahead = pass_on((second_out + got.astype(wide)).astype(half), "zhi", 1)
 

time: 249 us -> 246 us (0.988)
  waiting for transfers between devices: 75.2 us -> 61 us
  blocking collectives: 16.6 us -> 29.8 us
  starting transfers between devices: 103 us -> 90.6 us
  between operations: 5.44 us -> 10.7 us
  local copies, waits for them, and re-layouts: 5.12 us -> 8.31 us
  Pallas kernels: 30.3 us -> 33.1 us
    ppermute x5 -> x2, starting transfers between devices: 31.4 us -> 5.97 us  [shift(): return lax.ppermute(a, axis, [(i, (i + by) % n) for i in range(n)])]
    all_to_all x1 -> x2, blocking collectives: 16.6 us -> 29.8 us  [swap(): return lax.all_to_all(a, axis, split_axis=0, concat_axis=0, tiled=True)]
    ppermute x12, waiting for transfers between devices: 68.8 us -> 60.3 us  [pass_on(): lax.ppermute(a, ('core', axis), [(c * n + i, c * n + (i + by * (1 - 2 * c...]
    ppermute x12, starting transfers between devices: 54.9 us -> 62.4 us  [pass_on(): lax.ppermute(a, ('core', axis), [(c * n + i, c * n + (i + by * (1 - 2 * c...]
    all_to_all x4 -> x5, starting transfers between devices: 16.6 us -> 22.2 us  [swap(): return lax.all_to_all(a, axis, split_axis=0, concat_axis=0, tiled=True)]
    all_to_all x4 -> x5, waiting for transfers between devices: 4.89 us -> 0.47 us  [swap(): return lax.all_to_all(a, axis, split_axis=0, concat_axis=0, tiled=True)]
    pallas_call x2 -> x3, Pallas kernels: 8.13 us -> 10.9 us  [down(): pl.pallas_call(kernel, grid=(2,), in_specs=[pl.BlockSpec((4, 32 * n, 1792...]
    unnamed x32 -> x30, local copies, waits for them, and re-layouts: 4.94 us -> 6.35 us
  transfers between devices with their start and end apart: 21 -> 19, of which waited for: 11 -> 7; matrix products, arithmetic and copies ran while one was open for 4% -> 3% of each run, Pallas kernels for 6% -> 10%
where the time goes in v7:
time: 246 us; the launch traced here: 245 us
  starting transfers between devices  90.6 us (37%)
  waiting for transfers between devices  61 us (25%)
  Pallas kernels  33.1 us (13%)
  blocking collectives  29.8 us (12%)
  other arithmetic  11.3 us (5%)
  between operations  10.7 us (4%)
  local copies, waits for them, and re-layouts  8.31 us (3%)
    ppermute x12, starting transfers between devices, pass_on(): lax.ppermute(a, ('core', axis), [(c * n + i, c * n + (i + by * (1 - 2 * c...  62.4 us
    ppermute x12, waiting for transfers between devices, pass_on(): lax.ppermute(a, ('core', axis), [(c * n + i, c * n + (i + by * (1 - 2 * c...  60.3 us
    all_to_all x2, blocking collectives, swap(): return lax.all_to_all(a, axis, split_axis=0, concat_axis=0, tiled=True)  29.8 us
    all_to_all x5, starting transfers between devices, swap(): return lax.all_to_all(a, axis, split_axis=0, concat_axis=0, tiled=True)  22.2 us
    pallas_call x3, Pallas kernels, down(): pl.pallas_call(kernel, grid=(2,), in_specs=[pl.BlockSpec((4, 32 * n, 1792...  10.9 us
    pallas_call x1, Pallas kernels, early(): pl.pallas_call(kernel, in_specs=[WHOLE] * 3 + [ANY] * 4, out_specs=[ANY]...  6.72 us
    unnamed x30, local copies, waits for them, and re-layouts  6.35 us
    ppermute x2, starting transfers between devices, shift(): return lax.ppermute(a, axis, [(i, (i + by) % n) for i in range(n)])  5.97 us
  transfers between devices with their start and end apart: 19, of which 7 were waited for; matrix products, arithmetic and copies ran while one was open for 3% of the time, Pallas kernels for 10%

profile of v7, /device:TPU:1, one launch (start us, length us, event | category | flops | bytes accessed | tf_op | source)
XLA Modules:
  0.0 244.7 jit_solution(10137683267547757466)
XLA Ops:
  0.0 1.8 broadcast_in_dim.76
  1.8 6.4 %all-to-all-start = ((bf16[4,64,1024]{2,1,0:T(8,128)(2,1)}), bf16[4,64,1024]{2,1,0:T(8,128)(2,1)S(1)}, u32[]{:S(2)}, u32[]{:S(2)}) async-start(bf16[4,64,1024]{2,1,0:T(8,128)(2,1)} %broadcast_in_dim.76), calls=%async_computation | async-start | bytes 1048576 | tf_op jit(solution)/shard_map/all_to_all | solution.py:29
  8.2 4.6 %collective-permute-start.3 = (bf16[896,1024]{1,0:T(8,128)(2,1)}, bf16[896,1024]{1,0:T(8,128)(2,1)S(1)}, u32[]{:S(2)}, u32[]{:S(2)}) collective-permute-start(bf16[896,1024]{1,0:T(8,128)(2,1)} %bitcast.21), channel_id=1, source_target_pairs={{0,4},{4,8},{8,12},{12,0},{64,76},{68,64},{72,68},{76,72},{1,5},{5... | collective-permute-start | bytes 5505032 | tf_op jit(solution)/shard_map/ppermute | solution.py:23
  12.8 1.9 collective-permute-start.4
  14.8 4.6 %collective-permute-start.5 = (bf16[448,1024]{1,0:T(8,128)(2,1)}, bf16[448,1024]{1,0:T(8,128)(2,1)S(1)}, u32[]{:S(2)}, u32[]{:S(2)}) collective-permute-start(bf16[448,1024]{1,0:T(8,128)(2,1)} %bitcast.16), channel_id=1, source_target_pairs={{0,4},{4,8},{8,12},{12,0},{64,76},{68,64},{72,68},{76,72},{1,5},{5... | collective-permute-start | bytes 2752520 | tf_op jit(solution)/shard_map/ppermute | solution.py:23
  19.4 0.8 convert_reduce_fusion
  20.5 0.7 select_reduce_fusion.4
  25.2 0.7 pad_maximum_fusion
  26.0 3.7 %collective-permute-start = (bf16[128,1024]{1,0:T(8,128)(2,1)}, bf16[128,1024]{1,0:T(8,128)(2,1)S(1)}, u32[]{:S(2)}, u32[]{:S(2)}) collective-permute-start(bf16[128,1024]{1,0:T(8,128)(2,1)} %pad_maximum_fusion), channel_id=1, source_target_pairs={{0,64},{64,0},{1,65},{65,1},{2,66},{66,2},{3,67},{67,3},{4,68},{68... | collective-permute-start | bytes 786440 | tf_op jit(solution)/shard_map/ppermute | solution.py:18
  29.6 0.7 select_reduce_fusion.3
  35.4 8.6 %collective-permute-start.1 = (bf16[128,1024]{1,0:T(8,128)(2,1)S(1)}, bf16[128,1024]{1,0:T(8,128)(2,1)S(1)}, u32[]{:S(2)}, u32[]{:S(2)}) collective-permute-start(bf16[128,1024]{1,0:T(8,128)(2,1)S(1)} %pad_maximum_fusion.1.refs_2_.refs_3_), channel_id=1, source_target_pairs={{0,1},{1,2},{2,3},{3,0},{64,67},{65,64},{66,65},{67,66},{4,5},{5,6... | collective-permute-start | bytes 786440 | tf_op jit(solution)/shard_map/ppermute | solution.py:23
  44.0 1.9 collective-permute-start.2
  46.0 16.8 %collective-permute-done.5.refs_6_.refs_2_ = bf16[448,1024]{1,0:T(8,128)(2,1)S(1)} collective-permute-done((bf16[448,1024]{1,0:T(8,128)(2,1)}, bf16[448,1024]{1,0:T(8,128)(2,1)S(1)}, u32[]{:S(2)}, u32[]{:S(2)}) %collective-permute-start.5) | collective-permute-done | bytes 917536 | tf_op jit(solution)/shard_map/ppermute | solution.py:23
  62.8 0.9 copy-done
  64.4 0.7 copy-done.10
  65.1 6.7 %shard_map.55 = (bf16[4,96,2688]{2,1,0:T(8,128)(2,1)}, bf16[128,1024]{1,0:T(8,128)(2,1)}, bf16[896,1024]{1,0:T(8,128)(2,1)}) custom-call(bf16[128,1024]{1,0:T(8,128)(2,1)} %copy-done.9, bf16[128,1024]{1,0:T(8,128)(2,1)} %copy-done.10, bf16[128,1024]{1,0:T(8,128)(2,1)} %copy-done.7, bf16[896,1024]{1,0:T(8,128)(2,1)} %bitcast.23, bf16[896,1024]{1,0:T(8,128)(2,1)} %copy-done.5, ...), custom_call_target="tpu_custom_call" | custom-call | flops 1024 | bytes 1024 | tf_op jit(solution)/shard_map/pallas_call | solution.py:64
  71.8 4.9 %collective-permute-start.7 = (bf16[896,1024]{1,0:T(8,128)(2,1)}, bf16[896,1024]{1,0:T(8,128)(2,1)}, u32[]{:S(2)}, u32[]{:S(2)}) collective-permute-start(bf16[896,1024]{1,0:T(8,128)(2,1)} %get-tuple-element.14), channel_id=1, source_target_pairs={{0,4},{4,8},{8,12},{12,0},{64,76},{68,64},{72,68},{76,72},{1,5},{5... | collective-permute-start | bytes 5505032 | tf_op jit(solution)/shard_map/ppermute | solution.py:23
  76.8 4.2 %all-to-all-start.2 = ((bf16[4,96,2688]{2,1,0:T(8,128)(2,1)}), bf16[4,96,2688]{2,1,0:T(8,128)(2,1)S(1)}, u32[]{:S(2)}, u32[]{:S(2)}) async-start(bf16[4,96,2688]{2,1,0:T(8,128)(2,1)} %get-tuple-element.15), calls=%async_computation.2 | async-start | bytes 4128768 | tf_op jit(solution)/shard_map/all_to_all | solution.py:29
  81.0 10.6 %collective-permute-start.6 = (bf16[128,1024]{1,0:T(8,128)(2,1)S(1)}, bf16[128,1024]{1,0:T(8,128)(2,1)S(1)}, u32[]{:S(2)}, u32[]{:S(2)}) collective-permute-start(bf16[128,1024]{1,0:T(8,128)(2,1)S(1)} %copy-done.14), channel_id=1, source_target_pairs={{0,1},{1,2},{2,3},{3,0},{64,67},{65,64},{66,65},{67,66},{4,5},{5,6... | collective-permute-start | bytes 786440 | tf_op jit(solution)/shard_map/ppermute | solution.py:23
  91.6 11.7 %collective-permute-done.6.far_ref.refs_0_ = bf16[128,1024]{1,0:T(8,128)(2,1)S(1)} collective-permute-done((bf16[128,1024]{1,0:T(8,128)(2,1)S(1)}, bf16[128,1024]{1,0:T(8,128)(2,1)S(1)}, u32[]{:S(2)}, u32[]{:S(2)}) %collective-permute-start.6) | collective-permute-done | bytes 262176 | tf_op jit(solution)/shard_map/ppermute | solution.py:23
  103.3 0.7 copy-done.11
  104.0 5.6 %shard_map.56.refs_5_ = bf16[4,32,6272]{2,1,0:T(8,128)(2,1)} custom-call(bf16[128,1024]{1,0:T(8,128)(2,1)} %copy-done.11, bf16[896,1024]{1,0:T(8,128)(2,1)} %bitcast.24, bf16[896,1024]{1,0:T(8,128)(2,1)} %copy-done.5, bf16[896,1024]{1,0:T(8,128)(2,1)} %collective-permute-done.4.refs_5_.refs_2_), custom_call_target="tpu_custom_call" | custom-call | flops 1024 | bytes 1024 | tf_op jit(solution)/shard_map/pallas_call | solution.py:99
  109.6 4.1 %shard_map.57 = bf16[4,32,6272]{2,1,0:T(8,128)(2,1)} custom-call(bf16[128,1024]{1,0:T(8,128)(2,1)} %copy-done.11, bf16[128,1024]{1,0:T(8,128)(2,1)} %copy-done.9, bf16[128,1024]{1,0:T(8,128)(2,1)} %copy-done.10, bf16[128,1024]{1,0:T(8,128)(2,1)} %copy-done.7, bf16[896,1024]{1,0:T(8,128)(2,1)} %collective-permute-done.7.refs_4_, ...), custom_call_target="tpu_custom_call", output_to_operand_aliasing={{}: (5, {})} | custom-call | flops 1024 | bytes 1024 | tf_op jit(solution)/shard_map/pallas_call | solution.py:126
  113.7 1.3 copy-done.4
  115.0 4.4 %all-to-all-start.1 = ((bf16[4,32,6272]{2,1,0:T(8,128)(2,1)}), bf16[4,32,6272]{2,1,0:T(8,128)(2,1)}, u32[]{:S(2)}, u32[]{:S(2)}) async-start(bf16[4,32,6272]{2,1,0:T(8,128)(2,1)} %shard_map.57), calls=%async_computation.1 | async-start | bytes 3211264 | tf_op jit(solution)/shard_map/all_to_all | solution.py:29
  119.4 1.9 collective-permute-start.8
  121.4 4.6 %collective-permute-start.9 = (bf16[448,1024]{1,0:T(8,128)(2,1)S(1)}, bf16[448,1024]{1,0:T(8,128)(2,1)S(1)}, u32[]{:S(2)}, u32[]{:S(2)}) collective-permute-start(bf16[448,1024]{1,0:T(8,128)(2,1)S(1)} %copy-done.1), channel_id=1, source_target_pairs={{0,4},{4,8},{8,12},{12,0},{64,76},{68,64},{72,68},{76,72},{1,5},{5... | collective-permute-start | bytes 2752520 | tf_op jit(solution)/shard_map/ppermute | solution.py:23
  126.0 2.7 %shard_map.58.begun_ref = bf16[96,1344]{1,0:T(8,128)(2,1)} custom-call(bf16[4,96,2688]{2,1,0:T(8,128)(2,1)} %copy-done.4), custom_call_target="tpu_custom_call" | custom-call | flops 1024 | bytes 1024 | tf_op jit(solution)/shard_map/pallas_call | solution.py:152
  128.7 14.3 %collective-permute-done.8.refs_0_.refs_3_ = bf16[448,1024]{1,0:T(8,128)(2,1)S(1)} collective-permute-done((bf16[448,1024]{1,0:T(8,128)(2,1)}, bf16[448,1024]{1,0:T(8,128)(2,1)S(1)}, u32[]{:S(2)}, u32[]{:S(2)}) %collective-permute-start.8) | collective-permute-done | bytes 917536 | tf_op jit(solution)/shard_map/ppermute | solution.py:23
  142.9 0.9 copy-done.2
  144.2 3.1 %shard_map.59 = (bf16[4,32,1792]{2,1,0:T(8,128)(2,1)}, bf16[4,64,1792]{2,1,0:T(8,128)(2,1)}, bf16[4,32,1792]{2,1,0:T(8,128)(2,1)}) custom-call(bf16[4,32,6272]{2,1,0:T(8,128)(2,1)} %all-to-all-done.1.sums_ref, bf16[96,1344]{1,0:T(8,128)(2,1)} %shard_map.58.begun_ref, bf16[448,1024]{1,0:T(8,128)(2,1)} %copy-done.2, bf16[448,1024]{1,0:T(8,128)(2,1)} %copy-done.3), custom_call_target="tpu_custom_call" | custom-call | flops 1024 | bytes 1024 | tf_op jit(solution)/shard_map/pallas_call | solution.py:175
  147.2 13.1 %all_to_all.35.refs_0_ = bf16[4,32,1792]{2,1,0:T(8,128)(2,1)} all-to-all(bf16[4,32,1792]{2,1,0:T(8,128)(2,1)} %get-tuple-element.19), channel_id=1, replica_groups=mesh['zlo'=4,'core'=2,'x'=4,'y'=4,'zhi'=4] {'x'}, dimensions={0} | all-to-all | bytes 917504 | tf_op jit(solution)/shard_map/all_to_all | solution.py:29
  160.4 3.5 %all-to-all-start.4 = ((bf16[4,64,1792]{2,1,0:T(8,128)(2,1)}), bf16[4,64,1792]{2,1,0:T(8,128)(2,1)S(1)}, u32[]{:S(2)}, u32[]{:S(2)}) async-start(bf16[4,64,1792]{2,1,0:T(8,128)(2,1)} %get-tuple-element.17), calls=%async_computation.4 | async-start | bytes 1835008 | tf_op jit(solution)/shard_map/all_to_all | solution.py:29
  163.9 3.4 %shard_map.62 = bf16[128,1024]{1,0:T(8,128)(2,1)} custom-call(bf16[4,32,1792]{2,1,0:T(8,128)(2,1)} %all_to_all.35.refs_0_, bf16[448,1024]{1,0:T(8,128)(2,1)} %bitcast.18, bf16[448,1024]{1,0:T(8,128)(2,1)} %copy-done, bf16[448,1024]{1,0:T(8,128)(2,1)} %copy-done.2, bf16[448,1024]{1,0:T(8,128)(2,1)} %copy-done.3), custom_call_target="tpu_custom_call" | custom-call | flops 1024 | bytes 1024 | tf_op jit(solution)/shard_map/pallas_call | solution.py:200
  167.3 9.0 %collective-permute-start.10 = (bf16[128,1024]{1,0:T(8,128)(2,1)}, bf16[128,1024]{1,0:T(8,128)(2,1)S(1)}, u32[]{:S(2)}, u32[]{:S(2)}) collective-permute-start(bf16[128,1024]{1,0:T(8,128)(2,1)} %shard_map.62), channel_id=1, source_target_pairs={{0,1},{1,2},{2,3},{3,0},{64,67},{65,64},{66,65},{67,66},{4,5},{5,6... | collective-permute-start | bytes 786440 | tf_op jit(solution)/shard_map/ppermute | solution.py:23
  177.5 3.7 %all-to-all-start.3 = ((bf16[4,32,1792]{2,1,0:T(8,128)(2,1)}), bf16[4,32,1792]{2,1,0:T(8,128)(2,1)S(1)}, u32[]{:S(2)}, u32[]{:S(2)}) async-start(bf16[4,32,1792]{2,1,0:T(8,128)(2,1)} %get-tuple-element.16), calls=%async_computation.3 | async-start | bytes 917504 | tf_op jit(solution)/shard_map/all_to_all | solution.py:29
  181.2 4.1 %shard_map.61 = (bf16[128,1024]{1,0:T(8,128)(2,1)}, f32[128,1024]{1,0:T(8,128)}) custom-call(bf16[4,64,1792]{2,1,0:T(8,128)(2,1)} %copy-done.6, bf16[448,1024]{1,0:T(8,128)(2,1)} %bitcast.19, bf16[448,1024]{1,0:T(8,128)(2,1)} %copy-done, bf16[448,1024]{1,0:T(8,128)(2,1)} %copy-done.2, bf16[448,1024]{1,0:T(8,128)(2,1)} %copy-done.3), custom_call_target="tpu_custom_call" | custom-call | flops 1024 | bytes 1024 | tf_op jit(solution)/shard_map/pallas_call | solution.py:200
  185.7 1.1 add_convert_fusion.2
  186.8 7.9 %collective-permute-start.11 = (bf16[128,1024]{1,0:T(8,128)(2,1)S(1)}, bf16[128,1024]{1,0:T(8,128)(2,1)S(1)}, u32[]{:S(2)}, u32[]{:S(2)}) collective-permute-start(bf16[128,1024]{1,0:T(8,128)(2,1)S(1)} %add_convert_fusion.2), channel_id=1, source_target_pairs={{0,1},{1,2},{2,3},{3,0},{64,67},{65,64},{66,65},{67,66},{4,5},{5,6... | collective-permute-start | bytes 786440 | tf_op jit(solution)/shard_map/ppermute | solution.py:23
  194.7 1.9 collective-permute-start.12
  199.3 0.8 copy-done.8
  200.1 3.4 %shard_map.60 = f32[128,1024]{1,0:T(8,128)} custom-call(bf16[4,32,1792]{2,1,0:T(8,128)(2,1)} %copy-done.8, bf16[448,1024]{1,0:T(8,128)(2,1)} %bitcast.20, bf16[448,1024]{1,0:T(8,128)(2,1)} %copy-done, bf16[448,1024]{1,0:T(8,128)(2,1)} %copy-done.2, bf16[448,1024]{1,0:T(8,128)(2,1)} %copy-done.3), custom_call_target="tpu_custom_call" | custom-call | flops 1024 | bytes 1024 | tf_op jit(solution)/shard_map/pallas_call | solution.py:200
  203.5 17.1 %collective-permute-done.12 = bf16[128,1024]{1,0:T(8,128)(2,1)S(1)} collective-permute-done((bf16[128,1024]{1,0:T(8,128)(2,1)}, bf16[128,1024]{1,0:T(8,128)(2,1)S(1)}, u32[]{:S(2)}, u32[]{:S(2)}) %collective-permute-start.12) | collective-permute-done | bytes 262176 | tf_op jit(solution)/shard_map/ppermute | solution.py:23
  220.6 1.1 convert_add_fusion
  221.7 1.3 slice_multiply_fusion.1
  223.2 2.3 collective-permute-start.13
  227.3 16.6 %all_to_all.36 = bf16[4,64,1024]{2,1,0:T(8,128)(2,1)S(1)} all-to-all(bf16[4,64,1024]{2,1,0:T(8,128)(2,1)S(1)} %add_convert_fusion), channel_id=1, replica_groups=mesh['zlo'=4,'core'=2,'x'=4,'y'=4,'zhi'=4] {'zlo'}, dimensions={0} | all-to-all | bytes 1048576 | tf_op jit(solution)/shard_map/all_to_all | solution.py:29
  244.0 0.7 reduce_sum.112
  (55 shorter events, 6.5 us)
Async XLA Ops:
  1.8 23.4 %all-to-all-start = ((bf16[4,64,1024]{2,1,0:T(8,128)(2,1)}), bf16[4,64,1024]{2,1,0:T(8,128)(2,1)S(1)}, u32[]{:S(2)}, u32[]{:S(2)}) async-start(bf16[4,64,1024]{2,1,0:T(8,128)(2,1)} %broadcast_in_dim.76), calls=%async_computation | async-start | bytes 1048576 | tf_op jit(solution)/shard_map/all_to_all | solution.py:29
  8.2 54.6 %collective-permute-start.3 = (bf16[896,1024]{1,0:T(8,128)(2,1)}, bf16[896,1024]{1,0:T(8,128)(2,1)S(1)}, u32[]{:S(2)}, u32[]{:S(2)}) collective-permute-start(bf16[896,1024]{1,0:T(8,128)(2,1)} %bitcast.21), channel_id=1, source_target_pairs={{0,4},{4,8},{8,12},{12,0},{64,76},{68,64},{72,68},{76,72},{1,5},{5... | collective-permute-start | bytes 5505032 | tf_op jit(solution)/shard_map/ppermute | solution.py:23
  12.8 50.0 %collective-permute-start.4 = (bf16[896,1024]{1,0:T(8,128)(2,1)}, bf16[896,1024]{1,0:T(8,128)(2,1)}, u32[]{:S(2)}, u32[]{:S(2)}) collective-permute-start(bf16[896,1024]{1,0:T(8,128)(2,1)} %bitcast.22), channel_id=1, source_target_pairs={{0,12},{4,0},{8,4},{12,8},{64,68},{68,72},{72,76},{76,64},{1,13},{... | collective-permute-start | bytes 5505032 | tf_op jit(solution)/shard_map/ppermute | solution.py:23
  14.8 48.0 %collective-permute-start.5 = (bf16[448,1024]{1,0:T(8,128)(2,1)}, bf16[448,1024]{1,0:T(8,128)(2,1)S(1)}, u32[]{:S(2)}, u32[]{:S(2)}) collective-permute-start(bf16[448,1024]{1,0:T(8,128)(2,1)} %bitcast.16), channel_id=1, source_target_pairs={{0,4},{4,8},{8,12},{12,0},{64,76},{68,64},{72,68},{76,72},{1,5},{5... | collective-permute-start | bytes 2752520 | tf_op jit(solution)/shard_map/ppermute | solution.py:23
  26.0 9.4 %collective-permute-start = (bf16[128,1024]{1,0:T(8,128)(2,1)}, bf16[128,1024]{1,0:T(8,128)(2,1)S(1)}, u32[]{:S(2)}, u32[]{:S(2)}) collective-permute-start(bf16[128,1024]{1,0:T(8,128)(2,1)} %pad_maximum_fusion), channel_id=1, source_target_pairs={{0,64},{64,0},{1,65},{65,1},{2,66},{66,2},{3,67},{67,3},{4,68},{68... | collective-permute-start | bytes 786440 | tf_op jit(solution)/shard_map/ppermute | solution.py:18
  35.4 27.4 %copy-start.7 = (bf16[128,1024]{1,0:T(8,128)(2,1)}, bf16[128,1024]{1,0:T(8,128)(2,1)S(1)}, u32[]{:S(2)}) copy-start(bf16[128,1024]{1,0:T(8,128)(2,1)S(1)} %pad_maximum_fusion.1.refs_2_.refs_3_) | copy-start | bytes 786436
  35.4 27.4 %collective-permute-start.1 = (bf16[128,1024]{1,0:T(8,128)(2,1)S(1)}, bf16[128,1024]{1,0:T(8,128)(2,1)S(1)}, u32[]{:S(2)}, u32[]{:S(2)}) collective-permute-start(bf16[128,1024]{1,0:T(8,128)(2,1)S(1)} %pad_maximum_fusion.1.refs_2_.refs_3_), channel_id=1, source_target_pairs={{0,1},{1,2},{2,3},{3,0},{64,67},{65,64},{66,65},{67,66},{4,5},{5,6... | collective-permute-start | bytes 786440 | tf_op jit(solution)/shard_map/ppermute | solution.py:23
  44.0 18.8 %collective-permute-start.2 = (bf16[128,1024]{1,0:T(8,128)(2,1)S(1)}, bf16[128,1024]{1,0:T(8,128)(2,1)S(1)}, u32[]{:S(2)}, u32[]{:S(2)}) collective-permute-start(bf16[128,1024]{1,0:T(8,128)(2,1)S(1)} %pad_maximum_fusion.1.refs_2_.refs_3_), channel_id=1, source_target_pairs={{0,3},{1,0},{2,1},{3,2},{64,65},{65,66},{66,67},{67,64},{4,7},{5,4... | collective-permute-start | bytes 786440 | tf_op jit(solution)/shard_map/ppermute | solution.py:23
  62.8 0.9 copy-start
  62.8 1.5 copy-start.5
  62.8 1.6 copy-start.9
  64.4 0.7 copy-start.10
  71.8 37.8 %collective-permute-start.7 = (bf16[896,1024]{1,0:T(8,128)(2,1)}, bf16[896,1024]{1,0:T(8,128)(2,1)}, u32[]{:S(2)}, u32[]{:S(2)}) collective-permute-start(bf16[896,1024]{1,0:T(8,128)(2,1)} %get-tuple-element.14), channel_id=1, source_target_pairs={{0,4},{4,8},{8,12},{12,0},{64,76},{68,64},{72,68},{76,72},{1,5},{5... | collective-permute-start | bytes 5505032 | tf_op jit(solution)/shard_map/ppermute | solution.py:23
  76.8 4.2 %copy-start.14 = (bf16[128,1024]{1,0:T(8,128)(2,1)S(1)}, bf16[128,1024]{1,0:T(8,128)(2,1)}, u32[]{:S(2)}) copy-start(bf16[128,1024]{1,0:T(8,128)(2,1)} %get-tuple-element.13) | copy-start | bytes 786436
  76.8 36.9 %all-to-all-start.2 = ((bf16[4,96,2688]{2,1,0:T(8,128)(2,1)}), bf16[4,96,2688]{2,1,0:T(8,128)(2,1)S(1)}, u32[]{:S(2)}, u32[]{:S(2)}) async-start(bf16[4,96,2688]{2,1,0:T(8,128)(2,1)} %get-tuple-element.15), calls=%async_computation.2 | async-start | bytes 4128768 | tf_op jit(solution)/shard_map/all_to_all | solution.py:29
  81.0 22.3 %collective-permute-start.6 = (bf16[128,1024]{1,0:T(8,128)(2,1)S(1)}, bf16[128,1024]{1,0:T(8,128)(2,1)S(1)}, u32[]{:S(2)}, u32[]{:S(2)}) collective-permute-start(bf16[128,1024]{1,0:T(8,128)(2,1)S(1)} %copy-done.14), channel_id=1, source_target_pairs={{0,1},{1,2},{2,3},{3,0},{64,67},{65,64},{66,65},{67,66},{4,5},{5,6... | collective-permute-start | bytes 786440 | tf_op jit(solution)/shard_map/ppermute | solution.py:23
  103.3 0.7 copy-start.11
  113.7 7.7 %copy-start.1 = (bf16[448,1024]{1,0:T(8,128)(2,1)S(1)}, bf16[448,1024]{1,0:T(8,128)(2,1)}, u32[]{:S(2)}) copy-start(bf16[448,1024]{1,0:T(8,128)(2,1)} %copy-done) | copy-start | bytes 2752516
  113.7 1.3 copy-start.4
  115.0 27.9 %all-to-all-start.1 = ((bf16[4,32,6272]{2,1,0:T(8,128)(2,1)}), bf16[4,32,6272]{2,1,0:T(8,128)(2,1)}, u32[]{:S(2)}, u32[]{:S(2)}) async-start(bf16[4,32,6272]{2,1,0:T(8,128)(2,1)} %shard_map.57), calls=%async_computation.1 | async-start | bytes 3211264 | tf_op jit(solution)/shard_map/all_to_all | solution.py:29
  119.4 23.5 %collective-permute-start.8 = (bf16[448,1024]{1,0:T(8,128)(2,1)}, bf16[448,1024]{1,0:T(8,128)(2,1)S(1)}, u32[]{:S(2)}, u32[]{:S(2)}) collective-permute-start(bf16[448,1024]{1,0:T(8,128)(2,1)} %bitcast.17), channel_id=1, source_target_pairs={{0,12},{4,0},{8,4},{12,8},{64,68},{68,72},{72,76},{76,64},{1,13},{... | collective-permute-start | bytes 2752520 | tf_op jit(solution)/shard_map/ppermute | solution.py:23
  121.4 21.5 %collective-permute-start.9 = (bf16[448,1024]{1,0:T(8,128)(2,1)S(1)}, bf16[448,1024]{1,0:T(8,128)(2,1)S(1)}, u32[]{:S(2)}, u32[]{:S(2)}) collective-permute-start(bf16[448,1024]{1,0:T(8,128)(2,1)S(1)} %copy-done.1), channel_id=1, source_target_pairs={{0,4},{4,8},{8,12},{12,0},{64,76},{68,64},{72,68},{76,72},{1,5},{5... | collective-permute-start | bytes 2752520 | tf_op jit(solution)/shard_map/ppermute | solution.py:23
  142.9 0.9 copy-start.2
  142.9 1.2 copy-start.3
  160.4 17.1 %all-to-all-start.4 = ((bf16[4,64,1792]{2,1,0:T(8,128)(2,1)}), bf16[4,64,1792]{2,1,0:T(8,128)(2,1)S(1)}, u32[]{:S(2)}, u32[]{:S(2)}) async-start(bf16[4,64,1792]{2,1,0:T(8,128)(2,1)} %get-tuple-element.17), calls=%async_computation.4 | async-start | bytes 1835008 | tf_op jit(solution)/shard_map/all_to_all | solution.py:29
  163.9 13.0 %copy-start.12 = (s32[8,2]{0,1:T(2,128)S(1)}, s32[8,2]{0,1:T(2,128)}, u32[]{:S(2)}) copy-start(s32[8,2]{0,1:T(2,128)} %param.6) | copy-start | bytes 196
  163.9 13.0 %copy-start.13 = (f32[8,2]{0,1:T(2,128)S(1)}, f32[8,2]{0,1:T(2,128)}, u32[]{:S(2)}) copy-start(f32[8,2]{0,1:T(2,128)} %param.7) | copy-start | bytes 196
  167.3 18.4 %collective-permute-start.10 = (bf16[128,1024]{1,0:T(8,128)(2,1)}, bf16[128,1024]{1,0:T(8,128)(2,1)S(1)}, u32[]{:S(2)}, u32[]{:S(2)}) collective-permute-start(bf16[128,1024]{1,0:T(8,128)(2,1)} %shard_map.62), channel_id=1, source_target_pairs={{0,1},{1,2},{2,3},{3,0},{64,67},{65,64},{66,65},{67,66},{4,5},{5,6... | collective-permute-start | bytes 786440 | tf_op jit(solution)/shard_map/ppermute | solution.py:23
  177.5 3.7 %copy-start.6 = (bf16[4,64,1792]{2,1,0:T(8,128)(2,1)}, bf16[4,64,1792]{2,1,0:T(8,128)(2,1)S(1)}, u32[]{:S(2)}) copy-start(bf16[4,64,1792]{2,1,0:T(8,128)(2,1)S(1)} %all-to-all-done.4.refs_0_) | copy-start | bytes 2752516
  177.5 21.8 %all-to-all-start.3 = ((bf16[4,32,1792]{2,1,0:T(8,128)(2,1)}), bf16[4,32,1792]{2,1,0:T(8,128)(2,1)S(1)}, u32[]{:S(2)}, u32[]{:S(2)}) async-start(bf16[4,32,1792]{2,1,0:T(8,128)(2,1)} %get-tuple-element.16), calls=%async_computation.3 | async-start | bytes 917504 | tf_op jit(solution)/shard_map/all_to_all | solution.py:29
  186.8 16.7 %collective-permute-start.11 = (bf16[128,1024]{1,0:T(8,128)(2,1)S(1)}, bf16[128,1024]{1,0:T(8,128)(2,1)S(1)}, u32[]{:S(2)}, u32[]{:S(2)}) collective-permute-start(bf16[128,1024]{1,0:T(8,128)(2,1)S(1)} %add_convert_fusion.2), channel_id=1, source_target_pairs={{0,1},{1,2},{2,3},{3,0},{64,67},{65,64},{66,65},{67,66},{4,5},{5,6... | collective-permute-start | bytes 786440 | tf_op jit(solution)/shard_map/ppermute | solution.py:23
  194.7 25.9 %collective-permute-start.12 = (bf16[128,1024]{1,0:T(8,128)(2,1)}, bf16[128,1024]{1,0:T(8,128)(2,1)S(1)}, u32[]{:S(2)}, u32[]{:S(2)}) collective-permute-start(bf16[128,1024]{1,0:T(8,128)(2,1)} %get-tuple-element.20), channel_id=1, source_target_pairs={{0,3},{1,0},{2,1},{3,2},{64,65},{65,66},{66,67},{67,64},{4,7},{5,4... | collective-permute-start | bytes 786440 | tf_op jit(solution)/shard_map/ppermute | solution.py:23
  199.3 0.8 copy-start.8
  223.2 3.8 %collective-permute-start.13 = (bf16[4,64,1024]{2,1,0:T(8,128)(2,1)S(1)}, bf16[4,64,1024]{2,1,0:T(8,128)(2,1)S(1)}, u32[]{:S(2)}, u32[]{:S(2)}) collective-permute-start(bf16[4,64,1024]{2,1,0:T(8,128)(2,1)S(1)} %add_convert_fusion.1), channel_id=1, source_target_pairs={{0,64},{64,0},{1,65},{65,1},{2,66},{66,2},{3,67},{67,3},{4,68},{68... | collective-permute-start | bytes 1572872 | tf_op jit(solution)/shard_map/ppermute | solution.py:18

commit v8 on v5

--- a/solution.py
+++ b/solution.py
@@ -8,6 +8,7 @@
 wide = jnp.float32
 half = jnp.bfloat16
 LIMIT = 60 * 2**20
+LONG = pl.CostEstimate(flops=10**11, bytes_accessed=1024, transcendentals=0)
 COST = pl.CostEstimate(flops=1024, bytes_accessed=1024, transcendentals=0)
 ANY = pl.BlockSpec(memory_space=pl.ANY)
 WHOLE = pl.BlockSpec(memory_space=pltpu.VMEM)
@@ -32,20 +33,6 @@
 DIMS = (((1,), (1,)), ((), ()))
 
 
-def hold(a, after):
-    def kernel(a_ref, after_ref, out_ref):
-        out_ref[...] = a_ref[...]
-
-    return pl.pallas_call(
-        kernel,
-        in_specs=[WHOLE, ANY],
-        out_specs=WHOLE,
-        out_shape=jax.ShapeDtypeStruct(a.shape, a.dtype),
-        compiler_params=pltpu.CompilerParams(vmem_limit_bytes=LIMIT),
-        cost_estimate=COST,
-    )(a, after)
-
-
 def fetch(refs, held, sems):
     copies = [pltpu.make_async_copy(ref, held.at[i], sems.at[i]) for i, ref in enumerate(refs)]
     for copy in copies:
@@ -53,86 +40,78 @@
     return copies
 
 
-def early(pieces, weights, after):
+def early(pieces, weights, spare, after):
+    n = len(pieces)
+
     def kernel(*refs):
-        out_ref, copy_ref, held, sems, sem = refs[-5:]
-        copies = fetch(refs[3:6], held, sems)
-        x = jnp.concatenate([ref[...] for ref in refs[:3]])
-        spare = pltpu.make_async_copy(held.at[1], copy_ref, sem)
+        out_ref, held, sums, sems, out_sems = refs[-5:]
+        copies = fetch(refs[n : n + 3], held, sems)
+        x = jnp.concatenate([ref[...] for ref in refs[:n]])
+        going = []
         for i in range(3):
             copies[i].wait()
-            if i == 1:
-                spare.start()
+            if i == 1 and spare:
+                going.append(pltpu.make_async_copy(held.at[1], refs[-6], out_sems.at[3]))
+                going[-1].start()
+            columns = pl.ds(896 * i, 896)
             out = lax.dot_general(x, held[i], DIMS, preferred_element_type=wide).astype(half)
-            for p in range(3):
-                out_ref[:, pl.ds(32 * p, 32), pl.ds(896 * i, 896)] = out[128 * p : 128 * p + 128].reshape(4, 32, 896)
-        spare.wait()
-
-    return pl.pallas_call(
-        kernel,
-        in_specs=[WHOLE] * 3 + [ANY] * (3 + len(after)),
-        out_specs=[WHOLE, ANY],
-        out_shape=[jax.ShapeDtypeStruct((4, 96, 2688), half), jax.ShapeDtypeStruct((896, 1024), half)],
+            for p in range(n):
+                sums[:, pl.ds(32 * p, 32), columns] = out[128 * p : 128 * p + 128].reshape(4, 32, 896)
+            going.append(pltpu.make_async_copy(sums.at[:, :, columns], out_ref.at[:, :, columns], out_sems.at[i]))
+            going[-1].start()
+        for copy in going:
+            copy.wait()
+
+    shapes = [(896, 1024)] * spare + [(4, 32 * n, 2688)]
+    return pl.pallas_call(
+        kernel,
+        in_specs=[WHOLE] * n + [ANY] * (3 + len(after)),
+        out_specs=[ANY] * len(shapes),
+        out_shape=[jax.ShapeDtypeStruct(shape, half) for shape in shapes],
         scratch_shapes=[
             pltpu.VMEM((3, 896, 1024), half),
+            pltpu.VMEM((4, 32 * n, 2688), half),
             pltpu.SemaphoreType.DMA((3,)),
-            pltpu.SemaphoreType.DMA,
+            pltpu.SemaphoreType.DMA((4,)),
         ],
         compiler_params=pltpu.CompilerParams(vmem_limit_bytes=LIMIT),
-        cost_estimate=COST,
+        cost_estimate=LONG,
     )(*pieces, *weights, *after)
 
 
-def late_near(far, weights):
-    def kernel(far_ref, *refs):
-        out_ref, held, sums, sems, sem = refs[-5:]
-        copies = fetch(refs[:3], held, sems)
-        x = far_ref[...]
-        for i in range(3):
+def late(pieces, weights, after):
+    def kernel(*refs):
+        out_ref, held, sums, sems, out_sems = refs[-5:]
+        copies = fetch(refs[4:8], held, sems)
+        x = jnp.concatenate([ref[...] for ref in refs[:4]])
+        going = []
+        for i in range(4):
             copies[i].wait()
-            out = lax.dot_general(x, held[i], DIMS, preferred_element_type=wide).astype(half)
-            sums[:, :, pl.ds(896 * i, 896)] = out.reshape(4, 32, 896)
-        copy = pltpu.make_async_copy(sums, out_ref.at[:, :, pl.ds(0, 2688)], sem)
-        copy.start()
-        copy.wait()
-
-    return pl.pallas_call(
-        kernel,
-        in_specs=[WHOLE] + [ANY] * 3,
+            rows = x[:128] if i < 3 else x
+            out = lax.dot_general(rows, held[i], DIMS, preferred_element_type=wide).astype(half)
+            for p in range(1 if i < 3 else 4):
+                columns = pl.ds(896 * (i + p), 896)
+                sums[:, :, columns] = out[128 * p : 128 * p + 128].reshape(4, 32, 896)
+            columns = pl.ds(896 * i, 896 if i < 3 else 3584)
+            going.append(pltpu.make_async_copy(sums.at[:, :, columns], out_ref.at[:, :, columns], out_sems.at[i]))
+            going[-1].start()
+        for copy in going:
+            copy.wait()
+
+    return pl.pallas_call(
+        kernel,
+        in_specs=[WHOLE] * 4 + [ANY] * (4 + len(after)),
         out_specs=ANY,
         out_shape=jax.ShapeDtypeStruct((4, 32, 6272), half),
         scratch_shapes=[
-            pltpu.VMEM((3, 896, 1024), half),
-            pltpu.VMEM((4, 32, 2688), half),
-            pltpu.SemaphoreType.DMA((3,)),
-            pltpu.SemaphoreType.DMA,
+            pltpu.VMEM((4, 896, 1024), half),
+            pltpu.VMEM((4, 32, 6272), half),
+            pltpu.SemaphoreType.DMA((4,)),
+            pltpu.SemaphoreType.DMA((4,)),
         ],
         compiler_params=pltpu.CompilerParams(vmem_limit_bytes=LIMIT),
         cost_estimate=COST,
-    )(far, *weights)
-
-
-def late_far(pieces, w_far, begun):
-    def kernel(*refs):
-        w_ref, out_ref, sums, sem = refs[4], refs[6], refs[7], refs[8]
-        x = jnp.concatenate([ref[...] for ref in refs[:4]])
-        out = lax.dot_general(x, w_ref[...], DIMS, preferred_element_type=wide).astype(half)
-        for p in range(4):
-            sums[:, :, pl.ds(896 * p, 896)] = out[128 * p : 128 * p + 128].reshape(4, 32, 896)
-        copy = pltpu.make_async_copy(sums, out_ref.at[:, :, pl.ds(2688, 3584)], sem)
-        copy.start()
-        copy.wait()
-
-    return pl.pallas_call(
-        kernel,
-        in_specs=[WHOLE] * 5 + [ANY],
-        out_specs=ANY,
-        out_shape=jax.ShapeDtypeStruct((4, 32, 6272), half),
-        scratch_shapes=[pltpu.VMEM((4, 32, 3584), half), pltpu.SemaphoreType.DMA],
-        input_output_aliases={5: 0},
-        compiler_params=pltpu.CompilerParams(vmem_limit_bytes=LIMIT),
-        cost_estimate=COST,
-    )(*pieces, w_far, begun)
+    )(*pieces, *weights, *after)
 
 
 def act(gate, up):
@@ -145,6 +124,8 @@
 
 
 def activate_early(sums, after):
+    rows = sums.shape[1]
+
     def kernel(sums_ref, *refs):
         out_ref = refs[-1]
         total = jnp.sum(sums_ref[...].astype(wide), axis=0)
@@ -152,30 +133,41 @@
 
     return pl.pallas_call(
         kernel,
-        in_specs=[WHOLE] + [ANY] * len(after),
-        out_specs=WHOLE,
-        out_shape=jax.ShapeDtypeStruct((96, 1344), half),
+        grid=(1,),
+        in_specs=[pl.BlockSpec((4, rows, 2688), lambda i: (0, 0, 0))] + [ANY] * len(after),
+        out_specs=pl.BlockSpec((rows, 1344), lambda i: (0, 0)),
+        out_shape=jax.ShapeDtypeStruct((rows, 1344), half),
         compiler_params=pltpu.CompilerParams(vmem_limit_bytes=LIMIT),
         cost_estimate=COST,
     )(sums, *after)
 
 
-def activate_late(sums, first):
-    def kernel(sums_ref, first_ref, *outs):
+def activate_late(sums, near, own, after):
+    def kernel(sums_ref, near_ref, own_ref, *refs):
+        outs = refs[-3:]
         total = jnp.sum(sums_ref[...].astype(wide), axis=0)
         blocks = [block(total, i) for i in range(7)]
         far = jnp.concatenate(blocks[:4], axis=1)
-        rest = jnp.concatenate([first_ref[...], jnp.concatenate(blocks[4:])], axis=1)
-        for part, out in zip((far, rest[:64], rest[64:]), outs):
+        near = jnp.concatenate([near_ref[...], jnp.concatenate(blocks[4:6])], axis=1)
+        own = jnp.concatenate([own_ref[...], blocks[6]], axis=1)
+        for part, out in zip((far, near, own), outs):
             for j in range(4):
                 out[j] = part
 
     return pl.pallas_call(
         kernel,
+        grid=(1,),
+        in_specs=[
+            pl.BlockSpec((4, 32, 6272), lambda i: (0, 0, 0)),
+            pl.BlockSpec((64, 1344), lambda i: (0, 0)),
+            pl.BlockSpec((32, 1344), lambda i: (0, 0)),
+        ]
+        + [ANY] * len(after),
+        out_specs=[pl.BlockSpec((4, r, 1792), lambda i: (0, 0, 0)) for r in (32, 64, 32)],
         out_shape=[jax.ShapeDtypeStruct((4, r, 1792), half) for r in (32, 64, 32)],
         compiler_params=pltpu.CompilerParams(vmem_limit_bytes=LIMIT),
         cost_estimate=COST,
-    )(sums, first)
+    )(sums, near, own, *after)
 
 
 def down(hidden, weights, types):
@@ -244,15 +236,17 @@
     )
 
     first, second = pass_on(rows, "zhi", 1), pass_on(rows, "zhi", -1)
-    part, w_next = early([first, second, rows], weights, [v_first])
-
-    far = pass_on(hold(first, second), "zhi", 1)
+    w_next, own_part = early([rows], weights, True, [])
+    own_sums = swap(own_part, "x")
     w_far = pass_on(w_next, "y", 1)
+
+    (part,) = early([first, second], weights, False, [own_part])
+    far = pass_on(first, "zhi", 1)
     v_far = pass_on(v_first, "y", 1)
     v_all = [v_own, v_first, v_second, v_far]
-    begun = activate_early(swap(part, "x"), [v_second, v_far])
-    rest = swap(late_far([far, first, second, rows], w_far, late_near(far, weights)), "x")
-    far_h, near_h, own_h = activate_late(rest, begun)
+    own_h, near_h = activate_early(own_sums, []), activate_early(swap(part, "x"), [v_first])
+    rest = swap(late([far, first, second, rows], weights + [w_far], []), "x")
+    far_h, near_h, own_h = activate_late(rest, near_h, own_h, [v_second, v_far])
 
     (far_out,) = down(swap(far_h, "x"), v_all, (half,))
     got = pass_on(far_out, "zhi", 1)

time: 244 us -> 238 us (0.975)
  blocking collectives: 38.9 us -> 30.5 us
  starting transfers between devices: 95 us -> 99.4 us
  waiting for transfers between devices: 49.5 us -> 46.9 us
    all_to_all x2, blocking collectives: 38.9 us -> 30.5 us  [swap(): return lax.all_to_all(a, axis, split_axis=0, concat_axis=0, tiled=True)]
    ppermute x5, starting transfers between devices: 26 us -> 18.7 us  [shift(): return lax.ppermute(a, axis, [(i, (i + by) % n) for i in range(n)])]
    ppermute x12, starting transfers between devices: 54.1 us -> 61.2 us  [pass_on(): lax.ppermute(a, ('core', axis), [(c * n + i, c * n + (i + by * (1 - 2 * c...]
    all_to_all x4 -> x5, starting transfers between devices: 15 us -> 19.5 us  [swap(): return lax.all_to_all(a, axis, split_axis=0, concat_axis=0, tiled=True)]
    all_to_all x4 -> x5, waiting for transfers between devices: 4 us -> 1.23 us  [swap(): return lax.all_to_all(a, axis, split_axis=0, concat_axis=0, tiled=True)]
    unnamed x28 -> x38, local copies, waits for them, and re-layouts: 5.45 us -> 5.29 us
  transfers between devices with their start and end apart: 21 -> 22, of which waited for: 8 -> 9; matrix products, arithmetic and copies ran while one was open for 4% -> 4% of each run, Pallas kernels for 10% -> 14%
where the time goes in v8:
time: 238 us; the launch traced here: 237 us
  starting transfers between devices  99.4 us (42%)
  waiting for transfers between devices  46.9 us (20%)
  Pallas kernels  36.8 us (15%)
  blocking collectives  30.5 us (13%)
  other arithmetic  12.1 us (5%)
  local copies, waits for them, and re-layouts  5.47 us (2%)
  between operations  5.41 us (2%)
    ppermute x12, starting transfers between devices, pass_on(): lax.ppermute(a, ('core', axis), [(c * n + i, c * n + (i + by * (1 - 2 * c...  61.2 us
    ppermute x12, waiting for transfers between devices, pass_on(): lax.ppermute(a, ('core', axis), [(c * n + i, c * n + (i + by * (1 - 2 * c...  43.5 us
    all_to_all x2, blocking collectives, swap(): return lax.all_to_all(a, axis, split_axis=0, concat_axis=0, tiled=True)  30.5 us
    all_to_all x5, starting transfers between devices, swap(): return lax.all_to_all(a, axis, split_axis=0, concat_axis=0, tiled=True)  19.5 us
    ppermute x5, starting transfers between devices, shift(): return lax.ppermute(a, axis, [(i, (i + by) % n) for i in range(n)])  18.7 us
    pallas_call x2, Pallas kernels, early(): pl.pallas_call(kernel, in_specs=[WHOLE] * n + [ANY] * (3 + len(after)), o...  11.2 us
    pallas_call x3, Pallas kernels, down(): pl.pallas_call(kernel, grid=(2,), in_specs=[pl.BlockSpec((4, 32 * n, 1792...  11 us
    pallas_call x1, Pallas kernels, late(): pl.pallas_call(kernel, in_specs=[WHOLE] * 4 + [ANY] * (4 + len(after)), o...  7.23 us
  transfers between devices with their start and end apart: 22, of which 9 were waited for; matrix products, arithmetic and copies ran while one was open for 4% of the time, Pallas kernels for 14%

profile of v8, /device:TPU:1, one launch (start us, length us, event | category | flops | bytes accessed | tf_op | source)
XLA Modules:
  0.0 236.6 jit_solution(12615777951065237818)
XLA Ops:
  0.0 5.5 %collective-permute-start.7 = (bf16[896,1024]{1,0:T(8,128)(2,1)}, bf16[896,1024]{1,0:T(8,128)(2,1)S(1)}, u32[]{:S(2)}, u32[]{:S(2)}) collective-permute-start(bf16[896,1024]{1,0:T(8,128)(2,1)} %bitcast.12), channel_id=1, source_target_pairs={{0,4},{4,8},{8,12},{12,0},{64,76},{68,64},{72,68},{76,72},{1,5},{5... | collective-permute-start | bytes 5505032 | tf_op jit(solution)/shard_map/ppermute | solution.py:24
  5.5 1.9 collective-permute-start.8
  7.4 4.9 %collective-permute-start.1 = (bf16[64,1024]{1,0:T(8,128)(2,1)}, bf16[64,1024]{1,0:T(8,128)(2,1)S(1)}, u32[]{:S(2)}, u32[]{:S(2)}) collective-permute-start(bf16[64,1024]{1,0:T(8,128)(2,1)} %bitcast.17), channel_id=1, source_target_pairs={{0,256},{128,384},{256,0},{384,128},{1,257},{129,385},{257,1},{385... | collective-permute-start | bytes 393224 | tf_op jit(solution)/shard_map/ppermute | solution.py:19
  12.3 3.3 %collective-permute-start.2 = (bf16[64,1024]{1,0:T(8,128)(2,1)}, bf16[64,1024]{1,0:T(8,128)(2,1)S(1)}, u32[]{:S(2)}, u32[]{:S(2)}) collective-permute-start(bf16[64,1024]{1,0:T(8,128)(2,1)} %bitcast.18), channel_id=1, source_target_pairs={{0,384},{128,0},{256,128},{384,256},{1,385},{129,1},{257,129},{385... | collective-permute-start | bytes 393224 | tf_op jit(solution)/shard_map/ppermute | solution.py:19
  15.6 2.2 collective-permute-start
  21.6 1.9 collective-permute-done
  23.5 0.9 select_select_fusion.1
  24.5 5.6 %collective-permute-start.3 = (bf16[128,1024]{1,0:T(8,128)(2,1)S(1)}, bf16[128,1024]{1,0:T(8,128)(2,1)S(1)}, u32[]{:S(2)}, u32[]{:S(2)}) collective-permute-start(bf16[128,1024]{1,0:T(8,128)(2,1)S(1)} %pad_maximum_fusion), channel_id=1, source_target_pairs={{0,64},{64,0},{1,65},{65,1},{2,66},{66,2},{3,67},{67,3},{4,68},{68... | collective-permute-start | bytes 786440 | tf_op jit(solution)/shard_map/ppermute | solution.py:19
  32.5 0.9 slice_select_fusion.1
  33.5 10.0 %collective-permute-start.4 = (bf16[128,1024]{1,0:T(8,128)(2,1)S(1)}, bf16[128,1024]{1,0:T(8,128)(2,1)S(1)}, u32[]{:S(2)}, u32[]{:S(2)}) collective-permute-start(bf16[128,1024]{1,0:T(8,128)(2,1)S(1)} %pad_maximum_fusion.1.refs_0_.refs_3_), channel_id=1, source_target_pairs={{0,1},{1,2},{2,3},{3,0},{64,67},{65,64},{66,65},{67,66},{4,5},{5,6... | collective-permute-start | bytes 786440 | tf_op jit(solution)/shard_map/ppermute | solution.py:24
  43.5 1.9 collective-permute-start.6
  45.5 3.4 %collective-permute-done.8.refs_3_.refs_6_.refs_4_ = bf16[896,1024]{1,0:T(8,128)(2,1)} collective-permute-done((bf16[896,1024]{1,0:T(8,128)(2,1)}, bf16[896,1024]{1,0:T(8,128)(2,1)}, u32[]{:S(2)}, u32[]{:S(2)}) %collective-permute-start.8) | collective-permute-done | bytes 1835040 | tf_op jit(solution)/shard_map/ppermute | solution.py:24
  48.9 5.5 %shard_map.55 = (bf16[896,1024]{1,0:T(8,128)(2,1)}, bf16[4,32,2688]{2,1,0:T(8,128)(2,1)}) custom-call(bf16[128,1024]{1,0:T(8,128)(2,1)} %copy-done.8, bf16[896,1024]{1,0:T(8,128)(2,1)} %bitcast.14, bf16[896,1024]{1,0:T(8,128)(2,1)} %copy-done.7, bf16[896,1024]{1,0:T(8,128)(2,1)} %collective-permute-done.8.refs_3_.refs_6_.refs_4_), custom_call_target="tpu_custom_call" | custom-call | flops 99999997952 | bytes 1024 | tf_op jit(solution)/shard_map/pallas_call | solution.py:66
  54.4 1.9 collective-permute-start.9
  56.3 4.0 %all-to-all-start.2 = ((bf16[4,32,2688]{2,1,0:T(8,128)(2,1)}), bf16[4,32,2688]{2,1,0:T(8,128)(2,1)S(1)}, u32[]{:S(2)}, u32[]{:S(2)}) async-start(bf16[4,32,2688]{2,1,0:T(8,128)(2,1)} %get-tuple-element.13.refs_5_), calls=%async_computation.2 | async-start | bytes 1376256 | tf_op jit(solution)/shard_map/all_to_all | solution.py:30
  60.4 1.6 collective-permute-done.4.refs_1_.refs_0_
  63.4 5.7 %shard_map.57 = bf16[4,64,2688]{2,1,0:T(8,128)(2,1)} custom-call(bf16[128,1024]{1,0:T(8,128)(2,1)} %copy-done.9, bf16[128,1024]{1,0:T(8,128)(2,1)} %copy-done.11, bf16[896,1024]{1,0:T(8,128)(2,1)} %bitcast.15, bf16[896,1024]{1,0:T(8,128)(2,1)} %copy-done.7, bf16[896,1024]{1,0:T(8,128)(2,1)} %collective-permute-done.8.refs_3_.refs_6_.refs_4_, ...), custom_call_target="tpu_custom_call" | custom-call | flops 99999997952 | bytes 1024 | tf_op jit(solution)/shard_map/pallas_call | solution.py:66
  69.1 4.2 %all-to-all-start.1 = ((bf16[4,64,2688]{2,1,0:T(8,128)(2,1)}), bf16[4,64,2688]{2,1,0:T(8,128)(2,1)S(1)}, u32[]{:S(2)}, u32[]{:S(2)}) async-start(bf16[4,64,2688]{2,1,0:T(8,128)(2,1)} %shard_map.57), calls=%async_computation.1 | async-start | bytes 2752512 | tf_op jit(solution)/shard_map/all_to_all | solution.py:30
  73.2 3.8 %collective-permute-start.10 = (bf16[448,1024]{1,0:T(8,128)(2,1)}, bf16[448,1024]{1,0:T(8,128)(2,1)S(1)}, u32[]{:S(2)}, u32[]{:S(2)}) collective-permute-start(bf16[448,1024]{1,0:T(8,128)(2,1)} %bitcast.6.refs_1_), channel_id=1, source_target_pairs={{0,4},{4,8},{8,12},{12,0},{64,76},{68,64},{72,68},{76,72},{1,5},{5... | collective-permute-start | bytes 2752520 | tf_op jit(solution)/shard_map/ppermute | solution.py:24
  77.1 12.5 %collective-permute-start.5 = (bf16[128,1024]{1,0:T(8,128)(2,1)S(1)}, bf16[128,1024]{1,0:T(8,128)(2,1)S(1)}, u32[]{:S(2)}, u32[]{:S(2)}) collective-permute-start(bf16[128,1024]{1,0:T(8,128)(2,1)S(1)} %copy-done.10), channel_id=1, source_target_pairs={{0,1},{1,2},{2,3},{3,0},{64,67},{65,64},{66,65},{67,66},{4,5},{5,6... | collective-permute-start | bytes 786440 | tf_op jit(solution)/shard_map/ppermute | solution.py:24
  89.6 11.7 %collective-permute-done.5.refs_0_ = bf16[128,1024]{1,0:T(8,128)(2,1)S(1)} collective-permute-done((bf16[128,1024]{1,0:T(8,128)(2,1)S(1)}, bf16[128,1024]{1,0:T(8,128)(2,1)S(1)}, u32[]{:S(2)}, u32[]{:S(2)}) %collective-permute-start.5) | collective-permute-done | bytes 262176 | tf_op jit(solution)/shard_map/ppermute | solution.py:24
  102.0 7.2 %shard_map.56 = bf16[4,32,6272]{2,1,0:T(8,128)(2,1)} custom-call(bf16[128,1024]{1,0:T(8,128)(2,1)} %copy-done.12, bf16[128,1024]{1,0:T(8,128)(2,1)} %copy-done.9, bf16[128,1024]{1,0:T(8,128)(2,1)} %copy-done.11, bf16[128,1024]{1,0:T(8,128)(2,1)} %copy-done.8, bf16[896,1024]{1,0:T(8,128)(2,1)} %bitcast.16, bf16[896,1024]{1,0:T(8,128)(2,1)} %copy-done.7, ...), custom_call_target="tpu_custom_call" | custom-call | flops 1024 | bytes 1024 | tf_op jit(solution)/shard_map/pallas_call | solution.py:101
  109.3 1.1 copy-done.3
  110.4 4.4 %all-to-all-start = ((bf16[4,32,6272]{2,1,0:T(8,128)(2,1)}), bf16[4,32,6272]{2,1,0:T(8,128)(2,1)}, u32[]{:S(2)}, u32[]{:S(2)}) async-start(bf16[4,32,6272]{2,1,0:T(8,128)(2,1)} %shard_map.56), calls=%async_computation | async-start | bytes 3211264 | tf_op jit(solution)/shard_map/all_to_all | solution.py:30
  114.7 3.0 %collective-permute-start.11 = (bf16[448,1024]{1,0:T(8,128)(2,1)}, bf16[448,1024]{1,0:T(8,128)(2,1)S(1)}, u32[]{:S(2)}, u32[]{:S(2)}) collective-permute-start(bf16[448,1024]{1,0:T(8,128)(2,1)} %bitcast.6.refs_1_), channel_id=1, source_target_pairs={{0,12},{4,0},{8,4},{12,8},{64,68},{68,72},{72,76},{76,64},{1,13},{... | collective-permute-start | bytes 2752520 | tf_op jit(solution)/shard_map/ppermute | solution.py:24
  117.8 3.5 %collective-permute-start.12 = (bf16[448,1024]{1,0:T(8,128)(2,1)S(1)}, bf16[448,1024]{1,0:T(8,128)(2,1)S(1)}, u32[]{:S(2)}, u32[]{:S(2)}) collective-permute-start(bf16[448,1024]{1,0:T(8,128)(2,1)S(1)} %collective-permute-done.10.refs_0_.refs_2_), channel_id=1, source_target_pairs={{0,4},{4,8},{8,12},{12,0},{64,76},{68,64},{72,68},{76,72},{1,5},{5... | collective-permute-start | bytes 2752520 | tf_op jit(solution)/shard_map/ppermute | solution.py:24
  121.3 1.9 shard_map.59.own_ref
  123.2 2.3 shard_map.58.near_ref
  125.5 13.3 %collective-permute-done.11.refs_0_.refs_3_ = bf16[448,1024]{1,0:T(8,128)(2,1)S(1)} collective-permute-done((bf16[448,1024]{1,0:T(8,128)(2,1)}, bf16[448,1024]{1,0:T(8,128)(2,1)S(1)}, u32[]{:S(2)}, u32[]{:S(2)}) %collective-permute-start.11) | collective-permute-done | bytes 917536 | tf_op jit(solution)/shard_map/ppermute | solution.py:24
  138.8 0.9 copy-done
  140.1 3.2 %shard_map.60 = (bf16[4,32,1792]{2,1,0:T(8,128)(2,1)}, bf16[4,64,1792]{2,1,0:T(8,128)(2,1)}, bf16[4,32,1792]{2,1,0:T(8,128)(2,1)}) custom-call(bf16[4,32,6272]{2,1,0:T(8,128)(2,1)} %all-to-all-done.sums_ref, bf16[64,1344]{1,0:T(8,128)(2,1)} %shard_map.58.near_ref, bf16[32,1344]{1,0:T(8,128)(2,1)} %shard_map.59.own_ref, bf16[448,1024]{1,0:T(8,128)(2,1)} %copy-done, ...), custom_call_target="tpu_custom_call" | custom-call | flops 1024 | bytes 1024 | tf_op jit(solution)/shard_map/pallas_call | solution.py:157
  143.3 13.9 %all_to_all.35.refs_0_ = bf16[4,32,1792]{2,1,0:T(8,128)(2,1)} all-to-all(bf16[4,32,1792]{2,1,0:T(8,128)(2,1)} %get-tuple-element.17), channel_id=1, replica_groups=mesh['zlo'=4,'core'=2,'x'=4,'y'=4,'zhi'=4] {'x'}, dimensions={0} | all-to-all | bytes 917504 | tf_op jit(solution)/shard_map/all_to_all | solution.py:30
  157.2 3.5 %all-to-all-start.4 = ((bf16[4,64,1792]{2,1,0:T(8,128)(2,1)}), bf16[4,64,1792]{2,1,0:T(8,128)(2,1)S(1)}, u32[]{:S(2)}, u32[]{:S(2)}) async-start(bf16[4,64,1792]{2,1,0:T(8,128)(2,1)} %get-tuple-element.15), calls=%async_computation.4 | async-start | bytes 1835008 | tf_op jit(solution)/shard_map/all_to_all | solution.py:30
  160.7 3.4 %shard_map.63 = bf16[128,1024]{1,0:T(8,128)(2,1)} custom-call(bf16[4,32,1792]{2,1,0:T(8,128)(2,1)} %all_to_all.35.refs_0_, bf16[448,1024]{1,0:T(8,128)(2,1)} %bitcast.6.refs_1_, bf16[448,1024]{1,0:T(8,128)(2,1)} %copy-done.2, bf16[448,1024]{1,0:T(8,128)(2,1)} %copy-done, bf16[448,1024]{1,0:T(8,128)(2,1)} %copy-done.1), custom_call_target="tpu_custom_call" | custom-call | flops 1024 | bytes 1024 | tf_op jit(solution)/shard_map/pallas_call | solution.py:183
  164.1 8.0 %collective-permute-start.13 = (bf16[128,1024]{1,0:T(8,128)(2,1)}, bf16[128,1024]{1,0:T(8,128)(2,1)S(1)}, u32[]{:S(2)}, u32[]{:S(2)}) collective-permute-start(bf16[128,1024]{1,0:T(8,128)(2,1)} %shard_map.63), channel_id=1, source_target_pairs={{0,1},{1,2},{2,3},{3,0},{64,67},{65,64},{66,65},{67,66},{4,5},{5,6... | collective-permute-start | bytes 786440 | tf_op jit(solution)/shard_map/ppermute | solution.py:24
  172.8 1.2 all-to-all-done.4.refs_0_
  174.0 3.5 %all-to-all-start.3 = ((bf16[4,32,1792]{2,1,0:T(8,128)(2,1)}), bf16[4,32,1792]{2,1,0:T(8,128)(2,1)S(1)}, u32[]{:S(2)}, u32[]{:S(2)}) async-start(bf16[4,32,1792]{2,1,0:T(8,128)(2,1)} %get-tuple-element.14), calls=%async_computation.3 | async-start | bytes 917504 | tf_op jit(solution)/shard_map/all_to_all | solution.py:30
  177.5 4.1 %shard_map.62 = (bf16[128,1024]{1,0:T(8,128)(2,1)}, f32[128,1024]{1,0:T(8,128)}) custom-call(bf16[4,64,1792]{2,1,0:T(8,128)(2,1)} %copy-done.4, bf16[448,1024]{1,0:T(8,128)(2,1)} %bitcast.6.refs_1_, bf16[448,1024]{1,0:T(8,128)(2,1)} %copy-done.2, bf16[448,1024]{1,0:T(8,128)(2,1)} %copy-done, bf16[448,1024]{1,0:T(8,128)(2,1)} %copy-done.1), custom_call_target="tpu_custom_call" | custom-call | flops 1024 | bytes 1024 | tf_op jit(solution)/shard_map/pallas_call | solution.py:183
  181.6 3.6 %collective-permute-start.15 = (bf16[128,1024]{1,0:T(8,128)(2,1)}, bf16[128,1024]{1,0:T(8,128)(2,1)S(1)}, u32[]{:S(2)}, u32[]{:S(2)}) collective-permute-start(bf16[128,1024]{1,0:T(8,128)(2,1)} %get-tuple-element.18), channel_id=1, source_target_pairs={{0,3},{1,0},{2,1},{3,2},{64,65},{65,66},{66,67},{67,64},{4,7},{5,4... | collective-permute-start | bytes 786440 | tf_op jit(solution)/shard_map/ppermute | solution.py:24
  185.3 1.1 add_convert_fusion.2
  186.4 5.5 %collective-permute-start.14 = (bf16[128,1024]{1,0:T(8,128)(2,1)S(1)}, bf16[128,1024]{1,0:T(8,128)(2,1)S(1)}, u32[]{:S(2)}, u32[]{:S(2)}) collective-permute-start(bf16[128,1024]{1,0:T(8,128)(2,1)S(1)} %add_convert_fusion.2), channel_id=1, source_target_pairs={{0,1},{1,2},{2,3},{3,0},{64,67},{65,64},{66,65},{67,66},{4,5},{5,6... | collective-permute-start | bytes 786440 | tf_op jit(solution)/shard_map/ppermute | solution.py:24
  194.5 0.8 copy-done.6
  195.3 3.4 %shard_map.61 = f32[128,1024]{1,0:T(8,128)} custom-call(bf16[4,32,1792]{2,1,0:T(8,128)(2,1)} %copy-done.6, bf16[448,1024]{1,0:T(8,128)(2,1)} %bitcast.6.refs_1_, bf16[448,1024]{1,0:T(8,128)(2,1)} %copy-done.2, bf16[448,1024]{1,0:T(8,128)(2,1)} %copy-done, bf16[448,1024]{1,0:T(8,128)(2,1)} %copy-done.1), custom_call_target="tpu_custom_call" | custom-call | flops 1024 | bytes 1024 | tf_op jit(solution)/shard_map/pallas_call | solution.py:183
  199.0 13.2 %collective-permute-done.14 = bf16[128,1024]{1,0:T(8,128)(2,1)S(1)} collective-permute-done((bf16[128,1024]{1,0:T(8,128)(2,1)S(1)}, bf16[128,1024]{1,0:T(8,128)(2,1)S(1)}, u32[]{:S(2)}, u32[]{:S(2)}) %collective-permute-start.14) | collective-permute-done | bytes 262176 | tf_op jit(solution)/shard_map/ppermute | solution.py:24
  212.1 1.1 convert_add_fusion
  213.3 1.3 slice_multiply_fusion.1
  214.7 2.7 %collective-permute-start.16 = (bf16[4,64,1024]{2,1,0:T(8,128)(2,1)S(1)}, bf16[4,64,1024]{2,1,0:T(8,128)(2,1)S(1)}, u32[]{:S(2)}, u32[]{:S(2)}) collective-permute-start(bf16[4,64,1024]{2,1,0:T(8,128)(2,1)S(1)} %add_convert_fusion.1), channel_id=1, source_target_pairs={{0,64},{64,0},{1,65},{65,1},{2,66},{66,2},{3,67},{67,3},{4,68},{68... | collective-permute-start | bytes 1572872 | tf_op jit(solution)/shard_map/ppermute | solution.py:19
  219.2 16.6 %all_to_all.36 = bf16[4,64,1024]{2,1,0:T(8,128)(2,1)S(1)} all-to-all(bf16[4,64,1024]{2,1,0:T(8,128)(2,1)S(1)} %add_convert_fusion), channel_id=1, replica_groups=mesh['zlo'=4,'core'=2,'x'=4,'y'=4,'zhi'=4] {'zlo'}, dimensions={0} | all-to-all | bytes 1048576 | tf_op jit(solution)/shard_map/all_to_all | solution.py:30
  (69 shorter events, 10.0 us)
Async XLA Ops:
  0.0 45.4 %collective-permute-start.7 = (bf16[896,1024]{1,0:T(8,128)(2,1)}, bf16[896,1024]{1,0:T(8,128)(2,1)S(1)}, u32[]{:S(2)}, u32[]{:S(2)}) collective-permute-start(bf16[896,1024]{1,0:T(8,128)(2,1)} %bitcast.12), channel_id=1, source_target_pairs={{0,4},{4,8},{8,12},{12,0},{64,76},{68,64},{72,68},{76,72},{1,5},{5... | collective-permute-start | bytes 5505032 | tf_op jit(solution)/shard_map/ppermute | solution.py:24
  5.5 43.4 %collective-permute-start.8 = (bf16[896,1024]{1,0:T(8,128)(2,1)}, bf16[896,1024]{1,0:T(8,128)(2,1)}, u32[]{:S(2)}, u32[]{:S(2)}) collective-permute-start(bf16[896,1024]{1,0:T(8,128)(2,1)} %bitcast.13), channel_id=1, source_target_pairs={{0,12},{4,0},{8,4},{12,8},{64,68},{68,72},{72,76},{76,64},{1,13},{... | collective-permute-start | bytes 5505032 | tf_op jit(solution)/shard_map/ppermute | solution.py:24
  7.4 14.2 %collective-permute-start.1 = (bf16[64,1024]{1,0:T(8,128)(2,1)}, bf16[64,1024]{1,0:T(8,128)(2,1)S(1)}, u32[]{:S(2)}, u32[]{:S(2)}) collective-permute-start(bf16[64,1024]{1,0:T(8,128)(2,1)} %bitcast.17), channel_id=1, source_target_pairs={{0,256},{128,384},{256,0},{384,128},{1,257},{129,385},{257,1},{385... | collective-permute-start | bytes 393224 | tf_op jit(solution)/shard_map/ppermute | solution.py:19
  12.3 9.3 %collective-permute-start.2 = (bf16[64,1024]{1,0:T(8,128)(2,1)}, bf16[64,1024]{1,0:T(8,128)(2,1)S(1)}, u32[]{:S(2)}, u32[]{:S(2)}) collective-permute-start(bf16[64,1024]{1,0:T(8,128)(2,1)} %bitcast.18), channel_id=1, source_target_pairs={{0,384},{128,0},{256,128},{384,256},{1,385},{129,1},{257,129},{385... | collective-permute-start | bytes 393224 | tf_op jit(solution)/shard_map/ppermute | solution.py:19
  15.6 7.9 %collective-permute-start = (bf16[64,1024]{1,0:T(8,128)(2,1)}, bf16[64,1024]{1,0:T(8,128)(2,1)S(1)}, u32[]{:S(2)}, u32[]{:S(2)}) collective-permute-start(bf16[64,1024]{1,0:T(8,128)(2,1)} %bitcast.19), channel_id=1, source_target_pairs={{0,128},{128,256},{256,384},{384,0},{1,129},{129,257},{257,385},{3... | collective-permute-start | bytes 393224 | tf_op jit(solution)/shard_map/ppermute | solution.py:19
  18.9 5.5 %copy-start.13 = (pred[8]{0:T(512)(128)(4,1)}, pred[8]{0:T(512)(128)(4,1)S(1)}, u32[]{:S(2)}) copy-start(pred[8]{0:T(512)(128)(4,1)S(1)} %get-tuple-element.19) | copy-start | bytes 28
  18.9 5.5 %copy-start.15 = (pred[8]{0:T(512)(128)(4,1)}, pred[8]{0:T(512)(128)(4,1)S(1)}, u32[]{:S(2)}) copy-start(pred[8]{0:T(512)(128)(4,1)S(1)} %get-tuple-element.20) | copy-start | bytes 28
  24.5 8.0 %collective-permute-start.3 = (bf16[128,1024]{1,0:T(8,128)(2,1)S(1)}, bf16[128,1024]{1,0:T(8,128)(2,1)S(1)}, u32[]{:S(2)}, u32[]{:S(2)}) collective-permute-start(bf16[128,1024]{1,0:T(8,128)(2,1)S(1)} %pad_maximum_fusion), channel_id=1, source_target_pairs={{0,64},{64,0},{1,65},{65,1},{2,66},{66,2},{3,67},{67,3},{4,68},{68... | collective-permute-start | bytes 786440 | tf_op jit(solution)/shard_map/ppermute | solution.py:19
  33.5 15.4 %copy-start.8 = (bf16[128,1024]{1,0:T(8,128)(2,1)}, bf16[128,1024]{1,0:T(8,128)(2,1)S(1)}, u32[]{:S(2)}) copy-start(bf16[128,1024]{1,0:T(8,128)(2,1)S(1)} %pad_maximum_fusion.1.refs_0_.refs_3_) | copy-start | bytes 786436
  33.5 28.5 %collective-permute-start.4 = (bf16[128,1024]{1,0:T(8,128)(2,1)S(1)}, bf16[128,1024]{1,0:T(8,128)(2,1)S(1)}, u32[]{:S(2)}, u32[]{:S(2)}) collective-permute-start(bf16[128,1024]{1,0:T(8,128)(2,1)S(1)} %pad_maximum_fusion.1.refs_0_.refs_3_), channel_id=1, source_target_pairs={{0,1},{1,2},{2,3},{3,0},{64,67},{65,64},{66,65},{67,66},{4,5},{5,6... | collective-permute-start | bytes 786440 | tf_op jit(solution)/shard_map/ppermute | solution.py:24
  43.5 18.5 %collective-permute-start.6 = (bf16[128,1024]{1,0:T(8,128)(2,1)S(1)}, bf16[128,1024]{1,0:T(8,128)(2,1)S(1)}, u32[]{:S(2)}, u32[]{:S(2)}) collective-permute-start(bf16[128,1024]{1,0:T(8,128)(2,1)S(1)} %pad_maximum_fusion.1.refs_0_.refs_3_), channel_id=1, source_target_pairs={{0,3},{1,0},{2,1},{3,2},{64,65},{65,66},{66,67},{67,64},{4,7},{5,4... | collective-permute-start | bytes 786440 | tf_op jit(solution)/shard_map/ppermute | solution.py:24
  45.4 3.5 %copy-start.7 = (bf16[896,1024]{1,0:T(8,128)(2,1)}, bf16[896,1024]{1,0:T(8,128)(2,1)S(1)}, u32[]{:S(2)}) copy-start(bf16[896,1024]{1,0:T(8,128)(2,1)S(1)} %collective-permute-done.7.refs_2_.refs_5_.refs_3_) | copy-start | bytes 5505028
  54.4 46.9 %collective-permute-start.9 = (bf16[896,1024]{1,0:T(8,128)(2,1)}, bf16[896,1024]{1,0:T(8,128)(2,1)}, u32[]{:S(2)}, u32[]{:S(2)}) collective-permute-start(bf16[896,1024]{1,0:T(8,128)(2,1)} %get-tuple-element.12), channel_id=1, source_target_pairs={{0,4},{4,8},{8,12},{12,0},{64,76},{68,64},{72,68},{76,72},{1,5},{5... | collective-permute-start | bytes 5505032 | tf_op jit(solution)/shard_map/ppermute | solution.py:24
  56.3 12.7 %all-to-all-start.2 = ((bf16[4,32,2688]{2,1,0:T(8,128)(2,1)}), bf16[4,32,2688]{2,1,0:T(8,128)(2,1)S(1)}, u32[]{:S(2)}, u32[]{:S(2)}) async-start(bf16[4,32,2688]{2,1,0:T(8,128)(2,1)} %get-tuple-element.13.refs_5_), calls=%async_computation.2 | async-start | bytes 1376256 | tf_op jit(solution)/shard_map/all_to_all | solution.py:30
  62.0 0.7 copy-start.9
  62.7 0.7 copy-start.11
  69.0 8.0 %copy-start.10 = (bf16[128,1024]{1,0:T(8,128)(2,1)S(1)}, bf16[128,1024]{1,0:T(8,128)(2,1)}, u32[]{:S(2)}) copy-start(bf16[128,1024]{1,0:T(8,128)(2,1)} %copy-done.9) | copy-start | bytes 786436
  69.1 40.2 %copy-start.5 = (bf16[4,32,2688]{2,1,0:T(8,128)(2,1)}, bf16[4,32,2688]{2,1,0:T(8,128)(2,1)S(1)}, u32[]{:S(2)}) copy-start(bf16[4,32,2688]{2,1,0:T(8,128)(2,1)S(1)} %all-to-all-done.2.sums_ref) | copy-start | bytes 2064388
  69.1 40.2 %all-to-all-start.1 = ((bf16[4,64,2688]{2,1,0:T(8,128)(2,1)}), bf16[4,64,2688]{2,1,0:T(8,128)(2,1)S(1)}, u32[]{:S(2)}, u32[]{:S(2)}) async-start(bf16[4,64,2688]{2,1,0:T(8,128)(2,1)} %shard_map.57), calls=%async_computation.1 | async-start | bytes 2752512 | tf_op jit(solution)/shard_map/all_to_all | solution.py:30
  73.2 44.5 %collective-permute-start.10 = (bf16[448,1024]{1,0:T(8,128)(2,1)}, bf16[448,1024]{1,0:T(8,128)(2,1)S(1)}, u32[]{:S(2)}, u32[]{:S(2)}) collective-permute-start(bf16[448,1024]{1,0:T(8,128)(2,1)} %bitcast.6.refs_1_), channel_id=1, source_target_pairs={{0,4},{4,8},{8,12},{12,0},{64,76},{68,64},{72,68},{76,72},{1,5},{5... | collective-permute-start | bytes 2752520 | tf_op jit(solution)/shard_map/ppermute | solution.py:24
  77.1 24.2 %collective-permute-start.5 = (bf16[128,1024]{1,0:T(8,128)(2,1)S(1)}, bf16[128,1024]{1,0:T(8,128)(2,1)S(1)}, u32[]{:S(2)}, u32[]{:S(2)}) collective-permute-start(bf16[128,1024]{1,0:T(8,128)(2,1)S(1)} %copy-done.10), channel_id=1, source_target_pairs={{0,1},{1,2},{2,3},{3,0},{64,67},{65,64},{66,65},{67,66},{4,5},{5,6... | collective-permute-start | bytes 786440 | tf_op jit(solution)/shard_map/ppermute | solution.py:24
  101.3 0.7 copy-start.12
  109.3 1.1 copy-start.3
  110.4 28.4 %all-to-all-start = ((bf16[4,32,6272]{2,1,0:T(8,128)(2,1)}), bf16[4,32,6272]{2,1,0:T(8,128)(2,1)}, u32[]{:S(2)}, u32[]{:S(2)}) async-start(bf16[4,32,6272]{2,1,0:T(8,128)(2,1)} %shard_map.56), calls=%async_computation | async-start | bytes 3211264 | tf_op jit(solution)/shard_map/all_to_all | solution.py:30
  114.7 24.0 %collective-permute-start.11 = (bf16[448,1024]{1,0:T(8,128)(2,1)}, bf16[448,1024]{1,0:T(8,128)(2,1)S(1)}, u32[]{:S(2)}, u32[]{:S(2)}) collective-permute-start(bf16[448,1024]{1,0:T(8,128)(2,1)} %bitcast.6.refs_1_), channel_id=1, source_target_pairs={{0,12},{4,0},{8,4},{12,8},{64,68},{68,72},{72,76},{76,64},{1,13},{... | collective-permute-start | bytes 2752520 | tf_op jit(solution)/shard_map/ppermute | solution.py:24
  117.7 5.4 %copy-start.2 = (bf16[448,1024]{1,0:T(8,128)(2,1)}, bf16[448,1024]{1,0:T(8,128)(2,1)S(1)}, u32[]{:S(2)}) copy-start(bf16[448,1024]{1,0:T(8,128)(2,1)S(1)} %collective-permute-done.10.refs_0_.refs_2_) | copy-start | bytes 2752516
  117.8 21.0 %collective-permute-start.12 = (bf16[448,1024]{1,0:T(8,128)(2,1)S(1)}, bf16[448,1024]{1,0:T(8,128)(2,1)S(1)}, u32[]{:S(2)}, u32[]{:S(2)}) collective-permute-start(bf16[448,1024]{1,0:T(8,128)(2,1)S(1)} %collective-permute-done.10.refs_0_.refs_2_), channel_id=1, source_target_pairs={{0,4},{4,8},{8,12},{12,0},{64,76},{68,64},{72,68},{76,72},{1,5},{5... | collective-permute-start | bytes 2752520 | tf_op jit(solution)/shard_map/ppermute | solution.py:24
  138.8 0.9 copy-start
  138.8 1.3 copy-start.1
  157.2 16.8 %all-to-all-start.4 = ((bf16[4,64,1792]{2,1,0:T(8,128)(2,1)}), bf16[4,64,1792]{2,1,0:T(8,128)(2,1)S(1)}, u32[]{:S(2)}, u32[]{:S(2)}) async-start(bf16[4,64,1792]{2,1,0:T(8,128)(2,1)} %get-tuple-element.15), calls=%async_computation.4 | async-start | bytes 1835008 | tf_op jit(solution)/shard_map/all_to_all | solution.py:30
  160.7 12.0 %copy-start.17 = (s32[8,2]{0,1:T(2,128)S(1)}, s32[8,2]{0,1:T(2,128)}, u32[]{:S(2)}) copy-start(s32[8,2]{0,1:T(2,128)} %param.6) | copy-start | bytes 196
  160.7 12.0 %copy-start.18 = (f32[8,2]{0,1:T(2,128)S(1)}, f32[8,2]{0,1:T(2,128)}, u32[]{:S(2)}) copy-start(f32[8,2]{0,1:T(2,128)} %param.7) | copy-start | bytes 196
  164.1 21.1 %collective-permute-start.13 = (bf16[128,1024]{1,0:T(8,128)(2,1)}, bf16[128,1024]{1,0:T(8,128)(2,1)S(1)}, u32[]{:S(2)}, u32[]{:S(2)}) collective-permute-start(bf16[128,1024]{1,0:T(8,128)(2,1)} %shard_map.63), channel_id=1, source_target_pairs={{0,1},{1,2},{2,3},{3,0},{64,67},{65,64},{66,65},{67,66},{4,5},{5,6... | collective-permute-start | bytes 786440 | tf_op jit(solution)/shard_map/ppermute | solution.py:24
  174.0 3.5 %copy-start.4 = (bf16[4,64,1792]{2,1,0:T(8,128)(2,1)}, bf16[4,64,1792]{2,1,0:T(8,128)(2,1)S(1)}, u32[]{:S(2)}) copy-start(bf16[4,64,1792]{2,1,0:T(8,128)(2,1)S(1)} %all-to-all-done.4.refs_0_) | copy-start | bytes 2752516
  174.0 20.5 %all-to-all-start.3 = ((bf16[4,32,1792]{2,1,0:T(8,128)(2,1)}), bf16[4,32,1792]{2,1,0:T(8,128)(2,1)S(1)}, u32[]{:S(2)}, u32[]{:S(2)}) async-start(bf16[4,32,1792]{2,1,0:T(8,128)(2,1)} %get-tuple-element.14), calls=%async_computation.3 | async-start | bytes 917504 | tf_op jit(solution)/shard_map/all_to_all | solution.py:30
  177.5 16.4 %copy-start.14 = (pred[8]{0:T(512)(128)(4,1)S(1)}, pred[8]{0:T(512)(128)(4,1)}, u32[]{:S(2)}) copy-start(pred[8]{0:T(512)(128)(4,1)} %copy-done.13) | copy-start | bytes 28
  177.5 16.4 %copy-start.16 = (pred[8]{0:T(512)(128)(4,1)S(1)}, pred[8]{0:T(512)(128)(4,1)}, u32[]{:S(2)}) copy-start(pred[8]{0:T(512)(128)(4,1)} %copy-done.15) | copy-start | bytes 28
  181.6 17.4 %collective-permute-start.15 = (bf16[128,1024]{1,0:T(8,128)(2,1)}, bf16[128,1024]{1,0:T(8,128)(2,1)S(1)}, u32[]{:S(2)}, u32[]{:S(2)}) collective-permute-start(bf16[128,1024]{1,0:T(8,128)(2,1)} %get-tuple-element.18), channel_id=1, source_target_pairs={{0,3},{1,0},{2,1},{3,2},{64,65},{65,66},{66,67},{67,64},{4,7},{5,4... | collective-permute-start | bytes 786440 | tf_op jit(solution)/shard_map/ppermute | solution.py:24
  186.4 25.8 %collective-permute-start.14 = (bf16[128,1024]{1,0:T(8,128)(2,1)S(1)}, bf16[128,1024]{1,0:T(8,128)(2,1)S(1)}, u32[]{:S(2)}, u32[]{:S(2)}) collective-permute-start(bf16[128,1024]{1,0:T(8,128)(2,1)S(1)} %add_convert_fusion.2), channel_id=1, source_target_pairs={{0,1},{1,2},{2,3},{3,0},{64,67},{65,64},{66,65},{67,66},{4,5},{5,6... | collective-permute-start | bytes 786440 | tf_op jit(solution)/shard_map/ppermute | solution.py:24
  194.5 0.8 copy-start.6
  214.7 4.2 %collective-permute-start.16 = (bf16[4,64,1024]{2,1,0:T(8,128)(2,1)S(1)}, bf16[4,64,1024]{2,1,0:T(8,128)(2,1)S(1)}, u32[]{:S(2)}, u32[]{:S(2)}) collective-permute-start(bf16[4,64,1024]{2,1,0:T(8,128)(2,1)S(1)} %add_convert_fusion.1), channel_id=1, source_target_pairs={{0,64},{64,0},{1,65},{65,1},{2,66},{66,2},{3,67},{67,3},{4,68},{68... | collective-permute-start | bytes 1572872 | tf_op jit(solution)/shard_map/ppermute | solution.py:19

commit v9 on v8

--- a/solution.py
+++ b/solution.py
@@ -8,6 +8,7 @@
 wide = jnp.float32
 half = jnp.bfloat16
 LIMIT = 60 * 2**20
+SOME = pl.CostEstimate(flops=10 * 10**9, bytes_accessed=1024, transcendentals=0)
 LONG = pl.CostEstimate(flops=10**11, bytes_accessed=1024, transcendentals=0)
 COST = pl.CostEstimate(flops=1024, bytes_accessed=1024, transcendentals=0)
 ANY = pl.BlockSpec(memory_space=pl.ANY)
@@ -31,6 +32,20 @@
 
 
 DIMS = (((1,), (1,)), ((), ()))
+
+
+def hold(a, after, cost):
+    def kernel(a_ref, *refs):
+        refs[-1][...] = a_ref[...]
+
+    return pl.pallas_call(
+        kernel,
+        in_specs=[WHOLE] + [ANY] * len(after),
+        out_specs=WHOLE,
+        out_shape=jax.ShapeDtypeStruct(a.shape, a.dtype),
+        compiler_params=pltpu.CompilerParams(vmem_limit_bytes=LIMIT),
+        cost_estimate=cost,
+    )(a, *after)
 
 
 def fetch(refs, held, sems):
@@ -75,7 +90,7 @@
             pltpu.SemaphoreType.DMA((4,)),
         ],
         compiler_params=pltpu.CompilerParams(vmem_limit_bytes=LIMIT),
-        cost_estimate=LONG,
+        cost_estimate=LONG if spare else SOME,
     )(*pieces, *weights, *after)
 
 
@@ -110,7 +125,7 @@
             pltpu.SemaphoreType.DMA((4,)),
         ],
         compiler_params=pltpu.CompilerParams(vmem_limit_bytes=LIMIT),
-        cost_estimate=COST,
+        cost_estimate=LONG,
     )(*pieces, *weights, *after)
 
 
@@ -200,7 +215,6 @@
     mine = [tokens[0]] + [shift(tokens[0], "zlo", d) for d in (1, 2, 3)]
     w_own, v_own = jnp.transpose(w_in[0], (1, 2, 0)).reshape(896, 1024), w_down[0]
     w_first, w_second = pass_on(w_own, "y", 1), pass_on(w_own, "y", -1)
-    v_first, v_second = pass_on(v_own, "y", 1), pass_on(v_own, "y", -1)
     weights = [w_own, w_first, w_second]
 
     matches = routes[:, :, None] == jnp.arange(8, dtype=jnp.int32)[None, None, :]
@@ -241,7 +255,9 @@
     w_far = pass_on(w_next, "y", 1)
 
     (part,) = early([first, second], weights, False, [own_part])
-    far = pass_on(first, "zhi", 1)
+    far = pass_on(hold(first, [own_part], SOME), "zhi", 1)
+    v_held = hold(v_own, [own_sums], COST)
+    v_first, v_second = pass_on(v_held, "y", 1), pass_on(v_held, "y", -1)
     v_far = pass_on(v_first, "y", 1)
     v_all = [v_own, v_first, v_second, v_far]
     own_h, near_h = activate_early(own_sums, []), activate_early(swap(part, "x"), [v_first])

time: 238 us -> 233 us (0.979)
  waiting for transfers between devices: 46.9 us -> 32.1 us
  blocking collectives: 30.5 us -> 35.5 us
  Pallas kernels: 36.8 us -> 40.6 us
    ppermute x12, waiting for transfers between devices: 43.5 us -> 27.1 us  [pass_on(): lax.ppermute(a, ('core', axis), [(c * n + i, c * n + (i + by * (1 - 2 * c...]
    ppermute x12, starting transfers between devices: 61.2 us -> 55.3 us  [pass_on(): lax.ppermute(a, ('core', axis), [(c * n + i, c * n + (i + by * (1 - 2 * c...]
    ppermute x5, starting transfers between devices: 18.7 us -> 23.7 us  [shift(): return lax.ppermute(a, axis, [(i, (i + by) % n) for i in range(n)])]
    all_to_all x2, blocking collectives: 30.5 us -> 35.5 us  [swap(): return lax.all_to_all(a, axis, split_axis=0, concat_axis=0, tiled=True)]
    pallas_call x0 -> x2, Pallas kernels: none -> 3.94 us  [hold(): pl.pallas_call(kernel, in_specs=[WHOLE] + [ANY] * len(after), out_specs=W...]
    unnamed x38 -> x34, local copies, waits for them, and re-layouts: 5.29 us -> 4.95 us
  transfers between devices with their start and end apart: 22 -> 22, of which waited for: 9 -> 9; matrix products, arithmetic and copies ran while one was open for 4% -> 4% of each run, Pallas kernels for 14% -> 16%
where the time goes in v9:
time: 233 us; the launch traced here: 230 us
  starting transfers between devices  98.8 us (42%)
  Pallas kernels  40.6 us (17%)
  blocking collectives  35.5 us (15%)
  waiting for transfers between devices  32.1 us (14%)
  other arithmetic  12.5 us (5%)
  between operations  5.42 us (2%)
  local copies, waits for them, and re-layouts  5.13 us (2%)
    ppermute x12, starting transfers between devices, pass_on(): lax.ppermute(a, ('core', axis), [(c * n + i, c * n + (i + by * (1 - 2 * c...  55.3 us
    all_to_all x2, blocking collectives, swap(): return lax.all_to_all(a, axis, split_axis=0, concat_axis=0, tiled=True)  35.5 us
    ppermute x12, waiting for transfers between devices, pass_on(): lax.ppermute(a, ('core', axis), [(c * n + i, c * n + (i + by * (1 - 2 * c...  27.1 us
    ppermute x5, starting transfers between devices, shift(): return lax.ppermute(a, axis, [(i, (i + by) % n) for i in range(n)])  23.7 us
    all_to_all x5, starting transfers between devices, swap(): return lax.all_to_all(a, axis, split_axis=0, concat_axis=0, tiled=True)  19.7 us
    pallas_call x2, Pallas kernels, early(): pl.pallas_call(kernel, in_specs=[WHOLE] * n + [ANY] * (3 + len(after)), o...  11.1 us
    pallas_call x3, Pallas kernels, down(): pl.pallas_call(kernel, grid=(2,), in_specs=[pl.BlockSpec((4, 32 * n, 1792...  10.9 us
    pallas_call x1, Pallas kernels, late(): pl.pallas_call(kernel, in_specs=[WHOLE] * 4 + [ANY] * (4 + len(after)), o...  7.28 us
  transfers between devices with their start and end apart: 22, of which 9 were waited for; matrix products, arithmetic and copies ran while one was open for 4% of the time, Pallas kernels for 16%

profile of v9, /device:TPU:1, one launch (start us, length us, event | category | flops | bytes accessed | tf_op | source)
XLA Modules:
  0.0 230.1 jit_solution(5929129430449257209)
XLA Ops:
  0.0 5.5 %collective-permute-start.5 = (bf16[896,1024]{1,0:T(8,128)(2,1)}, bf16[896,1024]{1,0:T(8,128)(2,1)}, u32[]{:S(2)}, u32[]{:S(2)}) collective-permute-start(bf16[896,1024]{1,0:T(8,128)(2,1)} %bitcast.19), channel_id=1, source_target_pairs={{0,4},{4,8},{8,12},{12,0},{64,76},{68,64},{72,68},{76,72},{1,5},{5... | collective-permute-start | bytes 5505032 | tf_op jit(solution)/shard_map/ppermute | solution.py:25
  5.5 1.9 collective-permute-start.6
  7.4 4.9 %collective-permute-start.1 = (bf16[64,1024]{1,0:T(8,128)(2,1)}, bf16[64,1024]{1,0:T(8,128)(2,1)S(1)}, u32[]{:S(2)}, u32[]{:S(2)}) collective-permute-start(bf16[64,1024]{1,0:T(8,128)(2,1)} %bitcast.16), channel_id=1, source_target_pairs={{0,256},{128,384},{256,0},{384,128},{1,257},{129,385},{257,1},{385... | collective-permute-start | bytes 393224 | tf_op jit(solution)/shard_map/ppermute | solution.py:20
  12.3 3.3 %collective-permute-start.2 = (bf16[64,1024]{1,0:T(8,128)(2,1)}, bf16[64,1024]{1,0:T(8,128)(2,1)S(1)}, u32[]{:S(2)}, u32[]{:S(2)}) collective-permute-start(bf16[64,1024]{1,0:T(8,128)(2,1)} %bitcast.17), channel_id=1, source_target_pairs={{0,384},{128,0},{256,128},{384,256},{1,385},{129,1},{257,129},{385... | collective-permute-start | bytes 393224 | tf_op jit(solution)/shard_map/ppermute | solution.py:20
  15.6 2.2 collective-permute-start
  21.6 2.0 collective-permute-done
  23.6 0.9 select_select_fusion.1
  24.6 5.5 %collective-permute-start.3 = (bf16[128,1024]{1,0:T(8,128)(2,1)S(1)}, bf16[128,1024]{1,0:T(8,128)(2,1)S(1)}, u32[]{:S(2)}, u32[]{:S(2)}) collective-permute-start(bf16[128,1024]{1,0:T(8,128)(2,1)S(1)} %pad_maximum_fusion), channel_id=1, source_target_pairs={{0,64},{64,0},{1,65},{65,1},{2,66},{66,2},{3,67},{67,3},{4,68},{68... | collective-permute-start | bytes 786440 | tf_op jit(solution)/shard_map/ppermute | solution.py:20
  32.6 0.9 slice_select_fusion.1
  33.6 10.0 %collective-permute-start.4 = (bf16[128,1024]{1,0:T(8,128)(2,1)S(1)}, bf16[128,1024]{1,0:T(8,128)(2,1)S(1)}, u32[]{:S(2)}, u32[]{:S(2)}) collective-permute-start(bf16[128,1024]{1,0:T(8,128)(2,1)S(1)} %pad_maximum_fusion.1.refs_0_.refs_3_), channel_id=1, source_target_pairs={{0,1},{1,2},{2,3},{3,0},{64,67},{65,64},{66,65},{67,66},{4,5},{5,6... | collective-permute-start | bytes 786440 | tf_op jit(solution)/shard_map/ppermute | solution.py:25
  43.6 1.9 collective-permute-start.8
  45.5 3.5 %collective-permute-done.6.refs_3_.refs_6_.refs_4_ = bf16[896,1024]{1,0:T(8,128)(2,1)} collective-permute-done((bf16[896,1024]{1,0:T(8,128)(2,1)}, bf16[896,1024]{1,0:T(8,128)(2,1)}, u32[]{:S(2)}, u32[]{:S(2)}) %collective-permute-start.6) | collective-permute-done | bytes 1835040 | tf_op jit(solution)/shard_map/ppermute | solution.py:25
  49.0 5.5 %shard_map.55 = (bf16[896,1024]{1,0:T(8,128)(2,1)}, bf16[4,32,2688]{2,1,0:T(8,128)(2,1)}) custom-call(bf16[128,1024]{1,0:T(8,128)(2,1)} %copy-done.7, bf16[896,1024]{1,0:T(8,128)(2,1)} %bitcast.21, bf16[896,1024]{1,0:T(8,128)(2,1)} %collective-permute-done.5.refs_2_.refs_5_.refs_3_, bf16[896,1024]{1,0:T(8,128)(2,1)} %collective-permute-done.6.refs_3_.refs_6_.refs_4_), custom_call_target="tpu_custom_call" | custom-call | flops 99999997952 | bytes 1024 | tf_op jit(solution)/shard_map/pallas_call | solution.py:81
  54.5 1.9 collective-permute-start.9
  56.4 3.9 %all-to-all-start.2 = ((bf16[4,32,2688]{2,1,0:T(8,128)(2,1)}), bf16[4,32,2688]{2,1,0:T(8,128)(2,1)S(1)}, u32[]{:S(2)}, u32[]{:S(2)}) async-start(bf16[4,32,2688]{2,1,0:T(8,128)(2,1)} %get-tuple-element.12.refs_0_.refs_5_), calls=%async_computation.2 | async-start | bytes 1376256 | tf_op jit(solution)/shard_map/all_to_all | solution.py:31
  60.3 1.7 collective-permute-done.4.a_ref.refs_1_.refs_0_
  62.7 1.7 shard_map.56
  64.4 10.8 %collective-permute-start.7 = (bf16[128,1024]{1,0:T(8,128)(2,1)}, bf16[128,1024]{1,0:T(8,128)(2,1)S(1)}, u32[]{:S(2)}, u32[]{:S(2)}) collective-permute-start(bf16[128,1024]{1,0:T(8,128)(2,1)} %shard_map.56), channel_id=1, source_target_pairs={{0,1},{1,2},{2,3},{3,0},{64,67},{65,64},{66,65},{67,66},{4,5},{5,6... | collective-permute-start | bytes 786440 | tf_op jit(solution)/shard_map/ppermute | solution.py:25
  75.9 5.7 %shard_map.58 = bf16[4,64,2688]{2,1,0:T(8,128)(2,1)} custom-call(bf16[128,1024]{1,0:T(8,128)(2,1)} %copy-done.14, bf16[128,1024]{1,0:T(8,128)(2,1)} %copy-done.15, bf16[896,1024]{1,0:T(8,128)(2,1)} %bitcast.22, bf16[896,1024]{1,0:T(8,128)(2,1)} %collective-permute-done.5.refs_2_.refs_5_.refs_3_, ...), custom_call_target="tpu_custom_call" | custom-call | flops 10000000000 | bytes 1024 | tf_op jit(solution)/shard_map/pallas_call | solution.py:81
  81.6 4.2 %all-to-all-start.1 = ((bf16[4,64,2688]{2,1,0:T(8,128)(2,1)}), bf16[4,64,2688]{2,1,0:T(8,128)(2,1)S(1)}, u32[]{:S(2)}, u32[]{:S(2)}) async-start(bf16[4,64,2688]{2,1,0:T(8,128)(2,1)} %shard_map.58), calls=%async_computation.1 | async-start | bytes 2752512 | tf_op jit(solution)/shard_map/all_to_all | solution.py:31
  85.9 2.2 shard_map.59
  88.1 2.2 collective-permute-start.10
  91.1 7.3 %shard_map.57 = bf16[4,32,6272]{2,1,0:T(8,128)(2,1)} custom-call(bf16[128,1024]{1,0:T(8,128)(2,1)} %copy-done.16, bf16[128,1024]{1,0:T(8,128)(2,1)} %copy-done.14, bf16[128,1024]{1,0:T(8,128)(2,1)} %copy-done.15, bf16[128,1024]{1,0:T(8,128)(2,1)} %copy-done.7, bf16[896,1024]{1,0:T(8,128)(2,1)} %bitcast.23, ...), custom_call_target="tpu_custom_call" | custom-call | flops 99999997952 | bytes 1024 | tf_op jit(solution)/shard_map/pallas_call | solution.py:116
  98.4 2.4 %all-to-all-done.1.sums_ref = bf16[4,64,2688]{2,1,0:T(8,128)(2,1)S(1)} async-done(((bf16[4,64,2688]{2,1,0:T(8,128)(2,1)}), bf16[4,64,2688]{2,1,0:T(8,128)(2,1)S(1)}, u32[]{:S(2)}, u32[]{:S(2)}) %all-to-all-start.1) | async-done | bytes 1376288 | tf_op jit(solution)/shard_map/all_to_all | solution.py:31
  100.8 1.1 copy-done.4
  101.8 4.3 %all-to-all-start = ((bf16[4,32,6272]{2,1,0:T(8,128)(2,1)}), bf16[4,32,6272]{2,1,0:T(8,128)(2,1)}, u32[]{:S(2)}, u32[]{:S(2)}) async-start(bf16[4,32,6272]{2,1,0:T(8,128)(2,1)} %shard_map.57), calls=%async_computation | async-start | bytes 3211264 | tf_op jit(solution)/shard_map/all_to_all | solution.py:31
  106.2 3.4 %collective-permute-start.11 = (bf16[448,1024]{1,0:T(8,128)(2,1)}, bf16[448,1024]{1,0:T(8,128)(2,1)S(1)}, u32[]{:S(2)}, u32[]{:S(2)}) collective-permute-start(bf16[448,1024]{1,0:T(8,128)(2,1)} %shard_map.59), channel_id=1, source_target_pairs={{0,12},{4,0},{8,4},{12,8},{64,68},{68,72},{72,76},{76,64},{1,13},{... | collective-permute-start | bytes 2752520 | tf_op jit(solution)/shard_map/ppermute | solution.py:25
  109.6 3.1 %collective-permute-start.12 = (bf16[448,1024]{1,0:T(8,128)(2,1)S(1)}, bf16[448,1024]{1,0:T(8,128)(2,1)S(1)}, u32[]{:S(2)}, u32[]{:S(2)}) collective-permute-start(bf16[448,1024]{1,0:T(8,128)(2,1)S(1)} %collective-permute-done.10.refs_0_.refs_2_), channel_id=1, source_target_pairs={{0,4},{4,8},{8,12},{12,0},{64,76},{68,64},{72,68},{76,72},{1,5},{5... | collective-permute-start | bytes 2752520 | tf_op jit(solution)/shard_map/ppermute | solution.py:25
  112.7 1.9 shard_map.61.own_ref
  114.6 2.3 %shard_map.60.near_ref = bf16[64,1344]{1,0:T(8,128)(2,1)} custom-call(bf16[4,64,2688]{2,1,0:T(8,128)(2,1)} %copy-done.4, bf16[448,1024]{1,0:T(8,128)(2,1)} %copy-done.2), custom_call_target="tpu_custom_call" | custom-call | flops 1024 | bytes 1024 | tf_op jit(solution)/shard_map/pallas_call | solution.py:149
  116.9 11.2 %collective-permute-done.11.refs_0_.refs_3_ = bf16[448,1024]{1,0:T(8,128)(2,1)S(1)} collective-permute-done((bf16[448,1024]{1,0:T(8,128)(2,1)}, bf16[448,1024]{1,0:T(8,128)(2,1)S(1)}, u32[]{:S(2)}, u32[]{:S(2)}) %collective-permute-start.11) | collective-permute-done | bytes 917536 | tf_op jit(solution)/shard_map/ppermute | solution.py:25
  128.2 1.9 collective-permute-done.12.refs_1_.refs_4_
  131.0 3.2 %shard_map.62 = (bf16[4,32,1792]{2,1,0:T(8,128)(2,1)}, bf16[4,64,1792]{2,1,0:T(8,128)(2,1)}, bf16[4,32,1792]{2,1,0:T(8,128)(2,1)}) custom-call(bf16[4,32,6272]{2,1,0:T(8,128)(2,1)} %all-to-all-done.sums_ref, bf16[64,1344]{1,0:T(8,128)(2,1)} %shard_map.60.near_ref, bf16[32,1344]{1,0:T(8,128)(2,1)} %shard_map.61.own_ref, bf16[448,1024]{1,0:T(8,128)(2,1)} %copy-done, ...), custom_call_target="tpu_custom_call" | custom-call | flops 1024 | bytes 1024 | tf_op jit(solution)/shard_map/pallas_call | solution.py:172
  134.2 11.2 %all_to_all.35.refs_0_ = bf16[4,32,1792]{2,1,0:T(8,128)(2,1)} all-to-all(bf16[4,32,1792]{2,1,0:T(8,128)(2,1)} %get-tuple-element.17), channel_id=1, replica_groups=mesh['zlo'=4,'core'=2,'x'=4,'y'=4,'zhi'=4] {'x'}, dimensions={0} | all-to-all | bytes 917504 | tf_op jit(solution)/shard_map/all_to_all | solution.py:31
  145.3 3.5 %all-to-all-start.4 = ((bf16[4,64,1792]{2,1,0:T(8,128)(2,1)}), bf16[4,64,1792]{2,1,0:T(8,128)(2,1)S(1)}, u32[]{:S(2)}, u32[]{:S(2)}) async-start(bf16[4,64,1792]{2,1,0:T(8,128)(2,1)} %get-tuple-element.15), calls=%async_computation.4 | async-start | bytes 1835008 | tf_op jit(solution)/shard_map/all_to_all | solution.py:31
  148.9 3.4 %shard_map.65 = bf16[128,1024]{1,0:T(8,128)(2,1)} custom-call(bf16[4,32,1792]{2,1,0:T(8,128)(2,1)} %all_to_all.35.refs_0_, bf16[448,1024]{1,0:T(8,128)(2,1)} %bitcast.13, bf16[448,1024]{1,0:T(8,128)(2,1)} %copy-done.2, bf16[448,1024]{1,0:T(8,128)(2,1)} %copy-done, bf16[448,1024]{1,0:T(8,128)(2,1)} %copy-done.1), custom_call_target="tpu_custom_call" | custom-call | flops 1024 | bytes 1024 | tf_op jit(solution)/shard_map/pallas_call | solution.py:198
  152.2 5.4 %collective-permute-start.13 = (bf16[128,1024]{1,0:T(8,128)(2,1)}, bf16[128,1024]{1,0:T(8,128)(2,1)S(1)}, u32[]{:S(2)}, u32[]{:S(2)}) collective-permute-start(bf16[128,1024]{1,0:T(8,128)(2,1)} %shard_map.65), channel_id=1, source_target_pairs={{0,1},{1,2},{2,3},{3,0},{64,67},{65,64},{66,65},{67,66},{4,5},{5,6... | collective-permute-start | bytes 786440 | tf_op jit(solution)/shard_map/ppermute | solution.py:25
  158.8 3.7 %all-to-all-start.3 = ((bf16[4,32,1792]{2,1,0:T(8,128)(2,1)}), bf16[4,32,1792]{2,1,0:T(8,128)(2,1)S(1)}, u32[]{:S(2)}, u32[]{:S(2)}) async-start(bf16[4,32,1792]{2,1,0:T(8,128)(2,1)} %get-tuple-element.14), calls=%async_computation.3 | async-start | bytes 917504 | tf_op jit(solution)/shard_map/all_to_all | solution.py:31
  162.6 4.1 %shard_map.64 = (bf16[128,1024]{1,0:T(8,128)(2,1)}, f32[128,1024]{1,0:T(8,128)}) custom-call(bf16[4,64,1792]{2,1,0:T(8,128)(2,1)} %copy-done.5, bf16[448,1024]{1,0:T(8,128)(2,1)} %bitcast.14, bf16[448,1024]{1,0:T(8,128)(2,1)} %copy-done.2, bf16[448,1024]{1,0:T(8,128)(2,1)} %copy-done, bf16[448,1024]{1,0:T(8,128)(2,1)} %copy-done.1), custom_call_target="tpu_custom_call" | custom-call | flops 1024 | bytes 1024 | tf_op jit(solution)/shard_map/pallas_call | solution.py:198
  166.7 3.8 %collective-permute-start.15 = (bf16[128,1024]{1,0:T(8,128)(2,1)}, bf16[128,1024]{1,0:T(8,128)(2,1)S(1)}, u32[]{:S(2)}, u32[]{:S(2)}) collective-permute-start(bf16[128,1024]{1,0:T(8,128)(2,1)} %get-tuple-element.18), channel_id=1, source_target_pairs={{0,3},{1,0},{2,1},{3,2},{64,65},{65,66},{66,67},{67,64},{4,7},{5,4... | collective-permute-start | bytes 786440 | tf_op jit(solution)/shard_map/ppermute | solution.py:25
  170.5 1.1 add_convert_fusion.2
  171.6 5.4 %collective-permute-start.14 = (bf16[128,1024]{1,0:T(8,128)(2,1)S(1)}, bf16[128,1024]{1,0:T(8,128)(2,1)S(1)}, u32[]{:S(2)}, u32[]{:S(2)}) collective-permute-start(bf16[128,1024]{1,0:T(8,128)(2,1)S(1)} %add_convert_fusion.2), channel_id=1, source_target_pairs={{0,1},{1,2},{2,3},{3,0},{64,67},{65,64},{66,65},{67,66},{4,5},{5,6... | collective-permute-start | bytes 786440 | tf_op jit(solution)/shard_map/ppermute | solution.py:25
  180.5 3.4 %shard_map.63 = f32[128,1024]{1,0:T(8,128)} custom-call(bf16[4,32,1792]{2,1,0:T(8,128)(2,1)} %copy-done.6, bf16[448,1024]{1,0:T(8,128)(2,1)} %bitcast.15, bf16[448,1024]{1,0:T(8,128)(2,1)} %copy-done.2, bf16[448,1024]{1,0:T(8,128)(2,1)} %copy-done, bf16[448,1024]{1,0:T(8,128)(2,1)} %copy-done.1), custom_call_target="tpu_custom_call" | custom-call | flops 1024 | bytes 1024 | tf_op jit(solution)/shard_map/pallas_call | solution.py:198
  183.9 8.8 %collective-permute-done.14 = bf16[128,1024]{1,0:T(8,128)(2,1)S(1)} collective-permute-done((bf16[128,1024]{1,0:T(8,128)(2,1)S(1)}, bf16[128,1024]{1,0:T(8,128)(2,1)S(1)}, u32[]{:S(2)}, u32[]{:S(2)}) %collective-permute-start.14) | collective-permute-done | bytes 262176 | tf_op jit(solution)/shard_map/ppermute | solution.py:25
  192.7 1.1 convert_add_fusion
  193.8 1.4 slice_multiply_fusion.1
  195.4 7.8 %collective-permute-start.16 = (bf16[4,64,1024]{2,1,0:T(8,128)(2,1)S(1)}, bf16[4,64,1024]{2,1,0:T(8,128)(2,1)S(1)}, u32[]{:S(2)}, u32[]{:S(2)}) collective-permute-start(bf16[4,64,1024]{2,1,0:T(8,128)(2,1)S(1)} %add_convert_fusion.1), channel_id=1, source_target_pairs={{0,64},{64,0},{1,65},{65,1},{2,66},{66,2},{3,67},{67,3},{4,68},{68... | collective-permute-start | bytes 1572872 | tf_op jit(solution)/shard_map/ppermute | solution.py:20
  205.0 24.3 %all_to_all.36 = bf16[4,64,1024]{2,1,0:T(8,128)(2,1)S(1)} all-to-all(bf16[4,64,1024]{2,1,0:T(8,128)(2,1)S(1)} %add_convert_fusion), channel_id=1, replica_groups=mesh['zlo'=4,'core'=2,'x'=4,'y'=4,'zhi'=4] {'zlo'}, dimensions={0} | all-to-all | bytes 1048576 | tf_op jit(solution)/shard_map/all_to_all | solution.py:31
  (67 shorter events, 11.8 us)
Async XLA Ops:
  0.0 45.5 %collective-permute-start.5 = (bf16[896,1024]{1,0:T(8,128)(2,1)}, bf16[896,1024]{1,0:T(8,128)(2,1)}, u32[]{:S(2)}, u32[]{:S(2)}) collective-permute-start(bf16[896,1024]{1,0:T(8,128)(2,1)} %bitcast.19), channel_id=1, source_target_pairs={{0,4},{4,8},{8,12},{12,0},{64,76},{68,64},{72,68},{76,72},{1,5},{5... | collective-permute-start | bytes 5505032 | tf_op jit(solution)/shard_map/ppermute | solution.py:25
  5.5 43.5 %collective-permute-start.6 = (bf16[896,1024]{1,0:T(8,128)(2,1)}, bf16[896,1024]{1,0:T(8,128)(2,1)}, u32[]{:S(2)}, u32[]{:S(2)}) collective-permute-start(bf16[896,1024]{1,0:T(8,128)(2,1)} %bitcast.20), channel_id=1, source_target_pairs={{0,12},{4,0},{8,4},{12,8},{64,68},{68,72},{72,76},{76,64},{1,13},{... | collective-permute-start | bytes 5505032 | tf_op jit(solution)/shard_map/ppermute | solution.py:25
  7.4 14.2 %collective-permute-start.1 = (bf16[64,1024]{1,0:T(8,128)(2,1)}, bf16[64,1024]{1,0:T(8,128)(2,1)S(1)}, u32[]{:S(2)}, u32[]{:S(2)}) collective-permute-start(bf16[64,1024]{1,0:T(8,128)(2,1)} %bitcast.16), channel_id=1, source_target_pairs={{0,256},{128,384},{256,0},{384,128},{1,257},{129,385},{257,1},{385... | collective-permute-start | bytes 393224 | tf_op jit(solution)/shard_map/ppermute | solution.py:20
  12.3 9.3 %collective-permute-start.2 = (bf16[64,1024]{1,0:T(8,128)(2,1)}, bf16[64,1024]{1,0:T(8,128)(2,1)S(1)}, u32[]{:S(2)}, u32[]{:S(2)}) collective-permute-start(bf16[64,1024]{1,0:T(8,128)(2,1)} %bitcast.17), channel_id=1, source_target_pairs={{0,384},{128,0},{256,128},{384,256},{1,385},{129,1},{257,129},{385... | collective-permute-start | bytes 393224 | tf_op jit(solution)/shard_map/ppermute | solution.py:20
  15.6 8.0 %collective-permute-start = (bf16[64,1024]{1,0:T(8,128)(2,1)}, bf16[64,1024]{1,0:T(8,128)(2,1)S(1)}, u32[]{:S(2)}, u32[]{:S(2)}) collective-permute-start(bf16[64,1024]{1,0:T(8,128)(2,1)} %bitcast.18), channel_id=1, source_target_pairs={{0,128},{128,256},{256,384},{384,0},{1,129},{129,257},{257,385},{3... | collective-permute-start | bytes 393224 | tf_op jit(solution)/shard_map/ppermute | solution.py:20
  18.9 5.6 %copy-start.8 = (pred[8]{0:T(512)(128)(4,1)}, pred[8]{0:T(512)(128)(4,1)S(1)}, u32[]{:S(2)}) copy-start(pred[8]{0:T(512)(128)(4,1)S(1)} %get-tuple-element.19) | copy-start | bytes 28
  18.9 5.6 %copy-start.10 = (pred[8]{0:T(512)(128)(4,1)}, pred[8]{0:T(512)(128)(4,1)S(1)}, u32[]{:S(2)}) copy-start(pred[8]{0:T(512)(128)(4,1)S(1)} %get-tuple-element.20) | copy-start | bytes 28
  24.6 8.0 %collective-permute-start.3 = (bf16[128,1024]{1,0:T(8,128)(2,1)S(1)}, bf16[128,1024]{1,0:T(8,128)(2,1)S(1)}, u32[]{:S(2)}, u32[]{:S(2)}) collective-permute-start(bf16[128,1024]{1,0:T(8,128)(2,1)S(1)} %pad_maximum_fusion), channel_id=1, source_target_pairs={{0,64},{64,0},{1,65},{65,1},{2,66},{66,2},{3,67},{67,3},{4,68},{68... | collective-permute-start | bytes 786440 | tf_op jit(solution)/shard_map/ppermute | solution.py:20
  33.6 15.4 %copy-start.7 = (bf16[128,1024]{1,0:T(8,128)(2,1)}, bf16[128,1024]{1,0:T(8,128)(2,1)S(1)}, u32[]{:S(2)}) copy-start(bf16[128,1024]{1,0:T(8,128)(2,1)S(1)} %pad_maximum_fusion.1.refs_0_.refs_3_) | copy-start | bytes 786436
  33.6 28.5 %collective-permute-start.4 = (bf16[128,1024]{1,0:T(8,128)(2,1)S(1)}, bf16[128,1024]{1,0:T(8,128)(2,1)S(1)}, u32[]{:S(2)}, u32[]{:S(2)}) collective-permute-start(bf16[128,1024]{1,0:T(8,128)(2,1)S(1)} %pad_maximum_fusion.1.refs_0_.refs_3_), channel_id=1, source_target_pairs={{0,1},{1,2},{2,3},{3,0},{64,67},{65,64},{66,65},{67,66},{4,5},{5,6... | collective-permute-start | bytes 786440 | tf_op jit(solution)/shard_map/ppermute | solution.py:25
  43.6 31.6 %collective-permute-start.8 = (bf16[128,1024]{1,0:T(8,128)(2,1)S(1)}, bf16[128,1024]{1,0:T(8,128)(2,1)S(1)}, u32[]{:S(2)}, u32[]{:S(2)}) collective-permute-start(bf16[128,1024]{1,0:T(8,128)(2,1)S(1)} %pad_maximum_fusion.1.refs_0_.refs_3_), channel_id=1, source_target_pairs={{0,3},{1,0},{2,1},{3,2},{64,65},{65,66},{66,67},{67,64},{4,7},{5,4... | collective-permute-start | bytes 786440 | tf_op jit(solution)/shard_map/ppermute | solution.py:25
  54.5 35.9 %collective-permute-start.9 = (bf16[896,1024]{1,0:T(8,128)(2,1)}, bf16[896,1024]{1,0:T(8,128)(2,1)}, u32[]{:S(2)}, u32[]{:S(2)}) collective-permute-start(bf16[896,1024]{1,0:T(8,128)(2,1)} %get-tuple-element.13), channel_id=1, source_target_pairs={{0,4},{4,8},{8,12},{12,0},{64,76},{68,64},{72,68},{76,72},{1,5},{5... | collective-permute-start | bytes 5505032 | tf_op jit(solution)/shard_map/ppermute | solution.py:25
  56.4 25.2 %all-to-all-start.2 = ((bf16[4,32,2688]{2,1,0:T(8,128)(2,1)}), bf16[4,32,2688]{2,1,0:T(8,128)(2,1)S(1)}, u32[]{:S(2)}, u32[]{:S(2)}) async-start(bf16[4,32,2688]{2,1,0:T(8,128)(2,1)} %get-tuple-element.12.refs_0_.refs_5_), calls=%async_computation.2 | async-start | bytes 1376256 | tf_op jit(solution)/shard_map/all_to_all | solution.py:31
  62.0 0.7 copy-start.14
  64.4 25.9 %collective-permute-start.7 = (bf16[128,1024]{1,0:T(8,128)(2,1)}, bf16[128,1024]{1,0:T(8,128)(2,1)S(1)}, u32[]{:S(2)}, u32[]{:S(2)}) collective-permute-start(bf16[128,1024]{1,0:T(8,128)(2,1)} %shard_map.56), channel_id=1, source_target_pairs={{0,1},{1,2},{2,3},{3,0},{64,67},{65,64},{66,65},{67,66},{4,5},{5,6... | collective-permute-start | bytes 786440 | tf_op jit(solution)/shard_map/ppermute | solution.py:25
  75.2 0.7 copy-start.15
  81.6 4.3 %copy-start.3 = (bf16[4,32,2688]{2,1,0:T(8,128)(2,1)}, bf16[4,32,2688]{2,1,0:T(8,128)(2,1)S(1)}, u32[]{:S(2)}) copy-start(bf16[4,32,2688]{2,1,0:T(8,128)(2,1)S(1)} %all-to-all-done.2.refs_0_.sums_ref) | copy-start | bytes 2064388
  81.6 19.2 %all-to-all-start.1 = ((bf16[4,64,2688]{2,1,0:T(8,128)(2,1)}), bf16[4,64,2688]{2,1,0:T(8,128)(2,1)S(1)}, u32[]{:S(2)}, u32[]{:S(2)}) async-start(bf16[4,64,2688]{2,1,0:T(8,128)(2,1)} %shard_map.58), calls=%async_computation.1 | async-start | bytes 2752512 | tf_op jit(solution)/shard_map/all_to_all | solution.py:31
  88.1 21.5 %collective-permute-start.10 = (bf16[448,1024]{1,0:T(8,128)(2,1)}, bf16[448,1024]{1,0:T(8,128)(2,1)S(1)}, u32[]{:S(2)}, u32[]{:S(2)}) collective-permute-start(bf16[448,1024]{1,0:T(8,128)(2,1)} %shard_map.59), channel_id=1, source_target_pairs={{0,4},{4,8},{8,12},{12,0},{64,76},{68,64},{72,68},{76,72},{1,5},{5... | collective-permute-start | bytes 2752520 | tf_op jit(solution)/shard_map/ppermute | solution.py:25
  90.4 0.7 copy-start.16
  100.8 1.1 copy-start.4
  101.8 28.2 %all-to-all-start = ((bf16[4,32,6272]{2,1,0:T(8,128)(2,1)}), bf16[4,32,6272]{2,1,0:T(8,128)(2,1)}, u32[]{:S(2)}, u32[]{:S(2)}) async-start(bf16[4,32,6272]{2,1,0:T(8,128)(2,1)} %shard_map.57), calls=%async_computation | async-start | bytes 3211264 | tf_op jit(solution)/shard_map/all_to_all | solution.py:31
  106.2 22.0 %collective-permute-start.11 = (bf16[448,1024]{1,0:T(8,128)(2,1)}, bf16[448,1024]{1,0:T(8,128)(2,1)S(1)}, u32[]{:S(2)}, u32[]{:S(2)}) collective-permute-start(bf16[448,1024]{1,0:T(8,128)(2,1)} %shard_map.59), channel_id=1, source_target_pairs={{0,12},{4,0},{8,4},{12,8},{64,68},{68,72},{72,76},{76,64},{1,13},{... | collective-permute-start | bytes 2752520 | tf_op jit(solution)/shard_map/ppermute | solution.py:25
  109.6 5.0 %copy-start.2 = (bf16[448,1024]{1,0:T(8,128)(2,1)}, bf16[448,1024]{1,0:T(8,128)(2,1)S(1)}, u32[]{:S(2)}) copy-start(bf16[448,1024]{1,0:T(8,128)(2,1)S(1)} %collective-permute-done.10.refs_0_.refs_2_) | copy-start | bytes 2752516
  109.6 20.4 %collective-permute-start.12 = (bf16[448,1024]{1,0:T(8,128)(2,1)S(1)}, bf16[448,1024]{1,0:T(8,128)(2,1)S(1)}, u32[]{:S(2)}, u32[]{:S(2)}) collective-permute-start(bf16[448,1024]{1,0:T(8,128)(2,1)S(1)} %collective-permute-done.10.refs_0_.refs_2_), channel_id=1, source_target_pairs={{0,4},{4,8},{8,12},{12,0},{64,76},{68,64},{72,68},{76,72},{1,5},{5... | collective-permute-start | bytes 2752520 | tf_op jit(solution)/shard_map/ppermute | solution.py:25
  128.2 1.9 copy-start
  130.0 0.9 copy-start.1
  145.3 13.5 %all-to-all-start.4 = ((bf16[4,64,1792]{2,1,0:T(8,128)(2,1)}), bf16[4,64,1792]{2,1,0:T(8,128)(2,1)S(1)}, u32[]{:S(2)}, u32[]{:S(2)}) async-start(bf16[4,64,1792]{2,1,0:T(8,128)(2,1)} %get-tuple-element.15), calls=%async_computation.4 | async-start | bytes 1835008 | tf_op jit(solution)/shard_map/all_to_all | solution.py:31
  148.8 9.4 %copy-start.12 = (s32[8,2]{0,1:T(2,128)S(1)}, s32[8,2]{0,1:T(2,128)}, u32[]{:S(2)}) copy-start(s32[8,2]{0,1:T(2,128)} %param.6) | copy-start | bytes 196
  148.8 9.4 %copy-start.13 = (f32[8,2]{0,1:T(2,128)S(1)}, f32[8,2]{0,1:T(2,128)}, u32[]{:S(2)}) copy-start(f32[8,2]{0,1:T(2,128)} %param.7) | copy-start | bytes 196
  152.2 18.2 %collective-permute-start.13 = (bf16[128,1024]{1,0:T(8,128)(2,1)}, bf16[128,1024]{1,0:T(8,128)(2,1)S(1)}, u32[]{:S(2)}, u32[]{:S(2)}) collective-permute-start(bf16[128,1024]{1,0:T(8,128)(2,1)} %shard_map.65), channel_id=1, source_target_pairs={{0,1},{1,2},{2,3},{3,0},{64,67},{65,64},{66,65},{67,66},{4,5},{5,6... | collective-permute-start | bytes 786440 | tf_op jit(solution)/shard_map/ppermute | solution.py:25
  158.8 3.7 %copy-start.5 = (bf16[4,64,1792]{2,1,0:T(8,128)(2,1)}, bf16[4,64,1792]{2,1,0:T(8,128)(2,1)S(1)}, u32[]{:S(2)}) copy-start(bf16[4,64,1792]{2,1,0:T(8,128)(2,1)S(1)} %all-to-all-done.4.refs_0_) | copy-start | bytes 2752516
  158.8 20.8 %all-to-all-start.3 = ((bf16[4,32,1792]{2,1,0:T(8,128)(2,1)}), bf16[4,32,1792]{2,1,0:T(8,128)(2,1)S(1)}, u32[]{:S(2)}, u32[]{:S(2)}) async-start(bf16[4,32,1792]{2,1,0:T(8,128)(2,1)} %get-tuple-element.14), calls=%async_computation.3 | async-start | bytes 917504 | tf_op jit(solution)/shard_map/all_to_all | solution.py:31
  162.5 16.4 %copy-start.9 = (pred[8]{0:T(512)(128)(4,1)S(1)}, pred[8]{0:T(512)(128)(4,1)}, u32[]{:S(2)}) copy-start(pred[8]{0:T(512)(128)(4,1)} %copy-done.8) | copy-start | bytes 28
  162.6 16.5 %copy-start.11 = (pred[8]{0:T(512)(128)(4,1)S(1)}, pred[8]{0:T(512)(128)(4,1)}, u32[]{:S(2)}) copy-start(pred[8]{0:T(512)(128)(4,1)} %copy-done.10) | copy-start | bytes 28
  166.7 17.2 %collective-permute-start.15 = (bf16[128,1024]{1,0:T(8,128)(2,1)}, bf16[128,1024]{1,0:T(8,128)(2,1)S(1)}, u32[]{:S(2)}, u32[]{:S(2)}) collective-permute-start(bf16[128,1024]{1,0:T(8,128)(2,1)} %get-tuple-element.18), channel_id=1, source_target_pairs={{0,3},{1,0},{2,1},{3,2},{64,65},{65,66},{66,67},{67,64},{4,7},{5,4... | collective-permute-start | bytes 786440 | tf_op jit(solution)/shard_map/ppermute | solution.py:25
  171.6 21.1 %collective-permute-start.14 = (bf16[128,1024]{1,0:T(8,128)(2,1)S(1)}, bf16[128,1024]{1,0:T(8,128)(2,1)S(1)}, u32[]{:S(2)}, u32[]{:S(2)}) collective-permute-start(bf16[128,1024]{1,0:T(8,128)(2,1)S(1)} %add_convert_fusion.2), channel_id=1, source_target_pairs={{0,1},{1,2},{2,3},{3,0},{64,67},{65,64},{66,65},{67,66},{4,5},{5,6... | collective-permute-start | bytes 786440 | tf_op jit(solution)/shard_map/ppermute | solution.py:25
  179.7 0.8 copy-start.6
  195.4 9.4 %collective-permute-start.16 = (bf16[4,64,1024]{2,1,0:T(8,128)(2,1)S(1)}, bf16[4,64,1024]{2,1,0:T(8,128)(2,1)S(1)}, u32[]{:S(2)}, u32[]{:S(2)}) collective-permute-start(bf16[4,64,1024]{2,1,0:T(8,128)(2,1)S(1)} %add_convert_fusion.1), channel_id=1, source_target_pairs={{0,64},{64,0},{1,65},{65,1},{2,66},{66,2},{3,67},{67,3},{4,68},{68... | collective-permute-start | bytes 1572872 | tf_op jit(solution)/shard_map/ppermute | solution.py:20

commit v10 on v9

--- a/solution.py
+++ b/solution.py
@@ -94,20 +94,16 @@
     )(*pieces, *weights, *after)
 
 
-def late(pieces, weights, after):
-    def kernel(*refs):
+def late_far(far, weights):
+    def kernel(far_ref, *refs):
         out_ref, held, sums, sems, out_sems = refs[-5:]
-        copies = fetch(refs[4:8], held, sems)
-        x = jnp.concatenate([ref[...] for ref in refs[:4]])
+        copies = fetch(refs[:4], held, sems)
         going = []
         for i in range(4):
             copies[i].wait()
-            rows = x[:128] if i < 3 else x
-            out = lax.dot_general(rows, held[i], DIMS, preferred_element_type=wide).astype(half)
-            for p in range(1 if i < 3 else 4):
-                columns = pl.ds(896 * (i + p), 896)
-                sums[:, :, columns] = out[128 * p : 128 * p + 128].reshape(4, 32, 896)
-            columns = pl.ds(896 * i, 896 if i < 3 else 3584)
+            columns = pl.ds(896 * i, 896)
+            out = lax.dot_general(far_ref[...], held[i], DIMS, preferred_element_type=wide).astype(half)
+            sums[:, :, columns] = out.reshape(4, 32, 896)
             going.append(pltpu.make_async_copy(sums.at[:, :, columns], out_ref.at[:, :, columns], out_sems.at[i]))
             going[-1].start()
         for copy in going:
@@ -115,18 +111,36 @@
 
     return pl.pallas_call(
         kernel,
-        in_specs=[WHOLE] * 4 + [ANY] * (4 + len(after)),
+        in_specs=[WHOLE] + [ANY] * 4,
         out_specs=ANY,
-        out_shape=jax.ShapeDtypeStruct((4, 32, 6272), half),
+        out_shape=jax.ShapeDtypeStruct((4, 32, 3584), half),
         scratch_shapes=[
             pltpu.VMEM((4, 896, 1024), half),
-            pltpu.VMEM((4, 32, 6272), half),
+            pltpu.VMEM((4, 32, 3584), half),
             pltpu.SemaphoreType.DMA((4,)),
             pltpu.SemaphoreType.DMA((4,)),
         ],
         compiler_params=pltpu.CompilerParams(vmem_limit_bytes=LIMIT),
         cost_estimate=LONG,
-    )(*pieces, *weights, *after)
+    )(far, *weights)
+
+
+def late_rest(pieces, w_far, after):
+    def kernel(*refs):
+        out_ref = refs[-1]
+        x = jnp.concatenate([ref[...] for ref in refs[:3]])
+        out = lax.dot_general(x, refs[3][...], DIMS, preferred_element_type=wide).astype(half)
+        for p in range(3):
+            out_ref[:, :, pl.ds(896 * p, 896)] = out[128 * p : 128 * p + 128].reshape(4, 32, 896)
+
+    return pl.pallas_call(
+        kernel,
+        in_specs=[WHOLE] * 4 + [ANY] * len(after),
+        out_specs=WHOLE,
+        out_shape=jax.ShapeDtypeStruct((4, 32, 2688), half),
+        compiler_params=pltpu.CompilerParams(vmem_limit_bytes=LIMIT),
+        cost_estimate=COST,
+    )(*pieces, w_far, *after)
 
 
 def act(gate, up):
@@ -157,15 +171,32 @@
     )(sums, *after)
 
 
-def activate_late(sums, near, own, after):
+def activate_far(sums):
+    def kernel(sums_ref, out_ref):
+        total = jnp.sum(sums_ref[...].astype(wide), axis=0)
+        hidden = jnp.concatenate([block(total, i) for i in range(4)], axis=1)
+        for j in range(4):
+            out_ref[j] = hidden
+
+    return pl.pallas_call(
+        kernel,
+        grid=(1,),
+        in_specs=[pl.BlockSpec((4, 32, 3584), lambda i: (0, 0, 0))],
+        out_specs=pl.BlockSpec((4, 32, 1792), lambda i: (0, 0, 0)),
+        out_shape=jax.ShapeDtypeStruct((4, 32, 1792), half),
+        compiler_params=pltpu.CompilerParams(vmem_limit_bytes=LIMIT),
+        cost_estimate=COST,
+    )(sums)
+
+
+def activate_rest(sums, near, own, after):
     def kernel(sums_ref, near_ref, own_ref, *refs):
-        outs = refs[-3:]
+        outs = refs[-2:]
         total = jnp.sum(sums_ref[...].astype(wide), axis=0)
-        blocks = [block(total, i) for i in range(7)]
-        far = jnp.concatenate(blocks[:4], axis=1)
-        near = jnp.concatenate([near_ref[...], jnp.concatenate(blocks[4:6])], axis=1)
-        own = jnp.concatenate([own_ref[...], blocks[6]], axis=1)
-        for part, out in zip((far, near, own), outs):
+        blocks = [block(total, i) for i in range(3)]
+        near = jnp.concatenate([near_ref[...], jnp.concatenate(blocks[:2])], axis=1)
+        own = jnp.concatenate([own_ref[...], blocks[2]], axis=1)
+        for part, out in zip((near, own), outs):
             for j in range(4):
                 out[j] = part
 
@@ -173,13 +204,13 @@
         kernel,
         grid=(1,),
         in_specs=[
-            pl.BlockSpec((4, 32, 6272), lambda i: (0, 0, 0)),
+            pl.BlockSpec((4, 32, 2688), lambda i: (0, 0, 0)),
             pl.BlockSpec((64, 1344), lambda i: (0, 0)),
             pl.BlockSpec((32, 1344), lambda i: (0, 0)),
         ]
         + [ANY] * len(after),
-        out_specs=[pl.BlockSpec((4, r, 1792), lambda i: (0, 0, 0)) for r in (32, 64, 32)],
-        out_shape=[jax.ShapeDtypeStruct((4, r, 1792), half) for r in (32, 64, 32)],
+        out_specs=[pl.BlockSpec((4, r, 1792), lambda i: (0, 0, 0)) for r in (64, 32)],
+        out_shape=[jax.ShapeDtypeStruct((4, r, 1792), half) for r in (64, 32)],
         compiler_params=pltpu.CompilerParams(vmem_limit_bytes=LIMIT),
         cost_estimate=COST,
     )(sums, near, own, *after)
@@ -261,8 +292,10 @@
     v_far = pass_on(v_first, "y", 1)
     v_all = [v_own, v_first, v_second, v_far]
     own_h, near_h = activate_early(own_sums, []), activate_early(swap(part, "x"), [v_first])
-    rest = swap(late([far, first, second, rows], weights + [w_far], []), "x")
-    far_h, near_h, own_h = activate_late(rest, near_h, own_h, [v_second, v_far])
+    far_part = late_far(far, weights + [w_far])
+    rest_part = late_rest([first, second, rows], w_far, [far_part])
+    far_h = activate_far(swap(far_part, "x"))
+    near_h, own_h = activate_rest(swap(rest_part, "x"), near_h, own_h, [v_second, v_far])
 
     (far_out,) = down(swap(far_h, "x"), v_all, (half,))
     got = pass_on(far_out, "zhi", 1)

time: 233 us -> 230 us (0.987)
  blocking collectives: 35.5 us -> 21.6 us
  starting transfers between devices: 98.8 us -> 107 us
  Pallas kernels: 40.6 us -> 44.8 us
    ppermute x12, waiting for transfers between devices: 27.1 us -> 10.9 us  [pass_on(): lax.ppermute(a, ('core', axis), [(c * n + i, c * n + (i + by * (1 - 2 * c...]
    all_to_all x5 -> x7, waiting for transfers between devices: 2.89 us -> 17.9 us  [swap(): return lax.all_to_all(a, axis, split_axis=0, concat_axis=0, tiled=True)]
    all_to_all x2 -> x1, blocking collectives: 35.5 us -> 21.6 us  [swap(): return lax.all_to_all(a, axis, split_axis=0, concat_axis=0, tiled=True)]
    all_to_all x5 -> x7, starting transfers between devices: 19.7 us -> 27.6 us  [swap(): return lax.all_to_all(a, axis, split_axis=0, concat_axis=0, tiled=True)]
    pallas_call x2 -> x4, Pallas kernels: 10.5 us -> 14.6 us  [the longest x1 6.28 us: late_far(): pl.pallas_call(kernel, in_specs=[WHOLE] + [ANY] * 4, out_specs=ANY, out_s...]
    unnamed x34 -> x38, local copies, waits for them, and re-layouts: 4.95 us -> 5.93 us
  transfers between devices with their start and end apart: 22 -> 24, of which waited for: 9 -> 11; matrix products, arithmetic and copies ran while one was open for 4% -> 4% of each run, Pallas kernels for 16% -> 20%
where the time goes in v10:
time: 230 us; the launch traced here: 228 us
  starting transfers between devices  107 us (47%)
  Pallas kernels  44.8 us (19%)
  waiting for transfers between devices  30.8 us (13%)
  blocking collectives  21.6 us (9%)
  other arithmetic  12.4 us (5%)
  local copies, waits for them, and re-layouts  6.12 us (3%)
  between operations  5.4 us (2%)
    ppermute x12, starting transfers between devices, pass_on(): lax.ppermute(a, ('core', axis), [(c * n + i, c * n + (i + by * (1 - 2 * c...  55.4 us
    all_to_all x7, starting transfers between devices, swap(): return lax.all_to_all(a, axis, split_axis=0, concat_axis=0, tiled=True)  27.6 us
    ppermute x5, starting transfers between devices, shift(): return lax.ppermute(a, axis, [(i, (i + by) % n) for i in range(n)])  23.9 us
    all_to_all x1, blocking collectives, swap(): return lax.all_to_all(a, axis, split_axis=0, concat_axis=0, tiled=True)  21.6 us
    all_to_all x7, waiting for transfers between devices, swap(): return lax.all_to_all(a, axis, split_axis=0, concat_axis=0, tiled=True)  17.9 us
    pallas_call x2, Pallas kernels, early(): pl.pallas_call(kernel, in_specs=[WHOLE] * n + [ANY] * (3 + len(after)), o...  11.2 us
    pallas_call x3, Pallas kernels, down(): pl.pallas_call(kernel, grid=(2,), in_specs=[pl.BlockSpec((4, 32 * n, 1792...  10.9 us
    ppermute x12, waiting for transfers between devices, pass_on(): lax.ppermute(a, ('core', axis), [(c * n + i, c * n + (i + by * (1 - 2 * c...  10.9 us
  transfers between devices with their start and end apart: 24, of which 11 were waited for; matrix products, arithmetic and copies ran while one was open for 4% of the time, Pallas kernels for 20%

profile of v10, /device:TPU:1, one launch (start us, length us, event | category | flops | bytes accessed | tf_op | source)
XLA Modules:
  0.0 228.0 jit_solution(8441081213506019632)
XLA Ops:
  0.0 5.5 %collective-permute-start.6 = (bf16[896,1024]{1,0:T(8,128)(2,1)}, bf16[896,1024]{1,0:T(8,128)(2,1)S(1)}, u32[]{:S(2)}, u32[]{:S(2)}) collective-permute-start(bf16[896,1024]{1,0:T(8,128)(2,1)} %bitcast.19), channel_id=1, source_target_pairs={{0,4},{4,8},{8,12},{12,0},{64,76},{68,64},{72,68},{76,72},{1,5},{5... | collective-permute-start | bytes 5505032 | tf_op jit(solution)/shard_map/ppermute | solution.py:25
  5.5 1.9 collective-permute-start.7
  7.4 4.9 %collective-permute-start.1 = (bf16[64,1024]{1,0:T(8,128)(2,1)}, bf16[64,1024]{1,0:T(8,128)(2,1)S(1)}, u32[]{:S(2)}, u32[]{:S(2)}) collective-permute-start(bf16[64,1024]{1,0:T(8,128)(2,1)} %bitcast.16), channel_id=1, source_target_pairs={{0,256},{128,384},{256,0},{384,128},{1,257},{129,385},{257,1},{385... | collective-permute-start | bytes 393224 | tf_op jit(solution)/shard_map/ppermute | solution.py:20
  12.3 3.3 %collective-permute-start.2 = (bf16[64,1024]{1,0:T(8,128)(2,1)}, bf16[64,1024]{1,0:T(8,128)(2,1)S(1)}, u32[]{:S(2)}, u32[]{:S(2)}) collective-permute-start(bf16[64,1024]{1,0:T(8,128)(2,1)} %bitcast.17), channel_id=1, source_target_pairs={{0,384},{128,0},{256,128},{384,256},{1,385},{129,1},{257,129},{385... | collective-permute-start | bytes 393224 | tf_op jit(solution)/shard_map/ppermute | solution.py:20
  15.6 2.2 collective-permute-start
  21.6 1.9 collective-permute-done
  24.5 5.6 %collective-permute-start.3 = (bf16[128,1024]{1,0:T(8,128)(2,1)S(1)}, bf16[128,1024]{1,0:T(8,128)(2,1)S(1)}, u32[]{:S(2)}, u32[]{:S(2)}) collective-permute-start(bf16[128,1024]{1,0:T(8,128)(2,1)S(1)} %pad_maximum_fusion), channel_id=1, source_target_pairs={{0,64},{64,0},{1,65},{65,1},{2,66},{66,2},{3,67},{67,3},{4,68},{68... | collective-permute-start | bytes 786440 | tf_op jit(solution)/shard_map/ppermute | solution.py:20
  33.6 10.0 %collective-permute-start.4 = (bf16[128,1024]{1,0:T(8,128)(2,1)S(1)}, bf16[128,1024]{1,0:T(8,128)(2,1)S(1)}, u32[]{:S(2)}, u32[]{:S(2)}) collective-permute-start(bf16[128,1024]{1,0:T(8,128)(2,1)S(1)} %pad_maximum_fusion.1.refs_0_.refs_2_), channel_id=1, source_target_pairs={{0,1},{1,2},{2,3},{3,0},{64,67},{65,64},{66,65},{67,66},{4,5},{5,6... | collective-permute-start | bytes 786440 | tf_op jit(solution)/shard_map/ppermute | solution.py:25
  43.6 1.9 collective-permute-start.5
  45.5 3.4 %collective-permute-done.7.refs_3_.refs_2_.refs_4_ = bf16[896,1024]{1,0:T(8,128)(2,1)} collective-permute-done((bf16[896,1024]{1,0:T(8,128)(2,1)}, bf16[896,1024]{1,0:T(8,128)(2,1)}, u32[]{:S(2)}, u32[]{:S(2)}) %collective-permute-start.7) | collective-permute-done | bytes 1835040 | tf_op jit(solution)/shard_map/ppermute | solution.py:25
  48.9 5.5 %shard_map.55 = (bf16[896,1024]{1,0:T(8,128)(2,1)}, bf16[4,32,2688]{2,1,0:T(8,128)(2,1)}) custom-call(bf16[128,1024]{1,0:T(8,128)(2,1)} %copy-done.8, bf16[896,1024]{1,0:T(8,128)(2,1)} %bitcast.21, bf16[896,1024]{1,0:T(8,128)(2,1)} %copy-done.17, bf16[896,1024]{1,0:T(8,128)(2,1)} %collective-permute-done.7.refs_3_.refs_2_.refs_4_), custom_call_target="tpu_custom_call" | custom-call | flops 99999997952 | bytes 1024 | tf_op jit(solution)/shard_map/pallas_call | solution.py:81
  54.4 1.9 collective-permute-start.8
  56.4 4.0 %all-to-all-start.2 = ((bf16[4,32,2688]{2,1,0:T(8,128)(2,1)}), bf16[4,32,2688]{2,1,0:T(8,128)(2,1)S(1)}, u32[]{:S(2)}, u32[]{:S(2)}) async-start(bf16[4,32,2688]{2,1,0:T(8,128)(2,1)} %get-tuple-element.12.refs_0_.refs_5_), calls=%async_computation.2 | async-start | bytes 1376256 | tf_op jit(solution)/shard_map/all_to_all | solution.py:31
  60.4 1.6 collective-permute-done.4.a_ref.refs_0_
  62.7 1.7 shard_map.56
  64.4 10.9 %collective-permute-start.9 = (bf16[128,1024]{1,0:T(8,128)(2,1)}, bf16[128,1024]{1,0:T(8,128)(2,1)S(1)}, u32[]{:S(2)}, u32[]{:S(2)}) collective-permute-start(bf16[128,1024]{1,0:T(8,128)(2,1)} %shard_map.56), channel_id=1, source_target_pairs={{0,1},{1,2},{2,3},{3,0},{64,67},{65,64},{66,65},{67,66},{4,5},{5,6... | collective-permute-start | bytes 786440 | tf_op jit(solution)/shard_map/ppermute | solution.py:25
  76.0 5.6 %shard_map.59 = bf16[4,64,2688]{2,1,0:T(8,128)(2,1)} custom-call(bf16[128,1024]{1,0:T(8,128)(2,1)} %copy-done.9, bf16[128,1024]{1,0:T(8,128)(2,1)} %copy-done.10, bf16[896,1024]{1,0:T(8,128)(2,1)} %bitcast.22, bf16[896,1024]{1,0:T(8,128)(2,1)} %copy-done.17, bf16[896,1024]{1,0:T(8,128)(2,1)} %collective-permute-done.7.refs_3_.refs_2_.refs_4_, ...), custom_call_target="tpu_custom_call" | custom-call | flops 10000000000 | bytes 1024 | tf_op jit(solution)/shard_map/pallas_call | solution.py:81
  81.7 4.2 %all-to-all-start.1 = ((bf16[4,64,2688]{2,1,0:T(8,128)(2,1)}), bf16[4,64,2688]{2,1,0:T(8,128)(2,1)S(1)}, u32[]{:S(2)}, u32[]{:S(2)}) async-start(bf16[4,64,2688]{2,1,0:T(8,128)(2,1)} %shard_map.59), calls=%async_computation.1 | async-start | bytes 2752512 | tf_op jit(solution)/shard_map/all_to_all | solution.py:31
  85.9 2.2 shard_map.60
  88.2 2.3 collective-permute-start.10
  91.1 6.3 %shard_map.57.refs_4_ = bf16[4,32,3584]{2,1,0:T(8,128)(2,1)} custom-call(bf16[128,1024]{1,0:T(8,128)(2,1)} %copy-done.18, bf16[896,1024]{1,0:T(8,128)(2,1)} %bitcast.23, bf16[896,1024]{1,0:T(8,128)(2,1)} %copy-done.17, bf16[896,1024]{1,0:T(8,128)(2,1)} %collective-permute-done.7.refs_3_.refs_2_.refs_4_, bf16[896,1024]{1,0:T(8,128)(2,1)} %collective-permute-done.8.refs_3_), custom_call_target="tpu_custom_call" | custom-call | flops 99999997952 | bytes 1024 | tf_op jit(solution)/shard_map/pallas_call | solution.py:112
  97.4 4.0 %all-to-all-done.1.sums_ref = bf16[4,64,2688]{2,1,0:T(8,128)(2,1)S(1)} async-done(((bf16[4,64,2688]{2,1,0:T(8,128)(2,1)}), bf16[4,64,2688]{2,1,0:T(8,128)(2,1)S(1)}, u32[]{:S(2)}, u32[]{:S(2)}) %all-to-all-start.1) | async-done | bytes 1376288 | tf_op jit(solution)/shard_map/all_to_all | solution.py:31
  102.5 4.2 %all-to-all-start.5 = ((bf16[4,32,3584]{2,1,0:T(8,128)(2,1)}), bf16[4,32,3584]{2,1,0:T(8,128)(2,1)}, u32[]{:S(2)}, u32[]{:S(2)}) async-start(bf16[4,32,3584]{2,1,0:T(8,128)(2,1)} %shard_map.57.refs_4_), calls=%async_computation.5 | async-start | bytes 1835008 | tf_op jit(solution)/shard_map/all_to_all | solution.py:31
  106.7 4.0 %collective-permute-start.11 = (bf16[448,1024]{1,0:T(8,128)(2,1)}, bf16[448,1024]{1,0:T(8,128)(2,1)S(1)}, u32[]{:S(2)}, u32[]{:S(2)}) collective-permute-start(bf16[448,1024]{1,0:T(8,128)(2,1)} %shard_map.60), channel_id=1, source_target_pairs={{0,12},{4,0},{8,4},{12,8},{64,68},{68,72},{72,76},{76,64},{1,13},{... | collective-permute-start | bytes 2752520 | tf_op jit(solution)/shard_map/ppermute | solution.py:25
  110.7 2.5 %collective-permute-start.12 = (bf16[448,1024]{1,0:T(8,128)(2,1)S(1)}, bf16[448,1024]{1,0:T(8,128)(2,1)S(1)}, u32[]{:S(2)}, u32[]{:S(2)}) collective-permute-start(bf16[448,1024]{1,0:T(8,128)(2,1)S(1)} %collective-permute-done.10.refs_0_.refs_2_), channel_id=1, source_target_pairs={{0,4},{4,8},{8,12},{12,0},{64,76},{68,64},{72,68},{76,72},{1,5},{5... | collective-permute-start | bytes 2752520 | tf_op jit(solution)/shard_map/ppermute | solution.py:25
  113.2 3.6 %shard_map.58 = bf16[4,32,2688]{2,1,0:T(8,128)(2,1)} custom-call(bf16[128,1024]{1,0:T(8,128)(2,1)} %copy-done.9, bf16[128,1024]{1,0:T(8,128)(2,1)} %copy-done.10, bf16[128,1024]{1,0:T(8,128)(2,1)} %copy-done.8, bf16[896,1024]{1,0:T(8,128)(2,1)} %collective-permute-done.8.refs_3_, bf16[4,32,3584]{2,1,0:T(8,128)(2,1)} %shard_map.57.refs_4_), custom_call_target="tpu_custom_call" | custom-call | flops 1024 | bytes 1024 | tf_op jit(solution)/shard_map/pallas_call | solution.py:136
  116.9 1.5 all-to-all-done.5.sums_ref
  118.4 3.5 %all-to-all-start = ((bf16[4,32,2688]{2,1,0:T(8,128)(2,1)}), bf16[4,32,2688]{2,1,0:T(8,128)(2,1)S(1)}, u32[]{:S(2)}, u32[]{:S(2)}) async-start(bf16[4,32,2688]{2,1,0:T(8,128)(2,1)} %shard_map.58), calls=%async_computation | async-start | bytes 1376256 | tf_op jit(solution)/shard_map/all_to_all | solution.py:31
  121.9 2.2 shard_map.66
  124.1 8.7 %all-to-all-done.sums_ref = bf16[4,32,2688]{2,1,0:T(8,128)(2,1)S(1)} async-done(((bf16[4,32,2688]{2,1,0:T(8,128)(2,1)}), bf16[4,32,2688]{2,1,0:T(8,128)(2,1)S(1)}, u32[]{:S(2)}, u32[]{:S(2)}) %all-to-all-start) | async-done | bytes 688160 | tf_op jit(solution)/shard_map/all_to_all | solution.py:31
  132.8 4.1 %all-to-all-start.6 = ((bf16[4,32,1792]{2,1,0:T(8,128)(2,1)}), bf16[4,32,1792]{2,1,0:T(8,128)(2,1)}, u32[]{:S(2)}, u32[]{:S(2)}) async-start(bf16[4,32,1792]{2,1,0:T(8,128)(2,1)} %shard_map.66), calls=%async_computation.6 | async-start | bytes 917504 | tf_op jit(solution)/shard_map/all_to_all | solution.py:31
  137.0 1.9 shard_map.62.own_ref
  138.9 2.3 shard_map.61.near_ref
  143.1 2.5 %shard_map.63 = (bf16[4,64,1792]{2,1,0:T(8,128)(2,1)}, bf16[4,32,1792]{2,1,0:T(8,128)(2,1)}) custom-call(bf16[4,32,2688]{2,1,0:T(8,128)(2,1)} %copy-done.6, bf16[64,1344]{1,0:T(8,128)(2,1)} %shard_map.61.near_ref, bf16[32,1344]{1,0:T(8,128)(2,1)} %shard_map.62.own_ref, bf16[448,1024]{1,0:T(8,128)(2,1)} %copy-done.1, bf16[448,1024]{1,0:T(8,128)(2,1)} %copy-done.2), custom_call_target="tpu_custom_call" | custom-call | flops 1024 | bytes 1024 | tf_op jit(solution)/shard_map/pallas_call | solution.py:203
  145.7 4.0 %all-to-all-start.4 = ((bf16[4,64,1792]{2,1,0:T(8,128)(2,1)}), bf16[4,64,1792]{2,1,0:T(8,128)(2,1)S(1)}, u32[]{:S(2)}, u32[]{:S(2)}) async-start(bf16[4,64,1792]{2,1,0:T(8,128)(2,1)} %get-tuple-element.14), calls=%async_computation.4 | async-start | bytes 1835008 | tf_op jit(solution)/shard_map/all_to_all | solution.py:31
  149.7 3.4 %shard_map.67 = bf16[128,1024]{1,0:T(8,128)(2,1)} custom-call(bf16[4,32,1792]{2,1,0:T(8,128)(2,1)} %all-to-all-done.6.refs_0_, bf16[448,1024]{1,0:T(8,128)(2,1)} %bitcast.13, bf16[448,1024]{1,0:T(8,128)(2,1)} %copy-done, bf16[448,1024]{1,0:T(8,128)(2,1)} %copy-done.1, bf16[448,1024]{1,0:T(8,128)(2,1)} %copy-done.2), custom_call_target="tpu_custom_call" | custom-call | flops 1024 | bytes 1024 | tf_op jit(solution)/shard_map/pallas_call | solution.py:229
  153.2 5.4 %collective-permute-start.13 = (bf16[128,1024]{1,0:T(8,128)(2,1)}, bf16[128,1024]{1,0:T(8,128)(2,1)S(1)}, u32[]{:S(2)}, u32[]{:S(2)}) collective-permute-start(bf16[128,1024]{1,0:T(8,128)(2,1)} %shard_map.67), channel_id=1, source_target_pairs={{0,1},{1,2},{2,3},{3,0},{64,67},{65,64},{66,65},{67,66},{4,5},{5,6... | collective-permute-start | bytes 786440 | tf_op jit(solution)/shard_map/ppermute | solution.py:25
  159.2 3.5 %all-to-all-done.4.refs_0_ = bf16[4,64,1792]{2,1,0:T(8,128)(2,1)S(1)} async-done(((bf16[4,64,1792]{2,1,0:T(8,128)(2,1)}), bf16[4,64,1792]{2,1,0:T(8,128)(2,1)S(1)}, u32[]{:S(2)}, u32[]{:S(2)}) %all-to-all-start.4) | async-done | bytes 917536 | tf_op jit(solution)/shard_map/all_to_all | solution.py:31
  162.7 3.5 %all-to-all-start.3 = ((bf16[4,32,1792]{2,1,0:T(8,128)(2,1)}), bf16[4,32,1792]{2,1,0:T(8,128)(2,1)S(1)}, u32[]{:S(2)}, u32[]{:S(2)}) async-start(bf16[4,32,1792]{2,1,0:T(8,128)(2,1)} %get-tuple-element.13), calls=%async_computation.3 | async-start | bytes 917504 | tf_op jit(solution)/shard_map/all_to_all | solution.py:31
  166.2 4.1 %shard_map.65 = (bf16[128,1024]{1,0:T(8,128)(2,1)}, f32[128,1024]{1,0:T(8,128)}) custom-call(bf16[4,64,1792]{2,1,0:T(8,128)(2,1)} %copy-done.5, bf16[448,1024]{1,0:T(8,128)(2,1)} %bitcast.14, bf16[448,1024]{1,0:T(8,128)(2,1)} %copy-done, bf16[448,1024]{1,0:T(8,128)(2,1)} %copy-done.1, bf16[448,1024]{1,0:T(8,128)(2,1)} %copy-done.2), custom_call_target="tpu_custom_call" | custom-call | flops 1024 | bytes 1024 | tf_op jit(solution)/shard_map/pallas_call | solution.py:229
  170.3 1.9 collective-permute-start.15
  173.4 7.3 %collective-permute-start.14 = (bf16[128,1024]{1,0:T(8,128)(2,1)S(1)}, bf16[128,1024]{1,0:T(8,128)(2,1)S(1)}, u32[]{:S(2)}, u32[]{:S(2)}) collective-permute-start(bf16[128,1024]{1,0:T(8,128)(2,1)S(1)} %add_convert_fusion.2), channel_id=1, source_target_pairs={{0,1},{1,2},{2,3},{3,0},{64,67},{65,64},{66,65},{67,66},{4,5},{5,6... | collective-permute-start | bytes 786440 | tf_op jit(solution)/shard_map/ppermute | solution.py:25
  184.1 3.4 %shard_map.64 = f32[128,1024]{1,0:T(8,128)} custom-call(bf16[4,32,1792]{2,1,0:T(8,128)(2,1)} %copy-done.7, bf16[448,1024]{1,0:T(8,128)(2,1)} %bitcast.15, bf16[448,1024]{1,0:T(8,128)(2,1)} %copy-done, bf16[448,1024]{1,0:T(8,128)(2,1)} %copy-done.1, bf16[448,1024]{1,0:T(8,128)(2,1)} %copy-done.2), custom_call_target="tpu_custom_call" | custom-call | flops 1024 | bytes 1024 | tf_op jit(solution)/shard_map/pallas_call | solution.py:229
  187.5 2.0 collective-permute-done.15
  189.5 3.9 %collective-permute-done.14 = bf16[128,1024]{1,0:T(8,128)(2,1)S(1)} collective-permute-done((bf16[128,1024]{1,0:T(8,128)(2,1)S(1)}, bf16[128,1024]{1,0:T(8,128)(2,1)S(1)}, u32[]{:S(2)}, u32[]{:S(2)}) %collective-permute-start.14) | collective-permute-done | bytes 262176 | tf_op jit(solution)/shard_map/ppermute | solution.py:25
  194.6 1.3 slice_multiply_fusion.1
  196.1 7.8 %collective-permute-start.16 = (bf16[4,64,1024]{2,1,0:T(8,128)(2,1)S(1)}, bf16[4,64,1024]{2,1,0:T(8,128)(2,1)S(1)}, u32[]{:S(2)}, u32[]{:S(2)}) collective-permute-start(bf16[4,64,1024]{2,1,0:T(8,128)(2,1)S(1)} %add_convert_fusion.1), channel_id=1, source_target_pairs={{0,64},{64,0},{1,65},{65,1},{2,66},{66,2},{3,67},{67,3},{4,68},{68... | collective-permute-start | bytes 1572872 | tf_op jit(solution)/shard_map/ppermute | solution.py:20
  205.7 21.6 %all_to_all.40 = bf16[4,64,1024]{2,1,0:T(8,128)(2,1)S(1)} all-to-all(bf16[4,64,1024]{2,1,0:T(8,128)(2,1)S(1)} %add_convert_fusion), channel_id=1, replica_groups=mesh['zlo'=4,'core'=2,'x'=4,'y'=4,'zhi'=4] {'zlo'}, dimensions={0} | all-to-all | bytes 1048576 | tf_op jit(solution)/shard_map/all_to_all | solution.py:31
  (76 shorter events, 17.6 us)
Async XLA Ops:
  0.0 45.5 %collective-permute-start.6 = (bf16[896,1024]{1,0:T(8,128)(2,1)}, bf16[896,1024]{1,0:T(8,128)(2,1)S(1)}, u32[]{:S(2)}, u32[]{:S(2)}) collective-permute-start(bf16[896,1024]{1,0:T(8,128)(2,1)} %bitcast.19), channel_id=1, source_target_pairs={{0,4},{4,8},{8,12},{12,0},{64,76},{68,64},{72,68},{76,72},{1,5},{5... | collective-permute-start | bytes 5505032 | tf_op jit(solution)/shard_map/ppermute | solution.py:25
  5.5 43.4 %collective-permute-start.7 = (bf16[896,1024]{1,0:T(8,128)(2,1)}, bf16[896,1024]{1,0:T(8,128)(2,1)}, u32[]{:S(2)}, u32[]{:S(2)}) collective-permute-start(bf16[896,1024]{1,0:T(8,128)(2,1)} %bitcast.20), channel_id=1, source_target_pairs={{0,12},{4,0},{8,4},{12,8},{64,68},{68,72},{72,76},{76,64},{1,13},{... | collective-permute-start | bytes 5505032 | tf_op jit(solution)/shard_map/ppermute | solution.py:25
  7.4 14.2 %collective-permute-start.1 = (bf16[64,1024]{1,0:T(8,128)(2,1)}, bf16[64,1024]{1,0:T(8,128)(2,1)S(1)}, u32[]{:S(2)}, u32[]{:S(2)}) collective-permute-start(bf16[64,1024]{1,0:T(8,128)(2,1)} %bitcast.16), channel_id=1, source_target_pairs={{0,256},{128,384},{256,0},{384,128},{1,257},{129,385},{257,1},{385... | collective-permute-start | bytes 393224 | tf_op jit(solution)/shard_map/ppermute | solution.py:20
  12.3 9.3 %collective-permute-start.2 = (bf16[64,1024]{1,0:T(8,128)(2,1)}, bf16[64,1024]{1,0:T(8,128)(2,1)S(1)}, u32[]{:S(2)}, u32[]{:S(2)}) collective-permute-start(bf16[64,1024]{1,0:T(8,128)(2,1)} %bitcast.17), channel_id=1, source_target_pairs={{0,384},{128,0},{256,128},{384,256},{1,385},{129,1},{257,129},{385... | collective-permute-start | bytes 393224 | tf_op jit(solution)/shard_map/ppermute | solution.py:20
  15.6 7.9 %collective-permute-start = (bf16[64,1024]{1,0:T(8,128)(2,1)}, bf16[64,1024]{1,0:T(8,128)(2,1)S(1)}, u32[]{:S(2)}, u32[]{:S(2)}) collective-permute-start(bf16[64,1024]{1,0:T(8,128)(2,1)} %bitcast.18), channel_id=1, source_target_pairs={{0,128},{128,256},{256,384},{384,0},{1,129},{129,257},{257,385},{3... | collective-permute-start | bytes 393224 | tf_op jit(solution)/shard_map/ppermute | solution.py:20
  18.9 5.5 %copy-start.11 = (pred[8]{0:T(512)(128)(4,1)}, pred[8]{0:T(512)(128)(4,1)S(1)}, u32[]{:S(2)}) copy-start(pred[8]{0:T(512)(128)(4,1)S(1)} %get-tuple-element.17) | copy-start | bytes 28
  18.9 5.5 %copy-start.13 = (pred[8]{0:T(512)(128)(4,1)}, pred[8]{0:T(512)(128)(4,1)S(1)}, u32[]{:S(2)}) copy-start(pred[8]{0:T(512)(128)(4,1)S(1)} %get-tuple-element.18) | copy-start | bytes 28
  24.5 8.1 %collective-permute-start.3 = (bf16[128,1024]{1,0:T(8,128)(2,1)S(1)}, bf16[128,1024]{1,0:T(8,128)(2,1)S(1)}, u32[]{:S(2)}, u32[]{:S(2)}) collective-permute-start(bf16[128,1024]{1,0:T(8,128)(2,1)S(1)} %pad_maximum_fusion), channel_id=1, source_target_pairs={{0,64},{64,0},{1,65},{65,1},{2,66},{66,2},{3,67},{67,3},{4,68},{68... | collective-permute-start | bytes 786440 | tf_op jit(solution)/shard_map/ppermute | solution.py:20
  33.6 15.3 %copy-start.8 = (bf16[128,1024]{1,0:T(8,128)(2,1)}, bf16[128,1024]{1,0:T(8,128)(2,1)S(1)}, u32[]{:S(2)}) copy-start(bf16[128,1024]{1,0:T(8,128)(2,1)S(1)} %pad_maximum_fusion.1.refs_0_.refs_2_) | copy-start | bytes 786436
  33.6 28.5 %collective-permute-start.4 = (bf16[128,1024]{1,0:T(8,128)(2,1)S(1)}, bf16[128,1024]{1,0:T(8,128)(2,1)S(1)}, u32[]{:S(2)}, u32[]{:S(2)}) collective-permute-start(bf16[128,1024]{1,0:T(8,128)(2,1)S(1)} %pad_maximum_fusion.1.refs_0_.refs_2_), channel_id=1, source_target_pairs={{0,1},{1,2},{2,3},{3,0},{64,67},{65,64},{66,65},{67,66},{4,5},{5,6... | collective-permute-start | bytes 786440 | tf_op jit(solution)/shard_map/ppermute | solution.py:25
  43.6 31.7 %collective-permute-start.5 = (bf16[128,1024]{1,0:T(8,128)(2,1)S(1)}, bf16[128,1024]{1,0:T(8,128)(2,1)S(1)}, u32[]{:S(2)}, u32[]{:S(2)}) collective-permute-start(bf16[128,1024]{1,0:T(8,128)(2,1)S(1)} %pad_maximum_fusion.1.refs_0_.refs_2_), channel_id=1, source_target_pairs={{0,3},{1,0},{2,1},{3,2},{64,65},{65,66},{66,67},{67,64},{4,7},{5,4... | collective-permute-start | bytes 786440 | tf_op jit(solution)/shard_map/ppermute | solution.py:25
  45.5 3.4 %copy-start.17 = (bf16[896,1024]{1,0:T(8,128)(2,1)}, bf16[896,1024]{1,0:T(8,128)(2,1)S(1)}, u32[]{:S(2)}) copy-start(bf16[896,1024]{1,0:T(8,128)(2,1)S(1)} %collective-permute-done.6.refs_2_.refs_1_.refs_3_) | copy-start | bytes 5505028
  54.4 36.0 %collective-permute-start.8 = (bf16[896,1024]{1,0:T(8,128)(2,1)}, bf16[896,1024]{1,0:T(8,128)(2,1)}, u32[]{:S(2)}, u32[]{:S(2)}) collective-permute-start(bf16[896,1024]{1,0:T(8,128)(2,1)} %get-tuple-element.11), channel_id=1, source_target_pairs={{0,4},{4,8},{8,12},{12,0},{64,76},{68,64},{72,68},{76,72},{1,5},{5... | collective-permute-start | bytes 5505032 | tf_op jit(solution)/shard_map/ppermute | solution.py:25
  56.4 25.2 %all-to-all-start.2 = ((bf16[4,32,2688]{2,1,0:T(8,128)(2,1)}), bf16[4,32,2688]{2,1,0:T(8,128)(2,1)S(1)}, u32[]{:S(2)}, u32[]{:S(2)}) async-start(bf16[4,32,2688]{2,1,0:T(8,128)(2,1)} %get-tuple-element.12.refs_0_.refs_5_), calls=%async_computation.2 | async-start | bytes 1376256 | tf_op jit(solution)/shard_map/all_to_all | solution.py:31
  62.0 0.7 copy-start.9
  64.4 26.0 %collective-permute-start.9 = (bf16[128,1024]{1,0:T(8,128)(2,1)}, bf16[128,1024]{1,0:T(8,128)(2,1)S(1)}, u32[]{:S(2)}, u32[]{:S(2)}) collective-permute-start(bf16[128,1024]{1,0:T(8,128)(2,1)} %shard_map.56), channel_id=1, source_target_pairs={{0,1},{1,2},{2,3},{3,0},{64,67},{65,64},{66,65},{67,66},{4,5},{5,6... | collective-permute-start | bytes 786440 | tf_op jit(solution)/shard_map/ppermute | solution.py:25
  75.3 0.7 copy-start.10
  81.6 4.3 %copy-start.3 = (bf16[4,32,2688]{2,1,0:T(8,128)(2,1)}, bf16[4,32,2688]{2,1,0:T(8,128)(2,1)S(1)}, u32[]{:S(2)}) copy-start(bf16[4,32,2688]{2,1,0:T(8,128)(2,1)S(1)} %all-to-all-done.2.refs_0_.sums_ref) | copy-start | bytes 2064388
  81.7 19.7 %all-to-all-start.1 = ((bf16[4,64,2688]{2,1,0:T(8,128)(2,1)}), bf16[4,64,2688]{2,1,0:T(8,128)(2,1)S(1)}, u32[]{:S(2)}, u32[]{:S(2)}) async-start(bf16[4,64,2688]{2,1,0:T(8,128)(2,1)} %shard_map.59), calls=%async_computation.1 | async-start | bytes 2752512 | tf_op jit(solution)/shard_map/all_to_all | solution.py:31
  88.2 22.6 %collective-permute-start.10 = (bf16[448,1024]{1,0:T(8,128)(2,1)}, bf16[448,1024]{1,0:T(8,128)(2,1)S(1)}, u32[]{:S(2)}, u32[]{:S(2)}) collective-permute-start(bf16[448,1024]{1,0:T(8,128)(2,1)} %shard_map.60), channel_id=1, source_target_pairs={{0,4},{4,8},{8,12},{12,0},{64,76},{68,64},{72,68},{76,72},{1,5},{5... | collective-permute-start | bytes 2752520 | tf_op jit(solution)/shard_map/ppermute | solution.py:25
  90.4 0.7 copy-start.18
  101.4 1.1 copy-start.4
  102.5 15.9 %all-to-all-start.5 = ((bf16[4,32,3584]{2,1,0:T(8,128)(2,1)}), bf16[4,32,3584]{2,1,0:T(8,128)(2,1)}, u32[]{:S(2)}, u32[]{:S(2)}) async-start(bf16[4,32,3584]{2,1,0:T(8,128)(2,1)} %shard_map.57.refs_4_), calls=%async_computation.5 | async-start | bytes 1835008 | tf_op jit(solution)/shard_map/all_to_all | solution.py:31
  106.7 34.5 %collective-permute-start.11 = (bf16[448,1024]{1,0:T(8,128)(2,1)}, bf16[448,1024]{1,0:T(8,128)(2,1)S(1)}, u32[]{:S(2)}, u32[]{:S(2)}) collective-permute-start(bf16[448,1024]{1,0:T(8,128)(2,1)} %shard_map.60), channel_id=1, source_target_pairs={{0,12},{4,0},{8,4},{12,8},{64,68},{68,72},{72,76},{76,64},{1,13},{... | collective-permute-start | bytes 2752520 | tf_op jit(solution)/shard_map/ppermute | solution.py:25
  110.7 6.1 %copy-start = (bf16[448,1024]{1,0:T(8,128)(2,1)}, bf16[448,1024]{1,0:T(8,128)(2,1)S(1)}, u32[]{:S(2)}) copy-start(bf16[448,1024]{1,0:T(8,128)(2,1)S(1)} %collective-permute-done.10.refs_0_.refs_2_) | copy-start | bytes 2752516
  110.7 30.4 %collective-permute-start.12 = (bf16[448,1024]{1,0:T(8,128)(2,1)S(1)}, bf16[448,1024]{1,0:T(8,128)(2,1)S(1)}, u32[]{:S(2)}, u32[]{:S(2)}) collective-permute-start(bf16[448,1024]{1,0:T(8,128)(2,1)S(1)} %collective-permute-done.10.refs_0_.refs_2_), channel_id=1, source_target_pairs={{0,4},{4,8},{8,12},{12,0},{64,76},{68,64},{72,68},{76,72},{1,5},{5... | collective-permute-start | bytes 2752520 | tf_op jit(solution)/shard_map/ppermute | solution.py:25
  118.4 14.4 %all-to-all-start = ((bf16[4,32,2688]{2,1,0:T(8,128)(2,1)}), bf16[4,32,2688]{2,1,0:T(8,128)(2,1)S(1)}, u32[]{:S(2)}, u32[]{:S(2)}) async-start(bf16[4,32,2688]{2,1,0:T(8,128)(2,1)} %shard_map.58), calls=%async_computation | async-start | bytes 1376256 | tf_op jit(solution)/shard_map/all_to_all | solution.py:31
  132.8 8.3 %copy-start.6 = (bf16[4,32,2688]{2,1,0:T(8,128)(2,1)}, bf16[4,32,2688]{2,1,0:T(8,128)(2,1)S(1)}, u32[]{:S(2)}) copy-start(bf16[4,32,2688]{2,1,0:T(8,128)(2,1)S(1)} %all-to-all-done.sums_ref) | copy-start | bytes 2064388
  132.8 12.9 %all-to-all-start.6 = ((bf16[4,32,1792]{2,1,0:T(8,128)(2,1)}), bf16[4,32,1792]{2,1,0:T(8,128)(2,1)}, u32[]{:S(2)}, u32[]{:S(2)}) async-start(bf16[4,32,1792]{2,1,0:T(8,128)(2,1)} %shard_map.66), calls=%async_computation.6 | async-start | bytes 917504 | tf_op jit(solution)/shard_map/all_to_all | solution.py:31
  141.1 0.9 copy-start.1
  142.1 1.0 copy-start.2
  145.7 17.0 %all-to-all-start.4 = ((bf16[4,64,1792]{2,1,0:T(8,128)(2,1)}), bf16[4,64,1792]{2,1,0:T(8,128)(2,1)S(1)}, u32[]{:S(2)}, u32[]{:S(2)}) async-start(bf16[4,64,1792]{2,1,0:T(8,128)(2,1)} %get-tuple-element.14), calls=%async_computation.4 | async-start | bytes 1835008 | tf_op jit(solution)/shard_map/all_to_all | solution.py:31
  149.7 9.4 %copy-start.15 = (s32[8,2]{0,1:T(2,128)S(1)}, s32[8,2]{0,1:T(2,128)}, u32[]{:S(2)}) copy-start(s32[8,2]{0,1:T(2,128)} %param.6) | copy-start | bytes 196
  149.7 9.4 %copy-start.16 = (f32[8,2]{0,1:T(2,128)S(1)}, f32[8,2]{0,1:T(2,128)}, u32[]{:S(2)}) copy-start(f32[8,2]{0,1:T(2,128)} %param.7) | copy-start | bytes 196
  153.2 19.1 %collective-permute-start.13 = (bf16[128,1024]{1,0:T(8,128)(2,1)}, bf16[128,1024]{1,0:T(8,128)(2,1)S(1)}, u32[]{:S(2)}, u32[]{:S(2)}) collective-permute-start(bf16[128,1024]{1,0:T(8,128)(2,1)} %shard_map.67), channel_id=1, source_target_pairs={{0,1},{1,2},{2,3},{3,0},{64,67},{65,64},{66,65},{67,66},{4,5},{5,6... | collective-permute-start | bytes 786440 | tf_op jit(solution)/shard_map/ppermute | solution.py:25
  162.7 3.5 %copy-start.5 = (bf16[4,64,1792]{2,1,0:T(8,128)(2,1)}, bf16[4,64,1792]{2,1,0:T(8,128)(2,1)S(1)}, u32[]{:S(2)}) copy-start(bf16[4,64,1792]{2,1,0:T(8,128)(2,1)S(1)} %all-to-all-done.4.refs_0_) | copy-start | bytes 2752516
  162.7 20.6 %all-to-all-start.3 = ((bf16[4,32,1792]{2,1,0:T(8,128)(2,1)}), bf16[4,32,1792]{2,1,0:T(8,128)(2,1)S(1)}, u32[]{:S(2)}, u32[]{:S(2)}) async-start(bf16[4,32,1792]{2,1,0:T(8,128)(2,1)} %get-tuple-element.13), calls=%async_computation.3 | async-start | bytes 917504 | tf_op jit(solution)/shard_map/all_to_all | solution.py:31
  166.2 16.5 %copy-start.12 = (pred[8]{0:T(512)(128)(4,1)S(1)}, pred[8]{0:T(512)(128)(4,1)}, u32[]{:S(2)}) copy-start(pred[8]{0:T(512)(128)(4,1)} %copy-done.11) | copy-start | bytes 28
  166.2 16.5 %copy-start.14 = (pred[8]{0:T(512)(128)(4,1)S(1)}, pred[8]{0:T(512)(128)(4,1)}, u32[]{:S(2)}) copy-start(pred[8]{0:T(512)(128)(4,1)} %copy-done.13) | copy-start | bytes 28
  170.3 19.2 %collective-permute-start.15 = (bf16[128,1024]{1,0:T(8,128)(2,1)}, bf16[128,1024]{1,0:T(8,128)(2,1)S(1)}, u32[]{:S(2)}, u32[]{:S(2)}) collective-permute-start(bf16[128,1024]{1,0:T(8,128)(2,1)} %get-tuple-element.16), channel_id=1, source_target_pairs={{0,3},{1,0},{2,1},{3,2},{64,65},{65,66},{66,67},{67,64},{4,7},{5,4... | collective-permute-start | bytes 786440 | tf_op jit(solution)/shard_map/ppermute | solution.py:25
  173.4 20.1 %collective-permute-start.14 = (bf16[128,1024]{1,0:T(8,128)(2,1)S(1)}, bf16[128,1024]{1,0:T(8,128)(2,1)S(1)}, u32[]{:S(2)}, u32[]{:S(2)}) collective-permute-start(bf16[128,1024]{1,0:T(8,128)(2,1)S(1)} %add_convert_fusion.2), channel_id=1, source_target_pairs={{0,1},{1,2},{2,3},{3,0},{64,67},{65,64},{66,65},{67,66},{4,5},{5,6... | collective-permute-start | bytes 786440 | tf_op jit(solution)/shard_map/ppermute | solution.py:25
  183.3 0.8 copy-start.7
  196.1 9.4 %collective-permute-start.16 = (bf16[4,64,1024]{2,1,0:T(8,128)(2,1)S(1)}, bf16[4,64,1024]{2,1,0:T(8,128)(2,1)S(1)}, u32[]{:S(2)}, u32[]{:S(2)}) collective-permute-start(bf16[4,64,1024]{2,1,0:T(8,128)(2,1)S(1)} %add_convert_fusion.1), channel_id=1, source_target_pairs={{0,64},{64,0},{1,65},{65,1},{2,66},{66,2},{3,67},{67,3},{4,68},{68... | collective-permute-start | bytes 1572872 | tf_op jit(solution)/shard_map/ppermute | solution.py:20

commit v11 on v10

--- a/solution.py
+++ b/solution.py
@@ -174,46 +174,42 @@
 def activate_far(sums):
     def kernel(sums_ref, out_ref):
         total = jnp.sum(sums_ref[...].astype(wide), axis=0)
-        hidden = jnp.concatenate([block(total, i) for i in range(4)], axis=1)
-        for j in range(4):
-            out_ref[j] = hidden
+        out_ref[...] = jnp.concatenate([block(total, i) for i in range(4)], axis=1)
 
     return pl.pallas_call(
         kernel,
         grid=(1,),
         in_specs=[pl.BlockSpec((4, 32, 3584), lambda i: (0, 0, 0))],
-        out_specs=pl.BlockSpec((4, 32, 1792), lambda i: (0, 0, 0)),
-        out_shape=jax.ShapeDtypeStruct((4, 32, 1792), half),
-        compiler_params=pltpu.CompilerParams(vmem_limit_bytes=LIMIT),
-        cost_estimate=COST,
+        out_specs=pl.BlockSpec((32, 1792), lambda i: (0, 0)),
+        out_shape=jax.ShapeDtypeStruct((32, 1792), half),
+        compiler_params=pltpu.CompilerParams(vmem_limit_bytes=LIMIT),
+        cost_estimate=LONG,
     )(sums)
 
 
-def activate_rest(sums, near, own, after):
-    def kernel(sums_ref, near_ref, own_ref, *refs):
-        outs = refs[-2:]
-        total = jnp.sum(sums_ref[...].astype(wide), axis=0)
-        blocks = [block(total, i) for i in range(3)]
-        near = jnp.concatenate([near_ref[...], jnp.concatenate(blocks[:2])], axis=1)
-        own = jnp.concatenate([own_ref[...], blocks[2]], axis=1)
-        for part, out in zip((near, own), outs):
-            for j in range(4):
-                out[j] = part
+def activate_rest(sums, begun, at, after):
+    n = begun.shape[0] // 32
+
+    def kernel(sums_ref, begun_ref, *refs):
+        total = jnp.sum(sums_ref[:, :, 896 * at : 896 * (at + n)].astype(wide), axis=0)
+        blocks = jnp.concatenate([block(total, i) for i in range(n)])
+        hidden = jnp.concatenate([begun_ref[...], blocks], axis=1)
+        for j in range(4):
+            refs[-1][j] = hidden
 
     return pl.pallas_call(
         kernel,
         grid=(1,),
         in_specs=[
             pl.BlockSpec((4, 32, 2688), lambda i: (0, 0, 0)),
-            pl.BlockSpec((64, 1344), lambda i: (0, 0)),
-            pl.BlockSpec((32, 1344), lambda i: (0, 0)),
+            pl.BlockSpec((32 * n, 1344), lambda i: (0, 0)),
         ]
         + [ANY] * len(after),
-        out_specs=[pl.BlockSpec((4, r, 1792), lambda i: (0, 0, 0)) for r in (64, 32)],
-        out_shape=[jax.ShapeDtypeStruct((4, r, 1792), half) for r in (64, 32)],
+        out_specs=pl.BlockSpec((4, 32 * n, 1792), lambda i: (0, 0, 0)),
+        out_shape=jax.ShapeDtypeStruct((4, 32 * n, 1792), half),
         compiler_params=pltpu.CompilerParams(vmem_limit_bytes=LIMIT),
         cost_estimate=COST,
-    )(sums, near, own, *after)
+    )(sums, begun, *after)
 
 
 def down(hidden, weights, types):
@@ -236,6 +232,43 @@
         compiler_params=pltpu.CompilerParams(vmem_limit_bytes=LIMIT),
         cost_estimate=COST,
     )(hidden, *weights)
+
+
+def down_far(pieces, weights, x):
+    def kernel(x_ref, *refs):
+        v_refs, out_ref = refs[4:8], refs[8]
+        v = jnp.concatenate([ref[...] for ref in v_refs])
+        rows = jnp.concatenate([ref[...] for ref in refs[:4]])
+        out = jnp.dot(rows, v, preferred_element_type=wide).astype(half)
+        for d in range(4):
+            at = pl.multiple_of(((x_ref[0] - d) & 3) * 32, 32)
+            out_ref[pl.ds(at, 32), :] = out[32 * d : 32 * d + 32]
+
+    return pl.pallas_call(
+        kernel,
+        grid=(2,),
+        in_specs=[pl.BlockSpec(memory_space=pltpu.SMEM)]
+        + [pl.BlockSpec((32, 1792), lambda i: (0, 0))] * 4
+        + [pl.BlockSpec((448, 512), lambda i: (0, i))] * 4,
+        out_specs=pl.BlockSpec((128, 512), lambda i: (0, i)),
+        out_shape=jax.ShapeDtypeStruct((128, 1024), half),
+        compiler_params=pltpu.CompilerParams(vmem_limit_bytes=LIMIT),
+        cost_estimate=LONG,
+    )(x.reshape(1), *pieces, *weights)
+
+
+def join(a, b):
+    def kernel(a_ref, b_ref, out_ref):
+        out_ref[...] = (a_ref[...] + b_ref[...].astype(wide)).astype(half)
+
+    return pl.pallas_call(
+        kernel,
+        in_specs=[WHOLE] * 2,
+        out_specs=WHOLE,
+        out_shape=jax.ShapeDtypeStruct(a.shape, half),
+        compiler_params=pltpu.CompilerParams(vmem_limit_bytes=LIMIT),
+        cost_estimate=LONG,
+    )(a, b)
 
 
 def on_device(tokens, routes, route_gates, w_in, w_down):
@@ -295,14 +328,17 @@
     far_part = late_far(far, weights + [w_far])
     rest_part = late_rest([first, second, rows], w_far, [far_part])
     far_h = activate_far(swap(far_part, "x"))
-    near_h, own_h = activate_rest(swap(rest_part, "x"), near_h, own_h, [v_second, v_far])
-
-    (far_out,) = down(swap(far_h, "x"), v_all, (half,))
+    rest = swap(rest_part, "x")
+    near_h = activate_rest(rest, near_h, 0, [v_second, v_far])
+
+    far_out = down_far([far_h] + [shift(far_h, "x", d) for d in (1, 2, 3)], v_all, lax.axis_index("x"))
     got = pass_on(far_out, "zhi", 1)
     first_out, second_out = down(swap(near_h, "x"), v_all, (half, wide))
     back = pass_on(first_out, "zhi", -1)
-    ahead = pass_on((second_out + got.astype(wide)).astype(half), "zhi", 1)
-
+    joined = join(second_out, got)
+    ahead = pass_on(joined, "zhi", 1)
+
+    own_h = activate_rest(rest, own_h, 2, [first_out])
     (own_out,) = down(swap(own_h, "x"), v_all, (wide,))
     result = (own_out + ahead.astype(wide) + back.astype(wide)).reshape(2, 64, 1024)
 

time: 230 us -> 228 us (level)
  waiting for transfers between devices: 30.8 us -> 16 us
  blocking collectives: 21.6 us -> 25 us
  Pallas kernels: 44.8 us -> 48.1 us
  starting transfers between devices: 107 us -> 110 us
  local copies, waits for them, and re-layouts: 6.12 us -> 8.74 us
    all_to_all x7 -> x6, waiting for transfers between devices: 17.9 us -> 4.35 us  [swap(): return lax.all_to_all(a, axis, split_axis=0, concat_axis=0, tiled=True)]
    ppermute x5 -> x8, starting transfers between devices: 23.9 us -> 29 us  [shift(): return lax.ppermute(a, axis, [(i, (i + by) % n) for i in range(n)])]
    pallas_call x0 -> x2, Pallas kernels: none -> 5.09 us  [the longest x1 3.23 us: down_far(): pl.pallas_call(kernel, grid=(2,), in_specs=[pl.BlockSpec(memory_space=plt...]
    all_to_all x7 -> x6, starting transfers between devices: 27.6 us -> 23.8 us  [swap(): return lax.all_to_all(a, axis, split_axis=0, concat_axis=0, tiled=True)]
    all_to_all x1, blocking collectives: 21.6 us -> 25 us  [swap(): return lax.all_to_all(a, axis, split_axis=0, concat_axis=0, tiled=True)]
    pallas_call x3 -> x2, Pallas kernels: 10.9 us -> 7.53 us  [down(): pl.pallas_call(kernel, grid=(2,), in_specs=[pl.BlockSpec((4, 32 * n, 1792...]
    unnamed x38 -> x42, local copies, waits for them, and re-layouts: 5.93 us -> 8.55 us
  transfers between devices with their start and end apart: 24 -> 26, of which waited for: 11 -> 8; matrix products, arithmetic and copies ran while one was open for 4% -> 4% of each run, Pallas kernels for 20% -> 21%
where the time goes in v11:
time: 228 us; the launch traced here: 224 us
  starting transfers between devices  110 us (48%)
  Pallas kernels  48.1 us (21%)
  blocking collectives  25 us (11%)
  waiting for transfers between devices  16 us (7%)
  other arithmetic  11.4 us (5%)
  local copies, waits for them, and re-layouts  8.74 us (4%)
  between operations  5.54 us (2%)
    ppermute x12, starting transfers between devices, pass_on(): lax.ppermute(a, ('core', axis), [(c * n + i, c * n + (i + by * (1 - 2 * c...  56.8 us
    ppermute x8, starting transfers between devices, shift(): return lax.ppermute(a, axis, [(i, (i + by) % n) for i in range(n)])  29 us
    all_to_all x1, blocking collectives, swap(): return lax.all_to_all(a, axis, split_axis=0, concat_axis=0, tiled=True)  25 us
    all_to_all x6, starting transfers between devices, swap(): return lax.all_to_all(a, axis, split_axis=0, concat_axis=0, tiled=True)  23.8 us
    pallas_call x2, Pallas kernels, early(): pl.pallas_call(kernel, in_specs=[WHOLE] * n + [ANY] * (3 + len(after)), o...  11.1 us
    ppermute x12, waiting for transfers between devices, pass_on(): lax.ppermute(a, ('core', axis), [(c * n + i, c * n + (i + by * (1 - 2 * c...  9.59 us
    unnamed x42, local copies, waits for them, and re-layouts  8.55 us
    pallas_call x2, Pallas kernels, down(): pl.pallas_call(kernel, grid=(2,), in_specs=[pl.BlockSpec((4, 32 * n, 1792...  7.53 us
  transfers between devices with their start and end apart: 26, of which 8 were waited for; matrix products, arithmetic and copies ran while one was open for 4% of the time, Pallas kernels for 21%

profile of v11, /device:TPU:1, one launch (start us, length us, event | category | flops | bytes accessed | tf_op | source)
XLA Modules:
  0.0 224.3 jit_solution(5701555661566393027)
XLA Ops:
  0.0 5.5 %collective-permute-start.6 = (bf16[896,1024]{1,0:T(8,128)(2,1)}, bf16[896,1024]{1,0:T(8,128)(2,1)S(1)}, u32[]{:S(2)}, u32[]{:S(2)}) collective-permute-start(bf16[896,1024]{1,0:T(8,128)(2,1)} %bitcast.20), channel_id=1, source_target_pairs={{0,4},{4,8},{8,12},{12,0},{64,76},{68,64},{72,68},{76,72},{1,5},{5... | collective-permute-start | bytes 5505032 | tf_op jit(solution)/shard_map/ppermute | solution.py:25
  5.5 1.9 collective-permute-start.7
  7.4 4.9 %collective-permute-start.1 = (bf16[64,1024]{1,0:T(8,128)(2,1)}, bf16[64,1024]{1,0:T(8,128)(2,1)S(1)}, u32[]{:S(2)}, u32[]{:S(2)}) collective-permute-start(bf16[64,1024]{1,0:T(8,128)(2,1)} %bitcast.17), channel_id=1, source_target_pairs={{0,256},{128,384},{256,0},{384,128},{1,257},{129,385},{257,1},{385... | collective-permute-start | bytes 393224 | tf_op jit(solution)/shard_map/ppermute | solution.py:20
  12.3 3.3 %collective-permute-start.2 = (bf16[64,1024]{1,0:T(8,128)(2,1)}, bf16[64,1024]{1,0:T(8,128)(2,1)S(1)}, u32[]{:S(2)}, u32[]{:S(2)}) collective-permute-start(bf16[64,1024]{1,0:T(8,128)(2,1)} %bitcast.18), channel_id=1, source_target_pairs={{0,384},{128,0},{256,128},{384,256},{1,385},{129,1},{257,129},{385... | collective-permute-start | bytes 393224 | tf_op jit(solution)/shard_map/ppermute | solution.py:20
  15.6 2.2 collective-permute-start
  21.7 1.8 collective-permute-done
  24.5 5.6 %collective-permute-start.3 = (bf16[128,1024]{1,0:T(8,128)(2,1)S(1)}, bf16[128,1024]{1,0:T(8,128)(2,1)S(1)}, u32[]{:S(2)}, u32[]{:S(2)}) collective-permute-start(bf16[128,1024]{1,0:T(8,128)(2,1)S(1)} %pad_maximum_fusion), channel_id=1, source_target_pairs={{0,64},{64,0},{1,65},{65,1},{2,66},{66,2},{3,67},{67,3},{4,68},{68... | collective-permute-start | bytes 786440 | tf_op jit(solution)/shard_map/ppermute | solution.py:20
  33.6 10.0 %collective-permute-start.4 = (bf16[128,1024]{1,0:T(8,128)(2,1)S(1)}, bf16[128,1024]{1,0:T(8,128)(2,1)S(1)}, u32[]{:S(2)}, u32[]{:S(2)}) collective-permute-start(bf16[128,1024]{1,0:T(8,128)(2,1)S(1)} %pad_maximum_fusion.1.refs_0_.refs_2_), channel_id=1, source_target_pairs={{0,1},{1,2},{2,3},{3,0},{64,67},{65,64},{66,65},{67,66},{4,5},{5,6... | collective-permute-start | bytes 786440 | tf_op jit(solution)/shard_map/ppermute | solution.py:25
  43.6 1.9 collective-permute-start.5
  45.6 3.3 %collective-permute-done.7.refs_3_.refs_2_.refs_4_ = bf16[896,1024]{1,0:T(8,128)(2,1)} collective-permute-done((bf16[896,1024]{1,0:T(8,128)(2,1)}, bf16[896,1024]{1,0:T(8,128)(2,1)}, u32[]{:S(2)}, u32[]{:S(2)}) %collective-permute-start.7) | collective-permute-done | bytes 1835040 | tf_op jit(solution)/shard_map/ppermute | solution.py:25
  48.9 5.5 %shard_map.55 = (bf16[896,1024]{1,0:T(8,128)(2,1)}, bf16[4,32,2688]{2,1,0:T(8,128)(2,1)}) custom-call(bf16[128,1024]{1,0:T(8,128)(2,1)} %copy-done.8, bf16[896,1024]{1,0:T(8,128)(2,1)} %bitcast.22, bf16[896,1024]{1,0:T(8,128)(2,1)} %copy-done.17, bf16[896,1024]{1,0:T(8,128)(2,1)} %collective-permute-done.7.refs_3_.refs_2_.refs_4_), custom_call_target="tpu_custom_call" | custom-call | flops 99999997952 | bytes 1024 | tf_op jit(solution)/shard_map/pallas_call | solution.py:81
  54.4 1.9 collective-permute-start.8
  56.3 4.0 %all-to-all-start.1 = ((bf16[4,32,2688]{2,1,0:T(8,128)(2,1)}), bf16[4,32,2688]{2,1,0:T(8,128)(2,1)S(1)}, u32[]{:S(2)}, u32[]{:S(2)}) async-start(bf16[4,32,2688]{2,1,0:T(8,128)(2,1)} %get-tuple-element.10.refs_0_.refs_5_), calls=%async_computation.1 | async-start | bytes 1376256 | tf_op jit(solution)/shard_map/all_to_all | solution.py:31
  60.3 1.7 collective-permute-done.4.a_ref.refs_0_
  62.8 1.7 shard_map.56
  64.5 10.7 %collective-permute-start.9 = (bf16[128,1024]{1,0:T(8,128)(2,1)}, bf16[128,1024]{1,0:T(8,128)(2,1)S(1)}, u32[]{:S(2)}, u32[]{:S(2)}) collective-permute-start(bf16[128,1024]{1,0:T(8,128)(2,1)} %shard_map.56), channel_id=1, source_target_pairs={{0,1},{1,2},{2,3},{3,0},{64,67},{65,64},{66,65},{67,66},{4,5},{5,6... | collective-permute-start | bytes 786440 | tf_op jit(solution)/shard_map/ppermute | solution.py:25
  75.9 5.6 %shard_map.60 = bf16[4,64,2688]{2,1,0:T(8,128)(2,1)} custom-call(bf16[128,1024]{1,0:T(8,128)(2,1)} %copy-done.9, bf16[128,1024]{1,0:T(8,128)(2,1)} %copy-done.10, bf16[896,1024]{1,0:T(8,128)(2,1)} %bitcast.23, bf16[896,1024]{1,0:T(8,128)(2,1)} %copy-done.17, bf16[896,1024]{1,0:T(8,128)(2,1)} %collective-permute-done.7.refs_3_.refs_2_.refs_4_, ...), custom_call_target="tpu_custom_call" | custom-call | flops 10000000000 | bytes 1024 | tf_op jit(solution)/shard_map/pallas_call | solution.py:81
  81.5 4.3 %all-to-all-start.2 = ((bf16[4,64,2688]{2,1,0:T(8,128)(2,1)}), bf16[4,64,2688]{2,1,0:T(8,128)(2,1)}, u32[]{:S(2)}, u32[]{:S(2)}) async-start(bf16[4,64,2688]{2,1,0:T(8,128)(2,1)} %shard_map.60), calls=%async_computation.2 | async-start | bytes 2752512 | tf_op jit(solution)/shard_map/all_to_all | solution.py:31
  85.9 2.2 shard_map.61
  88.1 2.3 %collective-permute-start.10 = (bf16[448,1024]{1,0:T(8,128)(2,1)}, bf16[448,1024]{1,0:T(8,128)(2,1)S(1)}, u32[]{:S(2)}, u32[]{:S(2)}) collective-permute-start(bf16[448,1024]{1,0:T(8,128)(2,1)} %shard_map.61), channel_id=1, source_target_pairs={{0,4},{4,8},{8,12},{12,0},{64,76},{68,64},{72,68},{76,72},{1,5},{5... | collective-permute-start | bytes 2752520 | tf_op jit(solution)/shard_map/ppermute | solution.py:25
  92.4 6.3 %shard_map.57.refs_4_ = bf16[4,32,3584]{2,1,0:T(8,128)(2,1)} custom-call(bf16[128,1024]{1,0:T(8,128)(2,1)} %copy-done.19, bf16[896,1024]{1,0:T(8,128)(2,1)} %bitcast.24, bf16[896,1024]{1,0:T(8,128)(2,1)} %copy-done.17, bf16[896,1024]{1,0:T(8,128)(2,1)} %collective-permute-done.7.refs_3_.refs_2_.refs_4_, bf16[896,1024]{1,0:T(8,128)(2,1)} %copy-done.7), custom_call_target="tpu_custom_call" | custom-call | flops 99999997952 | bytes 1024 | tf_op jit(solution)/shard_map/pallas_call | solution.py:112
  98.7 2.7 %all-to-all-done.2.sums_ref = bf16[4,64,2688]{2,1,0:T(8,128)(2,1)} async-done(((bf16[4,64,2688]{2,1,0:T(8,128)(2,1)}), bf16[4,64,2688]{2,1,0:T(8,128)(2,1)}, u32[]{:S(2)}, u32[]{:S(2)}) %all-to-all-start.2) | async-done | bytes 1376288 | tf_op jit(solution)/shard_map/all_to_all | solution.py:31
  101.3 4.2 %all-to-all-start.5 = ((bf16[4,32,3584]{2,1,0:T(8,128)(2,1)}), bf16[4,32,3584]{2,1,0:T(8,128)(2,1)}, u32[]{:S(2)}, u32[]{:S(2)}) async-start(bf16[4,32,3584]{2,1,0:T(8,128)(2,1)} %shard_map.57.refs_4_), calls=%async_computation.5 | async-start | bytes 1835008 | tf_op jit(solution)/shard_map/all_to_all | solution.py:31
  105.6 4.0 %collective-permute-start.11 = (bf16[448,1024]{1,0:T(8,128)(2,1)}, bf16[448,1024]{1,0:T(8,128)(2,1)S(1)}, u32[]{:S(2)}, u32[]{:S(2)}) collective-permute-start(bf16[448,1024]{1,0:T(8,128)(2,1)} %shard_map.61), channel_id=1, source_target_pairs={{0,12},{4,0},{8,4},{12,8},{64,68},{68,72},{72,76},{76,64},{1,13},{... | collective-permute-start | bytes 2752520 | tf_op jit(solution)/shard_map/ppermute | solution.py:25
  109.6 2.5 %collective-permute-start.12 = (bf16[448,1024]{1,0:T(8,128)(2,1)S(1)}, bf16[448,1024]{1,0:T(8,128)(2,1)S(1)}, u32[]{:S(2)}, u32[]{:S(2)}) collective-permute-start(bf16[448,1024]{1,0:T(8,128)(2,1)S(1)} %collective-permute-done.10.refs_0_.refs_2_.refs_5_), channel_id=1, source_target_pairs={{0,4},{4,8},{8,12},{12,0},{64,76},{68,64},{72,68},{76,72},{1,5},{5... | collective-permute-start | bytes 2752520 | tf_op jit(solution)/shard_map/ppermute | solution.py:25
  112.1 3.6 %shard_map.58 = bf16[4,32,2688]{2,1,0:T(8,128)(2,1)} custom-call(bf16[128,1024]{1,0:T(8,128)(2,1)} %copy-done.9, bf16[128,1024]{1,0:T(8,128)(2,1)} %copy-done.10, bf16[128,1024]{1,0:T(8,128)(2,1)} %copy-done.8, bf16[896,1024]{1,0:T(8,128)(2,1)} %copy-done.7, bf16[4,32,3584]{2,1,0:T(8,128)(2,1)} %shard_map.57.refs_4_), custom_call_target="tpu_custom_call" | custom-call | flops 1024 | bytes 1024 | tf_op jit(solution)/shard_map/pallas_call | solution.py:136
  115.7 1.5 all-to-all-done.5.sums_ref
  117.2 3.5 %all-to-all-start = ((bf16[4,32,2688]{2,1,0:T(8,128)(2,1)}), bf16[4,32,2688]{2,1,0:T(8,128)(2,1)S(1)}, u32[]{:S(2)}, u32[]{:S(2)}) async-start(bf16[4,32,2688]{2,1,0:T(8,128)(2,1)} %shard_map.58), calls=%async_computation | async-start | bytes 1376256 | tf_op jit(solution)/shard_map/all_to_all | solution.py:31
  120.7 2.1 shard_map.67.refs_0_
  122.7 3.3 %collective-permute-start.13 = (bf16[32,1792]{1,0:T(8,128)(2,1)}, bf16[32,1792]{1,0:T(8,128)(2,1)S(1)}, u32[]{:S(2)}, u32[]{:S(2)}) collective-permute-start(bf16[32,1792]{1,0:T(8,128)(2,1)} %shard_map.67.refs_0_), channel_id=1, source_target_pairs={{0,16},{16,32},{32,48},{48,0},{1,17},{17,33},{33,49},{49,1},{2,18}... | collective-permute-start | bytes 344072 | tf_op jit(solution)/shard_map/ppermute | solution.py:20
  126.1 4.3 %collective-permute-start.14 = (bf16[32,1792]{1,0:T(8,128)(2,1)}, bf16[32,1792]{1,0:T(8,128)(2,1)}, u32[]{:S(2)}, u32[]{:S(2)}) collective-permute-start(bf16[32,1792]{1,0:T(8,128)(2,1)} %shard_map.67.refs_0_), channel_id=1, source_target_pairs={{0,32},{16,48},{32,0},{48,16},{1,33},{17,49},{33,1},{49,17},{2,34}... | collective-permute-start | bytes 344072 | tf_op jit(solution)/shard_map/ppermute | solution.py:20
  130.4 3.1 %collective-permute-start.15 = (bf16[32,1792]{1,0:T(8,128)(2,1)}, bf16[32,1792]{1,0:T(8,128)(2,1)}, u32[]{:S(2)}, u32[]{:S(2)}) collective-permute-start(bf16[32,1792]{1,0:T(8,128)(2,1)} %shard_map.67.refs_0_), channel_id=1, source_target_pairs={{0,48},{16,0},{32,16},{48,32},{1,49},{17,1},{33,17},{49,33},{2,50}... | collective-permute-start | bytes 344072 | tf_op jit(solution)/shard_map/ppermute | solution.py:20
  133.5 2.3 %shard_map.62.begun_ref = bf16[64,1344]{1,0:T(8,128)(2,1)} custom-call(bf16[4,64,2688]{2,1,0:T(8,128)(2,1)} %all-to-all-done.2.sums_ref, bf16[448,1024]{1,0:T(8,128)(2,1)} %copy-done.2), custom_call_target="tpu_custom_call" | custom-call | flops 1024 | bytes 1024 | tf_op jit(solution)/shard_map/pallas_call | solution.py:163
  138.0 2.2 %shard_map.63 = bf16[4,64,1792]{2,1,0:T(8,128)(2,1)} custom-call(bf16[4,32,2688]{2,1,0:T(8,128)(2,1)} %copy-done.3, bf16[64,1344]{1,0:T(8,128)(2,1)} %shard_map.62.begun_ref, bf16[448,1024]{1,0:T(8,128)(2,1)} %copy-done, bf16[448,1024]{1,0:T(8,128)(2,1)} %copy-done.1), custom_call_target="tpu_custom_call" | custom-call | flops 1024 | bytes 1024 | tf_op jit(solution)/shard_map/pallas_call | solution.py:200
  140.2 3.5 %all-to-all-start.3 = ((bf16[4,64,1792]{2,1,0:T(8,128)(2,1)}), bf16[4,64,1792]{2,1,0:T(8,128)(2,1)S(1)}, u32[]{:S(2)}, u32[]{:S(2)}) async-start(bf16[4,64,1792]{2,1,0:T(8,128)(2,1)} %shard_map.63), calls=%async_computation.3 | async-start | bytes 1835008 | tf_op jit(solution)/shard_map/all_to_all | solution.py:31
  144.4 3.2 %shard_map.68 = bf16[128,1024]{1,0:T(8,128)(2,1)} custom-call(s32[1]{0:T(128)} %bitcast.7.x_ref, bf16[32,1792]{1,0:T(8,128)(2,1)} %shard_map.67.refs_0_, bf16[32,1792]{1,0:T(8,128)(2,1)} %copy-done.20, bf16[32,1792]{1,0:T(8,128)(2,1)} %collective-permute-done.14.refs_2_, bf16[32,1792]{1,0:T(8,128)(2,1)} %collective-permute-done.15.refs_3_, ...), custom_call_target="tpu_custom_call" | custom-call | flops 99999997952 | bytes 1024 | tf_op jit(solution)/shard_map/pallas_call | solution.py:247
  147.6 7.1 %collective-permute-start.16 = (bf16[128,1024]{1,0:T(8,128)(2,1)}, bf16[128,1024]{1,0:T(8,128)(2,1)S(1)}, u32[]{:S(2)}, u32[]{:S(2)}) collective-permute-start(bf16[128,1024]{1,0:T(8,128)(2,1)} %shard_map.68), channel_id=1, source_target_pairs={{0,1},{1,2},{2,3},{3,0},{64,67},{65,64},{66,65},{67,66},{4,5},{5,6... | collective-permute-start | bytes 786440 | tf_op jit(solution)/shard_map/ppermute | solution.py:25
  155.4 1.9 shard_map.59.begun_ref
  158.4 4.1 %shard_map.64 = (bf16[128,1024]{1,0:T(8,128)(2,1)}, f32[128,1024]{1,0:T(8,128)}) custom-call(bf16[4,64,1792]{2,1,0:T(8,128)(2,1)} %copy-done.5, bf16[448,1024]{1,0:T(8,128)(2,1)} %bitcast.15, bf16[448,1024]{1,0:T(8,128)(2,1)} %copy-done.2, bf16[448,1024]{1,0:T(8,128)(2,1)} %copy-done, bf16[448,1024]{1,0:T(8,128)(2,1)} %copy-done.1), custom_call_target="tpu_custom_call" | custom-call | flops 1024 | bytes 1024 | tf_op jit(solution)/shard_map/pallas_call | solution.py:225
  162.5 1.9 collective-permute-start.18
  164.4 2.1 shard_map.65
  166.5 4.2 %all-to-all-start.4 = ((bf16[4,32,1792]{2,1,0:T(8,128)(2,1)}), bf16[4,32,1792]{2,1,0:T(8,128)(2,1)S(1)}, u32[]{:S(2)}, u32[]{:S(2)}) async-start(bf16[4,32,1792]{2,1,0:T(8,128)(2,1)} %shard_map.65), calls=%async_computation.4 | async-start | bytes 917504 | tf_op jit(solution)/shard_map/all_to_all | solution.py:31
  171.3 1.9 shard_map.69
  173.2 7.1 %collective-permute-start.17 = (bf16[128,1024]{1,0:T(8,128)(2,1)}, bf16[128,1024]{1,0:T(8,128)(2,1)S(1)}, u32[]{:S(2)}, u32[]{:S(2)}) collective-permute-start(bf16[128,1024]{1,0:T(8,128)(2,1)} %shard_map.69), channel_id=1, source_target_pairs={{0,1},{1,2},{2,3},{3,0},{64,67},{65,64},{66,65},{67,66},{4,5},{5,6... | collective-permute-start | bytes 786440 | tf_op jit(solution)/shard_map/ppermute | solution.py:25
  183.9 3.4 %shard_map.66 = f32[128,1024]{1,0:T(8,128)} custom-call(bf16[4,32,1792]{2,1,0:T(8,128)(2,1)} %copy-done.6, bf16[448,1024]{1,0:T(8,128)(2,1)} %bitcast.16, bf16[448,1024]{1,0:T(8,128)(2,1)} %copy-done.2, bf16[448,1024]{1,0:T(8,128)(2,1)} %copy-done, bf16[448,1024]{1,0:T(8,128)(2,1)} %copy-done.1), custom_call_target="tpu_custom_call" | custom-call | flops 1024 | bytes 1024 | tf_op jit(solution)/shard_map/pallas_call | solution.py:225
  187.3 4.5 %collective-permute-done.17 = bf16[128,1024]{1,0:T(8,128)(2,1)S(1)} collective-permute-done((bf16[128,1024]{1,0:T(8,128)(2,1)}, bf16[128,1024]{1,0:T(8,128)(2,1)S(1)}, u32[]{:S(2)}, u32[]{:S(2)}) %collective-permute-start.17) | collective-permute-done | bytes 262176 | tf_op jit(solution)/shard_map/ppermute | solution.py:25
  194.4 2.2 collective-permute-start.19
  198.5 25.0 %all_to_all.35 = bf16[4,64,1024]{2,1,0:T(8,128)(2,1)S(1)} all-to-all(bf16[4,64,1024]{2,1,0:T(8,128)(2,1)S(1)} %add_convert_fusion), channel_id=1, replica_groups=mesh['zlo'=4,'core'=2,'x'=4,'y'=4,'zhi'=4] {'zlo'}, dimensions={0} | all-to-all | bytes 1048576 | tf_op jit(solution)/shard_map/all_to_all | solution.py:31
  (85 shorter events, 20.6 us)
Async XLA Ops:
  0.0 45.5 %collective-permute-start.6 = (bf16[896,1024]{1,0:T(8,128)(2,1)}, bf16[896,1024]{1,0:T(8,128)(2,1)S(1)}, u32[]{:S(2)}, u32[]{:S(2)}) collective-permute-start(bf16[896,1024]{1,0:T(8,128)(2,1)} %bitcast.20), channel_id=1, source_target_pairs={{0,4},{4,8},{8,12},{12,0},{64,76},{68,64},{72,68},{76,72},{1,5},{5... | collective-permute-start | bytes 5505032 | tf_op jit(solution)/shard_map/ppermute | solution.py:25
  5.5 43.4 %collective-permute-start.7 = (bf16[896,1024]{1,0:T(8,128)(2,1)}, bf16[896,1024]{1,0:T(8,128)(2,1)}, u32[]{:S(2)}, u32[]{:S(2)}) collective-permute-start(bf16[896,1024]{1,0:T(8,128)(2,1)} %bitcast.21), channel_id=1, source_target_pairs={{0,12},{4,0},{8,4},{12,8},{64,68},{68,72},{72,76},{76,64},{1,13},{... | collective-permute-start | bytes 5505032 | tf_op jit(solution)/shard_map/ppermute | solution.py:25
  7.4 14.3 %collective-permute-start.1 = (bf16[64,1024]{1,0:T(8,128)(2,1)}, bf16[64,1024]{1,0:T(8,128)(2,1)S(1)}, u32[]{:S(2)}, u32[]{:S(2)}) collective-permute-start(bf16[64,1024]{1,0:T(8,128)(2,1)} %bitcast.17), channel_id=1, source_target_pairs={{0,256},{128,384},{256,0},{384,128},{1,257},{129,385},{257,1},{385... | collective-permute-start | bytes 393224 | tf_op jit(solution)/shard_map/ppermute | solution.py:20
  12.3 9.4 %collective-permute-start.2 = (bf16[64,1024]{1,0:T(8,128)(2,1)}, bf16[64,1024]{1,0:T(8,128)(2,1)S(1)}, u32[]{:S(2)}, u32[]{:S(2)}) collective-permute-start(bf16[64,1024]{1,0:T(8,128)(2,1)} %bitcast.18), channel_id=1, source_target_pairs={{0,384},{128,0},{256,128},{384,256},{1,385},{129,1},{257,129},{385... | collective-permute-start | bytes 393224 | tf_op jit(solution)/shard_map/ppermute | solution.py:20
  15.6 7.9 %collective-permute-start = (bf16[64,1024]{1,0:T(8,128)(2,1)}, bf16[64,1024]{1,0:T(8,128)(2,1)S(1)}, u32[]{:S(2)}, u32[]{:S(2)}) collective-permute-start(bf16[64,1024]{1,0:T(8,128)(2,1)} %bitcast.19), channel_id=1, source_target_pairs={{0,128},{128,256},{256,384},{384,0},{1,129},{129,257},{257,385},{3... | collective-permute-start | bytes 393224 | tf_op jit(solution)/shard_map/ppermute | solution.py:20
  18.9 5.5 %copy-start.11 = (pred[8]{0:T(512)(128)(4,1)}, pred[8]{0:T(512)(128)(4,1)S(1)}, u32[]{:S(2)}) copy-start(pred[8]{0:T(512)(128)(4,1)S(1)} %get-tuple-element.13) | copy-start | bytes 28
  18.9 5.5 %copy-start.13 = (pred[8]{0:T(512)(128)(4,1)}, pred[8]{0:T(512)(128)(4,1)S(1)}, u32[]{:S(2)}) copy-start(pred[8]{0:T(512)(128)(4,1)S(1)} %get-tuple-element.14) | copy-start | bytes 28
  24.5 8.1 %collective-permute-start.3 = (bf16[128,1024]{1,0:T(8,128)(2,1)S(1)}, bf16[128,1024]{1,0:T(8,128)(2,1)S(1)}, u32[]{:S(2)}, u32[]{:S(2)}) collective-permute-start(bf16[128,1024]{1,0:T(8,128)(2,1)S(1)} %pad_maximum_fusion), channel_id=1, source_target_pairs={{0,64},{64,0},{1,65},{65,1},{2,66},{66,2},{3,67},{67,3},{4,68},{68... | collective-permute-start | bytes 786440 | tf_op jit(solution)/shard_map/ppermute | solution.py:20
  33.6 15.3 %copy-start.8 = (bf16[128,1024]{1,0:T(8,128)(2,1)}, bf16[128,1024]{1,0:T(8,128)(2,1)S(1)}, u32[]{:S(2)}) copy-start(bf16[128,1024]{1,0:T(8,128)(2,1)S(1)} %pad_maximum_fusion.1.refs_0_.refs_2_) | copy-start | bytes 786436
  33.6 28.5 %collective-permute-start.4 = (bf16[128,1024]{1,0:T(8,128)(2,1)S(1)}, bf16[128,1024]{1,0:T(8,128)(2,1)S(1)}, u32[]{:S(2)}, u32[]{:S(2)}) collective-permute-start(bf16[128,1024]{1,0:T(8,128)(2,1)S(1)} %pad_maximum_fusion.1.refs_0_.refs_2_), channel_id=1, source_target_pairs={{0,1},{1,2},{2,3},{3,0},{64,67},{65,64},{66,65},{67,66},{4,5},{5,6... | collective-permute-start | bytes 786440 | tf_op jit(solution)/shard_map/ppermute | solution.py:25
  43.6 31.6 %collective-permute-start.5 = (bf16[128,1024]{1,0:T(8,128)(2,1)S(1)}, bf16[128,1024]{1,0:T(8,128)(2,1)S(1)}, u32[]{:S(2)}, u32[]{:S(2)}) collective-permute-start(bf16[128,1024]{1,0:T(8,128)(2,1)S(1)} %pad_maximum_fusion.1.refs_0_.refs_2_), channel_id=1, source_target_pairs={{0,3},{1,0},{2,1},{3,2},{64,65},{65,66},{66,67},{67,64},{4,7},{5,4... | collective-permute-start | bytes 786440 | tf_op jit(solution)/shard_map/ppermute | solution.py:25
  45.5 3.4 %copy-start.17 = (bf16[896,1024]{1,0:T(8,128)(2,1)}, bf16[896,1024]{1,0:T(8,128)(2,1)S(1)}, u32[]{:S(2)}) copy-start(bf16[896,1024]{1,0:T(8,128)(2,1)S(1)} %collective-permute-done.6.refs_2_.refs_1_.refs_3_) | copy-start | bytes 5505028
  54.4 36.0 %collective-permute-start.8 = (bf16[896,1024]{1,0:T(8,128)(2,1)}, bf16[896,1024]{1,0:T(8,128)(2,1)S(1)}, u32[]{:S(2)}, u32[]{:S(2)}) collective-permute-start(bf16[896,1024]{1,0:T(8,128)(2,1)} %get-tuple-element.9), channel_id=1, source_target_pairs={{0,4},{4,8},{8,12},{12,0},{64,76},{68,64},{72,68},{76,72},{1,5},{5... | collective-permute-start | bytes 5505032 | tf_op jit(solution)/shard_map/ppermute | solution.py:25
  56.3 25.2 %all-to-all-start.1 = ((bf16[4,32,2688]{2,1,0:T(8,128)(2,1)}), bf16[4,32,2688]{2,1,0:T(8,128)(2,1)S(1)}, u32[]{:S(2)}, u32[]{:S(2)}) async-start(bf16[4,32,2688]{2,1,0:T(8,128)(2,1)} %get-tuple-element.10.refs_0_.refs_5_), calls=%async_computation.1 | async-start | bytes 1376256 | tf_op jit(solution)/shard_map/all_to_all | solution.py:31
  62.1 0.7 copy-start.9
  64.5 25.9 %collective-permute-start.9 = (bf16[128,1024]{1,0:T(8,128)(2,1)}, bf16[128,1024]{1,0:T(8,128)(2,1)S(1)}, u32[]{:S(2)}, u32[]{:S(2)}) collective-permute-start(bf16[128,1024]{1,0:T(8,128)(2,1)} %shard_map.56), channel_id=1, source_target_pairs={{0,1},{1,2},{2,3},{3,0},{64,67},{65,64},{66,65},{67,66},{4,5},{5,6... | collective-permute-start | bytes 786440 | tf_op jit(solution)/shard_map/ppermute | solution.py:25
  75.2 0.7 copy-start.10
  81.5 4.4 %copy-start.4 = (bf16[4,32,2688]{2,1,0:T(8,128)(2,1)}, bf16[4,32,2688]{2,1,0:T(8,128)(2,1)S(1)}, u32[]{:S(2)}) copy-start(bf16[4,32,2688]{2,1,0:T(8,128)(2,1)S(1)} %all-to-all-done.1.sums_ref.refs_0_) | copy-start | bytes 2064388
  81.5 19.8 %all-to-all-start.2 = ((bf16[4,64,2688]{2,1,0:T(8,128)(2,1)}), bf16[4,64,2688]{2,1,0:T(8,128)(2,1)}, u32[]{:S(2)}, u32[]{:S(2)}) async-start(bf16[4,64,2688]{2,1,0:T(8,128)(2,1)} %shard_map.60), calls=%async_computation.2 | async-start | bytes 2752512 | tf_op jit(solution)/shard_map/all_to_all | solution.py:31
  88.1 21.5 %collective-permute-start.10 = (bf16[448,1024]{1,0:T(8,128)(2,1)}, bf16[448,1024]{1,0:T(8,128)(2,1)S(1)}, u32[]{:S(2)}, u32[]{:S(2)}) collective-permute-start(bf16[448,1024]{1,0:T(8,128)(2,1)} %shard_map.61), channel_id=1, source_target_pairs={{0,4},{4,8},{8,12},{12,0},{64,76},{68,64},{72,68},{76,72},{1,5},{5... | collective-permute-start | bytes 2752520 | tf_op jit(solution)/shard_map/ppermute | solution.py:25
  90.4 0.7 copy-start.19
  91.1 1.3 copy-start.7
  101.3 15.9 %all-to-all-start.5 = ((bf16[4,32,3584]{2,1,0:T(8,128)(2,1)}), bf16[4,32,3584]{2,1,0:T(8,128)(2,1)}, u32[]{:S(2)}, u32[]{:S(2)}) async-start(bf16[4,32,3584]{2,1,0:T(8,128)(2,1)} %shard_map.57.refs_4_), calls=%async_computation.5 | async-start | bytes 1835008 | tf_op jit(solution)/shard_map/all_to_all | solution.py:31
  105.6 30.2 %collective-permute-start.11 = (bf16[448,1024]{1,0:T(8,128)(2,1)}, bf16[448,1024]{1,0:T(8,128)(2,1)S(1)}, u32[]{:S(2)}, u32[]{:S(2)}) collective-permute-start(bf16[448,1024]{1,0:T(8,128)(2,1)} %shard_map.61), channel_id=1, source_target_pairs={{0,12},{4,0},{8,4},{12,8},{64,68},{68,72},{72,76},{76,64},{1,13},{... | collective-permute-start | bytes 2752520 | tf_op jit(solution)/shard_map/ppermute | solution.py:25
  109.6 6.1 %copy-start.2 = (bf16[448,1024]{1,0:T(8,128)(2,1)}, bf16[448,1024]{1,0:T(8,128)(2,1)S(1)}, u32[]{:S(2)}) copy-start(bf16[448,1024]{1,0:T(8,128)(2,1)S(1)} %collective-permute-done.10.refs_0_.refs_2_.refs_5_) | copy-start | bytes 2752516
  109.6 26.2 %collective-permute-start.12 = (bf16[448,1024]{1,0:T(8,128)(2,1)S(1)}, bf16[448,1024]{1,0:T(8,128)(2,1)S(1)}, u32[]{:S(2)}, u32[]{:S(2)}) collective-permute-start(bf16[448,1024]{1,0:T(8,128)(2,1)S(1)} %collective-permute-done.10.refs_0_.refs_2_.refs_5_), channel_id=1, source_target_pairs={{0,4},{4,8},{8,12},{12,0},{64,76},{68,64},{72,68},{76,72},{1,5},{5... | collective-permute-start | bytes 2752520 | tf_op jit(solution)/shard_map/ppermute | solution.py:25
  117.2 18.6 %all-to-all-start = ((bf16[4,32,2688]{2,1,0:T(8,128)(2,1)}), bf16[4,32,2688]{2,1,0:T(8,128)(2,1)S(1)}, u32[]{:S(2)}, u32[]{:S(2)}) async-start(bf16[4,32,2688]{2,1,0:T(8,128)(2,1)} %shard_map.58), calls=%async_computation | async-start | bytes 1376256 | tf_op jit(solution)/shard_map/all_to_all | solution.py:31
  122.7 21.0 %collective-permute-start.13 = (bf16[32,1792]{1,0:T(8,128)(2,1)}, bf16[32,1792]{1,0:T(8,128)(2,1)S(1)}, u32[]{:S(2)}, u32[]{:S(2)}) collective-permute-start(bf16[32,1792]{1,0:T(8,128)(2,1)} %shard_map.67.refs_0_), channel_id=1, source_target_pairs={{0,16},{16,32},{32,48},{48,0},{1,17},{17,33},{33,49},{49,1},{2,18}... | collective-permute-start | bytes 344072 | tf_op jit(solution)/shard_map/ppermute | solution.py:20
  126.1 17.7 %collective-permute-start.14 = (bf16[32,1792]{1,0:T(8,128)(2,1)}, bf16[32,1792]{1,0:T(8,128)(2,1)}, u32[]{:S(2)}, u32[]{:S(2)}) collective-permute-start(bf16[32,1792]{1,0:T(8,128)(2,1)} %shard_map.67.refs_0_), channel_id=1, source_target_pairs={{0,32},{16,48},{32,0},{48,16},{1,33},{17,49},{33,1},{49,17},{2,34}... | collective-permute-start | bytes 344072 | tf_op jit(solution)/shard_map/ppermute | solution.py:20
  130.4 13.4 %collective-permute-start.15 = (bf16[32,1792]{1,0:T(8,128)(2,1)}, bf16[32,1792]{1,0:T(8,128)(2,1)}, u32[]{:S(2)}, u32[]{:S(2)}) collective-permute-start(bf16[32,1792]{1,0:T(8,128)(2,1)} %shard_map.67.refs_0_), channel_id=1, source_target_pairs={{0,48},{16,0},{32,16},{48,32},{1,49},{17,1},{33,17},{49,33},{2,50}... | collective-permute-start | bytes 344072 | tf_op jit(solution)/shard_map/ppermute | solution.py:20
  135.8 1.0 copy-start
  135.8 1.2 copy-start.3
  137.0 0.9 copy-start.1
  140.2 17.3 %all-to-all-start.3 = ((bf16[4,64,1792]{2,1,0:T(8,128)(2,1)}), bf16[4,64,1792]{2,1,0:T(8,128)(2,1)S(1)}, u32[]{:S(2)}, u32[]{:S(2)}) async-start(bf16[4,64,1792]{2,1,0:T(8,128)(2,1)} %shard_map.63), calls=%async_computation.3 | async-start | bytes 1835008 | tf_op jit(solution)/shard_map/all_to_all | solution.py:31
  143.7 0.6 copy-start.20
  144.4 10.9 %copy-start.15 = (s32[8,2]{0,1:T(2,128)S(1)}, s32[8,2]{0,1:T(2,128)}, u32[]{:S(2)}) copy-start(s32[8,2]{0,1:T(2,128)} %param.6) | copy-start | bytes 196
  144.4 10.9 %copy-start.16 = (f32[8,2]{0,1:T(2,128)S(1)}, f32[8,2]{0,1:T(2,128)}, u32[]{:S(2)}) copy-start(f32[8,2]{0,1:T(2,128)} %param.7) | copy-start | bytes 196
  147.6 23.0 %collective-permute-start.16 = (bf16[128,1024]{1,0:T(8,128)(2,1)}, bf16[128,1024]{1,0:T(8,128)(2,1)S(1)}, u32[]{:S(2)}, u32[]{:S(2)}) collective-permute-start(bf16[128,1024]{1,0:T(8,128)(2,1)} %shard_map.68), channel_id=1, source_target_pairs={{0,1},{1,2},{2,3},{3,0},{64,67},{65,64},{66,65},{67,66},{4,5},{5,6... | collective-permute-start | bytes 786440 | tf_op jit(solution)/shard_map/ppermute | solution.py:25
  157.5 0.9 copy-start.5
  162.5 24.8 %collective-permute-start.18 = (bf16[128,1024]{1,0:T(8,128)(2,1)}, bf16[128,1024]{1,0:T(8,128)(2,1)S(1)}, u32[]{:S(2)}, u32[]{:S(2)}) collective-permute-start(bf16[128,1024]{1,0:T(8,128)(2,1)} %get-tuple-element.11.refs_0_), channel_id=1, source_target_pairs={{0,3},{1,0},{2,1},{3,2},{64,65},{65,66},{66,67},{67,64},{4,7},{5,4... | collective-permute-start | bytes 786440 | tf_op jit(solution)/shard_map/ppermute | solution.py:25
  166.5 16.6 %all-to-all-start.4 = ((bf16[4,32,1792]{2,1,0:T(8,128)(2,1)}), bf16[4,32,1792]{2,1,0:T(8,128)(2,1)S(1)}, u32[]{:S(2)}, u32[]{:S(2)}) async-start(bf16[4,32,1792]{2,1,0:T(8,128)(2,1)} %shard_map.65), calls=%async_computation.4 | async-start | bytes 917504 | tf_op jit(solution)/shard_map/all_to_all | solution.py:31
  170.7 0.7 copy-start.18
  171.3 11.1 %copy-start.12 = (pred[8]{0:T(512)(128)(4,1)S(1)}, pred[8]{0:T(512)(128)(4,1)}, u32[]{:S(2)}) copy-start(pred[8]{0:T(512)(128)(4,1)} %copy-done.11) | copy-start | bytes 28
  171.3 11.1 %copy-start.14 = (pred[8]{0:T(512)(128)(4,1)S(1)}, pred[8]{0:T(512)(128)(4,1)}, u32[]{:S(2)}) copy-start(pred[8]{0:T(512)(128)(4,1)} %copy-done.13) | copy-start | bytes 28
  173.2 18.6 %collective-permute-start.17 = (bf16[128,1024]{1,0:T(8,128)(2,1)}, bf16[128,1024]{1,0:T(8,128)(2,1)S(1)}, u32[]{:S(2)}, u32[]{:S(2)}) collective-permute-start(bf16[128,1024]{1,0:T(8,128)(2,1)} %shard_map.69), channel_id=1, source_target_pairs={{0,1},{1,2},{2,3},{3,0},{64,67},{65,64},{66,65},{67,66},{4,5},{5,6... | collective-permute-start | bytes 786440 | tf_op jit(solution)/shard_map/ppermute | solution.py:25
  183.1 0.8 copy-start.6
  194.4 3.8 %collective-permute-start.19 = (bf16[4,64,1024]{2,1,0:T(8,128)(2,1)S(1)}, bf16[4,64,1024]{2,1,0:T(8,128)(2,1)S(1)}, u32[]{:S(2)}, u32[]{:S(2)}) collective-permute-start(bf16[4,64,1024]{2,1,0:T(8,128)(2,1)S(1)} %add_convert_fusion.1), channel_id=1, source_target_pairs={{0,64},{64,0},{1,65},{65,1},{2,66},{66,2},{3,67},{67,3},{4,68},{68... | collective-permute-start | bytes 1572872 | tf_op jit(solution)/shard_map/ppermute | solution.py:20

commit v12 on v11

--- a/solution.py
+++ b/solution.py
@@ -94,53 +94,42 @@
     )(*pieces, *weights, *after)
 
 
-def late_far(far, weights):
-    def kernel(far_ref, *refs):
-        out_ref, held, sums, sems, out_sems = refs[-5:]
-        copies = fetch(refs[:4], held, sems)
+def late(pieces, weights):
+    def kernel(*refs):
+        out_ref, rest_ref, held, sums, rest, sems, out_sems = refs[-7:]
+        copies = fetch(refs[4:8], held, sems)
         going = []
         for i in range(4):
             copies[i].wait()
             columns = pl.ds(896 * i, 896)
-            out = lax.dot_general(far_ref[...], held[i], DIMS, preferred_element_type=wide).astype(half)
+            out = lax.dot_general(refs[0][...], held[i], DIMS, preferred_element_type=wide).astype(half)
             sums[:, :, columns] = out.reshape(4, 32, 896)
             going.append(pltpu.make_async_copy(sums.at[:, :, columns], out_ref.at[:, :, columns], out_sems.at[i]))
             going[-1].start()
+        x = jnp.concatenate([ref[...] for ref in refs[1:4]])
+        out = lax.dot_general(x, held[3], DIMS, preferred_element_type=wide).astype(half)
+        for p in range(3):
+            rest[:, :, pl.ds(896 * p, 896)] = out[128 * p : 128 * p + 128].reshape(4, 32, 896)
+        going.append(pltpu.make_async_copy(rest, rest_ref, out_sems.at[4]))
+        going[-1].start()
         for copy in going:
             copy.wait()
 
     return pl.pallas_call(
         kernel,
-        in_specs=[WHOLE] + [ANY] * 4,
-        out_specs=ANY,
-        out_shape=jax.ShapeDtypeStruct((4, 32, 3584), half),
+        in_specs=[WHOLE] * 4 + [ANY] * 4,
+        out_specs=[ANY] * 2,
+        out_shape=[jax.ShapeDtypeStruct((4, 32, n), half) for n in (3584, 2688)],
         scratch_shapes=[
             pltpu.VMEM((4, 896, 1024), half),
             pltpu.VMEM((4, 32, 3584), half),
+            pltpu.VMEM((4, 32, 2688), half),
             pltpu.SemaphoreType.DMA((4,)),
-            pltpu.SemaphoreType.DMA((4,)),
+            pltpu.SemaphoreType.DMA((5,)),
         ],
         compiler_params=pltpu.CompilerParams(vmem_limit_bytes=LIMIT),
         cost_estimate=LONG,
-    )(far, *weights)
-
-
-def late_rest(pieces, w_far, after):
-    def kernel(*refs):
-        out_ref = refs[-1]
-        x = jnp.concatenate([ref[...] for ref in refs[:3]])
-        out = lax.dot_general(x, refs[3][...], DIMS, preferred_element_type=wide).astype(half)
-        for p in range(3):
-            out_ref[:, :, pl.ds(896 * p, 896)] = out[128 * p : 128 * p + 128].reshape(4, 32, 896)
-
-    return pl.pallas_call(
-        kernel,
-        in_specs=[WHOLE] * 4 + [ANY] * len(after),
-        out_specs=WHOLE,
-        out_shape=jax.ShapeDtypeStruct((4, 32, 2688), half),
-        compiler_params=pltpu.CompilerParams(vmem_limit_bytes=LIMIT),
-        cost_estimate=COST,
-    )(*pieces, w_far, *after)
+    )(*pieces, *weights)
 
 
 def act(gate, up):
@@ -171,20 +160,20 @@
     )(sums, *after)
 
 
-def activate_far(sums):
-    def kernel(sums_ref, out_ref):
+def activate_far(sums, after):
+    def kernel(sums_ref, after_ref, out_ref):
         total = jnp.sum(sums_ref[...].astype(wide), axis=0)
         out_ref[...] = jnp.concatenate([block(total, i) for i in range(4)], axis=1)
 
     return pl.pallas_call(
         kernel,
         grid=(1,),
-        in_specs=[pl.BlockSpec((4, 32, 3584), lambda i: (0, 0, 0))],
+        in_specs=[pl.BlockSpec((4, 32, 3584), lambda i: (0, 0, 0)), ANY],
         out_specs=pl.BlockSpec((32, 1792), lambda i: (0, 0)),
         out_shape=jax.ShapeDtypeStruct((32, 1792), half),
         compiler_params=pltpu.CompilerParams(vmem_limit_bytes=LIMIT),
         cost_estimate=LONG,
-    )(sums)
+    )(sums, after)
 
 
 def activate_rest(sums, begun, at, after):
@@ -325,9 +314,8 @@
     v_far = pass_on(v_first, "y", 1)
     v_all = [v_own, v_first, v_second, v_far]
     own_h, near_h = activate_early(own_sums, []), activate_early(swap(part, "x"), [v_first])
-    far_part = late_far(far, weights + [w_far])
-    rest_part = late_rest([first, second, rows], w_far, [far_part])
-    far_h = activate_far(swap(far_part, "x"))
+    far_part, rest_part = late([far, first, second, rows], weights + [w_far])
+    far_h = activate_far(swap(far_part, "x"), near_h)
     rest = swap(rest_part, "x")
     near_h = activate_rest(rest, near_h, 0, [v_second, v_far])
 

time: 228 us -> 225 us (0.987)
  Pallas kernels: 48.1 us -> 45.7 us
    pallas_call x2 -> x1, Pallas kernels: 9.91 us -> 7.56 us  [late(): pl.pallas_call(kernel, in_specs=[WHOLE] * 4 + [ANY] * 4, out_specs=[ANY]...]
  transfers between devices with their start and end apart: 26 -> 26, of which waited for: 8 -> 8; matrix products, arithmetic and copies ran while one was open for 4% -> 3% of each run, Pallas kernels for 21% -> 21%
where the time goes in v12:
time: 225 us; the launch traced here: 222 us
  starting transfers between devices  109 us (48%)
  Pallas kernels  45.7 us (20%)
  blocking collectives  24.9 us (11%)
  waiting for transfers between devices  17 us (8%)
  other arithmetic  11.2 us (5%)
  local copies, waits for them, and re-layouts  8.71 us (4%)
  between operations  5.56 us (2%)
    ppermute x12, starting transfers between devices, pass_on(): lax.ppermute(a, ('core', axis), [(c * n + i, c * n + (i + by * (1 - 2 * c...  56.7 us
    ppermute x8, starting transfers between devices, shift(): return lax.ppermute(a, axis, [(i, (i + by) % n) for i in range(n)])  29 us
    all_to_all x1, blocking collectives, swap(): return lax.all_to_all(a, axis, split_axis=0, concat_axis=0, tiled=True)  24.9 us
    all_to_all x6, starting transfers between devices, swap(): return lax.all_to_all(a, axis, split_axis=0, concat_axis=0, tiled=True)  23.4 us
    pallas_call x2, Pallas kernels, early(): pl.pallas_call(kernel, in_specs=[WHOLE] * n + [ANY] * (3 + len(after)), o...  11.1 us
    ppermute x12, waiting for transfers between devices, pass_on(): lax.ppermute(a, ('core', axis), [(c * n + i, c * n + (i + by * (1 - 2 * c...  9.82 us
    unnamed x42, local copies, waits for them, and re-layouts  8.52 us
    pallas_call x1, Pallas kernels, late(): pl.pallas_call(kernel, in_specs=[WHOLE] * 4 + [ANY] * 4, out_specs=[ANY]...  7.56 us
  transfers between devices with their start and end apart: 26, of which 8 were waited for; matrix products, arithmetic and copies ran while one was open for 3% of the time, Pallas kernels for 21%

profile of v12, /device:TPU:1, one launch (start us, length us, event | category | flops | bytes accessed | tf_op | source)
XLA Modules:
  0.0 222.1 jit_solution(14396521738837047426)
XLA Ops:
  0.0 5.5 %collective-permute-start.5 = (bf16[896,1024]{1,0:T(8,128)(2,1)}, bf16[896,1024]{1,0:T(8,128)(2,1)S(1)}, u32[]{:S(2)}, u32[]{:S(2)}) collective-permute-start(bf16[896,1024]{1,0:T(8,128)(2,1)} %bitcast.20), channel_id=1, source_target_pairs={{0,4},{4,8},{8,12},{12,0},{64,76},{68,64},{72,68},{76,72},{1,5},{5... | collective-permute-start | bytes 5505032 | tf_op jit(solution)/shard_map/ppermute | solution.py:25
  5.5 1.9 collective-permute-start.6
  7.4 4.9 %collective-permute-start.1 = (bf16[64,1024]{1,0:T(8,128)(2,1)}, bf16[64,1024]{1,0:T(8,128)(2,1)S(1)}, u32[]{:S(2)}, u32[]{:S(2)}) collective-permute-start(bf16[64,1024]{1,0:T(8,128)(2,1)} %bitcast.17), channel_id=1, source_target_pairs={{0,256},{128,384},{256,0},{384,128},{1,257},{129,385},{257,1},{385... | collective-permute-start | bytes 393224 | tf_op jit(solution)/shard_map/ppermute | solution.py:20
  12.3 3.3 %collective-permute-start.2 = (bf16[64,1024]{1,0:T(8,128)(2,1)}, bf16[64,1024]{1,0:T(8,128)(2,1)S(1)}, u32[]{:S(2)}, u32[]{:S(2)}) collective-permute-start(bf16[64,1024]{1,0:T(8,128)(2,1)} %bitcast.18), channel_id=1, source_target_pairs={{0,384},{128,0},{256,128},{384,256},{1,385},{129,1},{257,129},{385... | collective-permute-start | bytes 393224 | tf_op jit(solution)/shard_map/ppermute | solution.py:20
  15.6 2.2 collective-permute-start
  21.6 1.9 collective-permute-done
  24.5 5.6 %collective-permute-start.3 = (bf16[128,1024]{1,0:T(8,128)(2,1)S(1)}, bf16[128,1024]{1,0:T(8,128)(2,1)S(1)}, u32[]{:S(2)}, u32[]{:S(2)}) collective-permute-start(bf16[128,1024]{1,0:T(8,128)(2,1)S(1)} %pad_maximum_fusion), channel_id=1, source_target_pairs={{0,64},{64,0},{1,65},{65,1},{2,66},{66,2},{3,67},{67,3},{4,68},{68... | collective-permute-start | bytes 786440 | tf_op jit(solution)/shard_map/ppermute | solution.py:20
  33.5 10.0 %collective-permute-start.4 = (bf16[128,1024]{1,0:T(8,128)(2,1)S(1)}, bf16[128,1024]{1,0:T(8,128)(2,1)S(1)}, u32[]{:S(2)}, u32[]{:S(2)}) collective-permute-start(bf16[128,1024]{1,0:T(8,128)(2,1)S(1)} %pad_maximum_fusion.1.refs_0_.refs_3_), channel_id=1, source_target_pairs={{0,1},{1,2},{2,3},{3,0},{64,67},{65,64},{66,65},{67,66},{4,5},{5,6... | collective-permute-start | bytes 786440 | tf_op jit(solution)/shard_map/ppermute | solution.py:25
  43.5 1.9 collective-permute-start.8
  45.5 3.4 %collective-permute-done.6.refs_3_.refs_6_.refs_4_ = bf16[896,1024]{1,0:T(8,128)(2,1)} collective-permute-done((bf16[896,1024]{1,0:T(8,128)(2,1)}, bf16[896,1024]{1,0:T(8,128)(2,1)}, u32[]{:S(2)}, u32[]{:S(2)}) %collective-permute-start.6) | collective-permute-done | bytes 1835040 | tf_op jit(solution)/shard_map/ppermute | solution.py:25
  48.9 5.4 %shard_map.55 = (bf16[896,1024]{1,0:T(8,128)(2,1)}, bf16[4,32,2688]{2,1,0:T(8,128)(2,1)}) custom-call(bf16[128,1024]{1,0:T(8,128)(2,1)} %copy-done.7, bf16[896,1024]{1,0:T(8,128)(2,1)} %bitcast.22, bf16[896,1024]{1,0:T(8,128)(2,1)} %copy-done.14, bf16[896,1024]{1,0:T(8,128)(2,1)} %collective-permute-done.6.refs_3_.refs_6_.refs_4_), custom_call_target="tpu_custom_call" | custom-call | flops 99999997952 | bytes 1024 | tf_op jit(solution)/shard_map/pallas_call | solution.py:81
  54.3 1.9 collective-permute-start.9
  56.3 4.0 %all-to-all-start.1 = ((bf16[4,32,2688]{2,1,0:T(8,128)(2,1)}), bf16[4,32,2688]{2,1,0:T(8,128)(2,1)S(1)}, u32[]{:S(2)}, u32[]{:S(2)}) async-start(bf16[4,32,2688]{2,1,0:T(8,128)(2,1)} %get-tuple-element.11.refs_0_.refs_5_), calls=%async_computation.1 | async-start | bytes 1376256 | tf_op jit(solution)/shard_map/all_to_all | solution.py:31
  60.3 1.7 collective-permute-done.4.a_ref.refs_1_.refs_0_
  62.7 1.7 shard_map.56
  64.4 10.8 %collective-permute-start.7 = (bf16[128,1024]{1,0:T(8,128)(2,1)}, bf16[128,1024]{1,0:T(8,128)(2,1)S(1)}, u32[]{:S(2)}, u32[]{:S(2)}) collective-permute-start(bf16[128,1024]{1,0:T(8,128)(2,1)} %shard_map.56), channel_id=1, source_target_pairs={{0,1},{1,2},{2,3},{3,0},{64,67},{65,64},{66,65},{67,66},{4,5},{5,6... | collective-permute-start | bytes 786440 | tf_op jit(solution)/shard_map/ppermute | solution.py:25
  75.8 5.6 %shard_map.59 = bf16[4,64,2688]{2,1,0:T(8,128)(2,1)} custom-call(bf16[128,1024]{1,0:T(8,128)(2,1)} %copy-done.16, bf16[128,1024]{1,0:T(8,128)(2,1)} %copy-done.17, bf16[896,1024]{1,0:T(8,128)(2,1)} %bitcast.23, bf16[896,1024]{1,0:T(8,128)(2,1)} %copy-done.14, bf16[896,1024]{1,0:T(8,128)(2,1)} %collective-permute-done.6.refs_3_.refs_6_.refs_4_, ...), custom_call_target="tpu_custom_call" | custom-call | flops 10000000000 | bytes 1024 | tf_op jit(solution)/shard_map/pallas_call | solution.py:81
  81.5 4.3 %all-to-all-start.2 = ((bf16[4,64,2688]{2,1,0:T(8,128)(2,1)}), bf16[4,64,2688]{2,1,0:T(8,128)(2,1)}, u32[]{:S(2)}, u32[]{:S(2)}) async-start(bf16[4,64,2688]{2,1,0:T(8,128)(2,1)} %shard_map.59), calls=%async_computation.2 | async-start | bytes 2752512 | tf_op jit(solution)/shard_map/all_to_all | solution.py:31
  85.9 2.2 %shard_map.60 = bf16[448,1024]{1,0:T(8,128)(2,1)} custom-call(bf16[448,1024]{1,0:T(8,128)(2,1)} %bitcast.13, bf16[4,32,2688]{2,1,0:T(8,128)(2,1)} %copy-done.4), custom_call_target="tpu_custom_call" | custom-call | flops 1024 | bytes 1024 | tf_op jit(solution)/shard_map/pallas_call | solution.py:41
  88.1 2.3 %collective-permute-start.10 = (bf16[448,1024]{1,0:T(8,128)(2,1)}, bf16[448,1024]{1,0:T(8,128)(2,1)S(1)}, u32[]{:S(2)}, u32[]{:S(2)}) collective-permute-start(bf16[448,1024]{1,0:T(8,128)(2,1)} %shard_map.60), channel_id=1, source_target_pairs={{0,4},{4,8},{8,12},{12,0},{64,76},{68,64},{72,68},{76,72},{1,5},{5... | collective-permute-start | bytes 2752520 | tf_op jit(solution)/shard_map/ppermute | solution.py:25
  92.4 7.6 %shard_map.57 = (bf16[4,32,3584]{2,1,0:T(8,128)(2,1)}, bf16[4,32,2688]{2,1,0:T(8,128)(2,1)}) custom-call(bf16[128,1024]{1,0:T(8,128)(2,1)} %copy-done.18, bf16[128,1024]{1,0:T(8,128)(2,1)} %copy-done.16, bf16[128,1024]{1,0:T(8,128)(2,1)} %copy-done.17, bf16[128,1024]{1,0:T(8,128)(2,1)} %copy-done.7, bf16[896,1024]{1,0:T(8,128)(2,1)} %bitcast.24, ...), custom_call_target="tpu_custom_call" | custom-call | flops 99999997952 | bytes 1024 | tf_op jit(solution)/shard_map/pallas_call | solution.py:118
  99.9 1.4 all-to-all-done.2.sums_ref
  101.3 4.2 %all-to-all-start.5 = ((bf16[4,32,3584]{2,1,0:T(8,128)(2,1)}), bf16[4,32,3584]{2,1,0:T(8,128)(2,1)}, u32[]{:S(2)}, u32[]{:S(2)}) async-start(bf16[4,32,3584]{2,1,0:T(8,128)(2,1)} %get-tuple-element.16), calls=%async_computation.5 | async-start | bytes 1835008 | tf_op jit(solution)/shard_map/all_to_all | solution.py:31
  105.6 4.0 %collective-permute-start.11 = (bf16[448,1024]{1,0:T(8,128)(2,1)}, bf16[448,1024]{1,0:T(8,128)(2,1)S(1)}, u32[]{:S(2)}, u32[]{:S(2)}) collective-permute-start(bf16[448,1024]{1,0:T(8,128)(2,1)} %shard_map.60), channel_id=1, source_target_pairs={{0,12},{4,0},{8,4},{12,8},{64,68},{68,72},{72,76},{76,64},{1,13},{... | collective-permute-start | bytes 2752520 | tf_op jit(solution)/shard_map/ppermute | solution.py:25
  109.6 2.5 %collective-permute-start.12 = (bf16[448,1024]{1,0:T(8,128)(2,1)S(1)}, bf16[448,1024]{1,0:T(8,128)(2,1)S(1)}, u32[]{:S(2)}, u32[]{:S(2)}) collective-permute-start(bf16[448,1024]{1,0:T(8,128)(2,1)S(1)} %collective-permute-done.10.refs_0_.refs_2_.refs_5_), channel_id=1, source_target_pairs={{0,4},{4,8},{8,12},{12,0},{64,76},{68,64},{72,68},{76,72},{1,5},{5... | collective-permute-start | bytes 2752520 | tf_op jit(solution)/shard_map/ppermute | solution.py:25
  112.1 2.3 %shard_map.61.begun_ref.after_ref = bf16[64,1344]{1,0:T(8,128)(2,1)} custom-call(bf16[4,64,2688]{2,1,0:T(8,128)(2,1)} %all-to-all-done.2.sums_ref, bf16[448,1024]{1,0:T(8,128)(2,1)} %copy-done.2), custom_call_target="tpu_custom_call" | custom-call | flops 1024 | bytes 1024 | tf_op jit(solution)/shard_map/pallas_call | solution.py:152
  114.4 2.9 %all-to-all-done.5.sums_ref = bf16[4,32,3584]{2,1,0:T(8,128)(2,1)} async-done(((bf16[4,32,3584]{2,1,0:T(8,128)(2,1)}), bf16[4,32,3584]{2,1,0:T(8,128)(2,1)}, u32[]{:S(2)}, u32[]{:S(2)}) %all-to-all-start.5) | async-done | bytes 917536 | tf_op jit(solution)/shard_map/all_to_all | solution.py:31
  117.3 3.5 %all-to-all-start = ((bf16[4,32,2688]{2,1,0:T(8,128)(2,1)}), bf16[4,32,2688]{2,1,0:T(8,128)(2,1)S(1)}, u32[]{:S(2)}, u32[]{:S(2)}) async-start(bf16[4,32,2688]{2,1,0:T(8,128)(2,1)} %get-tuple-element.13), calls=%async_computation | async-start | bytes 1376256 | tf_op jit(solution)/shard_map/all_to_all | solution.py:31
  120.8 2.1 shard_map.66.refs_0_
  122.8 3.3 %collective-permute-start.13 = (bf16[32,1792]{1,0:T(8,128)(2,1)}, bf16[32,1792]{1,0:T(8,128)(2,1)S(1)}, u32[]{:S(2)}, u32[]{:S(2)}) collective-permute-start(bf16[32,1792]{1,0:T(8,128)(2,1)} %shard_map.66.refs_0_), channel_id=1, source_target_pairs={{0,16},{16,32},{32,48},{48,0},{1,17},{17,33},{33,49},{49,1},{2,18}... | collective-permute-start | bytes 344072 | tf_op jit(solution)/shard_map/ppermute | solution.py:20
  126.2 4.3 %collective-permute-start.14 = (bf16[32,1792]{1,0:T(8,128)(2,1)}, bf16[32,1792]{1,0:T(8,128)(2,1)}, u32[]{:S(2)}, u32[]{:S(2)}) collective-permute-start(bf16[32,1792]{1,0:T(8,128)(2,1)} %shard_map.66.refs_0_), channel_id=1, source_target_pairs={{0,32},{16,48},{32,0},{48,16},{1,33},{17,49},{33,1},{49,17},{2,34}... | collective-permute-start | bytes 344072 | tf_op jit(solution)/shard_map/ppermute | solution.py:20
  130.5 3.1 %collective-permute-start.15 = (bf16[32,1792]{1,0:T(8,128)(2,1)}, bf16[32,1792]{1,0:T(8,128)(2,1)}, u32[]{:S(2)}, u32[]{:S(2)}) collective-permute-start(bf16[32,1792]{1,0:T(8,128)(2,1)} %shard_map.66.refs_0_), channel_id=1, source_target_pairs={{0,48},{16,0},{32,16},{48,32},{1,49},{17,1},{33,17},{49,33},{2,50}... | collective-permute-start | bytes 344072 | tf_op jit(solution)/shard_map/ppermute | solution.py:20
  135.8 2.3 %shard_map.62 = bf16[4,64,1792]{2,1,0:T(8,128)(2,1)} custom-call(bf16[4,32,2688]{2,1,0:T(8,128)(2,1)} %copy-done.3, bf16[64,1344]{1,0:T(8,128)(2,1)} %shard_map.61.begun_ref.after_ref, bf16[448,1024]{1,0:T(8,128)(2,1)} %copy-done, bf16[448,1024]{1,0:T(8,128)(2,1)} %copy-done.1), custom_call_target="tpu_custom_call" | custom-call | flops 1024 | bytes 1024 | tf_op jit(solution)/shard_map/pallas_call | solution.py:189
  138.0 3.5 %all-to-all-start.3 = ((bf16[4,64,1792]{2,1,0:T(8,128)(2,1)}), bf16[4,64,1792]{2,1,0:T(8,128)(2,1)S(1)}, u32[]{:S(2)}, u32[]{:S(2)}) async-start(bf16[4,64,1792]{2,1,0:T(8,128)(2,1)} %shard_map.62), calls=%async_computation.3 | async-start | bytes 1835008 | tf_op jit(solution)/shard_map/all_to_all | solution.py:31
  142.2 3.2 %shard_map.67 = bf16[128,1024]{1,0:T(8,128)(2,1)} custom-call(s32[1]{0:T(128)} %bitcast.7.x_ref, bf16[32,1792]{1,0:T(8,128)(2,1)} %shard_map.66.refs_0_, bf16[32,1792]{1,0:T(8,128)(2,1)} %copy-done.20, bf16[32,1792]{1,0:T(8,128)(2,1)} %collective-permute-done.14.refs_2_, bf16[32,1792]{1,0:T(8,128)(2,1)} %collective-permute-done.15.refs_3_, ...), custom_call_target="tpu_custom_call" | custom-call | flops 99999997952 | bytes 1024 | tf_op jit(solution)/shard_map/pallas_call | solution.py:236
  145.5 7.0 %collective-permute-start.16 = (bf16[128,1024]{1,0:T(8,128)(2,1)}, bf16[128,1024]{1,0:T(8,128)(2,1)S(1)}, u32[]{:S(2)}, u32[]{:S(2)}) collective-permute-start(bf16[128,1024]{1,0:T(8,128)(2,1)} %shard_map.67), channel_id=1, source_target_pairs={{0,1},{1,2},{2,3},{3,0},{64,67},{65,64},{66,65},{67,66},{4,5},{5,6... | collective-permute-start | bytes 786440 | tf_op jit(solution)/shard_map/ppermute | solution.py:25
  153.2 1.9 shard_map.58.begun_ref
  156.6 4.1 %shard_map.63 = (bf16[128,1024]{1,0:T(8,128)(2,1)}, f32[128,1024]{1,0:T(8,128)}) custom-call(bf16[4,64,1792]{2,1,0:T(8,128)(2,1)} %copy-done.5, bf16[448,1024]{1,0:T(8,128)(2,1)} %bitcast.15, bf16[448,1024]{1,0:T(8,128)(2,1)} %copy-done.2, bf16[448,1024]{1,0:T(8,128)(2,1)} %copy-done, bf16[448,1024]{1,0:T(8,128)(2,1)} %copy-done.1), custom_call_target="tpu_custom_call" | custom-call | flops 1024 | bytes 1024 | tf_op jit(solution)/shard_map/pallas_call | solution.py:214
  160.7 1.9 collective-permute-start.18
  162.6 2.1 shard_map.64
  164.7 3.8 %all-to-all-start.4 = ((bf16[4,32,1792]{2,1,0:T(8,128)(2,1)}), bf16[4,32,1792]{2,1,0:T(8,128)(2,1)S(1)}, u32[]{:S(2)}, u32[]{:S(2)}) async-start(bf16[4,32,1792]{2,1,0:T(8,128)(2,1)} %shard_map.64), calls=%async_computation.4 | async-start | bytes 917504 | tf_op jit(solution)/shard_map/all_to_all | solution.py:31
  169.2 1.9 shard_map.68
  171.1 7.0 %collective-permute-start.17 = (bf16[128,1024]{1,0:T(8,128)(2,1)}, bf16[128,1024]{1,0:T(8,128)(2,1)S(1)}, u32[]{:S(2)}, u32[]{:S(2)}) collective-permute-start(bf16[128,1024]{1,0:T(8,128)(2,1)} %shard_map.68), channel_id=1, source_target_pairs={{0,1},{1,2},{2,3},{3,0},{64,67},{65,64},{66,65},{67,66},{4,5},{5,6... | collective-permute-start | bytes 786440 | tf_op jit(solution)/shard_map/ppermute | solution.py:25
  181.6 3.4 %shard_map.65 = f32[128,1024]{1,0:T(8,128)} custom-call(bf16[4,32,1792]{2,1,0:T(8,128)(2,1)} %copy-done.6, bf16[448,1024]{1,0:T(8,128)(2,1)} %bitcast.16, bf16[448,1024]{1,0:T(8,128)(2,1)} %copy-done.2, bf16[448,1024]{1,0:T(8,128)(2,1)} %copy-done, bf16[448,1024]{1,0:T(8,128)(2,1)} %copy-done.1), custom_call_target="tpu_custom_call" | custom-call | flops 1024 | bytes 1024 | tf_op jit(solution)/shard_map/pallas_call | solution.py:214
  185.0 4.7 %collective-permute-done.17 = bf16[128,1024]{1,0:T(8,128)(2,1)S(1)} collective-permute-done((bf16[128,1024]{1,0:T(8,128)(2,1)}, bf16[128,1024]{1,0:T(8,128)(2,1)S(1)}, u32[]{:S(2)}, u32[]{:S(2)}) %collective-permute-start.17) | collective-permute-done | bytes 262176 | tf_op jit(solution)/shard_map/ppermute | solution.py:25
  190.9 1.4 slice_multiply_fusion.1
  192.4 2.2 collective-permute-start.19
  196.5 24.9 %all_to_all.35 = bf16[4,64,1024]{2,1,0:T(8,128)(2,1)S(1)} all-to-all(bf16[4,64,1024]{2,1,0:T(8,128)(2,1)S(1)} %add_convert_fusion), channel_id=1, replica_groups=mesh['zlo'=4,'core'=2,'x'=4,'y'=4,'zhi'=4] {'zlo'}, dimensions={0} | all-to-all | bytes 1048576 | tf_op jit(solution)/shard_map/all_to_all | solution.py:31
  (84 shorter events, 19.6 us)
Async XLA Ops:
  0.0 45.5 %collective-permute-start.5 = (bf16[896,1024]{1,0:T(8,128)(2,1)}, bf16[896,1024]{1,0:T(8,128)(2,1)S(1)}, u32[]{:S(2)}, u32[]{:S(2)}) collective-permute-start(bf16[896,1024]{1,0:T(8,128)(2,1)} %bitcast.20), channel_id=1, source_target_pairs={{0,4},{4,8},{8,12},{12,0},{64,76},{68,64},{72,68},{76,72},{1,5},{5... | collective-permute-start | bytes 5505032 | tf_op jit(solution)/shard_map/ppermute | solution.py:25
  5.5 43.4 %collective-permute-start.6 = (bf16[896,1024]{1,0:T(8,128)(2,1)}, bf16[896,1024]{1,0:T(8,128)(2,1)}, u32[]{:S(2)}, u32[]{:S(2)}) collective-permute-start(bf16[896,1024]{1,0:T(8,128)(2,1)} %bitcast.21), channel_id=1, source_target_pairs={{0,12},{4,0},{8,4},{12,8},{64,68},{68,72},{72,76},{76,64},{1,13},{... | collective-permute-start | bytes 5505032 | tf_op jit(solution)/shard_map/ppermute | solution.py:25
  7.4 14.2 %collective-permute-start.1 = (bf16[64,1024]{1,0:T(8,128)(2,1)}, bf16[64,1024]{1,0:T(8,128)(2,1)S(1)}, u32[]{:S(2)}, u32[]{:S(2)}) collective-permute-start(bf16[64,1024]{1,0:T(8,128)(2,1)} %bitcast.17), channel_id=1, source_target_pairs={{0,256},{128,384},{256,0},{384,128},{1,257},{129,385},{257,1},{385... | collective-permute-start | bytes 393224 | tf_op jit(solution)/shard_map/ppermute | solution.py:20
  12.3 9.3 %collective-permute-start.2 = (bf16[64,1024]{1,0:T(8,128)(2,1)}, bf16[64,1024]{1,0:T(8,128)(2,1)S(1)}, u32[]{:S(2)}, u32[]{:S(2)}) collective-permute-start(bf16[64,1024]{1,0:T(8,128)(2,1)} %bitcast.18), channel_id=1, source_target_pairs={{0,384},{128,0},{256,128},{384,256},{1,385},{129,1},{257,129},{385... | collective-permute-start | bytes 393224 | tf_op jit(solution)/shard_map/ppermute | solution.py:20
  15.6 7.9 %collective-permute-start = (bf16[64,1024]{1,0:T(8,128)(2,1)}, bf16[64,1024]{1,0:T(8,128)(2,1)S(1)}, u32[]{:S(2)}, u32[]{:S(2)}) collective-permute-start(bf16[64,1024]{1,0:T(8,128)(2,1)} %bitcast.19), channel_id=1, source_target_pairs={{0,128},{128,256},{256,384},{384,0},{1,129},{129,257},{257,385},{3... | collective-permute-start | bytes 393224 | tf_op jit(solution)/shard_map/ppermute | solution.py:20
  18.9 5.5 %copy-start.8 = (pred[8]{0:T(512)(128)(4,1)}, pred[8]{0:T(512)(128)(4,1)S(1)}, u32[]{:S(2)}) copy-start(pred[8]{0:T(512)(128)(4,1)S(1)} %get-tuple-element.17) | copy-start | bytes 28
  18.9 5.5 %copy-start.10 = (pred[8]{0:T(512)(128)(4,1)}, pred[8]{0:T(512)(128)(4,1)S(1)}, u32[]{:S(2)}) copy-start(pred[8]{0:T(512)(128)(4,1)S(1)} %get-tuple-element.18) | copy-start | bytes 28
  24.5 8.1 %collective-permute-start.3 = (bf16[128,1024]{1,0:T(8,128)(2,1)S(1)}, bf16[128,1024]{1,0:T(8,128)(2,1)S(1)}, u32[]{:S(2)}, u32[]{:S(2)}) collective-permute-start(bf16[128,1024]{1,0:T(8,128)(2,1)S(1)} %pad_maximum_fusion), channel_id=1, source_target_pairs={{0,64},{64,0},{1,65},{65,1},{2,66},{66,2},{3,67},{67,3},{4,68},{68... | collective-permute-start | bytes 786440 | tf_op jit(solution)/shard_map/ppermute | solution.py:20
  33.5 15.4 %copy-start.7 = (bf16[128,1024]{1,0:T(8,128)(2,1)}, bf16[128,1024]{1,0:T(8,128)(2,1)S(1)}, u32[]{:S(2)}) copy-start(bf16[128,1024]{1,0:T(8,128)(2,1)S(1)} %pad_maximum_fusion.1.refs_0_.refs_3_) | copy-start | bytes 786436
  33.5 28.5 %collective-permute-start.4 = (bf16[128,1024]{1,0:T(8,128)(2,1)S(1)}, bf16[128,1024]{1,0:T(8,128)(2,1)S(1)}, u32[]{:S(2)}, u32[]{:S(2)}) collective-permute-start(bf16[128,1024]{1,0:T(8,128)(2,1)S(1)} %pad_maximum_fusion.1.refs_0_.refs_3_), channel_id=1, source_target_pairs={{0,1},{1,2},{2,3},{3,0},{64,67},{65,64},{66,65},{67,66},{4,5},{5,6... | collective-permute-start | bytes 786440 | tf_op jit(solution)/shard_map/ppermute | solution.py:25
  43.5 31.6 %collective-permute-start.8 = (bf16[128,1024]{1,0:T(8,128)(2,1)S(1)}, bf16[128,1024]{1,0:T(8,128)(2,1)S(1)}, u32[]{:S(2)}, u32[]{:S(2)}) collective-permute-start(bf16[128,1024]{1,0:T(8,128)(2,1)S(1)} %pad_maximum_fusion.1.refs_0_.refs_3_), channel_id=1, source_target_pairs={{0,3},{1,0},{2,1},{3,2},{64,65},{65,66},{66,67},{67,64},{4,7},{5,4... | collective-permute-start | bytes 786440 | tf_op jit(solution)/shard_map/ppermute | solution.py:25
  45.5 3.4 %copy-start.14 = (bf16[896,1024]{1,0:T(8,128)(2,1)}, bf16[896,1024]{1,0:T(8,128)(2,1)S(1)}, u32[]{:S(2)}) copy-start(bf16[896,1024]{1,0:T(8,128)(2,1)S(1)} %collective-permute-done.5.refs_2_.refs_5_.refs_3_) | copy-start | bytes 5505028
  54.3 36.1 %collective-permute-start.9 = (bf16[896,1024]{1,0:T(8,128)(2,1)}, bf16[896,1024]{1,0:T(8,128)(2,1)S(1)}, u32[]{:S(2)}, u32[]{:S(2)}) collective-permute-start(bf16[896,1024]{1,0:T(8,128)(2,1)} %get-tuple-element.12), channel_id=1, source_target_pairs={{0,4},{4,8},{8,12},{12,0},{64,76},{68,64},{72,68},{76,72},{1,5},{5... | collective-permute-start | bytes 5505032 | tf_op jit(solution)/shard_map/ppermute | solution.py:25
  56.3 25.2 %all-to-all-start.1 = ((bf16[4,32,2688]{2,1,0:T(8,128)(2,1)}), bf16[4,32,2688]{2,1,0:T(8,128)(2,1)S(1)}, u32[]{:S(2)}, u32[]{:S(2)}) async-start(bf16[4,32,2688]{2,1,0:T(8,128)(2,1)} %get-tuple-element.11.refs_0_.refs_5_), calls=%async_computation.1 | async-start | bytes 1376256 | tf_op jit(solution)/shard_map/all_to_all | solution.py:31
  62.0 0.7 copy-start.16
  64.4 26.0 %collective-permute-start.7 = (bf16[128,1024]{1,0:T(8,128)(2,1)}, bf16[128,1024]{1,0:T(8,128)(2,1)S(1)}, u32[]{:S(2)}, u32[]{:S(2)}) collective-permute-start(bf16[128,1024]{1,0:T(8,128)(2,1)} %shard_map.56), channel_id=1, source_target_pairs={{0,1},{1,2},{2,3},{3,0},{64,67},{65,64},{66,65},{67,66},{4,5},{5,6... | collective-permute-start | bytes 786440 | tf_op jit(solution)/shard_map/ppermute | solution.py:25
  75.2 0.7 copy-start.17
  81.5 4.3 %copy-start.4 = (bf16[4,32,2688]{2,1,0:T(8,128)(2,1)}, bf16[4,32,2688]{2,1,0:T(8,128)(2,1)S(1)}, u32[]{:S(2)}) copy-start(bf16[4,32,2688]{2,1,0:T(8,128)(2,1)S(1)} %all-to-all-done.1.sums_ref.refs_0_) | copy-start | bytes 2064388
  81.5 19.8 %all-to-all-start.2 = ((bf16[4,64,2688]{2,1,0:T(8,128)(2,1)}), bf16[4,64,2688]{2,1,0:T(8,128)(2,1)}, u32[]{:S(2)}, u32[]{:S(2)}) async-start(bf16[4,64,2688]{2,1,0:T(8,128)(2,1)} %shard_map.59), calls=%async_computation.2 | async-start | bytes 2752512 | tf_op jit(solution)/shard_map/all_to_all | solution.py:31
  88.1 21.5 %collective-permute-start.10 = (bf16[448,1024]{1,0:T(8,128)(2,1)}, bf16[448,1024]{1,0:T(8,128)(2,1)S(1)}, u32[]{:S(2)}, u32[]{:S(2)}) collective-permute-start(bf16[448,1024]{1,0:T(8,128)(2,1)} %shard_map.60), channel_id=1, source_target_pairs={{0,4},{4,8},{8,12},{12,0},{64,76},{68,64},{72,68},{76,72},{1,5},{5... | collective-permute-start | bytes 2752520 | tf_op jit(solution)/shard_map/ppermute | solution.py:25
  90.4 0.7 copy-start.18
  91.1 1.3 copy-start.15
  101.3 16.0 %all-to-all-start.5 = ((bf16[4,32,3584]{2,1,0:T(8,128)(2,1)}), bf16[4,32,3584]{2,1,0:T(8,128)(2,1)}, u32[]{:S(2)}, u32[]{:S(2)}) async-start(bf16[4,32,3584]{2,1,0:T(8,128)(2,1)} %get-tuple-element.16), calls=%async_computation.5 | async-start | bytes 1835008 | tf_op jit(solution)/shard_map/all_to_all | solution.py:31
  105.6 28.0 %collective-permute-start.11 = (bf16[448,1024]{1,0:T(8,128)(2,1)}, bf16[448,1024]{1,0:T(8,128)(2,1)S(1)}, u32[]{:S(2)}, u32[]{:S(2)}) collective-permute-start(bf16[448,1024]{1,0:T(8,128)(2,1)} %shard_map.60), channel_id=1, source_target_pairs={{0,12},{4,0},{8,4},{12,8},{64,68},{68,72},{72,76},{76,64},{1,13},{... | collective-permute-start | bytes 2752520 | tf_op jit(solution)/shard_map/ppermute | solution.py:25
  109.6 2.5 %copy-start.2 = (bf16[448,1024]{1,0:T(8,128)(2,1)}, bf16[448,1024]{1,0:T(8,128)(2,1)S(1)}, u32[]{:S(2)}) copy-start(bf16[448,1024]{1,0:T(8,128)(2,1)S(1)} %collective-permute-done.10.refs_0_.refs_2_.refs_5_) | copy-start | bytes 2752516
  109.6 24.0 %collective-permute-start.12 = (bf16[448,1024]{1,0:T(8,128)(2,1)S(1)}, bf16[448,1024]{1,0:T(8,128)(2,1)S(1)}, u32[]{:S(2)}, u32[]{:S(2)}) collective-permute-start(bf16[448,1024]{1,0:T(8,128)(2,1)S(1)} %collective-permute-done.10.refs_0_.refs_2_.refs_5_), channel_id=1, source_target_pairs={{0,4},{4,8},{8,12},{12,0},{64,76},{68,64},{72,68},{76,72},{1,5},{5... | collective-permute-start | bytes 2752520 | tf_op jit(solution)/shard_map/ppermute | solution.py:25
  117.3 16.3 %all-to-all-start = ((bf16[4,32,2688]{2,1,0:T(8,128)(2,1)}), bf16[4,32,2688]{2,1,0:T(8,128)(2,1)S(1)}, u32[]{:S(2)}, u32[]{:S(2)}) async-start(bf16[4,32,2688]{2,1,0:T(8,128)(2,1)} %get-tuple-element.13), calls=%async_computation | async-start | bytes 1376256 | tf_op jit(solution)/shard_map/all_to_all | solution.py:31
  122.8 18.7 %collective-permute-start.13 = (bf16[32,1792]{1,0:T(8,128)(2,1)}, bf16[32,1792]{1,0:T(8,128)(2,1)S(1)}, u32[]{:S(2)}, u32[]{:S(2)}) collective-permute-start(bf16[32,1792]{1,0:T(8,128)(2,1)} %shard_map.66.refs_0_), channel_id=1, source_target_pairs={{0,16},{16,32},{32,48},{48,0},{1,17},{17,33},{33,49},{49,1},{2,18}... | collective-permute-start | bytes 344072 | tf_op jit(solution)/shard_map/ppermute | solution.py:20
  126.2 15.4 %collective-permute-start.14 = (bf16[32,1792]{1,0:T(8,128)(2,1)}, bf16[32,1792]{1,0:T(8,128)(2,1)}, u32[]{:S(2)}, u32[]{:S(2)}) collective-permute-start(bf16[32,1792]{1,0:T(8,128)(2,1)} %shard_map.66.refs_0_), channel_id=1, source_target_pairs={{0,32},{16,48},{32,0},{48,16},{1,33},{17,49},{33,1},{49,17},{2,34}... | collective-permute-start | bytes 344072 | tf_op jit(solution)/shard_map/ppermute | solution.py:20
  130.5 11.1 %collective-permute-start.15 = (bf16[32,1792]{1,0:T(8,128)(2,1)}, bf16[32,1792]{1,0:T(8,128)(2,1)}, u32[]{:S(2)}, u32[]{:S(2)}) collective-permute-start(bf16[32,1792]{1,0:T(8,128)(2,1)} %shard_map.66.refs_0_), channel_id=1, source_target_pairs={{0,48},{16,0},{32,16},{48,32},{1,49},{17,1},{33,17},{49,33},{2,50}... | collective-permute-start | bytes 344072 | tf_op jit(solution)/shard_map/ppermute | solution.py:20
  133.6 1.0 copy-start
  133.6 1.2 copy-start.3
  134.8 0.9 copy-start.1
  138.0 17.6 %all-to-all-start.3 = ((bf16[4,64,1792]{2,1,0:T(8,128)(2,1)}), bf16[4,64,1792]{2,1,0:T(8,128)(2,1)S(1)}, u32[]{:S(2)}, u32[]{:S(2)}) async-start(bf16[4,64,1792]{2,1,0:T(8,128)(2,1)} %shard_map.62), calls=%async_computation.3 | async-start | bytes 1835008 | tf_op jit(solution)/shard_map/all_to_all | solution.py:31
  141.6 0.6 copy-start.20
  142.2 10.9 %copy-start.12 = (s32[8,2]{0,1:T(2,128)S(1)}, s32[8,2]{0,1:T(2,128)}, u32[]{:S(2)}) copy-start(s32[8,2]{0,1:T(2,128)} %param.6) | copy-start | bytes 196
  142.2 10.9 %copy-start.13 = (f32[8,2]{0,1:T(2,128)S(1)}, f32[8,2]{0,1:T(2,128)}, u32[]{:S(2)}) copy-start(f32[8,2]{0,1:T(2,128)} %param.7) | copy-start | bytes 196
  145.5 23.1 %collective-permute-start.16 = (bf16[128,1024]{1,0:T(8,128)(2,1)}, bf16[128,1024]{1,0:T(8,128)(2,1)S(1)}, u32[]{:S(2)}, u32[]{:S(2)}) collective-permute-start(bf16[128,1024]{1,0:T(8,128)(2,1)} %shard_map.67), channel_id=1, source_target_pairs={{0,1},{1,2},{2,3},{3,0},{64,67},{65,64},{66,65},{67,66},{4,5},{5,6... | collective-permute-start | bytes 786440 | tf_op jit(solution)/shard_map/ppermute | solution.py:25
  155.7 0.9 copy-start.5
  160.7 24.3 %collective-permute-start.18 = (bf16[128,1024]{1,0:T(8,128)(2,1)}, bf16[128,1024]{1,0:T(8,128)(2,1)S(1)}, u32[]{:S(2)}, u32[]{:S(2)}) collective-permute-start(bf16[128,1024]{1,0:T(8,128)(2,1)} %get-tuple-element.14.refs_0_), channel_id=1, source_target_pairs={{0,3},{1,0},{2,1},{3,2},{64,65},{65,66},{66,67},{67,64},{4,7},{5,4... | collective-permute-start | bytes 786440 | tf_op jit(solution)/shard_map/ppermute | solution.py:25
  164.7 16.1 %all-to-all-start.4 = ((bf16[4,32,1792]{2,1,0:T(8,128)(2,1)}), bf16[4,32,1792]{2,1,0:T(8,128)(2,1)S(1)}, u32[]{:S(2)}, u32[]{:S(2)}) async-start(bf16[4,32,1792]{2,1,0:T(8,128)(2,1)} %shard_map.64), calls=%async_computation.4 | async-start | bytes 917504 | tf_op jit(solution)/shard_map/all_to_all | solution.py:31
  168.5 0.7 copy-start.19
  169.2 10.9 %copy-start.9 = (pred[8]{0:T(512)(128)(4,1)S(1)}, pred[8]{0:T(512)(128)(4,1)}, u32[]{:S(2)}) copy-start(pred[8]{0:T(512)(128)(4,1)} %copy-done.8) | copy-start | bytes 28
  169.2 10.9 %copy-start.11 = (pred[8]{0:T(512)(128)(4,1)S(1)}, pred[8]{0:T(512)(128)(4,1)}, u32[]{:S(2)}) copy-start(pred[8]{0:T(512)(128)(4,1)} %copy-done.10) | copy-start | bytes 28
  171.1 18.7 %collective-permute-start.17 = (bf16[128,1024]{1,0:T(8,128)(2,1)}, bf16[128,1024]{1,0:T(8,128)(2,1)S(1)}, u32[]{:S(2)}, u32[]{:S(2)}) collective-permute-start(bf16[128,1024]{1,0:T(8,128)(2,1)} %shard_map.68), channel_id=1, source_target_pairs={{0,1},{1,2},{2,3},{3,0},{64,67},{65,64},{66,65},{67,66},{4,5},{5,6... | collective-permute-start | bytes 786440 | tf_op jit(solution)/shard_map/ppermute | solution.py:25
  180.8 0.8 copy-start.6
  192.4 3.8 %collective-permute-start.19 = (bf16[4,64,1024]{2,1,0:T(8,128)(2,1)S(1)}, bf16[4,64,1024]{2,1,0:T(8,128)(2,1)S(1)}, u32[]{:S(2)}, u32[]{:S(2)}) collective-permute-start(bf16[4,64,1024]{2,1,0:T(8,128)(2,1)S(1)} %add_convert_fusion.1), channel_id=1, source_target_pairs={{0,64},{64,0},{1,65},{65,1},{2,66},{66,2},{3,67},{67,3},{4,68},{68... | collective-permute-start | bytes 1572872 | tf_op jit(solution)/shard_map/ppermute | solution.py:20

commit v13 on v12

--- a/solution.py
+++ b/solution.py
@@ -201,15 +201,22 @@
     )(sums, begun, *after)
 
 
+def times_blocks(rows, blocks):
+    return sum(
+        jnp.dot(rows[:, 448 * i : 448 * i + 448], ref[...], preferred_element_type=wide)
+        for i, ref in enumerate(blocks)
+    )
+
+
 def down(hidden, weights, types):
     n = len(types)
 
     def kernel(*refs):
         hidden_ref, v_refs, outs = refs[0], refs[1:5], refs[5:]
-        v = jnp.concatenate([ref[...] for ref in v_refs])
+        rows = jnp.concatenate([hidden_ref[:, pl.ds(32 * i, 32), :].reshape(128, 1792) for i in range(n)])
+        sums = times_blocks(rows, v_refs)
         for i, out in enumerate(outs):
-            rows = hidden_ref[:, pl.ds(32 * i, 32), :].reshape(128, 1792)
-            out[...] = jnp.dot(rows, v, preferred_element_type=wide).astype(out.dtype)
+            out[...] = sums[128 * i : 128 * i + 128].astype(out.dtype)
 
     return pl.pallas_call(
         kernel,
@@ -226,9 +233,8 @@
 def down_far(pieces, weights, x):
     def kernel(x_ref, *refs):
         v_refs, out_ref = refs[4:8], refs[8]
-        v = jnp.concatenate([ref[...] for ref in v_refs])
         rows = jnp.concatenate([ref[...] for ref in refs[:4]])
-        out = jnp.dot(rows, v, preferred_element_type=wide).astype(half)
+        out = times_blocks(rows, v_refs).astype(half)
         for d in range(4):
             at = pl.multiple_of(((x_ref[0] - d) & 3) * 32, 32)
             out_ref[pl.ds(at, 32), :] = out[32 * d : 32 * d + 32]

time: 225 us -> 226 us (level)
  no operation moved by 1% of the time
where the time goes in v13:
time: 226 us; the launch traced here: 222 us
  starting transfers between devices  109 us (48%)
  Pallas kernels  46.2 us (20%)
  blocking collectives  24.6 us (11%)
  waiting for transfers between devices  16.9 us (7%)
  other arithmetic  11.2 us (5%)
  local copies, waits for them, and re-layouts  8.71 us (4%)
  between operations  5.56 us (2%)
    ppermute x12, starting transfers between devices, pass_on(): lax.ppermute(a, ('core', axis), [(c * n + i, c * n + (i + by * (1 - 2 * c...  56.7 us
    ppermute x8, starting transfers between devices, shift(): return lax.ppermute(a, axis, [(i, (i + by) % n) for i in range(n)])  28.8 us
    all_to_all x1, blocking collectives, swap(): return lax.all_to_all(a, axis, split_axis=0, concat_axis=0, tiled=True)  24.6 us
    all_to_all x6, starting transfers between devices, swap(): return lax.all_to_all(a, axis, split_axis=0, concat_axis=0, tiled=True)  23.6 us
    pallas_call x2, Pallas kernels, early(): pl.pallas_call(kernel, in_specs=[WHOLE] * n + [ANY] * (3 + len(after)), o...  11.1 us
    ppermute x12, waiting for transfers between devices, pass_on(): lax.ppermute(a, ('core', axis), [(c * n + i, c * n + (i + by * (1 - 2 * c...  9.8 us
    unnamed x42, local copies, waits for them, and re-layouts  8.52 us
    pallas_call x2, Pallas kernels, down(): pl.pallas_call(kernel, grid=(2,), in_specs=[pl.BlockSpec((4, 32 * n, 1792...  7.86 us
  transfers between devices with their start and end apart: 26, of which 8 were waited for; matrix products, arithmetic and copies ran while one was open for 3% of the time, Pallas kernels for 21%

profile of v13, /device:TPU:1, one launch (start us, length us, event | category | flops | bytes accessed | tf_op | source)
XLA Modules:
  0.0 222.4 jit_solution(6097489896284644408)
XLA Ops:
  0.0 5.5 %collective-permute-start.5 = (bf16[896,1024]{1,0:T(8,128)(2,1)}, bf16[896,1024]{1,0:T(8,128)(2,1)S(1)}, u32[]{:S(2)}, u32[]{:S(2)}) collective-permute-start(bf16[896,1024]{1,0:T(8,128)(2,1)} %bitcast.20), channel_id=1, source_target_pairs={{0,4},{4,8},{8,12},{12,0},{64,76},{68,64},{72,68},{76,72},{1,5},{5... | collective-permute-start | bytes 5505032 | tf_op jit(solution)/shard_map/ppermute | solution.py:25
  5.5 1.9 collective-permute-start.6
  7.4 4.9 %collective-permute-start.1 = (bf16[64,1024]{1,0:T(8,128)(2,1)}, bf16[64,1024]{1,0:T(8,128)(2,1)S(1)}, u32[]{:S(2)}, u32[]{:S(2)}) collective-permute-start(bf16[64,1024]{1,0:T(8,128)(2,1)} %bitcast.17), channel_id=1, source_target_pairs={{0,256},{128,384},{256,0},{384,128},{1,257},{129,385},{257,1},{385... | collective-permute-start | bytes 393224 | tf_op jit(solution)/shard_map/ppermute | solution.py:20
  12.3 3.3 %collective-permute-start.2 = (bf16[64,1024]{1,0:T(8,128)(2,1)}, bf16[64,1024]{1,0:T(8,128)(2,1)S(1)}, u32[]{:S(2)}, u32[]{:S(2)}) collective-permute-start(bf16[64,1024]{1,0:T(8,128)(2,1)} %bitcast.18), channel_id=1, source_target_pairs={{0,384},{128,0},{256,128},{384,256},{1,385},{129,1},{257,129},{385... | collective-permute-start | bytes 393224 | tf_op jit(solution)/shard_map/ppermute | solution.py:20
  15.6 2.2 collective-permute-start
  21.6 1.9 collective-permute-done
  24.5 5.6 %collective-permute-start.3 = (bf16[128,1024]{1,0:T(8,128)(2,1)S(1)}, bf16[128,1024]{1,0:T(8,128)(2,1)S(1)}, u32[]{:S(2)}, u32[]{:S(2)}) collective-permute-start(bf16[128,1024]{1,0:T(8,128)(2,1)S(1)} %pad_maximum_fusion), channel_id=1, source_target_pairs={{0,64},{64,0},{1,65},{65,1},{2,66},{66,2},{3,67},{67,3},{4,68},{68... | collective-permute-start | bytes 786440 | tf_op jit(solution)/shard_map/ppermute | solution.py:20
  33.5 10.0 %collective-permute-start.4 = (bf16[128,1024]{1,0:T(8,128)(2,1)S(1)}, bf16[128,1024]{1,0:T(8,128)(2,1)S(1)}, u32[]{:S(2)}, u32[]{:S(2)}) collective-permute-start(bf16[128,1024]{1,0:T(8,128)(2,1)S(1)} %pad_maximum_fusion.1.refs_0_.refs_3_), channel_id=1, source_target_pairs={{0,1},{1,2},{2,3},{3,0},{64,67},{65,64},{66,65},{67,66},{4,5},{5,6... | collective-permute-start | bytes 786440 | tf_op jit(solution)/shard_map/ppermute | solution.py:25
  43.5 1.9 collective-permute-start.8
  45.5 3.4 %collective-permute-done.6.refs_3_.refs_6_.refs_4_ = bf16[896,1024]{1,0:T(8,128)(2,1)} collective-permute-done((bf16[896,1024]{1,0:T(8,128)(2,1)}, bf16[896,1024]{1,0:T(8,128)(2,1)}, u32[]{:S(2)}, u32[]{:S(2)}) %collective-permute-start.6) | collective-permute-done | bytes 1835040 | tf_op jit(solution)/shard_map/ppermute | solution.py:25
  48.9 5.4 %shard_map.55 = (bf16[896,1024]{1,0:T(8,128)(2,1)}, bf16[4,32,2688]{2,1,0:T(8,128)(2,1)}) custom-call(bf16[128,1024]{1,0:T(8,128)(2,1)} %copy-done.7, bf16[896,1024]{1,0:T(8,128)(2,1)} %bitcast.22, bf16[896,1024]{1,0:T(8,128)(2,1)} %copy-done.14, bf16[896,1024]{1,0:T(8,128)(2,1)} %collective-permute-done.6.refs_3_.refs_6_.refs_4_), custom_call_target="tpu_custom_call" | custom-call | flops 99999997952 | bytes 1024 | tf_op jit(solution)/shard_map/pallas_call | solution.py:81
  54.3 1.9 collective-permute-start.9
  56.3 4.0 %all-to-all-start.1 = ((bf16[4,32,2688]{2,1,0:T(8,128)(2,1)}), bf16[4,32,2688]{2,1,0:T(8,128)(2,1)S(1)}, u32[]{:S(2)}, u32[]{:S(2)}) async-start(bf16[4,32,2688]{2,1,0:T(8,128)(2,1)} %get-tuple-element.11.refs_0_.refs_5_), calls=%async_computation.1 | async-start | bytes 1376256 | tf_op jit(solution)/shard_map/all_to_all | solution.py:31
  60.3 1.7 collective-permute-done.4.a_ref.refs_1_.refs_0_
  62.7 1.7 shard_map.56
  64.4 10.8 %collective-permute-start.7 = (bf16[128,1024]{1,0:T(8,128)(2,1)}, bf16[128,1024]{1,0:T(8,128)(2,1)S(1)}, u32[]{:S(2)}, u32[]{:S(2)}) collective-permute-start(bf16[128,1024]{1,0:T(8,128)(2,1)} %shard_map.56), channel_id=1, source_target_pairs={{0,1},{1,2},{2,3},{3,0},{64,67},{65,64},{66,65},{67,66},{4,5},{5,6... | collective-permute-start | bytes 786440 | tf_op jit(solution)/shard_map/ppermute | solution.py:25
  75.8 5.6 %shard_map.59 = bf16[4,64,2688]{2,1,0:T(8,128)(2,1)} custom-call(bf16[128,1024]{1,0:T(8,128)(2,1)} %copy-done.16, bf16[128,1024]{1,0:T(8,128)(2,1)} %copy-done.17, bf16[896,1024]{1,0:T(8,128)(2,1)} %bitcast.23, bf16[896,1024]{1,0:T(8,128)(2,1)} %copy-done.14, bf16[896,1024]{1,0:T(8,128)(2,1)} %collective-permute-done.6.refs_3_.refs_6_.refs_4_, ...), custom_call_target="tpu_custom_call" | custom-call | flops 10000000000 | bytes 1024 | tf_op jit(solution)/shard_map/pallas_call | solution.py:81
  81.5 4.3 %all-to-all-start.2 = ((bf16[4,64,2688]{2,1,0:T(8,128)(2,1)}), bf16[4,64,2688]{2,1,0:T(8,128)(2,1)}, u32[]{:S(2)}, u32[]{:S(2)}) async-start(bf16[4,64,2688]{2,1,0:T(8,128)(2,1)} %shard_map.59), calls=%async_computation.2 | async-start | bytes 2752512 | tf_op jit(solution)/shard_map/all_to_all | solution.py:31
  85.9 2.2 %shard_map.60 = bf16[448,1024]{1,0:T(8,128)(2,1)} custom-call(bf16[448,1024]{1,0:T(8,128)(2,1)} %bitcast.13, bf16[4,32,2688]{2,1,0:T(8,128)(2,1)} %copy-done.4), custom_call_target="tpu_custom_call" | custom-call | flops 1024 | bytes 1024 | tf_op jit(solution)/shard_map/pallas_call | solution.py:41
  88.1 2.3 %collective-permute-start.10 = (bf16[448,1024]{1,0:T(8,128)(2,1)}, bf16[448,1024]{1,0:T(8,128)(2,1)S(1)}, u32[]{:S(2)}, u32[]{:S(2)}) collective-permute-start(bf16[448,1024]{1,0:T(8,128)(2,1)} %shard_map.60), channel_id=1, source_target_pairs={{0,4},{4,8},{8,12},{12,0},{64,76},{68,64},{72,68},{76,72},{1,5},{5... | collective-permute-start | bytes 2752520 | tf_op jit(solution)/shard_map/ppermute | solution.py:25
  92.4 7.6 %shard_map.57 = (bf16[4,32,3584]{2,1,0:T(8,128)(2,1)}, bf16[4,32,2688]{2,1,0:T(8,128)(2,1)}) custom-call(bf16[128,1024]{1,0:T(8,128)(2,1)} %copy-done.18, bf16[128,1024]{1,0:T(8,128)(2,1)} %copy-done.16, bf16[128,1024]{1,0:T(8,128)(2,1)} %copy-done.17, bf16[128,1024]{1,0:T(8,128)(2,1)} %copy-done.7, bf16[896,1024]{1,0:T(8,128)(2,1)} %bitcast.24, ...), custom_call_target="tpu_custom_call" | custom-call | flops 99999997952 | bytes 1024 | tf_op jit(solution)/shard_map/pallas_call | solution.py:118
  99.9 1.4 all-to-all-done.2.sums_ref
  101.3 4.2 %all-to-all-start.5 = ((bf16[4,32,3584]{2,1,0:T(8,128)(2,1)}), bf16[4,32,3584]{2,1,0:T(8,128)(2,1)}, u32[]{:S(2)}, u32[]{:S(2)}) async-start(bf16[4,32,3584]{2,1,0:T(8,128)(2,1)} %get-tuple-element.16), calls=%async_computation.5 | async-start | bytes 1835008 | tf_op jit(solution)/shard_map/all_to_all | solution.py:31
  105.6 4.0 %collective-permute-start.11 = (bf16[448,1024]{1,0:T(8,128)(2,1)}, bf16[448,1024]{1,0:T(8,128)(2,1)S(1)}, u32[]{:S(2)}, u32[]{:S(2)}) collective-permute-start(bf16[448,1024]{1,0:T(8,128)(2,1)} %shard_map.60), channel_id=1, source_target_pairs={{0,12},{4,0},{8,4},{12,8},{64,68},{68,72},{72,76},{76,64},{1,13},{... | collective-permute-start | bytes 2752520 | tf_op jit(solution)/shard_map/ppermute | solution.py:25
  109.6 2.5 %collective-permute-start.12 = (bf16[448,1024]{1,0:T(8,128)(2,1)S(1)}, bf16[448,1024]{1,0:T(8,128)(2,1)S(1)}, u32[]{:S(2)}, u32[]{:S(2)}) collective-permute-start(bf16[448,1024]{1,0:T(8,128)(2,1)S(1)} %collective-permute-done.10.refs_0_.refs_2_.refs_5_), channel_id=1, source_target_pairs={{0,4},{4,8},{8,12},{12,0},{64,76},{68,64},{72,68},{76,72},{1,5},{5... | collective-permute-start | bytes 2752520 | tf_op jit(solution)/shard_map/ppermute | solution.py:25
  112.1 2.3 %shard_map.61.begun_ref.after_ref = bf16[64,1344]{1,0:T(8,128)(2,1)} custom-call(bf16[4,64,2688]{2,1,0:T(8,128)(2,1)} %all-to-all-done.2.sums_ref, bf16[448,1024]{1,0:T(8,128)(2,1)} %copy-done.2), custom_call_target="tpu_custom_call" | custom-call | flops 1024 | bytes 1024 | tf_op jit(solution)/shard_map/pallas_call | solution.py:152
  114.4 2.9 %all-to-all-done.5.sums_ref = bf16[4,32,3584]{2,1,0:T(8,128)(2,1)} async-done(((bf16[4,32,3584]{2,1,0:T(8,128)(2,1)}), bf16[4,32,3584]{2,1,0:T(8,128)(2,1)}, u32[]{:S(2)}, u32[]{:S(2)}) %all-to-all-start.5) | async-done | bytes 917536 | tf_op jit(solution)/shard_map/all_to_all | solution.py:31
  117.3 3.5 %all-to-all-start = ((bf16[4,32,2688]{2,1,0:T(8,128)(2,1)}), bf16[4,32,2688]{2,1,0:T(8,128)(2,1)S(1)}, u32[]{:S(2)}, u32[]{:S(2)}) async-start(bf16[4,32,2688]{2,1,0:T(8,128)(2,1)} %get-tuple-element.13), calls=%async_computation | async-start | bytes 1376256 | tf_op jit(solution)/shard_map/all_to_all | solution.py:31
  120.8 2.1 shard_map.66.refs_0_
  122.8 3.3 %collective-permute-start.13 = (bf16[32,1792]{1,0:T(8,128)(2,1)}, bf16[32,1792]{1,0:T(8,128)(2,1)S(1)}, u32[]{:S(2)}, u32[]{:S(2)}) collective-permute-start(bf16[32,1792]{1,0:T(8,128)(2,1)} %shard_map.66.refs_0_), channel_id=1, source_target_pairs={{0,16},{16,32},{32,48},{48,0},{1,17},{17,33},{33,49},{49,1},{2,18}... | collective-permute-start | bytes 344072 | tf_op jit(solution)/shard_map/ppermute | solution.py:20
  126.2 4.3 %collective-permute-start.14 = (bf16[32,1792]{1,0:T(8,128)(2,1)}, bf16[32,1792]{1,0:T(8,128)(2,1)}, u32[]{:S(2)}, u32[]{:S(2)}) collective-permute-start(bf16[32,1792]{1,0:T(8,128)(2,1)} %shard_map.66.refs_0_), channel_id=1, source_target_pairs={{0,32},{16,48},{32,0},{48,16},{1,33},{17,49},{33,1},{49,17},{2,34}... | collective-permute-start | bytes 344072 | tf_op jit(solution)/shard_map/ppermute | solution.py:20
  130.5 3.1 %collective-permute-start.15 = (bf16[32,1792]{1,0:T(8,128)(2,1)}, bf16[32,1792]{1,0:T(8,128)(2,1)}, u32[]{:S(2)}, u32[]{:S(2)}) collective-permute-start(bf16[32,1792]{1,0:T(8,128)(2,1)} %shard_map.66.refs_0_), channel_id=1, source_target_pairs={{0,48},{16,0},{32,16},{48,32},{1,49},{17,1},{33,17},{49,33},{2,50}... | collective-permute-start | bytes 344072 | tf_op jit(solution)/shard_map/ppermute | solution.py:20
  135.8 2.3 %shard_map.62 = bf16[4,64,1792]{2,1,0:T(8,128)(2,1)} custom-call(bf16[4,32,2688]{2,1,0:T(8,128)(2,1)} %copy-done.3, bf16[64,1344]{1,0:T(8,128)(2,1)} %shard_map.61.begun_ref.after_ref, bf16[448,1024]{1,0:T(8,128)(2,1)} %copy-done, bf16[448,1024]{1,0:T(8,128)(2,1)} %copy-done.1), custom_call_target="tpu_custom_call" | custom-call | flops 1024 | bytes 1024 | tf_op jit(solution)/shard_map/pallas_call | solution.py:189
  138.0 3.5 %all-to-all-start.3 = ((bf16[4,64,1792]{2,1,0:T(8,128)(2,1)}), bf16[4,64,1792]{2,1,0:T(8,128)(2,1)S(1)}, u32[]{:S(2)}, u32[]{:S(2)}) async-start(bf16[4,64,1792]{2,1,0:T(8,128)(2,1)} %shard_map.62), calls=%async_computation.3 | async-start | bytes 1835008 | tf_op jit(solution)/shard_map/all_to_all | solution.py:31
  142.2 3.4 %shard_map.67 = bf16[128,1024]{1,0:T(8,128)(2,1)} custom-call(s32[1]{0:T(128)} %bitcast.7.x_ref, bf16[32,1792]{1,0:T(8,128)(2,1)} %shard_map.66.refs_0_, bf16[32,1792]{1,0:T(8,128)(2,1)} %copy-done.20, bf16[32,1792]{1,0:T(8,128)(2,1)} %collective-permute-done.14.refs_2_, bf16[32,1792]{1,0:T(8,128)(2,1)} %collective-permute-done.15.refs_3_, ...), custom_call_target="tpu_custom_call" | custom-call | flops 99999997952 | bytes 1024 | tf_op jit(solution)/shard_map/pallas_call | solution.py:242
  145.6 7.0 %collective-permute-start.16 = (bf16[128,1024]{1,0:T(8,128)(2,1)}, bf16[128,1024]{1,0:T(8,128)(2,1)S(1)}, u32[]{:S(2)}, u32[]{:S(2)}) collective-permute-start(bf16[128,1024]{1,0:T(8,128)(2,1)} %shard_map.67), channel_id=1, source_target_pairs={{0,1},{1,2},{2,3},{3,0},{64,67},{65,64},{66,65},{67,66},{4,5},{5,6... | collective-permute-start | bytes 786440 | tf_op jit(solution)/shard_map/ppermute | solution.py:25
  153.3 1.9 shard_map.58.begun_ref
  156.6 4.3 %shard_map.63 = (bf16[128,1024]{1,0:T(8,128)(2,1)}, f32[128,1024]{1,0:T(8,128)}) custom-call(bf16[4,64,1792]{2,1,0:T(8,128)(2,1)} %copy-done.5, bf16[448,1024]{1,0:T(8,128)(2,1)} %bitcast.15, bf16[448,1024]{1,0:T(8,128)(2,1)} %copy-done.2, bf16[448,1024]{1,0:T(8,128)(2,1)} %copy-done, bf16[448,1024]{1,0:T(8,128)(2,1)} %copy-done.1), custom_call_target="tpu_custom_call" | custom-call | flops 1024 | bytes 1024 | tf_op jit(solution)/shard_map/pallas_call | solution.py:221
  160.9 1.9 collective-permute-start.18
  162.8 2.1 shard_map.64
  164.9 4.0 %all-to-all-start.4 = ((bf16[4,32,1792]{2,1,0:T(8,128)(2,1)}), bf16[4,32,1792]{2,1,0:T(8,128)(2,1)S(1)}, u32[]{:S(2)}, u32[]{:S(2)}) async-start(bf16[4,32,1792]{2,1,0:T(8,128)(2,1)} %shard_map.64), calls=%async_computation.4 | async-start | bytes 917504 | tf_op jit(solution)/shard_map/all_to_all | solution.py:31
  169.5 1.9 shard_map.68
  171.4 7.0 %collective-permute-start.17 = (bf16[128,1024]{1,0:T(8,128)(2,1)}, bf16[128,1024]{1,0:T(8,128)(2,1)S(1)}, u32[]{:S(2)}, u32[]{:S(2)}) collective-permute-start(bf16[128,1024]{1,0:T(8,128)(2,1)} %shard_map.68), channel_id=1, source_target_pairs={{0,1},{1,2},{2,3},{3,0},{64,67},{65,64},{66,65},{67,66},{4,5},{5,6... | collective-permute-start | bytes 786440 | tf_op jit(solution)/shard_map/ppermute | solution.py:25
  181.9 3.6 %shard_map.65 = f32[128,1024]{1,0:T(8,128)} custom-call(bf16[4,32,1792]{2,1,0:T(8,128)(2,1)} %copy-done.6, bf16[448,1024]{1,0:T(8,128)(2,1)} %bitcast.16, bf16[448,1024]{1,0:T(8,128)(2,1)} %copy-done.2, bf16[448,1024]{1,0:T(8,128)(2,1)} %copy-done, bf16[448,1024]{1,0:T(8,128)(2,1)} %copy-done.1), custom_call_target="tpu_custom_call" | custom-call | flops 1024 | bytes 1024 | tf_op jit(solution)/shard_map/pallas_call | solution.py:221
  185.5 4.7 %collective-permute-done.17 = bf16[128,1024]{1,0:T(8,128)(2,1)S(1)} collective-permute-done((bf16[128,1024]{1,0:T(8,128)(2,1)}, bf16[128,1024]{1,0:T(8,128)(2,1)S(1)}, u32[]{:S(2)}, u32[]{:S(2)}) %collective-permute-start.17) | collective-permute-done | bytes 262176 | tf_op jit(solution)/shard_map/ppermute | solution.py:25
  191.3 1.4 slice_multiply_fusion.1
  192.9 2.1 collective-permute-start.19
  197.0 24.6 %all_to_all.35 = bf16[4,64,1024]{2,1,0:T(8,128)(2,1)S(1)} all-to-all(bf16[4,64,1024]{2,1,0:T(8,128)(2,1)S(1)} %add_convert_fusion), channel_id=1, replica_groups=mesh['zlo'=4,'core'=2,'x'=4,'y'=4,'zhi'=4] {'zlo'}, dimensions={0} | all-to-all | bytes 1048576 | tf_op jit(solution)/shard_map/all_to_all | solution.py:31
  (84 shorter events, 19.5 us)
Async XLA Ops:
  0.0 45.5 %collective-permute-start.5 = (bf16[896,1024]{1,0:T(8,128)(2,1)}, bf16[896,1024]{1,0:T(8,128)(2,1)S(1)}, u32[]{:S(2)}, u32[]{:S(2)}) collective-permute-start(bf16[896,1024]{1,0:T(8,128)(2,1)} %bitcast.20), channel_id=1, source_target_pairs={{0,4},{4,8},{8,12},{12,0},{64,76},{68,64},{72,68},{76,72},{1,5},{5... | collective-permute-start | bytes 5505032 | tf_op jit(solution)/shard_map/ppermute | solution.py:25
  5.5 43.4 %collective-permute-start.6 = (bf16[896,1024]{1,0:T(8,128)(2,1)}, bf16[896,1024]{1,0:T(8,128)(2,1)}, u32[]{:S(2)}, u32[]{:S(2)}) collective-permute-start(bf16[896,1024]{1,0:T(8,128)(2,1)} %bitcast.21), channel_id=1, source_target_pairs={{0,12},{4,0},{8,4},{12,8},{64,68},{68,72},{72,76},{76,64},{1,13},{... | collective-permute-start | bytes 5505032 | tf_op jit(solution)/shard_map/ppermute | solution.py:25
  7.4 14.2 %collective-permute-start.1 = (bf16[64,1024]{1,0:T(8,128)(2,1)}, bf16[64,1024]{1,0:T(8,128)(2,1)S(1)}, u32[]{:S(2)}, u32[]{:S(2)}) collective-permute-start(bf16[64,1024]{1,0:T(8,128)(2,1)} %bitcast.17), channel_id=1, source_target_pairs={{0,256},{128,384},{256,0},{384,128},{1,257},{129,385},{257,1},{385... | collective-permute-start | bytes 393224 | tf_op jit(solution)/shard_map/ppermute | solution.py:20
  12.3 9.3 %collective-permute-start.2 = (bf16[64,1024]{1,0:T(8,128)(2,1)}, bf16[64,1024]{1,0:T(8,128)(2,1)S(1)}, u32[]{:S(2)}, u32[]{:S(2)}) collective-permute-start(bf16[64,1024]{1,0:T(8,128)(2,1)} %bitcast.18), channel_id=1, source_target_pairs={{0,384},{128,0},{256,128},{384,256},{1,385},{129,1},{257,129},{385... | collective-permute-start | bytes 393224 | tf_op jit(solution)/shard_map/ppermute | solution.py:20
  15.6 7.9 %collective-permute-start = (bf16[64,1024]{1,0:T(8,128)(2,1)}, bf16[64,1024]{1,0:T(8,128)(2,1)S(1)}, u32[]{:S(2)}, u32[]{:S(2)}) collective-permute-start(bf16[64,1024]{1,0:T(8,128)(2,1)} %bitcast.19), channel_id=1, source_target_pairs={{0,128},{128,256},{256,384},{384,0},{1,129},{129,257},{257,385},{3... | collective-permute-start | bytes 393224 | tf_op jit(solution)/shard_map/ppermute | solution.py:20
  18.9 5.5 %copy-start.8 = (pred[8]{0:T(512)(128)(4,1)}, pred[8]{0:T(512)(128)(4,1)S(1)}, u32[]{:S(2)}) copy-start(pred[8]{0:T(512)(128)(4,1)S(1)} %get-tuple-element.17) | copy-start | bytes 28
  18.9 5.5 %copy-start.10 = (pred[8]{0:T(512)(128)(4,1)}, pred[8]{0:T(512)(128)(4,1)S(1)}, u32[]{:S(2)}) copy-start(pred[8]{0:T(512)(128)(4,1)S(1)} %get-tuple-element.18) | copy-start | bytes 28
  24.5 8.1 %collective-permute-start.3 = (bf16[128,1024]{1,0:T(8,128)(2,1)S(1)}, bf16[128,1024]{1,0:T(8,128)(2,1)S(1)}, u32[]{:S(2)}, u32[]{:S(2)}) collective-permute-start(bf16[128,1024]{1,0:T(8,128)(2,1)S(1)} %pad_maximum_fusion), channel_id=1, source_target_pairs={{0,64},{64,0},{1,65},{65,1},{2,66},{66,2},{3,67},{67,3},{4,68},{68... | collective-permute-start | bytes 786440 | tf_op jit(solution)/shard_map/ppermute | solution.py:20
  33.5 15.4 %copy-start.7 = (bf16[128,1024]{1,0:T(8,128)(2,1)}, bf16[128,1024]{1,0:T(8,128)(2,1)S(1)}, u32[]{:S(2)}) copy-start(bf16[128,1024]{1,0:T(8,128)(2,1)S(1)} %pad_maximum_fusion.1.refs_0_.refs_3_) | copy-start | bytes 786436
  33.5 28.5 %collective-permute-start.4 = (bf16[128,1024]{1,0:T(8,128)(2,1)S(1)}, bf16[128,1024]{1,0:T(8,128)(2,1)S(1)}, u32[]{:S(2)}, u32[]{:S(2)}) collective-permute-start(bf16[128,1024]{1,0:T(8,128)(2,1)S(1)} %pad_maximum_fusion.1.refs_0_.refs_3_), channel_id=1, source_target_pairs={{0,1},{1,2},{2,3},{3,0},{64,67},{65,64},{66,65},{67,66},{4,5},{5,6... | collective-permute-start | bytes 786440 | tf_op jit(solution)/shard_map/ppermute | solution.py:25
  43.5 31.6 %collective-permute-start.8 = (bf16[128,1024]{1,0:T(8,128)(2,1)S(1)}, bf16[128,1024]{1,0:T(8,128)(2,1)S(1)}, u32[]{:S(2)}, u32[]{:S(2)}) collective-permute-start(bf16[128,1024]{1,0:T(8,128)(2,1)S(1)} %pad_maximum_fusion.1.refs_0_.refs_3_), channel_id=1, source_target_pairs={{0,3},{1,0},{2,1},{3,2},{64,65},{65,66},{66,67},{67,64},{4,7},{5,4... | collective-permute-start | bytes 786440 | tf_op jit(solution)/shard_map/ppermute | solution.py:25
  45.5 3.4 %copy-start.14 = (bf16[896,1024]{1,0:T(8,128)(2,1)}, bf16[896,1024]{1,0:T(8,128)(2,1)S(1)}, u32[]{:S(2)}) copy-start(bf16[896,1024]{1,0:T(8,128)(2,1)S(1)} %collective-permute-done.5.refs_2_.refs_5_.refs_3_) | copy-start | bytes 5505028
  54.3 36.1 %collective-permute-start.9 = (bf16[896,1024]{1,0:T(8,128)(2,1)}, bf16[896,1024]{1,0:T(8,128)(2,1)S(1)}, u32[]{:S(2)}, u32[]{:S(2)}) collective-permute-start(bf16[896,1024]{1,0:T(8,128)(2,1)} %get-tuple-element.12), channel_id=1, source_target_pairs={{0,4},{4,8},{8,12},{12,0},{64,76},{68,64},{72,68},{76,72},{1,5},{5... | collective-permute-start | bytes 5505032 | tf_op jit(solution)/shard_map/ppermute | solution.py:25
  56.3 25.2 %all-to-all-start.1 = ((bf16[4,32,2688]{2,1,0:T(8,128)(2,1)}), bf16[4,32,2688]{2,1,0:T(8,128)(2,1)S(1)}, u32[]{:S(2)}, u32[]{:S(2)}) async-start(bf16[4,32,2688]{2,1,0:T(8,128)(2,1)} %get-tuple-element.11.refs_0_.refs_5_), calls=%async_computation.1 | async-start | bytes 1376256 | tf_op jit(solution)/shard_map/all_to_all | solution.py:31
  62.0 0.7 copy-start.16
  64.4 26.0 %collective-permute-start.7 = (bf16[128,1024]{1,0:T(8,128)(2,1)}, bf16[128,1024]{1,0:T(8,128)(2,1)S(1)}, u32[]{:S(2)}, u32[]{:S(2)}) collective-permute-start(bf16[128,1024]{1,0:T(8,128)(2,1)} %shard_map.56), channel_id=1, source_target_pairs={{0,1},{1,2},{2,3},{3,0},{64,67},{65,64},{66,65},{67,66},{4,5},{5,6... | collective-permute-start | bytes 786440 | tf_op jit(solution)/shard_map/ppermute | solution.py:25
  75.2 0.7 copy-start.17
  81.5 4.3 %copy-start.4 = (bf16[4,32,2688]{2,1,0:T(8,128)(2,1)}, bf16[4,32,2688]{2,1,0:T(8,128)(2,1)S(1)}, u32[]{:S(2)}) copy-start(bf16[4,32,2688]{2,1,0:T(8,128)(2,1)S(1)} %all-to-all-done.1.sums_ref.refs_0_) | copy-start | bytes 2064388
  81.5 19.8 %all-to-all-start.2 = ((bf16[4,64,2688]{2,1,0:T(8,128)(2,1)}), bf16[4,64,2688]{2,1,0:T(8,128)(2,1)}, u32[]{:S(2)}, u32[]{:S(2)}) async-start(bf16[4,64,2688]{2,1,0:T(8,128)(2,1)} %shard_map.59), calls=%async_computation.2 | async-start | bytes 2752512 | tf_op jit(solution)/shard_map/all_to_all | solution.py:31
  88.1 21.5 %collective-permute-start.10 = (bf16[448,1024]{1,0:T(8,128)(2,1)}, bf16[448,1024]{1,0:T(8,128)(2,1)S(1)}, u32[]{:S(2)}, u32[]{:S(2)}) collective-permute-start(bf16[448,1024]{1,0:T(8,128)(2,1)} %shard_map.60), channel_id=1, source_target_pairs={{0,4},{4,8},{8,12},{12,0},{64,76},{68,64},{72,68},{76,72},{1,5},{5... | collective-permute-start | bytes 2752520 | tf_op jit(solution)/shard_map/ppermute | solution.py:25
  90.4 0.7 copy-start.18
  91.1 1.3 copy-start.15
  101.3 16.0 %all-to-all-start.5 = ((bf16[4,32,3584]{2,1,0:T(8,128)(2,1)}), bf16[4,32,3584]{2,1,0:T(8,128)(2,1)}, u32[]{:S(2)}, u32[]{:S(2)}) async-start(bf16[4,32,3584]{2,1,0:T(8,128)(2,1)} %get-tuple-element.16), calls=%async_computation.5 | async-start | bytes 1835008 | tf_op jit(solution)/shard_map/all_to_all | solution.py:31
  105.6 28.0 %collective-permute-start.11 = (bf16[448,1024]{1,0:T(8,128)(2,1)}, bf16[448,1024]{1,0:T(8,128)(2,1)S(1)}, u32[]{:S(2)}, u32[]{:S(2)}) collective-permute-start(bf16[448,1024]{1,0:T(8,128)(2,1)} %shard_map.60), channel_id=1, source_target_pairs={{0,12},{4,0},{8,4},{12,8},{64,68},{68,72},{72,76},{76,64},{1,13},{... | collective-permute-start | bytes 2752520 | tf_op jit(solution)/shard_map/ppermute | solution.py:25
  109.6 2.5 %copy-start.2 = (bf16[448,1024]{1,0:T(8,128)(2,1)}, bf16[448,1024]{1,0:T(8,128)(2,1)S(1)}, u32[]{:S(2)}) copy-start(bf16[448,1024]{1,0:T(8,128)(2,1)S(1)} %collective-permute-done.10.refs_0_.refs_2_.refs_5_) | copy-start | bytes 2752516
  109.6 24.0 %collective-permute-start.12 = (bf16[448,1024]{1,0:T(8,128)(2,1)S(1)}, bf16[448,1024]{1,0:T(8,128)(2,1)S(1)}, u32[]{:S(2)}, u32[]{:S(2)}) collective-permute-start(bf16[448,1024]{1,0:T(8,128)(2,1)S(1)} %collective-permute-done.10.refs_0_.refs_2_.refs_5_), channel_id=1, source_target_pairs={{0,4},{4,8},{8,12},{12,0},{64,76},{68,64},{72,68},{76,72},{1,5},{5... | collective-permute-start | bytes 2752520 | tf_op jit(solution)/shard_map/ppermute | solution.py:25
  117.3 16.3 %all-to-all-start = ((bf16[4,32,2688]{2,1,0:T(8,128)(2,1)}), bf16[4,32,2688]{2,1,0:T(8,128)(2,1)S(1)}, u32[]{:S(2)}, u32[]{:S(2)}) async-start(bf16[4,32,2688]{2,1,0:T(8,128)(2,1)} %get-tuple-element.13), calls=%async_computation | async-start | bytes 1376256 | tf_op jit(solution)/shard_map/all_to_all | solution.py:31
  122.8 18.7 %collective-permute-start.13 = (bf16[32,1792]{1,0:T(8,128)(2,1)}, bf16[32,1792]{1,0:T(8,128)(2,1)S(1)}, u32[]{:S(2)}, u32[]{:S(2)}) collective-permute-start(bf16[32,1792]{1,0:T(8,128)(2,1)} %shard_map.66.refs_0_), channel_id=1, source_target_pairs={{0,16},{16,32},{32,48},{48,0},{1,17},{17,33},{33,49},{49,1},{2,18}... | collective-permute-start | bytes 344072 | tf_op jit(solution)/shard_map/ppermute | solution.py:20
  126.2 15.4 %collective-permute-start.14 = (bf16[32,1792]{1,0:T(8,128)(2,1)}, bf16[32,1792]{1,0:T(8,128)(2,1)}, u32[]{:S(2)}, u32[]{:S(2)}) collective-permute-start(bf16[32,1792]{1,0:T(8,128)(2,1)} %shard_map.66.refs_0_), channel_id=1, source_target_pairs={{0,32},{16,48},{32,0},{48,16},{1,33},{17,49},{33,1},{49,17},{2,34}... | collective-permute-start | bytes 344072 | tf_op jit(solution)/shard_map/ppermute | solution.py:20
  130.5 11.1 %collective-permute-start.15 = (bf16[32,1792]{1,0:T(8,128)(2,1)}, bf16[32,1792]{1,0:T(8,128)(2,1)}, u32[]{:S(2)}, u32[]{:S(2)}) collective-permute-start(bf16[32,1792]{1,0:T(8,128)(2,1)} %shard_map.66.refs_0_), channel_id=1, source_target_pairs={{0,48},{16,0},{32,16},{48,32},{1,49},{17,1},{33,17},{49,33},{2,50}... | collective-permute-start | bytes 344072 | tf_op jit(solution)/shard_map/ppermute | solution.py:20
  133.6 1.0 copy-start
  133.6 1.2 copy-start.3
  134.8 0.9 copy-start.1
  138.0 17.6 %all-to-all-start.3 = ((bf16[4,64,1792]{2,1,0:T(8,128)(2,1)}), bf16[4,64,1792]{2,1,0:T(8,128)(2,1)S(1)}, u32[]{:S(2)}, u32[]{:S(2)}) async-start(bf16[4,64,1792]{2,1,0:T(8,128)(2,1)} %shard_map.62), calls=%async_computation.3 | async-start | bytes 1835008 | tf_op jit(solution)/shard_map/all_to_all | solution.py:31
  141.6 0.6 copy-start.20
  142.2 11.0 %copy-start.12 = (s32[8,2]{0,1:T(2,128)S(1)}, s32[8,2]{0,1:T(2,128)}, u32[]{:S(2)}) copy-start(s32[8,2]{0,1:T(2,128)} %param.6) | copy-start | bytes 196
  142.2 11.0 %copy-start.13 = (f32[8,2]{0,1:T(2,128)S(1)}, f32[8,2]{0,1:T(2,128)}, u32[]{:S(2)}) copy-start(f32[8,2]{0,1:T(2,128)} %param.7) | copy-start | bytes 196
  145.6 23.3 %collective-permute-start.16 = (bf16[128,1024]{1,0:T(8,128)(2,1)}, bf16[128,1024]{1,0:T(8,128)(2,1)S(1)}, u32[]{:S(2)}, u32[]{:S(2)}) collective-permute-start(bf16[128,1024]{1,0:T(8,128)(2,1)} %shard_map.67), channel_id=1, source_target_pairs={{0,1},{1,2},{2,3},{3,0},{64,67},{65,64},{66,65},{67,66},{4,5},{5,6... | collective-permute-start | bytes 786440 | tf_op jit(solution)/shard_map/ppermute | solution.py:25
  155.7 0.9 copy-start.5
  160.9 24.6 %collective-permute-start.18 = (bf16[128,1024]{1,0:T(8,128)(2,1)}, bf16[128,1024]{1,0:T(8,128)(2,1)S(1)}, u32[]{:S(2)}, u32[]{:S(2)}) collective-permute-start(bf16[128,1024]{1,0:T(8,128)(2,1)} %get-tuple-element.14.refs_0_), channel_id=1, source_target_pairs={{0,3},{1,0},{2,1},{3,2},{64,65},{65,66},{66,67},{67,64},{4,7},{5,4... | collective-permute-start | bytes 786440 | tf_op jit(solution)/shard_map/ppermute | solution.py:25
  164.9 16.3 %all-to-all-start.4 = ((bf16[4,32,1792]{2,1,0:T(8,128)(2,1)}), bf16[4,32,1792]{2,1,0:T(8,128)(2,1)S(1)}, u32[]{:S(2)}, u32[]{:S(2)}) async-start(bf16[4,32,1792]{2,1,0:T(8,128)(2,1)} %shard_map.64), calls=%async_computation.4 | async-start | bytes 917504 | tf_op jit(solution)/shard_map/all_to_all | solution.py:31
  168.8 0.7 copy-start.19
  169.5 10.9 %copy-start.9 = (pred[8]{0:T(512)(128)(4,1)S(1)}, pred[8]{0:T(512)(128)(4,1)}, u32[]{:S(2)}) copy-start(pred[8]{0:T(512)(128)(4,1)} %copy-done.8) | copy-start | bytes 28
  169.5 10.9 %copy-start.11 = (pred[8]{0:T(512)(128)(4,1)S(1)}, pred[8]{0:T(512)(128)(4,1)}, u32[]{:S(2)}) copy-start(pred[8]{0:T(512)(128)(4,1)} %copy-done.10) | copy-start | bytes 28
  171.4 18.8 %collective-permute-start.17 = (bf16[128,1024]{1,0:T(8,128)(2,1)}, bf16[128,1024]{1,0:T(8,128)(2,1)S(1)}, u32[]{:S(2)}, u32[]{:S(2)}) collective-permute-start(bf16[128,1024]{1,0:T(8,128)(2,1)} %shard_map.68), channel_id=1, source_target_pairs={{0,1},{1,2},{2,3},{3,0},{64,67},{65,64},{66,65},{67,66},{4,5},{5,6... | collective-permute-start | bytes 786440 | tf_op jit(solution)/shard_map/ppermute | solution.py:25
  181.2 0.8 copy-start.6
  192.9 3.8 %collective-permute-start.19 = (bf16[4,64,1024]{2,1,0:T(8,128)(2,1)S(1)}, bf16[4,64,1024]{2,1,0:T(8,128)(2,1)S(1)}, u32[]{:S(2)}, u32[]{:S(2)}) collective-permute-start(bf16[4,64,1024]{2,1,0:T(8,128)(2,1)S(1)} %add_convert_fusion.1), channel_id=1, source_target_pairs={{0,64},{64,0},{1,65},{65,1},{2,66},{66,2},{3,67},{67,3},{4,68},{68... | collective-permute-start | bytes 1572872 | tf_op jit(solution)/shard_map/ppermute | solution.py:20

commit v14 on v12

--- a/solution.py
+++ b/solution.py
@@ -260,6 +260,29 @@
     )(a, b)
 
 
+def finish(own, ahead, back, scales, places):
+    def kernel(scale_ref, place_ref, own_ref, ahead_ref, back_ref, scaled_ref, theirs_ref):
+        sums = own_ref[...] + ahead_ref[...].astype(wide) + back_ref[...].astype(wide)
+        slots = [scale_ref[k] * sums[64 * k : 64 * k + 64] for k in range(2)]
+        for k in range(2):
+            scaled_ref[64 * k : 64 * k + 64, :] = slots[k]
+        for z in range(4):
+            picked = [jnp.where(place_ref[k] == z, slots[k], 0.0) for k in range(2)]
+            theirs_ref[z] = (picked[0] + picked[1]).astype(half)
+
+    scalars = pl.BlockSpec(memory_space=pltpu.SMEM)
+    block = pl.BlockSpec((128, 1024), lambda i: (0, 0))
+    return pl.pallas_call(
+        kernel,
+        grid=(1,),
+        in_specs=[scalars] * 2 + [block] * 3,
+        out_specs=[block, pl.BlockSpec((4, 64, 1024), lambda i: (0, 0, 0))],
+        out_shape=[jax.ShapeDtypeStruct((128, 1024), wide), jax.ShapeDtypeStruct((4, 64, 1024), half)],
+        compiler_params=pltpu.CompilerParams(vmem_limit_bytes=LIMIT),
+        cost_estimate=COST,
+    )(scales, places, own, ahead, back)
+
+
 def on_device(tokens, routes, route_gates, w_in, w_down):
     core = lax.axis_index("core")
     zlo = lax.axis_index("zlo")
@@ -328,19 +351,15 @@
 
     own_h = activate_rest(rest, own_h, 2, [first_out])
     (own_out,) = down(swap(own_h, "x"), v_all, (wide,))
-    result = (own_out + ahead.astype(wide) + back.astype(wide)).reshape(2, 64, 1024)
-
+    places = jnp.stack([jnp.where(side[k] == core, -1, owner[k]) for k in range(2)])
+    scaled, theirs = finish(own_out, ahead, back, jnp.stack(scales), places)
+
+    got = shift(theirs, "core", 1)
     ids = jnp.arange(4, dtype=jnp.int32)[:, None, None]
-
-    def toward(parity):
-        return sum(
-            jnp.where((owner[k] == ids) & (side[k] == parity), scales[k] * result[k][None], 0.0)
-            for k in range(2)
-        )
-
-    got = shift(toward(1 - core).astype(half), "core", 1)
-    going = (toward(core) + got.astype(wide)).astype(half)
-    return jnp.sum(swap(going, "zlo").astype(wide), axis=0, keepdims=True).astype(half)
+    going = got.astype(wide)
+    for k in range(2):
+        going += jnp.where((owner[k] == ids) & (side[k] == core), scaled[None, 64 * k : 64 * k + 64], 0.0)
+    return jnp.sum(swap(going.astype(half), "zlo").astype(wide), axis=0, keepdims=True).astype(half)
 
 
 def solution(mesh):

time: 225 us -> 227 us (level)
  waiting for transfers between devices: 17 us -> 12.6 us
  local copies, waits for them, and re-layouts: 8.71 us -> 11.2 us
  Pallas kernels: 45.7 us -> 48 us
    ppermute x12, waiting for transfers between devices: 9.82 us -> 4.62 us  [pass_on(): lax.ppermute(a, ('core', axis), [(c * n + i, c * n + (i + by * (1 - 2 * c...]
    ppermute x8, starting transfers between devices: 29 us -> 31.6 us  [shift(): return lax.ppermute(a, axis, [(i, (i + by) % n) for i in range(n)])]
    another operation x0 -> x2, other arithmetic: none -> 2.57 us  [the longest x1 1.99 us: on_device(): scaled, theirs = finish(own_out, ahead, back, jnp.stack(scales), places)]
    unnamed x42 -> x46, local copies, waits for them, and re-layouts: 8.52 us -> 9.94 us
  transfers between devices with their start and end apart: 26 -> 26, of which waited for: 8 -> 6; matrix products, arithmetic and copies ran while one was open for 3% -> 5% of each run, Pallas kernels for 21% -> 20%
where the time goes in v14:
time: 227 us; the launch traced here: 224 us
  starting transfers between devices  111 us (49%)
  Pallas kernels  48 us (21%)
  blocking collectives  25.1 us (11%)
  waiting for transfers between devices  12.6 us (6%)
  local copies, waits for them, and re-layouts  11.2 us (5%)
  other arithmetic  9.98 us (4%)
  between operations  5.67 us (2%)
    ppermute x12, starting transfers between devices, pass_on(): lax.ppermute(a, ('core', axis), [(c * n + i, c * n + (i + by * (1 - 2 * c...  56.5 us
    ppermute x8, starting transfers between devices, shift(): return lax.ppermute(a, axis, [(i, (i + by) % n) for i in range(n)])  31.6 us
    all_to_all x1, blocking collectives, swap(): return lax.all_to_all(a, axis, split_axis=0, concat_axis=0, tiled=True)  25.1 us
    all_to_all x6, starting transfers between devices, swap(): return lax.all_to_all(a, axis, split_axis=0, concat_axis=0, tiled=True)  23 us
    pallas_call x2, Pallas kernels, early(): pl.pallas_call(kernel, in_specs=[WHOLE] * n + [ANY] * (3 + len(after)), o...  11.1 us
    unnamed x46, local copies, waits for them, and re-layouts  9.94 us
    pallas_call x1, Pallas kernels, late(): pl.pallas_call(kernel, in_specs=[WHOLE] * 4 + [ANY] * 4, out_specs=[ANY]...  7.56 us
    pallas_call x2, Pallas kernels, down(): pl.pallas_call(kernel, grid=(2,), in_specs=[pl.BlockSpec((4, 32 * n, 1792...  7.52 us
  transfers between devices with their start and end apart: 26, of which 6 were waited for; matrix products, arithmetic and copies ran while one was open for 5% of the time, Pallas kernels for 20%

profile of v14, /device:TPU:1, one launch (start us, length us, event | category | flops | bytes accessed | tf_op | source)
XLA Modules:
  0.0 223.8 jit_solution(15887234525995455616)
XLA Ops:
  0.0 5.5 %collective-permute-start.5 = (bf16[896,1024]{1,0:T(8,128)(2,1)}, bf16[896,1024]{1,0:T(8,128)(2,1)S(1)}, u32[]{:S(2)}, u32[]{:S(2)}) collective-permute-start(bf16[896,1024]{1,0:T(8,128)(2,1)} %bitcast.24), channel_id=1, source_target_pairs={{0,4},{4,8},{8,12},{12,0},{64,76},{68,64},{72,68},{76,72},{1,5},{5... | collective-permute-start | bytes 5505032 | tf_op jit(solution)/shard_map/ppermute | solution.py:25
  5.5 1.9 collective-permute-start.6
  7.4 4.9 %collective-permute-start.1 = (bf16[64,1024]{1,0:T(8,128)(2,1)}, bf16[64,1024]{1,0:T(8,128)(2,1)S(1)}, u32[]{:S(2)}, u32[]{:S(2)}) collective-permute-start(bf16[64,1024]{1,0:T(8,128)(2,1)} %bitcast.21), channel_id=1, source_target_pairs={{0,256},{128,384},{256,0},{384,128},{1,257},{129,385},{257,1},{385... | collective-permute-start | bytes 393224 | tf_op jit(solution)/shard_map/ppermute | solution.py:20
  12.3 3.3 %collective-permute-start.2 = (bf16[64,1024]{1,0:T(8,128)(2,1)}, bf16[64,1024]{1,0:T(8,128)(2,1)S(1)}, u32[]{:S(2)}, u32[]{:S(2)}) collective-permute-start(bf16[64,1024]{1,0:T(8,128)(2,1)} %bitcast.22), channel_id=1, source_target_pairs={{0,384},{128,0},{256,128},{384,256},{1,385},{129,1},{257,129},{385... | collective-permute-start | bytes 393224 | tf_op jit(solution)/shard_map/ppermute | solution.py:20
  15.6 2.2 collective-permute-start
  20.9 2.6 %collective-permute-done = bf16[64,1024]{1,0:T(8,128)(2,1)S(1)} collective-permute-done((bf16[64,1024]{1,0:T(8,128)(2,1)}, bf16[64,1024]{1,0:T(8,128)(2,1)S(1)}, u32[]{:S(2)}, u32[]{:S(2)}) %collective-permute-start) | collective-permute-done | bytes 131104 | tf_op jit(solution)/shard_map/ppermute | solution.py:20
  24.5 5.6 %collective-permute-start.3 = (bf16[128,1024]{1,0:T(8,128)(2,1)S(1)}, bf16[128,1024]{1,0:T(8,128)(2,1)S(1)}, u32[]{:S(2)}, u32[]{:S(2)}) collective-permute-start(bf16[128,1024]{1,0:T(8,128)(2,1)S(1)} %pad_maximum_fusion), channel_id=1, source_target_pairs={{0,64},{64,0},{1,65},{65,1},{2,66},{66,2},{3,67},{67,3},{4,68},{68... | collective-permute-start | bytes 786440 | tf_op jit(solution)/shard_map/ppermute | solution.py:20
  34.4 10.0 %collective-permute-start.4 = (bf16[128,1024]{1,0:T(8,128)(2,1)S(1)}, bf16[128,1024]{1,0:T(8,128)(2,1)S(1)}, u32[]{:S(2)}, u32[]{:S(2)}) collective-permute-start(bf16[128,1024]{1,0:T(8,128)(2,1)S(1)} %pad_maximum_fusion.1.refs_0_.refs_3_), channel_id=1, source_target_pairs={{0,1},{1,2},{2,3},{3,0},{64,67},{65,64},{66,65},{67,66},{4,5},{5,6... | collective-permute-start | bytes 786440 | tf_op jit(solution)/shard_map/ppermute | solution.py:25
  44.4 1.9 collective-permute-start.8
  46.3 2.6 %collective-permute-done.6.refs_3_.refs_6_.refs_4_ = bf16[896,1024]{1,0:T(8,128)(2,1)} collective-permute-done((bf16[896,1024]{1,0:T(8,128)(2,1)}, bf16[896,1024]{1,0:T(8,128)(2,1)}, u32[]{:S(2)}, u32[]{:S(2)}) %collective-permute-start.6) | collective-permute-done | bytes 1835040 | tf_op jit(solution)/shard_map/ppermute | solution.py:25
  48.9 5.4 %shard_map.55 = (bf16[896,1024]{1,0:T(8,128)(2,1)}, bf16[4,32,2688]{2,1,0:T(8,128)(2,1)}) custom-call(bf16[128,1024]{1,0:T(8,128)(2,1)} %copy-done.9, bf16[896,1024]{1,0:T(8,128)(2,1)} %bitcast.26, bf16[896,1024]{1,0:T(8,128)(2,1)} %copy-done.16, bf16[896,1024]{1,0:T(8,128)(2,1)} %collective-permute-done.6.refs_3_.refs_6_.refs_4_), custom_call_target="tpu_custom_call" | custom-call | flops 99999997952 | bytes 1024 | tf_op jit(solution)/shard_map/pallas_call | solution.py:81
  54.4 2.4 %collective-permute-start.9 = (bf16[896,1024]{1,0:T(8,128)(2,1)}, bf16[896,1024]{1,0:T(8,128)(2,1)S(1)}, u32[]{:S(2)}, u32[]{:S(2)}) collective-permute-start(bf16[896,1024]{1,0:T(8,128)(2,1)} %get-tuple-element.14), channel_id=1, source_target_pairs={{0,4},{4,8},{8,12},{12,0},{64,76},{68,64},{72,68},{76,72},{1,5},{5... | collective-permute-start | bytes 5505032 | tf_op jit(solution)/shard_map/ppermute | solution.py:25
  56.8 4.0 %all-to-all-start.1 = ((bf16[4,32,2688]{2,1,0:T(8,128)(2,1)}), bf16[4,32,2688]{2,1,0:T(8,128)(2,1)S(1)}, u32[]{:S(2)}, u32[]{:S(2)}) async-start(bf16[4,32,2688]{2,1,0:T(8,128)(2,1)} %get-tuple-element.13.refs_0_.refs_5_), calls=%async_computation.1 | async-start | bytes 1376256 | tf_op jit(solution)/shard_map/all_to_all | solution.py:31
  60.8 2.0 collective-permute-done.4.a_ref.refs_1_.refs_0_
  63.5 1.7 shard_map.56
  65.2 10.0 %collective-permute-start.7 = (bf16[128,1024]{1,0:T(8,128)(2,1)}, bf16[128,1024]{1,0:T(8,128)(2,1)S(1)}, u32[]{:S(2)}, u32[]{:S(2)}) collective-permute-start(bf16[128,1024]{1,0:T(8,128)(2,1)} %shard_map.56), channel_id=1, source_target_pairs={{0,1},{1,2},{2,3},{3,0},{64,67},{65,64},{66,65},{67,66},{4,5},{5,6... | collective-permute-start | bytes 786440 | tf_op jit(solution)/shard_map/ppermute | solution.py:25
  75.9 5.6 %shard_map.59 = bf16[4,64,2688]{2,1,0:T(8,128)(2,1)} custom-call(bf16[128,1024]{1,0:T(8,128)(2,1)} %copy-done.18, bf16[128,1024]{1,0:T(8,128)(2,1)} %copy-done.19, bf16[896,1024]{1,0:T(8,128)(2,1)} %bitcast.27, bf16[896,1024]{1,0:T(8,128)(2,1)} %copy-done.16, bf16[896,1024]{1,0:T(8,128)(2,1)} %collective-permute-done.6.refs_3_.refs_6_.refs_4_, ...), custom_call_target="tpu_custom_call" | custom-call | flops 10000000000 | bytes 1024 | tf_op jit(solution)/shard_map/pallas_call | solution.py:81
  81.5 4.3 %all-to-all-start.2 = ((bf16[4,64,2688]{2,1,0:T(8,128)(2,1)}), bf16[4,64,2688]{2,1,0:T(8,128)(2,1)}, u32[]{:S(2)}, u32[]{:S(2)}) async-start(bf16[4,64,2688]{2,1,0:T(8,128)(2,1)} %shard_map.59), calls=%async_computation.2 | async-start | bytes 2752512 | tf_op jit(solution)/shard_map/all_to_all | solution.py:31
  85.9 2.2 %shard_map.60 = bf16[448,1024]{1,0:T(8,128)(2,1)} custom-call(bf16[448,1024]{1,0:T(8,128)(2,1)} %bitcast.17, bf16[4,32,2688]{2,1,0:T(8,128)(2,1)} %copy-done.4), custom_call_target="tpu_custom_call" | custom-call | flops 1024 | bytes 1024 | tf_op jit(solution)/shard_map/pallas_call | solution.py:41
  88.1 2.3 %collective-permute-start.10 = (bf16[448,1024]{1,0:T(8,128)(2,1)}, bf16[448,1024]{1,0:T(8,128)(2,1)S(1)}, u32[]{:S(2)}, u32[]{:S(2)}) collective-permute-start(bf16[448,1024]{1,0:T(8,128)(2,1)} %shard_map.60), channel_id=1, source_target_pairs={{0,4},{4,8},{8,12},{12,0},{64,76},{68,64},{72,68},{76,72},{1,5},{5... | collective-permute-start | bytes 2752520 | tf_op jit(solution)/shard_map/ppermute | solution.py:25
  92.4 7.6 %shard_map.57 = (bf16[4,32,3584]{2,1,0:T(8,128)(2,1)}, bf16[4,32,2688]{2,1,0:T(8,128)(2,1)}) custom-call(bf16[128,1024]{1,0:T(8,128)(2,1)} %copy-done.20, bf16[128,1024]{1,0:T(8,128)(2,1)} %copy-done.18, bf16[128,1024]{1,0:T(8,128)(2,1)} %copy-done.19, bf16[128,1024]{1,0:T(8,128)(2,1)} %copy-done.9, bf16[896,1024]{1,0:T(8,128)(2,1)} %bitcast.28, ...), custom_call_target="tpu_custom_call" | custom-call | flops 99999997952 | bytes 1024 | tf_op jit(solution)/shard_map/pallas_call | solution.py:118
  99.9 1.4 all-to-all-done.2.sums_ref
  101.3 4.2 %all-to-all-start.5 = ((bf16[4,32,3584]{2,1,0:T(8,128)(2,1)}), bf16[4,32,3584]{2,1,0:T(8,128)(2,1)}, u32[]{:S(2)}, u32[]{:S(2)}) async-start(bf16[4,32,3584]{2,1,0:T(8,128)(2,1)} %get-tuple-element.18), calls=%async_computation.5 | async-start | bytes 1835008 | tf_op jit(solution)/shard_map/all_to_all | solution.py:31
  105.6 4.0 %collective-permute-start.11 = (bf16[448,1024]{1,0:T(8,128)(2,1)}, bf16[448,1024]{1,0:T(8,128)(2,1)S(1)}, u32[]{:S(2)}, u32[]{:S(2)}) collective-permute-start(bf16[448,1024]{1,0:T(8,128)(2,1)} %shard_map.60), channel_id=1, source_target_pairs={{0,12},{4,0},{8,4},{12,8},{64,68},{68,72},{72,76},{76,64},{1,13},{... | collective-permute-start | bytes 2752520 | tf_op jit(solution)/shard_map/ppermute | solution.py:25
  109.6 2.5 %collective-permute-start.12 = (bf16[448,1024]{1,0:T(8,128)(2,1)S(1)}, bf16[448,1024]{1,0:T(8,128)(2,1)S(1)}, u32[]{:S(2)}, u32[]{:S(2)}) collective-permute-start(bf16[448,1024]{1,0:T(8,128)(2,1)S(1)} %collective-permute-done.10.refs_0_.refs_2_.refs_5_), channel_id=1, source_target_pairs={{0,4},{4,8},{8,12},{12,0},{64,76},{68,64},{72,68},{76,72},{1,5},{5... | collective-permute-start | bytes 2752520 | tf_op jit(solution)/shard_map/ppermute | solution.py:25
  112.1 2.3 %shard_map.61.begun_ref.after_ref = bf16[64,1344]{1,0:T(8,128)(2,1)} custom-call(bf16[4,64,2688]{2,1,0:T(8,128)(2,1)} %all-to-all-done.2.sums_ref, bf16[448,1024]{1,0:T(8,128)(2,1)} %copy-done.2), custom_call_target="tpu_custom_call" | custom-call | flops 1024 | bytes 1024 | tf_op jit(solution)/shard_map/pallas_call | solution.py:152
  114.4 2.9 %all-to-all-done.5.sums_ref = bf16[4,32,3584]{2,1,0:T(8,128)(2,1)} async-done(((bf16[4,32,3584]{2,1,0:T(8,128)(2,1)}), bf16[4,32,3584]{2,1,0:T(8,128)(2,1)}, u32[]{:S(2)}, u32[]{:S(2)}) %all-to-all-start.5) | async-done | bytes 917536 | tf_op jit(solution)/shard_map/all_to_all | solution.py:31
  117.3 3.5 %all-to-all-start = ((bf16[4,32,2688]{2,1,0:T(8,128)(2,1)}), bf16[4,32,2688]{2,1,0:T(8,128)(2,1)S(1)}, u32[]{:S(2)}, u32[]{:S(2)}) async-start(bf16[4,32,2688]{2,1,0:T(8,128)(2,1)} %get-tuple-element.15), calls=%async_computation | async-start | bytes 1376256 | tf_op jit(solution)/shard_map/all_to_all | solution.py:31
  120.8 2.1 shard_map.66.refs_0_
  122.8 3.3 %collective-permute-start.13 = (bf16[32,1792]{1,0:T(8,128)(2,1)}, bf16[32,1792]{1,0:T(8,128)(2,1)S(1)}, u32[]{:S(2)}, u32[]{:S(2)}) collective-permute-start(bf16[32,1792]{1,0:T(8,128)(2,1)} %shard_map.66.refs_0_), channel_id=1, source_target_pairs={{0,16},{16,32},{32,48},{48,0},{1,17},{17,33},{33,49},{49,1},{2,18}... | collective-permute-start | bytes 344072 | tf_op jit(solution)/shard_map/ppermute | solution.py:20
  126.2 4.3 %collective-permute-start.14 = (bf16[32,1792]{1,0:T(8,128)(2,1)}, bf16[32,1792]{1,0:T(8,128)(2,1)}, u32[]{:S(2)}, u32[]{:S(2)}) collective-permute-start(bf16[32,1792]{1,0:T(8,128)(2,1)} %shard_map.66.refs_0_), channel_id=1, source_target_pairs={{0,32},{16,48},{32,0},{48,16},{1,33},{17,49},{33,1},{49,17},{2,34}... | collective-permute-start | bytes 344072 | tf_op jit(solution)/shard_map/ppermute | solution.py:20
  130.5 3.1 %collective-permute-start.15 = (bf16[32,1792]{1,0:T(8,128)(2,1)}, bf16[32,1792]{1,0:T(8,128)(2,1)}, u32[]{:S(2)}, u32[]{:S(2)}) collective-permute-start(bf16[32,1792]{1,0:T(8,128)(2,1)} %shard_map.66.refs_0_), channel_id=1, source_target_pairs={{0,48},{16,0},{32,16},{48,32},{1,49},{17,1},{33,17},{49,33},{2,50}... | collective-permute-start | bytes 344072 | tf_op jit(solution)/shard_map/ppermute | solution.py:20
  135.8 2.2 %shard_map.62 = bf16[4,64,1792]{2,1,0:T(8,128)(2,1)} custom-call(bf16[4,32,2688]{2,1,0:T(8,128)(2,1)} %copy-done.3, bf16[64,1344]{1,0:T(8,128)(2,1)} %shard_map.61.begun_ref.after_ref, bf16[448,1024]{1,0:T(8,128)(2,1)} %copy-done, bf16[448,1024]{1,0:T(8,128)(2,1)} %copy-done.1), custom_call_target="tpu_custom_call" | custom-call | flops 1024 | bytes 1024 | tf_op jit(solution)/shard_map/pallas_call | solution.py:189
  138.0 3.5 %all-to-all-start.3 = ((bf16[4,64,1792]{2,1,0:T(8,128)(2,1)}), bf16[4,64,1792]{2,1,0:T(8,128)(2,1)S(1)}, u32[]{:S(2)}, u32[]{:S(2)}) async-start(bf16[4,64,1792]{2,1,0:T(8,128)(2,1)} %shard_map.62), calls=%async_computation.3 | async-start | bytes 1835008 | tf_op jit(solution)/shard_map/all_to_all | solution.py:31
  142.2 3.3 %shard_map.67 = bf16[128,1024]{1,0:T(8,128)(2,1)} custom-call(s32[1]{0:T(128)} %bitcast.11.x_ref, bf16[32,1792]{1,0:T(8,128)(2,1)} %shard_map.66.refs_0_, bf16[32,1792]{1,0:T(8,128)(2,1)} %copy-done.22, bf16[32,1792]{1,0:T(8,128)(2,1)} %collective-permute-done.14.refs_2_, bf16[32,1792]{1,0:T(8,128)(2,1)} %collective-permute-done.15.refs_3_, ...), custom_call_target="tpu_custom_call" | custom-call | flops 99999997952 | bytes 1024 | tf_op jit(solution)/shard_map/pallas_call | solution.py:236
  145.4 6.9 %collective-permute-start.16 = (bf16[128,1024]{1,0:T(8,128)(2,1)}, bf16[128,1024]{1,0:T(8,128)(2,1)S(1)}, u32[]{:S(2)}, u32[]{:S(2)}) collective-permute-start(bf16[128,1024]{1,0:T(8,128)(2,1)} %shard_map.67), channel_id=1, source_target_pairs={{0,1},{1,2},{2,3},{3,0},{64,67},{65,64},{66,65},{67,66},{4,5},{5,6... | collective-permute-start | bytes 786440 | tf_op jit(solution)/shard_map/ppermute | solution.py:25
  152.7 1.9 shard_map.58.begun_ref
  156.6 4.1 %shard_map.63 = (bf16[128,1024]{1,0:T(8,128)(2,1)}, f32[128,1024]{1,0:T(8,128)}) custom-call(bf16[4,64,1792]{2,1,0:T(8,128)(2,1)} %copy-done.5, bf16[448,1024]{1,0:T(8,128)(2,1)} %bitcast.19, bf16[448,1024]{1,0:T(8,128)(2,1)} %copy-done.2, bf16[448,1024]{1,0:T(8,128)(2,1)} %copy-done, bf16[448,1024]{1,0:T(8,128)(2,1)} %copy-done.1), custom_call_target="tpu_custom_call" | custom-call | flops 1024 | bytes 1024 | tf_op jit(solution)/shard_map/pallas_call | solution.py:214
  160.7 1.9 collective-permute-start.18
  162.6 2.0 shard_map.64
  164.7 3.5 %all-to-all-start.4 = ((bf16[4,32,1792]{2,1,0:T(8,128)(2,1)}), bf16[4,32,1792]{2,1,0:T(8,128)(2,1)S(1)}, u32[]{:S(2)}, u32[]{:S(2)}) async-start(bf16[4,32,1792]{2,1,0:T(8,128)(2,1)} %shard_map.64), calls=%async_computation.4 | async-start | bytes 917504 | tf_op jit(solution)/shard_map/all_to_all | solution.py:31
  168.8 1.9 shard_map.68
  170.7 7.3 %collective-permute-start.17 = (bf16[128,1024]{1,0:T(8,128)(2,1)}, bf16[128,1024]{1,0:T(8,128)(2,1)S(1)}, u32[]{:S(2)}, u32[]{:S(2)}) collective-permute-start(bf16[128,1024]{1,0:T(8,128)(2,1)} %shard_map.68), channel_id=1, source_target_pairs={{0,1},{1,2},{2,3},{3,0},{64,67},{65,64},{66,65},{67,66},{4,5},{5,6... | collective-permute-start | bytes 786440 | tf_op jit(solution)/shard_map/ppermute | solution.py:25
  179.9 2.0 pad_maximum_fusion.2.scale_ref
  183.3 3.4 %shard_map.65.own_ref = f32[128,1024]{1,0:T(8,128)} custom-call(bf16[4,32,1792]{2,1,0:T(8,128)(2,1)} %copy-done.6, bf16[448,1024]{1,0:T(8,128)(2,1)} %bitcast.20, bf16[448,1024]{1,0:T(8,128)(2,1)} %copy-done.2, bf16[448,1024]{1,0:T(8,128)(2,1)} %copy-done, bf16[448,1024]{1,0:T(8,128)(2,1)} %copy-done.1), custom_call_target="tpu_custom_call" | custom-call | flops 1024 | bytes 1024 | tf_op jit(solution)/shard_map/pallas_call | solution.py:214
  188.1 2.3 %shard_map.69 = (f32[128,1024]{1,0:T(8,128)}, bf16[4,64,1024]{2,1,0:T(8,128)(2,1)}) custom-call(f32[2]{0:T(128)} %pad_maximum_fusion.2.scale_ref, s32[2]{0:T(128)} %pad_add_fusion.place_ref, f32[128,1024]{1,0:T(8,128)} %shard_map.65.own_ref, bf16[128,1024]{1,0:T(8,128)(2,1)} %copy-done.8, bf16[128,1024]{1,0:T(8,128)(2,1)} %copy-done.7), custom_call_target="tpu_custom_call" | custom-call | flops 1024 | bytes 1024 | tf_op jit(solution)/shard_map/pallas_call | solution.py:275
  190.4 4.9 %collective-permute-start.19 = (bf16[4,64,1024]{2,1,0:T(8,128)(2,1)}, bf16[4,64,1024]{2,1,0:T(8,128)(2,1)S(1)}, u32[]{:S(2)}, u32[]{:S(2)}) collective-permute-start(bf16[4,64,1024]{2,1,0:T(8,128)(2,1)} %get-tuple-element.19), channel_id=1, source_target_pairs={{0,64},{64,0},{1,65},{65,1},{2,66},{66,2},{3,67},{67,3},{4,68},{68... | collective-permute-start | bytes 1572872 | tf_op jit(solution)/shard_map/ppermute | solution.py:20
  197.9 25.1 %all_to_all.35 = bf16[4,64,1024]{2,1,0:T(8,128)(2,1)S(1)} all-to-all(bf16[4,64,1024]{2,1,0:T(8,128)(2,1)S(1)} %add_convert_fusion), channel_id=1, replica_groups=mesh['zlo'=4,'core'=2,'x'=4,'y'=4,'zhi'=4] {'zlo'}, dimensions={0} | all-to-all | bytes 1048576 | tf_op jit(solution)/shard_map/all_to_all | solution.py:31
  (87 shorter events, 20.3 us)
Async XLA Ops:
  0.0 46.3 %collective-permute-start.5 = (bf16[896,1024]{1,0:T(8,128)(2,1)}, bf16[896,1024]{1,0:T(8,128)(2,1)S(1)}, u32[]{:S(2)}, u32[]{:S(2)}) collective-permute-start(bf16[896,1024]{1,0:T(8,128)(2,1)} %bitcast.24), channel_id=1, source_target_pairs={{0,4},{4,8},{8,12},{12,0},{64,76},{68,64},{72,68},{76,72},{1,5},{5... | collective-permute-start | bytes 5505032 | tf_op jit(solution)/shard_map/ppermute | solution.py:25
  5.5 43.4 %collective-permute-start.6 = (bf16[896,1024]{1,0:T(8,128)(2,1)}, bf16[896,1024]{1,0:T(8,128)(2,1)}, u32[]{:S(2)}, u32[]{:S(2)}) collective-permute-start(bf16[896,1024]{1,0:T(8,128)(2,1)} %bitcast.25), channel_id=1, source_target_pairs={{0,12},{4,0},{8,4},{12,8},{64,68},{68,72},{72,76},{76,64},{1,13},{... | collective-permute-start | bytes 5505032 | tf_op jit(solution)/shard_map/ppermute | solution.py:25
  7.4 13.5 %collective-permute-start.1 = (bf16[64,1024]{1,0:T(8,128)(2,1)}, bf16[64,1024]{1,0:T(8,128)(2,1)S(1)}, u32[]{:S(2)}, u32[]{:S(2)}) collective-permute-start(bf16[64,1024]{1,0:T(8,128)(2,1)} %bitcast.21), channel_id=1, source_target_pairs={{0,256},{128,384},{256,0},{384,128},{1,257},{129,385},{257,1},{385... | collective-permute-start | bytes 393224 | tf_op jit(solution)/shard_map/ppermute | solution.py:20
  12.3 8.6 %collective-permute-start.2 = (bf16[64,1024]{1,0:T(8,128)(2,1)}, bf16[64,1024]{1,0:T(8,128)(2,1)S(1)}, u32[]{:S(2)}, u32[]{:S(2)}) collective-permute-start(bf16[64,1024]{1,0:T(8,128)(2,1)} %bitcast.22), channel_id=1, source_target_pairs={{0,384},{128,0},{256,128},{384,256},{1,385},{129,1},{257,129},{385... | collective-permute-start | bytes 393224 | tf_op jit(solution)/shard_map/ppermute | solution.py:20
  15.6 7.9 %collective-permute-start = (bf16[64,1024]{1,0:T(8,128)(2,1)}, bf16[64,1024]{1,0:T(8,128)(2,1)S(1)}, u32[]{:S(2)}, u32[]{:S(2)}) collective-permute-start(bf16[64,1024]{1,0:T(8,128)(2,1)} %bitcast.23), channel_id=1, source_target_pairs={{0,128},{128,256},{256,384},{384,0},{1,129},{129,257},{257,385},{3... | collective-permute-start | bytes 393224 | tf_op jit(solution)/shard_map/ppermute | solution.py:20
  18.9 15.4 %copy-start.10 = (pred[8]{0:T(512)(128)(4,1)}, pred[8]{0:T(512)(128)(4,1)S(1)}, u32[]{:S(2)}) copy-start(pred[8]{0:T(512)(128)(4,1)S(1)} %get-tuple-element.25) | copy-start | bytes 28
  18.9 15.4 %copy-start.12 = (pred[8]{0:T(512)(128)(4,1)}, pred[8]{0:T(512)(128)(4,1)S(1)}, u32[]{:S(2)}) copy-start(pred[8]{0:T(512)(128)(4,1)S(1)} %get-tuple-element.26) | copy-start | bytes 28
  24.5 8.9 %collective-permute-start.3 = (bf16[128,1024]{1,0:T(8,128)(2,1)S(1)}, bf16[128,1024]{1,0:T(8,128)(2,1)S(1)}, u32[]{:S(2)}, u32[]{:S(2)}) collective-permute-start(bf16[128,1024]{1,0:T(8,128)(2,1)S(1)} %pad_maximum_fusion), channel_id=1, source_target_pairs={{0,64},{64,0},{1,65},{65,1},{2,66},{66,2},{3,67},{67,3},{4,68},{68... | collective-permute-start | bytes 786440 | tf_op jit(solution)/shard_map/ppermute | solution.py:20
  34.3 14.6 %copy-start.9 = (bf16[128,1024]{1,0:T(8,128)(2,1)}, bf16[128,1024]{1,0:T(8,128)(2,1)S(1)}, u32[]{:S(2)}) copy-start(bf16[128,1024]{1,0:T(8,128)(2,1)S(1)} %pad_maximum_fusion.1.refs_0_.refs_3_) | copy-start | bytes 786436
  34.4 28.5 %collective-permute-start.4 = (bf16[128,1024]{1,0:T(8,128)(2,1)S(1)}, bf16[128,1024]{1,0:T(8,128)(2,1)S(1)}, u32[]{:S(2)}, u32[]{:S(2)}) collective-permute-start(bf16[128,1024]{1,0:T(8,128)(2,1)S(1)} %pad_maximum_fusion.1.refs_0_.refs_3_), channel_id=1, source_target_pairs={{0,1},{1,2},{2,3},{3,0},{64,67},{65,64},{66,65},{67,66},{4,5},{5,6... | collective-permute-start | bytes 786440 | tf_op jit(solution)/shard_map/ppermute | solution.py:25
  44.4 30.8 %collective-permute-start.8 = (bf16[128,1024]{1,0:T(8,128)(2,1)S(1)}, bf16[128,1024]{1,0:T(8,128)(2,1)S(1)}, u32[]{:S(2)}, u32[]{:S(2)}) collective-permute-start(bf16[128,1024]{1,0:T(8,128)(2,1)S(1)} %pad_maximum_fusion.1.refs_0_.refs_3_), channel_id=1, source_target_pairs={{0,3},{1,0},{2,1},{3,2},{64,65},{65,66},{66,67},{67,64},{4,7},{5,4... | collective-permute-start | bytes 786440 | tf_op jit(solution)/shard_map/ppermute | solution.py:25
  46.3 2.6 %copy-start.16 = (bf16[896,1024]{1,0:T(8,128)(2,1)}, bf16[896,1024]{1,0:T(8,128)(2,1)S(1)}, u32[]{:S(2)}) copy-start(bf16[896,1024]{1,0:T(8,128)(2,1)S(1)} %collective-permute-done.5.refs_2_.refs_5_.refs_3_) | copy-start | bytes 5505028
  54.4 36.1 %collective-permute-start.9 = (bf16[896,1024]{1,0:T(8,128)(2,1)}, bf16[896,1024]{1,0:T(8,128)(2,1)S(1)}, u32[]{:S(2)}, u32[]{:S(2)}) collective-permute-start(bf16[896,1024]{1,0:T(8,128)(2,1)} %get-tuple-element.14), channel_id=1, source_target_pairs={{0,4},{4,8},{8,12},{12,0},{64,76},{68,64},{72,68},{76,72},{1,5},{5... | collective-permute-start | bytes 5505032 | tf_op jit(solution)/shard_map/ppermute | solution.py:25
  56.8 24.7 %all-to-all-start.1 = ((bf16[4,32,2688]{2,1,0:T(8,128)(2,1)}), bf16[4,32,2688]{2,1,0:T(8,128)(2,1)S(1)}, u32[]{:S(2)}, u32[]{:S(2)}) async-start(bf16[4,32,2688]{2,1,0:T(8,128)(2,1)} %get-tuple-element.13.refs_0_.refs_5_), calls=%async_computation.1 | async-start | bytes 1376256 | tf_op jit(solution)/shard_map/all_to_all | solution.py:31
  62.8 0.7 copy-start.18
  65.2 25.2 %collective-permute-start.7 = (bf16[128,1024]{1,0:T(8,128)(2,1)}, bf16[128,1024]{1,0:T(8,128)(2,1)S(1)}, u32[]{:S(2)}, u32[]{:S(2)}) collective-permute-start(bf16[128,1024]{1,0:T(8,128)(2,1)} %shard_map.56), channel_id=1, source_target_pairs={{0,1},{1,2},{2,3},{3,0},{64,67},{65,64},{66,65},{67,66},{4,5},{5,6... | collective-permute-start | bytes 786440 | tf_op jit(solution)/shard_map/ppermute | solution.py:25
  75.2 0.7 copy-start.19
  81.5 4.3 %copy-start.4 = (bf16[4,32,2688]{2,1,0:T(8,128)(2,1)}, bf16[4,32,2688]{2,1,0:T(8,128)(2,1)S(1)}, u32[]{:S(2)}) copy-start(bf16[4,32,2688]{2,1,0:T(8,128)(2,1)S(1)} %all-to-all-done.1.sums_ref.refs_0_) | copy-start | bytes 2064388
  81.5 19.8 %all-to-all-start.2 = ((bf16[4,64,2688]{2,1,0:T(8,128)(2,1)}), bf16[4,64,2688]{2,1,0:T(8,128)(2,1)}, u32[]{:S(2)}, u32[]{:S(2)}) async-start(bf16[4,64,2688]{2,1,0:T(8,128)(2,1)} %shard_map.59), calls=%async_computation.2 | async-start | bytes 2752512 | tf_op jit(solution)/shard_map/all_to_all | solution.py:31
  88.1 21.4 %collective-permute-start.10 = (bf16[448,1024]{1,0:T(8,128)(2,1)}, bf16[448,1024]{1,0:T(8,128)(2,1)S(1)}, u32[]{:S(2)}, u32[]{:S(2)}) collective-permute-start(bf16[448,1024]{1,0:T(8,128)(2,1)} %shard_map.60), channel_id=1, source_target_pairs={{0,4},{4,8},{8,12},{12,0},{64,76},{68,64},{72,68},{76,72},{1,5},{5... | collective-permute-start | bytes 2752520 | tf_op jit(solution)/shard_map/ppermute | solution.py:25
  90.4 0.7 copy-start.20
  91.1 1.3 copy-start.17
  101.3 16.0 %all-to-all-start.5 = ((bf16[4,32,3584]{2,1,0:T(8,128)(2,1)}), bf16[4,32,3584]{2,1,0:T(8,128)(2,1)}, u32[]{:S(2)}, u32[]{:S(2)}) async-start(bf16[4,32,3584]{2,1,0:T(8,128)(2,1)} %get-tuple-element.18), calls=%async_computation.5 | async-start | bytes 1835008 | tf_op jit(solution)/shard_map/all_to_all | solution.py:31
  105.6 28.0 %collective-permute-start.11 = (bf16[448,1024]{1,0:T(8,128)(2,1)}, bf16[448,1024]{1,0:T(8,128)(2,1)S(1)}, u32[]{:S(2)}, u32[]{:S(2)}) collective-permute-start(bf16[448,1024]{1,0:T(8,128)(2,1)} %shard_map.60), channel_id=1, source_target_pairs={{0,12},{4,0},{8,4},{12,8},{64,68},{68,72},{72,76},{76,64},{1,13},{... | collective-permute-start | bytes 2752520 | tf_op jit(solution)/shard_map/ppermute | solution.py:25
  109.6 2.5 %copy-start.2 = (bf16[448,1024]{1,0:T(8,128)(2,1)}, bf16[448,1024]{1,0:T(8,128)(2,1)S(1)}, u32[]{:S(2)}) copy-start(bf16[448,1024]{1,0:T(8,128)(2,1)S(1)} %collective-permute-done.10.refs_0_.refs_2_.refs_5_) | copy-start | bytes 2752516
  109.6 24.1 %collective-permute-start.12 = (bf16[448,1024]{1,0:T(8,128)(2,1)S(1)}, bf16[448,1024]{1,0:T(8,128)(2,1)S(1)}, u32[]{:S(2)}, u32[]{:S(2)}) collective-permute-start(bf16[448,1024]{1,0:T(8,128)(2,1)S(1)} %collective-permute-done.10.refs_0_.refs_2_.refs_5_), channel_id=1, source_target_pairs={{0,4},{4,8},{8,12},{12,0},{64,76},{68,64},{72,68},{76,72},{1,5},{5... | collective-permute-start | bytes 2752520 | tf_op jit(solution)/shard_map/ppermute | solution.py:25
  117.3 16.3 %all-to-all-start = ((bf16[4,32,2688]{2,1,0:T(8,128)(2,1)}), bf16[4,32,2688]{2,1,0:T(8,128)(2,1)S(1)}, u32[]{:S(2)}, u32[]{:S(2)}) async-start(bf16[4,32,2688]{2,1,0:T(8,128)(2,1)} %get-tuple-element.15), calls=%async_computation | async-start | bytes 1376256 | tf_op jit(solution)/shard_map/all_to_all | solution.py:31
  122.8 18.7 %collective-permute-start.13 = (bf16[32,1792]{1,0:T(8,128)(2,1)}, bf16[32,1792]{1,0:T(8,128)(2,1)S(1)}, u32[]{:S(2)}, u32[]{:S(2)}) collective-permute-start(bf16[32,1792]{1,0:T(8,128)(2,1)} %shard_map.66.refs_0_), channel_id=1, source_target_pairs={{0,16},{16,32},{32,48},{48,0},{1,17},{17,33},{33,49},{49,1},{2,18}... | collective-permute-start | bytes 344072 | tf_op jit(solution)/shard_map/ppermute | solution.py:20
  126.2 15.4 %collective-permute-start.14 = (bf16[32,1792]{1,0:T(8,128)(2,1)}, bf16[32,1792]{1,0:T(8,128)(2,1)}, u32[]{:S(2)}, u32[]{:S(2)}) collective-permute-start(bf16[32,1792]{1,0:T(8,128)(2,1)} %shard_map.66.refs_0_), channel_id=1, source_target_pairs={{0,32},{16,48},{32,0},{48,16},{1,33},{17,49},{33,1},{49,17},{2,34}... | collective-permute-start | bytes 344072 | tf_op jit(solution)/shard_map/ppermute | solution.py:20
  130.5 11.1 %collective-permute-start.15 = (bf16[32,1792]{1,0:T(8,128)(2,1)}, bf16[32,1792]{1,0:T(8,128)(2,1)}, u32[]{:S(2)}, u32[]{:S(2)}) collective-permute-start(bf16[32,1792]{1,0:T(8,128)(2,1)} %shard_map.66.refs_0_), channel_id=1, source_target_pairs={{0,48},{16,0},{32,16},{48,32},{1,49},{17,1},{33,17},{49,33},{2,50}... | collective-permute-start | bytes 344072 | tf_op jit(solution)/shard_map/ppermute | solution.py:20
  133.6 1.0 copy-start
  133.6 1.2 copy-start.3
  134.8 0.9 copy-start.1
  138.0 17.7 %all-to-all-start.3 = ((bf16[4,64,1792]{2,1,0:T(8,128)(2,1)}), bf16[4,64,1792]{2,1,0:T(8,128)(2,1)S(1)}, u32[]{:S(2)}, u32[]{:S(2)}) async-start(bf16[4,64,1792]{2,1,0:T(8,128)(2,1)} %shard_map.62), calls=%async_computation.3 | async-start | bytes 1835008 | tf_op jit(solution)/shard_map/all_to_all | solution.py:31
  142.2 10.2 %copy-start.14 = (s32[8,2]{0,1:T(2,128)S(1)}, s32[8,2]{0,1:T(2,128)}, u32[]{:S(2)}) copy-start(s32[8,2]{0,1:T(2,128)} %param.6) | copy-start | bytes 196
  142.2 10.2 %copy-start.15 = (f32[8,2]{0,1:T(2,128)S(1)}, f32[8,2]{0,1:T(2,128)}, u32[]{:S(2)}) copy-start(f32[8,2]{0,1:T(2,128)} %param.7) | copy-start | bytes 196
  145.4 22.7 %collective-permute-start.16 = (bf16[128,1024]{1,0:T(8,128)(2,1)}, bf16[128,1024]{1,0:T(8,128)(2,1)S(1)}, u32[]{:S(2)}, u32[]{:S(2)}) collective-permute-start(bf16[128,1024]{1,0:T(8,128)(2,1)} %shard_map.67), channel_id=1, source_target_pairs={{0,1},{1,2},{2,3},{3,0},{64,67},{65,64},{66,65},{67,66},{4,5},{5,6... | collective-permute-start | bytes 786440 | tf_op jit(solution)/shard_map/ppermute | solution.py:25
  155.7 0.9 copy-start.5
  160.7 26.0 %collective-permute-start.18 = (bf16[128,1024]{1,0:T(8,128)(2,1)}, bf16[128,1024]{1,0:T(8,128)(2,1)S(1)}, u32[]{:S(2)}, u32[]{:S(2)}) collective-permute-start(bf16[128,1024]{1,0:T(8,128)(2,1)} %get-tuple-element.16.refs_0_), channel_id=1, source_target_pairs={{0,3},{1,0},{2,1},{3,2},{64,65},{65,66},{66,67},{67,64},{4,7},{5,4... | collective-permute-start | bytes 786440 | tf_op jit(solution)/shard_map/ppermute | solution.py:25
  164.7 17.8 %all-to-all-start.4 = ((bf16[4,32,1792]{2,1,0:T(8,128)(2,1)}), bf16[4,32,1792]{2,1,0:T(8,128)(2,1)S(1)}, u32[]{:S(2)}, u32[]{:S(2)}) async-start(bf16[4,32,1792]{2,1,0:T(8,128)(2,1)} %shard_map.64), calls=%async_computation.4 | async-start | bytes 917504 | tf_op jit(solution)/shard_map/all_to_all | solution.py:31
  168.1 0.7 copy-start.21
  168.8 9.1 %copy-start.11 = (pred[8]{0:T(512)(128)(4,1)S(1)}, pred[8]{0:T(512)(128)(4,1)}, u32[]{:S(2)}) copy-start(pred[8]{0:T(512)(128)(4,1)} %copy-done.10) | copy-start | bytes 28
  168.8 9.1 %copy-start.13 = (pred[8]{0:T(512)(128)(4,1)S(1)}, pred[8]{0:T(512)(128)(4,1)}, u32[]{:S(2)}) copy-start(pred[8]{0:T(512)(128)(4,1)} %copy-done.12) | copy-start | bytes 28
  170.7 16.0 %collective-permute-start.17 = (bf16[128,1024]{1,0:T(8,128)(2,1)}, bf16[128,1024]{1,0:T(8,128)(2,1)S(1)}, u32[]{:S(2)}, u32[]{:S(2)}) collective-permute-start(bf16[128,1024]{1,0:T(8,128)(2,1)} %shard_map.68), channel_id=1, source_target_pairs={{0,1},{1,2},{2,3},{3,0},{64,67},{65,64},{66,65},{67,66},{4,5},{5,6... | collective-permute-start | bytes 786440 | tf_op jit(solution)/shard_map/ppermute | solution.py:25
  182.5 0.8 copy-start.6
  186.7 0.7 copy-start.8
  187.4 0.7 copy-start.7
  190.4 7.3 %collective-permute-start.19 = (bf16[4,64,1024]{2,1,0:T(8,128)(2,1)}, bf16[4,64,1024]{2,1,0:T(8,128)(2,1)S(1)}, u32[]{:S(2)}, u32[]{:S(2)}) collective-permute-start(bf16[4,64,1024]{2,1,0:T(8,128)(2,1)} %get-tuple-element.19), channel_id=1, source_target_pairs={{0,64},{64,0},{1,65},{65,1},{2,66},{66,2},{3,67},{67,3},{4,68},{68... | collective-permute-start | bytes 1572872 | tf_op jit(solution)/shard_map/ppermute | solution.py:20
  (1 other events, 0.7 us)
